TPU v7x, 128 devices: a whole 4x4x4 slice. The times are simulated.
128 devices in a mesh: row: 8 (over x, core), col: 16 (over z, y).
Axes of the slice: x: 4, y: 4, z: 4, core: 2. Of those that a mesh axis runs over, the one named last changes fastest.
Arguments:
- kohn_blocks: bfloat16 [512, 16, 4, 4096], P('row', 'col'), may hold values from -0.1875 to 0.1875
- kohn_columns: int32 [512, 16, 4], P('row', 'col'), may hold values from 0 to 63
- density_blocks: bfloat16 [16, 64, 8, 4096], P('col', 'row'), may hold values from -6 to 6
- density_columns: int32 [16, 64, 8], P('col', 'row'), may hold values from 0 to 31, as said below
- owner_map: int32 [16384, 1], P(('row', 'col')), may hold values from 0 to 127; in each aligned block of 128 rows (0 to 127, 128 to 255, ...) at most 2 rows name the same one
Outputs:
- owned_blocks: float32 [32768, 4096], P(('row', 'col'))
Inputs may be any that keep to these rules, and one draw needn't show every extreme that they name: `density_columns`: the 8 window columns of one density block row are distinct. `owner_map`: the gradient blocks of one device's 4 rows name any one owner at most 2 times.
All inputs are finite; a program needn't handle non-finite values.
Results may differ from a plain program's by a relative error of at most 0.0003.
Values may be sent and summed in bfloat16 or wider, within the bound.
No kernel may reach another device: no remote copies, remote signals or barrier semaphores. Data moves between devices by JAX's collectives and lax.ppermute only.
A program may use at most 320 MiB of HBM per device.

v0:
```python
import jax
import jax.numpy as jnp
from jax import lax
from jax.sharding import PartitionSpec as P

B = 64
NCW = 32


def local(kohn_blocks, kohn_columns, density_blocks, density_columns, owner_map):
    panel_blocks, panel_columns = (
        lax.all_gather(density_blocks, "row", axis=1, tiled=True),
        lax.all_gather(density_columns, "row", axis=1, tiled=True),
    )
    panel_blocks = panel_blocks[0]
    panel_columns = panel_columns[0]
    local_blocks = kohn_blocks[:, 0]
    local_columns = kohn_columns[:, 0]
    slots_row = local_blocks.shape[1]
    slots_density = panel_blocks.shape[1]
    share = local_blocks.shape[0] // lax.axis_size("col")
    picked = panel_blocks[local_columns]
    picked_columns = panel_columns[local_columns]
    left = local_blocks.reshape(lax.axis_size("col") * share, slots_row, B, B)
    right = picked.reshape(lax.axis_size("col") * share, slots_row, slots_density, B, B)
    products = jnp.einsum("iaxy,iabyz->iabxz", left, right, preferred_element_type=jnp.float32)
    products = products.reshape(lax.axis_size("col") * share, slots_row, slots_density, B * B)
    onehot = (picked_columns[..., None] == jnp.arange(NCW, dtype=jnp.int32)).astype(jnp.float32)
    summed = jnp.einsum("iabj,iabe->ije", onehot, products, precision=lax.Precision.HIGHEST)
    gradient = lax.psum_scatter(summed, "col", scatter_dimension=0, tiled=True)
    rows_count = lax.axis_size("row")
    cols_count = lax.axis_size("col")
    devices = rows_count * cols_count
    capacity = max(2, share * NCW * 2 // devices)
    blocks = gradient.reshape(share * NCW, B * B)
    targets = owner_map.reshape(share * NCW)
    onehot_owner = (targets[:, None] == jnp.arange(devices, dtype=jnp.int32)).astype(jnp.int32)
    ranks = jnp.sum(jnp.cumsum(onehot_owner, axis=0) * onehot_owner, axis=1) - 1
    slots = targets * capacity + ranks
    outgoing = jnp.zeros((devices * capacity, B * B), jnp.float32).at[slots].set(blocks)
    owned_blocks = lax.all_to_all(outgoing, ("row", "col"), split_axis=0, concat_axis=0, tiled=True)
    return owned_blocks


def solution(mesh):
    return jax.shard_map(
        local,
        mesh=mesh,
        in_specs=(
            P("row", "col", None, None),
            P("row", "col", None),
            P("col", "row", None, None),
            P("col", "row", None),
            P(("row", "col"), None),
        ),
        out_specs=P(("row", "col"), None),
        check_vma=False,
    )
```

profile of v0, /device:TPU:1, one launch (start us, length us, event | category | flops | bytes accessed | tf_op | source)
XLA Modules:
  0.0 565.9 jit_solution(8959400753497321268)
XLA Ops:
  6.5 0.0 copy-start
  6.5 0.0 all-gather.2.cloned.1.call-start
  6.5 0.7 all-gather.2.cloned.1.call-update
  7.3 0.0 reduce-scatter.2.cloned.1.call-start
  7.3 0.7 compare_select_fusion
  8.0 0.1 copy.10
  8.1 0.1 reshape.55
  8.2 7.0 %reshape.80 = bf16[64,4,64,64,1]{3,2,1,0,4:T(8,128)(2,1)} reshape(bf16[64,1,4,4096]{3,2,1,0:T(4,128)(2,1)} %param.5) | data formatting | bytes 4194304 | tf_op jit(solution)/shard_map/reshape;squeeze | solution.py:24
  15.2 0.0 copy-done
  15.2 14.5 %all_gather.6 = s32[1,64,8]{2,1,0:T(8,128)S(1)} all-gather(s32[1,8,8]{2,1,0:T(8,128)S(1)} %copy-done), channel_id=1, replica_groups=mesh['row'=8,'col'=16] {'row'}, dimensions={1}, use_global_device_ids=true | all-gather | bytes 2304 | tf_op jit(solution)/shard_map/all_gather | solution.py:13
  29.7 0.7 gather_fusion
  30.4 14.5 %all-gather.2.cloned.1.call-done = bf16[1,64,8,4096]{3,2,0,1:T(8,128)(2,1)} async-done(((bf16[1,8,8,4096]{3,2,0,1:T(8,128)(2,1)}), bf16[1,64,8,4096]{3,2,0,1:T(8,128)(2,1)}) %all-gather.2.cloned.1.call-update) | async-done | bytes 4194320 | tf_op jit(solution)/shard_map/all_gather | solution.py:12
  44.9 11.9 %gather_fusion.1 = bf16[256,8,4096]{2,1,0:T(8,128)(2,1)} fusion(bf16[64,8,4096]{2,1,0:T(8,128)(2,1)} %bitcast.28, s32[1024]{0:T(1024)S(1)} %pad_clamp_fusion), kind=kCustom, calls=%fused_computation.1 | custom fusion | bytes 33555456 | tf_op jit(solution)/shard_map/gather | solution.py:22
  56.8 46.0 %reshape.50 = bf16[64,4,8,64,64]{4,3,2,1,0:T(8,128)(2,1)} reshape(bf16[256,8,4096]{2,1,0:T(8,128)(2,1)} %gather_fusion.1) | data formatting | bytes 33554432 | tf_op jit(solution)/shard_map/reshape | solution.py:25
  102.8 36.0 %convolution_bitcast_fusion = f32[64,4,8,64,64]{3,4,2,1,0:T(8,128)} fusion(bf16[64,4,8,64,64]{4,3,2,1,0:T(8,128)(2,1)} %reshape.50, bf16[64,4,64,64,1]{3,2,1,0,4:T(8,128)(2,1)} %reshape.80), kind=kOutput, calls=%fused_computation.3 | convolution fusion | flops 1073741824 | bytes 52428800 | tf_op jit(solution)/shard_map/iaxy,iabyz->iabxz/dot_general | solution.py:26
  138.8 66.1 %copy.13 = f32[64,4,8,64,64]{4,3,2,1,0:T(8,128)} copy(f32[64,4,8,64,64]{3,4,2,1,0:T(8,128)} %convolution_bitcast_fusion) | data formatting | bytes 67108864 | tf_op jit(solution)/shard_map/iaxy,iabyz->iabxz/transpose | solution.py:26
  205.0 54.7 %reshape.51 = f32[64,4,8,4096]{3,2,1,0:T(8,128)} reshape(f32[64,4,8,64,64]{4,3,2,1,0:T(8,128)} %copy.13) | data formatting | bytes 67108864 | tf_op jit(solution)/shard_map/reshape | solution.py:27
  259.7 28.6 %convolution_bitcast_fusion.1 = f32[64,32,4096]{2,1,0:T(8,128)} fusion(f32[64,4,8,4096]{3,2,1,0:T(8,128)} %reshape.51, s32[64,4,8]{2,1,0:T(4,128)S(1)} %bitcast.30), kind=kOutput, calls=%fused_computation.4 | convolution fusion | flops 3221291008 | bytes 67117056 | tf_op jit(solution)/shard_map/iabj,iabe->ije/dot_general | solution.py:29
  288.3 0.0 copy-start.1
  288.3 0.0 reduce-scatter.2.cloned.1.call-update
  288.3 0.6 copy-done.1
  289.0 0.1 fusion.4
  289.1 0.2 reduce_window_sum.11
  289.2 0.2 select_reduce_fusion
  289.4 193.7 %reduce-scatter.2.cloned.1.call-done = f32[4,32,4096]{2,1,0:T(8,128)} async-done(((f32[64,32,4096]{2,1,0:T(8,128)}), f32[4,32,4096]{2,1,0:T(8,128)}) %reduce-scatter.2.cloned.1.call-update) | async-done | bytes 2097168 | tf_op jit(solution)/shard_map/reduce_scatter | solution.py:30
  483.1 5.2 scatter_custom_fusion
  488.3 5.8 %all_to_all.8 = f32[128,2,4096]{2,1,0:T(2,128)} reshape(f32[256,4096]{1,0:T(8,128)} %scatter_custom_fusion) | data formatting | bytes 8388608 | tf_op jit(solution)/shard_map/all_to_all | solution.py:41
  494.1 58.8 %all_to_all.12 = f32[128,2,4096]{2,1,0:T(2,128)} all-to-all(f32[128,2,4096]{2,1,0:T(2,128)} %all_to_all.8), channel_id=1, replica_groups=mesh['row'=8,'col'=16] {'row','col'}, dimensions={0} | all-to-all | bytes 8388608 | tf_op jit(solution)/shard_map/all_to_all | solution.py:41
  553.0 6.0 %all_to_all.10 = f32[256,4096]{1,0:T(8,128)} reshape(f32[128,2,4096]{2,1,0:T(2,128)} %all_to_all.12) | data formatting | bytes 8388608 | tf_op jit(solution)/shard_map/all_to_all | solution.py:41
  (2 shorter events, 0.0 us)
Async XLA Ops:
  6.5 8.7 %copy-start = (s32[1,8,8]{2,1,0:T(8,128)S(1)}, s32[1,8,8]{2,1,0:T(8,128)}, u32[]{:S(2)}) copy-start(s32[1,8,8]{2,1,0:T(8,128)} %param.8) | copy-start | bytes 772
  6.5 38.3 %all-gather.2.cloned.1.call-start = ((), (), s32[]{:S(2)}) async-start(), calls=%async_computation.2 | async-start | bytes 4718592 | tf_op jit(solution)/shard_map/all_gather | solution.py:12
  7.3 475.8 %reduce-scatter.2.cloned.1.call-start = ((), (), s32[]{:S(2)}) async-start(), calls=%async_computation.3 | async-start | bytes 35651584 | tf_op jit(solution)/shard_map/reduce_scatter | solution.py:30
  288.3 0.7 copy-start.1
Sparse Core Ops, SparseCore 0:
  9.1 35.7 all-gather.1
  288.5 194.5 reduce-scatter.1
where the time goes:
time: 570 us; the launch traced here: 566 us
  waiting for transfers between devices  209 us (37%)
  local copies, waits for them, and re-layouts  204 us (36%)
  blocking collectives  73.3 us (13%)
  matrix products  64.7 us (11%)
  between operations  13.4 us (2%)
    reduce_scatter x1, waiting for transfers between devices, local(): gradient = lax.psum_scatter(summed, 'col', scatter_dimension=0, tiled=True)  194 us
    transpose x1, local copies, waits for them, and re-layouts, local(): jnp.einsum('iaxy,iabyz->iabxz', left, right, preferred_element_type=jnp.f...  66.1 us
    all_to_all x1, blocking collectives, local(): lax.all_to_all(outgoing, ('row', 'col'), split_axis=0, concat_axis=0, til...  58.8 us
    reshape x1, local copies, waits for them, and re-layouts, local(): products.reshape(lax.axis_size('col') * share, slots_row, slots_density,...  54.7 us
    reshape x1, local copies, waits for them, and re-layouts, local(): picked.reshape(lax.axis_size('col') * share, slots_row, slots_density, B, B)  46 us
    dot_general x1, matrix products, local(): jnp.einsum('iaxy,iabyz->iabxz', left, right, preferred_element_type=jnp.f...  36 us
    dot_general x1, matrix products, local(): jnp.einsum('iabj,iabe->ije', onehot, products, precision=lax.Precision.HI...  28.6 us
    all_gather x1, waiting for transfers between devices, local(): lax.all_gather(density_blocks, 'row', axis=1, tiled=True)  14.5 us
  transfers between devices with their start and end apart: 2, of which 2 were waited for; matrix products, arithmetic and copies ran while one was open for 2% of the time, Pallas kernels for 0%

commit v1 on v0

v1 whole, which is shorter than its diff:
```python
import functools

import jax
import jax.numpy as jnp
from jax import lax
from jax.experimental import pallas as pl
from jax.experimental.pallas import tpu as pltpu
from jax.sharding import Mesh, PartitionSpec as P

B = 64
HALF = 32
NCW = 32
SK = 4
SP = 8
X, C, Z, Y = 4, 2, 4, 4
ALL = ("x", "core", "z", "y")


def chunk_masks(shape):
    lane = lax.broadcasted_iota(jnp.int32, shape, len(shape) - 1)
    return (lane & 64) == 0, (lane & 32) == 0


def panel_kernel(kcol, jcol, k_ref, d_ref, o_ref):
    step = pl.program_id(0) * pl.num_programs(1) + pl.program_id(1)
    low64, low32 = chunk_masks((16, 128))
    o_ref[...] = jnp.zeros_like(o_ref)
    for p in range(Z * SK):
        z, a = p // SK, p % SK
        k = kcol[step * (Z * SK) + p]
        blk = k_ref[0, z, 0, 0, a * 32:(a + 1) * 32, :]
        left = jnp.concatenate([blk[:, :B], blk[:, B:]], axis=0)
        r = jnp.dot(left, d_ref[k], preferred_element_type=jnp.float32)
        for t in range(2):
            v = [r[ch * 16:(ch + 1) * 16, t * 128:(t + 1) * 128] for ch in range(4)]
            w = [None] * 4
            for c0 in range(2):
                lo, hi = v[c0], v[2 + c0]
                w[c0] = jnp.where(low64, lo, pltpu.roll(hi, 64, 1))
                w[2 + c0] = jnp.where(low64, pltpu.roll(lo, 64, 1), hi)
            u = [None] * 4
            for b1 in range(2):
                lo, hi = w[2 * b1], w[2 * b1 + 1]
                u[2 * b1] = jnp.where(low32, lo, pltpu.roll(hi, 32, 1))
                u[2 * b1 + 1] = jnp.where(low32, pltpu.roll(lo, 96, 1), hi)
            js = [jcol[k * SP + t * 4 + b] for b in range(4)]
            old = [o_ref[0, 0, js[b]] for b in range(4)]
            for b in range(4):
                o_ref[0, 0, js[b]] = old[b] + u[b]


def panel_sums(kcol, jcol, kohn, dens):
    grid_spec = pltpu.PrefetchScalarGridSpec(
        num_scalar_prefetch=2,
        grid=(Y, 8),
        in_specs=[
            pl.BlockSpec((1, Z, 1, 1, 128, 128), lambda y, r, *_: (r // 4, 0, y, r % 4, 0, 0)),
            pl.BlockSpec((Z * 64, 64, 256), lambda y, r, *_: (0, 0, 0), pipeline_mode=pl.Buffered(1)),
        ],
        out_specs=pl.BlockSpec((1, 1, NCW, 16, 128), lambda y, r, *_: (y, r, 0, 0, 0)),
    )
    return pl.pallas_call(
        panel_kernel,
        grid_spec=grid_spec,
        out_shape=jax.ShapeDtypeStruct((Y, 8, NCW, 16, 128), jnp.float32),
        compiler_params=pltpu.CompilerParams(vmem_limit_bytes=40 << 20),
        cost_estimate=pl.CostEstimate(flops=2 * 512 * 64 * 64 * 256, bytes_accessed=20 << 20, transcendentals=0),
        name="panel_sums",
    )(kcol, jcol, kohn, dens)


def pack_kernel(slots, g_ref, o_ref):
    def clear(n, _):
        o_ref[pl.ds(n * 16, 16)] = jnp.zeros((16, 16, 128), jnp.float32)
        return 0

    lax.fori_loop(0, 32, clear, 0)

    def place(n, _):
        for m in range(8):
            o_ref[slots[n * 8 + m]] = g_ref[n * 8 + m]
        return 0

    lax.fori_loop(0, 32, place, 0)


def pack(slots, blocks):
    return pl.pallas_call(
        pack_kernel,
        grid_spec=pltpu.PrefetchScalarGridSpec(
            num_scalar_prefetch=1,
            grid=(1,),
            in_specs=[pl.BlockSpec((256, 16, 128), lambda i, *_: (0, 0, 0), pipeline_mode=pl.Buffered(1))],
            out_specs=pl.BlockSpec((512, 16, 128), lambda i, *_: (0, 0, 0), pipeline_mode=pl.Buffered(1)),
        ),
        out_shape=jax.ShapeDtypeStruct((512, 16, 128), jnp.float32),
        compiler_params=pltpu.CompilerParams(vmem_limit_bytes=32 << 20),
        name="pack",
    )(slots, blocks)


def unpack_kernel(r_ref, o_ref, full):
    _, low32 = chunk_masks((16, 128))
    for n in range(16):
        for t in range(2):
            h0 = r_ref[0, 0, n, 0, t]
            h1 = r_ref[0, 1, n, 0, t]
            base = (n * 2 + t) * 32
            full[base:base + 16, :] = jnp.where(low32, h0, pltpu.roll(h1, 32, 1))
            full[base + 16:base + 32, :] = jnp.where(low32, pltpu.roll(h0, 96, 1), h1)
    for p in range(32):
        o_ref[:, p * 128:(p + 1) * 128] = full[pl.ds(p, 32, stride=32), :]


def unpack(received):
    return pl.pallas_call(
        unpack_kernel,
        grid=(X, C),
        in_specs=[pl.BlockSpec((1, C, 16, 1, 2, 16, 128), lambda x, s: (x, 0, 0, s, 0, 0, 0))],
        out_specs=pl.BlockSpec((32, 4096), lambda x, s: (x * 2 + s, 0)),
        out_shape=jax.ShapeDtypeStruct((256, 4096), jnp.float32),
        scratch_shapes=[pltpu.VMEM((32 * 32, 128), jnp.float32)],
        compiler_params=pltpu.CompilerParams(vmem_limit_bytes=32 << 20),
        name="unpack",
    )(received)


def local(kohn_blocks, kohn_columns, density_blocks, density_columns, owner_map):
    x, c, z = lax.axis_index("x"), lax.axis_index("core"), lax.axis_index("z")
    swap = [(0, 1), (1, 0)]

    halves = density_blocks.reshape(8, SP, B, 2, HALF).transpose(3, 0, 2, 1, 4).reshape(2, 8, B, SP * HALF)
    mine = lax.dynamic_index_in_dim(halves, c, 0, keepdims=False)
    theirs = lax.dynamic_index_in_dim(halves, 1 - c, 0, keepdims=False)
    shard = jnp.stack([mine, lax.ppermute(theirs, "core", swap)])
    dens = lax.all_gather(shard, ("z", "x"), axis=0, tiled=True).reshape(Z * 64, B, SP * HALF)

    ints = jnp.concatenate([kohn_columns.reshape(-1), density_columns.reshape(-1), owner_map.reshape(-1)])
    ints = lax.all_gather(ints, ("z", "x", "core")).reshape(Z, X, C, 448)

    def ordered(v, axis):
        return jnp.where(c == 1, jnp.flip(v, axis), v)

    kcol = lax.dynamic_index_in_dim(ints[..., :256], x, 1, keepdims=False).reshape(Z, C, Z, Y, 4, SK)
    kcol = ordered(lax.dynamic_index_in_dim(kcol, z, 2, keepdims=False), 1)
    kcol = (kcol ^ (8 * c)) + 64 * jnp.arange(Z, dtype=jnp.int32).reshape(Z, 1, 1, 1, 1)
    kcol = kcol.transpose(2, 1, 3, 0, 4).reshape(-1)
    jcol = ordered(ints[..., 256:320], 2).reshape(-1)
    owners = lax.dynamic_index_in_dim(ints[..., 320:], z, 0, keepdims=False)
    owners = ordered(lax.dynamic_index_in_dim(owners, x, 0, keepdims=False), 0)
    hit = (owners[..., None] == jnp.arange(128, dtype=jnp.int32)).astype(jnp.int32)
    ranks = jnp.sum(jnp.cumsum(hit, axis=1) * hit, axis=2) - 1
    source = jnp.arange(2, dtype=jnp.int32)[:, None] ^ c
    slots = (owners * 4 + source * 2 + ranks).reshape(-1)

    kohn = kohn_blocks.reshape(Z, 16, SK * 32, 128)
    kohn = lax.all_to_all(kohn, "z", split_axis=0, concat_axis=0, tiled=True)
    kohn = jnp.stack([kohn, lax.ppermute(kohn, "core", swap)]).reshape(2, Z, Y, 4, SK * 32, 128)

    sums = panel_sums(kcol, jcol, kohn, dens)
    gradient = lax.psum_scatter(sums, "y", scatter_dimension=0, tiled=True)
    outgoing = pack(slots, gradient.reshape(256, 16, 128))
    received = lax.all_to_all(outgoing.reshape(128, 4, 16, 128), ALL, split_axis=0, concat_axis=0, tiled=True)
    return unpack(received.reshape(X, C, 16, 2, 2, 16, 128))


def solution(mesh):
    grid = Mesh(mesh.devices.reshape(X, C, Z, Y), ALL)
    row, col = ("x", "core"), ("z", "y")
    return jax.shard_map(
        local,
        mesh=grid,
        in_specs=(
            P(row, col, None, None),
            P(row, col, None),
            P(col, row, None, None),
            P(col, row, None),
            P(ALL, None),
        ),
        out_specs=P(ALL, None),
        check_vma=False,
    )
```

time: 570 us -> 403 us (0.71)
  local copies, waits for them, and re-layouts: 204 us -> 17.8 us
  blocking collectives: 73.3 us -> 220 us
  waiting for transfers between devices: 209 us -> 83 us
  matrix products: 64.7 us -> 0 us
  Pallas kernels: 0 us -> 58.7 us
    unnamed x0 -> x1, blocking collectives: none -> 122 us
    reduce_scatter x1, waiting for transfers between devices: 194 us -> 81.4 us  [local(): gradient = lax.psum_scatter(sums, 'y', scatter_dimension=0, tiled=True)]
    reshape x2 -> x8, local copies, waits for them, and re-layouts: 101 us -> 7.11 us  [the longest x1 3.78 us: local(): kohn = kohn_blocks.reshape(Z, 16, SK * 32, 128)]
    dot_general x2 -> x0, matrix products: 64.7 us -> none  [the longest x1 36 us: local(): jnp.einsum('iaxy,iabyz->iabxz', left, right, preferred_element_type=jnp.f...]
    transpose x1 -> x2, local copies, waits for them, and re-layouts: 66.1 us -> 1.61 us  [the longest x1 1.56 us: local(): density_blocks.reshape(8, SP, B, 2, HALF).transpose(3, 0, 2, 1, 4)]
    pallas_call x0 -> x3, Pallas kernels: none -> 58.7 us  [the longest x1 51.5 us: panel_sums(): pl.pallas_call(panel_kernel, grid_spec=grid_spec, out_shape=jax.ShapeDtyp...]
    all_to_all x1 -> x2, blocking collectives: 58.8 us -> 97.7 us  [the longest x1 58.8 us: local(): lax.all_to_all(outgoing.reshape(128, 4, 16, 128), ALL, split_axis=0, conc...]
    all_gather x1, waiting for transfers between devices: 14.5 us -> 0.01 us  [local(): lax.all_gather(shard, ('z', 'x'), axis=0, tiled=True)]
  transfers between devices with their start and end apart: 2 -> 4, of which waited for: 2 -> 2; matrix products, arithmetic and copies ran while one was open for 2% -> 3% of each run, Pallas kernels for 0% -> 0%
where the time goes in v1:
time: 403 us; the launch traced here: 402 us
  blocking collectives  220 us (55%)
  waiting for transfers between devices  83 us (21%)
  Pallas kernels  58.7 us (15%)
  local copies, waits for them, and re-layouts  17.8 us (4%)
  between operations  14.3 us (4%)
  other arithmetic  5.08 us (1%)
    unnamed x1, blocking collectives  122 us
    reduce_scatter x1, waiting for transfers between devices, local(): gradient = lax.psum_scatter(sums, 'y', scatter_dimension=0, tiled=True)  81.4 us
    all_to_all x1, blocking collectives, local(): lax.all_to_all(outgoing.reshape(128, 4, 16, 128), ALL, split_axis=0, conc...  58.8 us
    pallas_call x1, Pallas kernels, panel_sums(): pl.pallas_call(panel_kernel, grid_spec=grid_spec, out_shape=jax.ShapeDtyp...  51.5 us
    all_to_all x1, blocking collectives, local(): kohn = lax.all_to_all(kohn, 'z', split_axis=0, concat_axis=0, tiled=True)  38.9 us
  transfers between devices with their start and end apart: 4, of which 2 were waited for; matrix products, arithmetic and copies ran while one was open for 3% of the time, Pallas kernels for 0%

profile of v1, /device:TPU:1, one launch (start us, length us, event | category | flops | bytes accessed | tf_op | source)
XLA Modules:
  0.0 402.4 jit_solution(9174439205361596143)
XLA Ops:
  6.5 2.5 reshape.76
  9.0 1.6 copy.19
  10.6 0.1 constant_dynamic-slice_fusion
  10.7 1.5 collective-permute-start.1
  12.2 1.5 collective-permute-done.1
  13.8 0.2 pad_maximum_fusion.1
  14.0 1.1 copy.20
  15.3 3.8 reshape.75
  19.0 38.9 %all_to_all.10 = bf16[4,16,128,128]{3,2,1,0:T(8,128)(2,1)} all-to-all(bf16[4,16,128,128]{3,2,1,0:T(8,128)(2,1)S(1)} %reshape.75), channel_id=1, replica_groups=mesh['x'=4,'core'=2,'z'=4,'y'=4] {'z'}, dimensions={0} | all-to-all | bytes 4194304 | tf_op jit(solution)/shard_map/all_to_all | solution.py:157
  58.0 1.8 collective-permute-start
  59.9 0.1 copy.17
  59.9 0.1 reshape.67
  60.1 0.6 dynamic-slice.2
  61.3 0.2 add_dynamic-update-slice_fusion
  61.5 122.5 %all-reduce = s32[14336]{0:T(1024)S(1)} all-reduce(s32[14336]{0:T(1024)S(1)} %add_dynamic-update-slice_fusion), channel_id=2, replica_groups=mesh['x'=4,'core'=2,'z'=4,'y'=4] {'z','x','core'}, use_global_device_ids=true, to_apply=%add | all-reduce | flops 14336 | bytes 114688
  184.0 0.1 reshape.70
  184.2 0.1 reshape.74.jcol
  184.3 0.4 reshape.72
  184.7 0.1 fusion.3
  184.9 0.1 reshape.73.kcol
  185.0 4.0 pad_maximum_fusion.k_ref
  189.0 2.2 copy-done.1
  191.2 51.5 %panel_sums.1 = f32[4,8,32,16,128]{4,3,2,1,0:T(8,128)S(1)} custom-call(s32[512]{0:T(512)S(1)} %reshape.73.kcol, s32[2048]{0:T(1024)S(1)} %reshape.74.jcol, bf16[2,4,4,4,128,128]{5,4,3,2,1,0:T(8,128)(2,1)S(1)} %copy-done.1, bf16[256,64,256]{2,1,0:T(8,128)(2,1)} %bitcast.30), custom_call_target="tpu_custom_call" | custom-call | flops 1073741824 | bytes 20971520 | tf_op jit(solution)/shard_map/panel_sums/pallas_call | solution.py:62
  242.7 3.2 copy-done
  246.1 0.1 fusion
  246.2 0.2 reduce_window_sum.11
  246.4 0.2 select_reduce_fusion
  246.6 81.4 %reduce-scatter.2.cloned.1.call-done = f32[1,8,32,16,128]{4,3,2,1,0:T(8,128)} async-done(((f32[4,8,32,16,128]{4,3,2,1,0:T(8,128)}), f32[1,8,32,16,128]{4,3,2,1,0:T(8,128)}) %reduce-scatter.2.cloned.1.call-update) | async-done | bytes 2097168 | tf_op jit(solution)/shard_map/reduce_scatter | solution.py:161
  328.1 1.6 copy-done.2
  329.7 1.3 pack.1
  331.0 58.8 %all_to_all.11 = f32[128,4,16,128]{3,2,1,0:T(8,128)S(1)} all-to-all(f32[128,4,16,128]{3,2,1,0:T(8,128)S(1)} %bitcast.27), channel_id=1, replica_groups=mesh['x'=4,'core'=2,'z'=4,'y'=4] {'x','core','z','y'}, dimensions={0} | all-to-all | bytes 8388608 | tf_op jit(solution)/shard_map/all_to_all | solution.py:163
  389.8 5.8 %unpack.1 = f32[256,4096]{1,0:T(8,128)} custom-call(f32[4,2,16,2,2,16,128]{6,5,4,3,2,1,0:T(8,128)S(1)} %bitcast.28), custom_call_target="tpu_custom_call" | custom-call | tf_op jit(solution)/shard_map/unpack/pallas_call | solution.py:116
  (33 shorter events, 0.5 us)
Async XLA Ops:
  6.5 182.4 %all-gather.3.cloned.1.call-start = ((), (), s32[]{:S(2)}) async-start(), calls=%async_computation.3 | async-start | bytes 8912896 | tf_op jit(solution)/shard_map/all_gather | solution.py:136
  10.7 3.0 collective-permute-start.1
  15.2 44.6 %copy-start.3 = (s32[1,8,8]{2,1,0:T(8,128)S(1)}, s32[1,8,8]{2,1,0:T(8,128)}, u32[]{:S(2)}) copy-start(s32[1,8,8]{2,1,0:T(8,128)} %param.8) | copy-start | bytes 772
  15.2 44.7 %copy-start.4 = (s32[64,1,4]{0,2,1:T(4,128)S(1)}, s32[64,1,4]{0,2,1:T(4,128)}, u32[]{:S(2)}) copy-start(s32[64,1,4]{0,2,1:T(4,128)} %param.6) | copy-start | bytes 3076
  15.2 44.9 %copy-start.6 = (u32[128]{0:T(128)S(1)}, u32[128]{0:T(128)}, u32[]{:S(2)}) copy-start(u32[128]{0:T(128)} %constant.84) | copy-start | bytes 1540
  15.2 46.1 %copy-start.5 = (s32[128,1]{0,1:T(1,128)S(1)}, s32[128,1]{0,1:T(1,128)}, u32[]{:S(2)}) copy-start(s32[128,1]{0,1:T(1,128)} %param.9) | copy-start | bytes 1540
  15.2 312.9 %reduce-scatter.2.cloned.1.call-start = ((), (), s32[]{:S(2)}) async-start(), calls=%async_computation.4 | async-start | bytes 10485760 | tf_op jit(solution)/shard_map/reduce_scatter | solution.py:161
  58.0 127.0 %collective-permute-start = (bf16[4,16,128,128]{3,2,1,0:T(8,128)(2,1)}, bf16[4,16,128,128]{3,2,1,0:T(8,128)(2,1)S(1)}, u32[]{:S(2)}, u32[]{:S(2)}) collective-permute-start(bf16[4,16,128,128]{3,2,1,0:T(8,128)(2,1)} %all_to_all.10), channel_id=1, source_target_pairs={{0,16},{16,0},{1,17},{17,1},{2,18},{18,2},{3,19},{19,3},{4,20},{20... | collective-permute-start | bytes 6291464 | tf_op jit(solution)/shard_map/ppermute | solution.py:158
  189.0 2.2 copy-start.1
  242.7 3.2 copy-start
  328.1 1.6 copy-start.2
Sparse Core Ops, SparseCore 0:
  15.3 87.2 all-gather.2
  246.1 81.9 reduce-scatter.1

commit v2 on v1

v2 whole, which is shorter than its diff:
```python
import jax
import jax.numpy as jnp
from jax import lax
from jax.experimental import pallas as pl
from jax.experimental.pallas import tpu as pltpu
from jax.sharding import Mesh, PartitionSpec as P

B = 64
HALF = 32
NCW = 32
SK = 4
SP = 8
X, C, Z, Y = 4, 2, 4, 4
ALL = ("x", "core", "z", "y")
PLANE = ("core", "z", "y")
TOP = 32766.0
MSG = 80


def line_pairs(step, along):
    pairs = []
    for c in range(C):
        for z in range(Z):
            for y in range(Y):
                to = ((z + step) % Z, y) if (c ^ along) == 0 else (z, (y + step) % Y)
                pairs.append(((c * Z + z) * Y + y, (c * Z + to[0]) * Y + to[1]))
    return pairs


def over_line(v, step):
    return lax.ppermute(v, PLANE, line_pairs(step, 0))


def over_cross(v, step):
    return lax.ppermute(v, PLANE, line_pairs(step, 1))


def over_x(v, step):
    return lax.ppermute(v, "x", [(i, (i + step) % X) for i in range(X)])


def over_core(v):
    return lax.ppermute(v, "core", [(0, 1), (1, 0)])


def chunk_masks(shape):
    lane = lax.broadcasted_iota(jnp.int32, shape, len(shape) - 1)
    return (lane & 64) == 0, (lane & 32) == 0


def panel_kernel(n, first, kcol, jcol, *refs):
    kohn, refs = refs[:n], refs[n:]
    halves, refs = refs[:2 * n], refs[2 * n:]
    if not first:
        p_ref, refs = refs[0], refs[1:]
    o_ref, dens, sems = refs
    step = pl.program_id(0)

    @pl.when(step == 0)
    def _():
        copies = [
            pltpu.make_async_copy(halves[h], dens.at[pl.ds(h * 32, 32)], sems.at[h]) for h in range(2 * n)
        ]
        for copy in copies:
            copy.start()
        for copy in copies:
            copy.wait()

    low64, low32 = chunk_masks((16, 128))
    if first:
        o_ref[...] = jnp.zeros_like(o_ref)
    else:
        o_ref[...] = p_ref[...]

    def product(row, s, a):
        k = kcol[((s * 4 + step) * 8 + row) * SK + a] + 64 * s
        blk = kohn[s][0, row // 4, row % 4, a * 32:(a + 1) * 32, :]
        left = jnp.concatenate([blk[:, :B], blk[:, B:]], axis=0)
        return k, jnp.dot(left, dens[k], preferred_element_type=jnp.float32)

    def add(row, k, r):
        us = []
        for t in range(2):
            v = [r[ch * 16:(ch + 1) * 16, t * 128:(t + 1) * 128] for ch in range(4)]
            w = [None] * 4
            for c0 in range(2):
                lo, hi = v[c0], v[2 + c0]
                w[c0] = jnp.where(low64, lo, pltpu.roll(hi, 64, 1))
                w[2 + c0] = jnp.where(low64, pltpu.roll(lo, 64, 1), hi)
            for b1 in range(2):
                lo, hi = w[2 * b1], w[2 * b1 + 1]
                us.append(jnp.where(low32, lo, pltpu.roll(hi, 32, 1)))
                us.append(jnp.where(low32, pltpu.roll(lo, 96, 1), hi))
        js = [jcol[k * SP + b] for b in range(SP)]
        old = [o_ref[0, row, j] for j in js]
        for b in range(SP):
            o_ref[0, row, js[b]] = old[b] + us[b]

    def one_row(row, _):
        todo = [(s, a) for s in range(n) for a in range(SK)]
        held = [product(row, *todo[0]), product(row, *todo[1])]
        for i in range(len(todo)):
            if i + 2 < len(todo):
                held.append(product(row, *todo[i + 2]))
            add(row, *held[i])
        return 0

    lax.fori_loop(0, 8, one_row, 0)


def panel_sums(kcol, jcol, kohn, halves, sums):
    n, first = len(kohn), sums is None
    k_spec = pl.BlockSpec((1, 2, 4, 128, 128), lambda o, *_: (o, 0, 0, 0, 0))
    s_spec = pl.BlockSpec((1, 8, NCW, 16, 128), lambda o, *_: (o, 0, 0, 0, 0))
    any_spec = pl.BlockSpec(memory_space=pl.ANY)
    return pl.pallas_call(
        lambda *refs: panel_kernel(n, first, *refs),
        grid_spec=pltpu.PrefetchScalarGridSpec(
            num_scalar_prefetch=2,
            grid=(4,),
            in_specs=[k_spec] * n + [any_spec] * (2 * n) + [s_spec] * (not first),
            out_specs=s_spec,
            scratch_shapes=[pltpu.VMEM((n * 64, B, SP * HALF), jnp.bfloat16), pltpu.SemaphoreType.DMA((2 * n,))],
        ),
        out_shape=jax.ShapeDtypeStruct((4, 8, NCW, 16, 128), jnp.float32),
        compiler_params=pltpu.CompilerParams(vmem_limit_bytes=40 << 20),
        cost_estimate=pl.CostEstimate(
            flops=2 * n * 128 * 64 * 64 * 256, bytes_accessed=(3 * n + 16) << 20, transcendentals=0
        ),
        name="panel_sums_%d" % n if not first else "panel_sums_first",
    )(kcol, jcol, *kohn, *halves, *(() if first else (sums,)))


def pack_kernel(slots, own, low_p, low_m, high_p, high_m, o_ref, total, codes):
    rows = lax.broadcasted_iota(jnp.int32, (16, 128), 0)

    def clear(n, _):
        for m in range(4):
            o_ref[n * 4 + m] = jnp.zeros((MSG, 128), jnp.int16)
            codes[n * 4 + m] = jnp.zeros((16, 128), jnp.int32)
        return 0

    lax.fori_loop(0, 32, clear, 0)

    def gather(m, p_ref, m_ref):
        def one(row, _):
            top = jnp.zeros((16, 128), jnp.float32)
            for j in range(NCW):
                g = own[0, m * 4 + row, j] + p_ref[row, j] + m_ref[row, j]
                total[j] = g
                top = jnp.maximum(top, jnp.abs(g))
            top = jnp.maximum(jnp.max(top, axis=0, keepdims=True), 2.0 ** -110)
            code = jnp.floor(jnp.log2(top) * 256.0) + 1.0
            scale = jnp.exp2(code * (-1.0 / 256.0)) * TOP
            code = jnp.broadcast_to(code.astype(jnp.int32), (16, 128))
            scale = jnp.broadcast_to(scale, (16, 128))
            for j in range(NCW):
                slot = slots[(m * 4 + row) * NCW + j]
                d, s = slot // 4, slot % 4
                q = jnp.floor(total[j] * scale + 0.5).astype(jnp.int32).astype(jnp.int16)
                o_ref[d, pl.ds(pl.multiple_of(s * 16, 16), 16), :] = q
                codes[d] = jnp.where(rows == s, code, codes[d])
            return 0

        lax.fori_loop(0, 4, one, 0)

    gather(0, low_p, low_m)
    gather(1, high_p, high_m)

    def finish(n, _):
        for m in range(4):
            o_ref[n * 4 + m, 64:80, :] = codes[n * 4 + m].astype(jnp.int16)
        return 0

    lax.fori_loop(0, 32, finish, 0)


def pack(slots, sums, low_p, low_m, high_p, high_m):
    part = pl.BlockSpec((4, NCW, 16, 128), lambda i, *_: (0, 0, 0, 0), pipeline_mode=pl.Buffered(1))
    return pl.pallas_call(
        pack_kernel,
        grid_spec=pltpu.PrefetchScalarGridSpec(
            num_scalar_prefetch=1,
            grid=(1,),
            in_specs=[
                pl.BlockSpec((1, 8, NCW, 16, 128), lambda i, *_: (3, 0, 0, 0, 0), pipeline_mode=pl.Buffered(1))
            ] + [part] * 4,
            out_specs=pl.BlockSpec((128, MSG, 128), lambda i, *_: (0, 0, 0), pipeline_mode=pl.Buffered(1)),
            scratch_shapes=[pltpu.VMEM((NCW, 16, 128), jnp.float32), pltpu.VMEM((128, 16, 128), jnp.int32)],
        ),
        out_shape=jax.ShapeDtypeStruct((128, MSG, 128), jnp.int16),
        compiler_params=pltpu.CompilerParams(vmem_limit_bytes=32 << 20),
        name="pack",
    )(slots, sums, low_p, low_m, high_p, high_m)


def unpack_kernel(r_ref, o_ref, full):
    _, low32 = chunk_masks((16, 128))
    for s in range(2):
        def one(n, _):
            scales = []
            for c in range(2):
                code = r_ref[0, c, n, 64:80, :].astype(jnp.int32).astype(jnp.float32)
                scales.append(jnp.exp2(code * (1.0 / 256.0)) * (1.0 / TOP))
            for t in range(2):
                h = []
                for c in range(2):
                    at = (s * 2 + t) * 16
                    q = r_ref[0, c, n, at:at + 16, :].astype(jnp.int32).astype(jnp.float32)
                    h.append(q * scales[c][s * 2 + t:s * 2 + t + 1, :])
                base = pl.multiple_of(((s * 16 + n) * 2 + t) * 32, 32)
                full[pl.ds(base, 16), :] = jnp.where(low32, h[0], pltpu.roll(h[1], 32, 1))
                full[pl.ds(base + 16, 16), :] = jnp.where(low32, pltpu.roll(h[0], 96, 1), h[1])
            return 0

        lax.fori_loop(0, 16, one, 0)
    for p in range(32):
        o_ref[:, p * 128:(p + 1) * 128] = full[pl.ds(p, 64, stride=32), :]


def unpack(received):
    return pl.pallas_call(
        unpack_kernel,
        grid=(X,),
        in_specs=[pl.BlockSpec((1, C, 16, MSG, 128), lambda x: (x, 0, 0, 0, 0))],
        out_specs=pl.BlockSpec((64, 4096), lambda x: (x, 0)),
        out_shape=jax.ShapeDtypeStruct((256, 4096), jnp.float32),
        scratch_shapes=[pltpu.VMEM((64 * 32, 128), jnp.float32)],
        compiler_params=pltpu.CompilerParams(vmem_limit_bytes=32 << 20),
        name="unpack",
    )(received)


def local(kohn_blocks, kohn_columns, density_blocks, density_columns, owner_map):
    x, c = lax.axis_index("x"), lax.axis_index("core")
    z, y = lax.axis_index("z"), lax.axis_index("y")
    on_line, on_cross = jnp.where(c == 0, z, y), jnp.where(c == 0, y, z)
    targets = (on_cross + jnp.array([2, 1, 3, 0], jnp.int32)) % 4

    def rows_of(t):
        return jnp.where(c == 0, t * Y + targets, targets * Y + t)

    ints = jnp.concatenate([kohn_columns.reshape(-1), density_columns.reshape(-1), owner_map.reshape(-1)])
    other = over_core(ints)
    columns = jnp.concatenate([ints[256:320], other[256:320]])
    columns = jnp.concatenate([columns, over_x(columns, 1), over_x(columns, -1), over_x(columns, 2)])
    words = jnp.concatenate([columns, ints[:256], other[:256]]).reshape(8, 128)
    words = [words, over_line(words, 1), over_line(words, -1), over_line(words, 2)]

    def indices(word):
        word = word.reshape(-1)
        k = word[512:].reshape(2, 16, 4, SK)[:, rows_of(on_line)].transpose(1, 0, 2, 3).reshape(-1)
        away = ((k >> 4) - x) & 3
        slot = jnp.where(away == 0, 0, jnp.where(away == 3, 1, away + 1))
        return slot * 16 + ((k & 15) ^ (8 * c)), word[:512]

    kcols, jcols = zip(*[indices(word) for word in words])

    owners = jnp.stack([ints[320:], other[320:]])
    hit = (owners[..., None] == jnp.arange(128, dtype=jnp.int32)).astype(jnp.int32)
    ranks = jnp.sum(jnp.cumsum(hit, axis=1) * hit, axis=2) - 1
    source = jnp.arange(2, dtype=jnp.int32)[:, None] ^ c
    slots = (owners * 4 + source * 2 + ranks).reshape(-1)

    halves = density_blocks.reshape(8, SP, B, 2, HALF).transpose(3, 0, 2, 1, 4).reshape(2, 8, B, SP * HALF)
    mine = lax.dynamic_index_in_dim(halves, c, 0, keepdims=False)
    theirs = over_core(lax.dynamic_index_in_dim(halves, 1 - c, 0, keepdims=False))
    left0, right0 = over_x(mine, 1), over_x(mine, -1)
    left1, right1 = over_x(theirs, 1), over_x(theirs, -1)
    far0, far1 = over_x(left0, 1), over_x(right1, -1)
    low = jnp.concatenate([mine, theirs, left0, left1])
    high = jnp.concatenate([right0, right1, far0, far1])

    prev_low, prev_high = over_line(low, 1), over_line(high, 1)
    next_high, next_low = over_line(high, -1), over_line(low, -1)
    far_low, far_high = over_line(prev_low, 1), over_line(next_high, -1)

    kohn = kohn_blocks.reshape(16, 4, SK * 32, 128)
    kohn_other = over_core(kohn)

    def rows_for(step):
        rows = rows_of((on_line + step) % 4)
        return jnp.stack([kohn[rows], kohn_other[rows]], axis=1)

    kohn_prev, kohn_next = over_line(rows_for(1), 1), over_line(rows_for(3), -1)
    opposite = rows_for(2)
    opposite0 = over_line(over_line(opposite[:2], 1), 1)
    opposite1 = over_line(over_line(opposite[2:], -1), -1)
    kohn_far = jnp.concatenate([opposite0, opposite1])

    sums = panel_sums(kcols[0], jcols[0], [rows_for(0)], [low, high], None)
    sums = panel_sums(
        jnp.concatenate(kcols[1:3]), jnp.concatenate(jcols[1:3]), [kohn_prev, kohn_next],
        [prev_low, prev_high, next_low, next_high], sums,
    )
    sums = panel_sums(kcols[3], jcols[3], [kohn_far], [far_low, far_high], sums)

    via_next, via_prev = over_cross(sums[0, :4], 1), over_cross(sums[0, 4:], -1)
    high_p, low_m = over_cross(sums[1, 4:], 1), over_cross(sums[2, :4], -1)
    low_p = over_cross(sums[1, :4] + via_next, 1)
    high_m = over_cross(sums[2, 4:] + via_prev, -1)

    outgoing = pack(slots, sums, low_p, low_m, high_p, high_m)
    received = lax.all_to_all(outgoing, ALL, split_axis=0, concat_axis=0, tiled=True)
    return unpack(received.reshape(X, C, 16, MSG, 128))


def solution(mesh):
    grid = Mesh(mesh.devices.reshape(X, C, Z, Y), ALL)
    row, col = ("x", "core"), ("z", "y")
    return jax.shard_map(
        local,
        mesh=grid,
        in_specs=(
            P(row, col, None, None),
            P(row, col, None),
            P(col, row, None, None),
            P(col, row, None),
            P(ALL, None),
        ),
        out_specs=P(ALL, None),
        check_vma=False,
    )
```

time: 403 us -> 282 us (0.70)
  blocking collectives: 220 us -> 43.5 us
  starting transfers between devices: 3.36 us -> 39.8 us
  local copies, waits for them, and re-layouts: 17.8 us -> 47 us
  waiting for transfers between devices: 83 us -> 62 us
  Pallas kernels: 58.7 us -> 75.5 us
  between operations: 14.3 us -> 0.37 us
  other arithmetic: 5.08 us -> 13.1 us
    unnamed x1 -> x0, blocking collectives: 122 us -> none
    reduce_scatter x1 -> x0, waiting for transfers between devices: 81.4 us -> none  [local(): gradient = lax.psum_scatter(sums, 'y', scatter_dimension=0, tiled=True)]
    ppermute x2 -> x33, waiting for transfers between devices: 1.54 us -> 62 us  [the longest x6 31.1 us: over_cross(): return lax.ppermute(v, PLANE, line_pairs(step, 1))]
    all_to_all x2 -> x1, blocking collectives: 97.7 us -> 43.5 us  [local(): lax.all_to_all(outgoing, ALL, split_axis=0, concat_axis=0, tiled=True)]
    ppermute x2 -> x33, starting transfers between devices: 3.32 us -> 39.8 us  [the longest x15 18.1 us: over_line(): return lax.ppermute(v, PLANE, line_pairs(step, 0))]
    gather x0 -> x12, local copies, waits for them, and re-layouts: none -> 26.3 us  [the longest x8 24 us: rows_for(): return jnp.stack([kohn[rows], kohn_other[rows]], axis=1)]
    pallas_call x2 -> x4, Pallas kernels: 57.4 us -> 70.9 us  [the longest x3 56.2 us: panel_sums(): pl.pallas_call(lambda *refs: panel_kernel(n, first, *refs), grid_spec=plt...]
    another operation x2 -> x5, other arithmetic: 4.22 us -> 8.1 us  [the longest x4 8.09 us: rows_for(): return jnp.stack([kohn[rows], kohn_other[rows]], axis=1)]
  transfers between devices with their start and end apart: 4 -> 33, of which waited for: 2 -> 13; matrix products, arithmetic and copies ran while one was open for 3% -> 17% of each run, Pallas kernels for 0% -> 14%
where the time goes in v2:
time: 282 us; the launch traced here: 281 us
  Pallas kernels  75.5 us (27%)
  waiting for transfers between devices  62 us (22%)
  local copies, waits for them, and re-layouts  47 us (17%)
  blocking collectives  43.5 us (15%)
  starting transfers between devices  39.8 us (14%)
  other arithmetic  13.1 us (5%)
    pallas_call x3, Pallas kernels, panel_sums(): pl.pallas_call(lambda *refs: panel_kernel(n, first, *refs), grid_spec=plt...  56.2 us
    all_to_all x1, blocking collectives, local(): lax.all_to_all(outgoing, ALL, split_axis=0, concat_axis=0, tiled=True)  43.5 us
    ppermute x6, waiting for transfers between devices, over_cross(): return lax.ppermute(v, PLANE, line_pairs(step, 1))  31.1 us
    gather x8, local copies, waits for them, and re-layouts, rows_for(): return jnp.stack([kohn[rows], kohn_other[rows]], axis=1)  24 us
    ppermute x15, waiting for transfers between devices, over_line(): return lax.ppermute(v, PLANE, line_pairs(step, 0))  19.4 us
    ppermute x15, starting transfers between devices, over_line(): return lax.ppermute(v, PLANE, line_pairs(step, 0))  18.1 us
    pallas_call x1, Pallas kernels, unpack(): pl.pallas_call(unpack_kernel, grid=(X,), in_specs=[pl.BlockSpec((1, C, 16...  14.7 us
    ppermute x9, starting transfers between devices, over_x(): return lax.ppermute(v, 'x', [(i, (i + step) % X) for i in range(X)])  10.2 us
  transfers between devices with their start and end apart: 33, of which 13 were waited for; matrix products, arithmetic and copies ran while one was open for 17% of the time, Pallas kernels for 14%

profile of v2, /device:TPU:1, one launch (start us, length us, event | category | flops | bytes accessed | tf_op | source)
XLA Modules:
  0.0 281.2 jit_solution(16831583014349430754)
XLA Ops:
  0.0 4.8 %reshape.141 = bf16[16,4,128,128]{3,2,1,0:T(8,128)(2,1)} reshape(bf16[64,1,4,4096]{3,2,1,0:T(4,128)(2,1)} %param.6) | data formatting | bytes 4194304 | tf_op jit(solution)/shard_map/reshape | solution.py:278
  9.8 2.6 collective-permute-start.15
  15.5 3.7 %collective-permute-start.3 = (s32[128]{0:T(128)S(1)}, s32[128]{0:T(128)S(1)}, u32[]{:S(2)}, u32[]{:S(2)}) collective-permute-start(s32[128]{0:T(128)S(1)} %pad_add_fusion.5), channel_id=1, source_target_pairs={{0,64},{32,96},{64,0},{96,32},{1,65},{33,97},{65,1},{97,33},{2,66}... | collective-permute-start | bytes 1544 | tf_op jit(solution)/shard_map/ppermute | solution.py:39
  19.2 6.5 %collective-permute-done.3 = s32[128]{0:T(128)S(1)} collective-permute-done((s32[128]{0:T(128)S(1)}, s32[128]{0:T(128)S(1)}, u32[]{:S(2)}, u32[]{:S(2)}) %collective-permute-start.3) | collective-permute-done | bytes 544 | tf_op jit(solution)/shard_map/ppermute | solution.py:39
  25.7 3.0 %gather_fusion.10 = bf16[4,4,128,128]{3,2,1,0:T(8,128)(2,1)} fusion(bf16[16,4,128,128]{3,2,1,0:T(8,128)(2,1)} %reshape.141, s32[1024]{0:T(1024)S(1)} %get-tuple-element.29), kind=kCustom, calls=%fused_computation.10 | custom fusion | bytes 1048592 | tf_op jit(solution)/shard_map/gather | solution.py:283
  28.7 3.0 %gather_fusion.7 = bf16[4,4,128,128]{3,2,1,0:T(8,128)(2,1)} fusion(bf16[16,4,128,128]{3,2,1,0:T(8,128)(2,1)} %reshape.141, s32[1024]{0:T(1024)S(1)} %get-tuple-element.27), kind=kCustom, calls=%fused_computation.7 | custom fusion | bytes 1048592 | tf_op jit(solution)/shard_map/gather | solution.py:283
  31.7 3.0 %gather_fusion.5 = bf16[4,4,128,128]{3,2,1,0:T(8,128)(2,1)} fusion(bf16[16,4,128,128]{3,2,1,0:T(8,128)(2,1)} %reshape.141, s32[1024]{0:T(1024)S(1)} %get-tuple-element.28), kind=kCustom, calls=%fused_computation.5 | custom fusion | bytes 1048592 | tf_op jit(solution)/shard_map/gather | solution.py:283
  34.7 3.0 %gather_fusion.1 = bf16[4,4,128,128]{3,2,1,0:T(8,128)(2,1)} fusion(bf16[16,4,128,128]{3,2,1,0:T(8,128)(2,1)} %reshape.141, s32[1024]{0:T(1024)S(1)} %get-tuple-element.30), kind=kCustom, calls=%fused_computation.1 | custom fusion | bytes 1048592 | tf_op jit(solution)/shard_map/gather | solution.py:283
  43.3 2.7 collective-permute-start.26
  54.0 3.9 %collective-permute-done.22 = s32[8,128]{1,0:T(8,128)S(1)} collective-permute-done((s32[8,128]{1,0:T(8,128)S(1)}, s32[8,128]{1,0:T(8,128)S(1)}, u32[]{:S(2)}, u32[]{:S(2)}) %collective-permute-start.22) | collective-permute-done | bytes 4128 | tf_op jit(solution)/shard_map/ppermute | solution.py:31
  61.2 3.0 %gather_fusion.6 = bf16[4,4,128,128]{3,2,1,0:T(8,128)(2,1)} fusion(bf16[16,4,128,128]{3,2,1,0:T(8,128)(2,1)} %collective-permute-done.5, s32[1024]{0:T(1024)S(1)} %get-tuple-element.28), kind=kCustom, calls=%fused_computation.6 | custom fusion | bytes 1048592 | tf_op jit(solution)/shard_map/gather | solution.py:283
  67.6 3.0 %gather_fusion.2 = bf16[4,4,128,128]{3,2,1,0:T(8,128)(2,1)} fusion(bf16[16,4,128,128]{3,2,1,0:T(8,128)(2,1)} %collective-permute-done.5, s32[1024]{0:T(1024)S(1)} %get-tuple-element.30), kind=kCustom, calls=%fused_computation.2 | custom fusion | bytes 1048592 | tf_op jit(solution)/shard_map/gather | solution.py:283
  70.6 7.3 %collective-permute-done.4 = s32[8,128]{1,0:T(8,128)S(1)} collective-permute-done((s32[8,128]{1,0:T(8,128)S(1)}, s32[8,128]{1,0:T(8,128)S(1)}, u32[]{:S(2)}, u32[]{:S(2)}) %collective-permute-start.4) | collective-permute-done | bytes 4128 | tf_op jit(solution)/shard_map/ppermute | solution.py:31
  80.2 2.5 collective-permute-start.6
  82.7 3.0 %gather_fusion.8 = bf16[4,4,128,128]{3,2,1,0:T(8,128)(2,1)} fusion(bf16[16,4,128,128]{3,2,1,0:T(8,128)(2,1)} %collective-permute-done.5, s32[1024]{0:T(1024)S(1)} %get-tuple-element.27), kind=kCustom, calls=%fused_computation.8 | custom fusion | bytes 1048592 | tf_op jit(solution)/shard_map/gather | solution.py:283
  90.9 8.2 %collective-permute-done.6 = bf16[2,2,4,128,128]{4,3,2,1,0:T(8,128)(2,1)} collective-permute-done((bf16[2,2,4,128,128]{4,3,2,1,0:T(8,128)(2,1)}, bf16[2,2,4,128,128]{4,3,2,1,0:T(8,128)(2,1)}, u32[]{:S(2)}, u32[]{:S(2)}) %collective-permute-start.6) | collective-permute-done | bytes 524320 | tf_op jit(solution)/shard_map/ppermute | solution.py:31
  104.8 3.0 %gather_fusion.11 = bf16[4,4,128,128]{3,2,1,0:T(8,128)(2,1)} fusion(bf16[16,4,128,128]{3,2,1,0:T(8,128)(2,1)} %collective-permute-done.5, s32[1024]{0:T(1024)S(1)} %get-tuple-element.29), kind=kCustom, calls=%fused_computation.11 | custom fusion | bytes 1048592 | tf_op jit(solution)/shard_map/gather | solution.py:283
  109.1 14.6 %panel_sums_first.1.refs_8_ = f32[4,8,32,16,128]{4,3,2,1,0:T(8,128)S(1)} custom-call(s32[128]{0:T(128)S(1)} %reshape.174.refs_0_, s32[512]{0:T(512)S(1)} %concatenate.48.refs_1_, bf16[4,2,4,128,128]{4,3,2,1,0:T(8,128)(2,1)S(1)} %pad_maximum_fusion.4.refs_2_, bf16[32,64,256]{2,1,0:T(8,128)(2,1)S(1)} %pad_maximum_fusion.1.refs_3_, ...), custom_call_target="tpu_custom_call" | custom-call | flops 268435456 | bytes 19922944 | tf_op jit(solution)/shard_map/panel_sums_first/pallas_call | solution.py:116
  123.7 3.3 %copy-done.2 = f32[4,8,32,16,128]{4,3,2,1,0:T(8,128)} copy-done((f32[4,8,32,16,128]{4,3,2,1,0:T(8,128)}, f32[4,8,32,16,128]{4,3,2,1,0:T(8,128)S(1)}, u32[]{:S(2)}) %copy-start.2) | copy-done | bytes 8388632
  127.0 23.9 %panel_sums_2.1.refs_5_ = f32[4,8,32,16,128]{4,3,2,1,0:T(8,128)} custom-call(s32[256]{0:T(256)S(1)} %pad_add_fusion.4.refs_0_, s32[1024]{0:T(1024)S(1)} %pad_add_fusion.1.refs_1_, bf16[4,2,4,128,128]{4,3,2,1,0:T(8,128)(2,1)} %collective-permute-done.23.refs_2_, bf16[4,2,4,128,128]{4,3,2,1,0:T(8,128)(2,1)} %collective-permute-done.24.refs_3_, ...), custom_call_target="tpu_custom_call" | custom-call | flops 536870912 | bytes 23068672 | tf_op jit(solution)/shard_map/panel_sums_2/pallas_call | solution.py:116
  152.2 17.7 %panel_sums_1.1.own = f32[4,8,32,16,128]{4,3,2,1,0:T(8,128)S(1)} custom-call(s32[128]{0:T(128)S(1)} %reshape.171.refs_0_, s32[512]{0:T(512)S(1)} %get-tuple-element.21.refs_1_, bf16[4,2,4,128,128]{4,3,2,1,0:T(8,128)(2,1)S(1)} %pad_maximum_fusion.refs_2_, bf16[32,64,256]{2,1,0:T(8,128)(2,1)} %collective-permute-done.14.refs_3_, ...), custom_call_target="tpu_custom_call" | custom-call | flops 268435456 | bytes 19922944 | tf_op jit(solution)/shard_map/panel_sums_1/pallas_call | solution.py:116
  172.0 5.3 %collective-permute-start.31 = (f32[4,32,16,128]{3,2,1,0:T(8,128)S(1)}, f32[4,32,16,128]{3,2,1,0:T(8,128)S(1)}, u32[]{:S(2)}, u32[]{:S(2)}) collective-permute-start(f32[4,32,16,128]{3,2,1,0:T(8,128)S(1)} %get-tuple-element.9), channel_id=1, source_target_pairs={{0,3},{1,0},{2,1},{3,2},{4,7},{5,4},{6,5},{7,6},{8,11},{9,8},{10,9... | collective-permute-start | bytes 3145736 | tf_op jit(solution)/shard_map/ppermute | solution.py:35
  177.3 2.7 collective-permute-start.29
  180.0 9.0 %collective-permute-done.31 = f32[4,32,16,128]{3,2,1,0:T(8,128)S(1)} collective-permute-done((f32[4,32,16,128]{3,2,1,0:T(8,128)S(1)}, f32[4,32,16,128]{3,2,1,0:T(8,128)S(1)}, u32[]{:S(2)}, u32[]{:S(2)}) %collective-permute-start.31) | collective-permute-done | bytes 1048608 | tf_op jit(solution)/shard_map/ppermute | solution.py:35
  189.1 3.4 %collective-permute-done.27 = f32[4,32,16,128]{3,2,1,0:T(8,128)S(1)} collective-permute-done((f32[4,32,16,128]{3,2,1,0:T(8,128)S(1)}, f32[4,32,16,128]{3,2,1,0:T(8,128)S(1)}, u32[]{:S(2)}, u32[]{:S(2)}) %collective-permute-start.27) | collective-permute-done | bytes 1048608 | tf_op jit(solution)/shard_map/ppermute | solution.py:35
  196.4 7.4 %collective-permute-done.30.high_p = f32[4,32,16,128]{3,2,1,0:T(8,128)S(1)} collective-permute-done((f32[4,32,16,128]{3,2,1,0:T(8,128)}, f32[4,32,16,128]{3,2,1,0:T(8,128)S(1)}, u32[]{:S(2)}, u32[]{:S(2)}) %collective-permute-start.30) | collective-permute-done | bytes 1048608 | tf_op jit(solution)/shard_map/ppermute | solution.py:35
  203.7 7.9 %collective-permute-done.32.high_m = f32[4,32,16,128]{3,2,1,0:T(8,128)S(1)} collective-permute-done((f32[4,32,16,128]{3,2,1,0:T(8,128)}, f32[4,32,16,128]{3,2,1,0:T(8,128)S(1)}, u32[]{:S(2)}, u32[]{:S(2)}) %collective-permute-start.32) | collective-permute-done | bytes 1048608 | tf_op jit(solution)/shard_map/ppermute | solution.py:35
  211.7 3.4 %collective-permute-done.28.low_p = f32[4,32,16,128]{3,2,1,0:T(8,128)} collective-permute-done((f32[4,32,16,128]{3,2,1,0:T(8,128)}, f32[4,32,16,128]{3,2,1,0:T(8,128)}, u32[]{:S(2)}, u32[]{:S(2)}) %collective-permute-start.28) | collective-permute-done | bytes 1048608 | tf_op jit(solution)/shard_map/ppermute | solution.py:35
  215.1 3.4 %copy-done.1 = f32[4,8,32,16,128]{4,3,2,1,0:T(8,128)S(1)} copy-done((f32[4,8,32,16,128]{4,3,2,1,0:T(8,128)S(1)}, f32[4,8,32,16,128]{4,3,2,1,0:T(8,128)}, u32[]{:S(2)}) %copy-start.1) | copy-done | bytes 8388632
  218.4 4.6 %pack.1 = s16[128,80,128]{2,1,0:T(8,128)(2,1)S(1)} custom-call(s32[256]{0:T(256)S(1)} %add_bitcast_fusion.slots, f32[4,8,32,16,128]{4,3,2,1,0:T(8,128)S(1)} %copy-done.1, f32[4,32,16,128]{3,2,1,0:T(8,128)} %collective-permute-done.28.low_p, f32[4,32,16,128]{3,2,1,0:T(8,128)S(1)} %collective-permute-done.29.low_m, ...), custom_call_target="tpu_custom_call" | custom-call | tf_op jit(solution)/shard_map/pack/pallas_call | solution.py:180
  223.0 43.5 %all_to_all.5 = s16[128,80,128]{2,1,0:T(8,128)(2,1)S(1)} all-to-all(s16[128,80,128]{2,1,0:T(8,128)(2,1)S(1)} %pack.1), channel_id=1, replica_groups=mesh['x'=4,'core'=2,'z'=4,'y'=4] {'x','core','z','y'}, dimensions={0} | all-to-all | bytes 5242880 | tf_op jit(solution)/shard_map/all_to_all | solution.py:304
  266.5 14.7 %unpack.1 = f32[256,4096]{1,0:T(8,128)} custom-call(s16[4,2,16,80,128]{4,3,2,1,0:T(8,128)(2,1)S(1)} %bitcast.79), custom_call_target="tpu_custom_call" | custom-call | tf_op jit(solution)/shard_map/unpack/pallas_call | solution.py:222
  (124 shorter events, 49.9 us)
Async XLA Ops:
  4.8 53.8 %collective-permute-start.5 = (bf16[16,4,128,128]{3,2,1,0:T(8,128)(2,1)}, bf16[16,4,128,128]{3,2,1,0:T(8,128)(2,1)}, u32[]{:S(2)}, u32[]{:S(2)}) collective-permute-start(bf16[16,4,128,128]{3,2,1,0:T(8,128)(2,1)} %reshape.141), channel_id=1, source_target_pairs={{0,16},{16,0},{1,17},{17,1},{2,18},{18,2},{3,19},{19,3},{4,20},{20... | collective-permute-start | bytes 6291464 | tf_op jit(solution)/shard_map/ppermute | solution.py:43
  9.8 36.9 %collective-permute-start.15 = (bf16[8,64,256]{2,1,0:T(8,128)(2,1)S(1)}, bf16[8,64,256]{2,1,0:T(8,128)(2,1)S(1)}, u32[]{:S(2)}, u32[]{:S(2)}) collective-permute-start(bf16[8,64,256]{2,1,0:T(8,128)(2,1)S(1)} %bitcast.90), channel_id=1, source_target_pairs={{0,96},{32,0},{64,32},{96,64},{1,97},{33,1},{65,33},{97,65},{2,98}... | collective-permute-start | bytes 786440 | tf_op jit(solution)/shard_map/ppermute | solution.py:39
  12.5 25.4 %collective-permute-start.11 = (bf16[8,64,256]{2,1,0:T(8,128)(2,1)S(1)}, bf16[8,64,256]{2,1,0:T(8,128)(2,1)}, u32[]{:S(2)}, u32[]{:S(2)}) collective-permute-start(bf16[8,64,256]{2,1,0:T(8,128)(2,1)S(1)} %bitcast.91), channel_id=1, source_target_pairs={{0,32},{32,64},{64,96},{96,0},{1,33},{33,65},{65,97},{97,1},{2,34}... | collective-permute-start | bytes 786440 | tf_op jit(solution)/shard_map/ppermute | solution.py:39
  13.3 1.6 collective-permute-start.10
  15.0 24.8 %collective-permute-start.12 = (bf16[8,64,256]{2,1,0:T(8,128)(2,1)S(1)}, bf16[8,64,256]{2,1,0:T(8,128)(2,1)S(1)}, u32[]{:S(2)}, u32[]{:S(2)}) collective-permute-start(bf16[8,64,256]{2,1,0:T(8,128)(2,1)S(1)} %collective-permute-done.10), channel_id=1, source_target_pairs={{0,32},{32,64},{64,96},{96,0},{1,33},{33,65},{65,97},{97,1},{2,34}... | collective-permute-start | bytes 786440 | tf_op jit(solution)/shard_map/ppermute | solution.py:39
  15.5 10.1 %collective-permute-start.3 = (s32[128]{0:T(128)S(1)}, s32[128]{0:T(128)S(1)}, u32[]{:S(2)}, u32[]{:S(2)}) collective-permute-start(s32[128]{0:T(128)S(1)} %pad_add_fusion.5), channel_id=1, source_target_pairs={{0,64},{32,96},{64,0},{96,32},{1,65},{33,97},{65,1},{97,33},{2,66}... | collective-permute-start | bytes 1544 | tf_op jit(solution)/shard_map/ppermute | solution.py:39
  25.7 21.6 %collective-permute-start.16 = (bf16[8,64,256]{2,1,0:T(8,128)(2,1)S(1)}, bf16[8,64,256]{2,1,0:T(8,128)(2,1)}, u32[]{:S(2)}, u32[]{:S(2)}) collective-permute-start(bf16[8,64,256]{2,1,0:T(8,128)(2,1)S(1)} %collective-permute-done.10), channel_id=1, source_target_pairs={{0,96},{32,0},{64,32},{96,64},{1,97},{33,1},{65,33},{97,65},{2,98}... | collective-permute-start | bytes 786440 | tf_op jit(solution)/shard_map/ppermute | solution.py:39
  37.8 3.0 %collective-permute-start.2 = (s32[128]{0:T(128)S(1)}, s32[128]{0:T(128)S(1)}, u32[]{:S(2)}, u32[]{:S(2)}) collective-permute-start(s32[128]{0:T(128)S(1)} %pad_add_fusion.5), channel_id=1, source_target_pairs={{0,96},{32,0},{64,32},{96,64},{1,97},{33,1},{65,33},{97,65},{2,98}... | collective-permute-start | bytes 1544 | tf_op jit(solution)/shard_map/ppermute | solution.py:39
  39.7 3.6 %collective-permute-start.1 = (s32[128]{0:T(128)S(1)}, s32[128]{0:T(128)S(1)}, u32[]{:S(2)}, u32[]{:S(2)}) collective-permute-start(s32[128]{0:T(128)S(1)} %pad_add_fusion.5), channel_id=1, source_target_pairs={{0,32},{32,64},{64,96},{96,0},{1,33},{33,65},{65,97},{97,1},{2,34}... | collective-permute-start | bytes 1544 | tf_op jit(solution)/shard_map/ppermute | solution.py:39
  40.8 7.7 %collective-permute-start.17 = (bf16[8,64,256]{2,1,0:T(8,128)(2,1)}, bf16[8,64,256]{2,1,0:T(8,128)(2,1)}, u32[]{:S(2)}, u32[]{:S(2)}) collective-permute-start(bf16[8,64,256]{2,1,0:T(8,128)(2,1)} %collective-permute-done.11), channel_id=1, source_target_pairs={{0,32},{32,64},{64,96},{96,0},{1,33},{33,65},{65,97},{97,1},{2,34}... | collective-permute-start | bytes 786440 | tf_op jit(solution)/shard_map/ppermute | solution.py:39
  43.3 36.9 %collective-permute-start.26 = (bf16[32,64,256]{2,1,0:T(8,128)(2,1)S(1)}, bf16[32,64,256]{2,1,0:T(8,128)(2,1)S(1)}, u32[]{:S(2)}, u32[]{:S(2)}) collective-permute-start(bf16[32,64,256]{2,1,0:T(8,128)(2,1)S(1)} %pad_maximum_fusion.1.refs_3_), channel_id=1, source_target_pairs={{0,12},{1,13},{2,14},{3,15},{4,0},{5,1},{6,2},{7,3},{8,4},{9,5},{1... | collective-permute-start | bytes 3145736 | tf_op jit(solution)/shard_map/ppermute | solution.py:31
  46.7 11.1 %collective-permute-start.22 = (s32[8,128]{1,0:T(8,128)S(1)}, s32[8,128]{1,0:T(8,128)S(1)}, u32[]{:S(2)}, u32[]{:S(2)}) collective-permute-start(s32[8,128]{1,0:T(8,128)S(1)} %bitcast.98), channel_id=1, source_target_pairs={{0,12},{1,13},{2,14},{3,15},{4,0},{5,1},{6,2},{7,3},{8,4},{9,5},{1... | collective-permute-start | bytes 12296 | tf_op jit(solution)/shard_map/ppermute | solution.py:31
  47.2 5.7 %collective-permute-start.18 = (bf16[8,64,256]{2,1,0:T(8,128)(2,1)}, bf16[8,64,256]{2,1,0:T(8,128)(2,1)S(1)}, u32[]{:S(2)}, u32[]{:S(2)}) collective-permute-start(bf16[8,64,256]{2,1,0:T(8,128)(2,1)} %collective-permute-done.16), channel_id=1, source_target_pairs={{0,96},{32,0},{64,32},{96,64},{1,97},{33,1},{65,33},{97,65},{2,98}... | collective-permute-start | bytes 786440 | tf_op jit(solution)/shard_map/ppermute | solution.py:39
  48.6 15.6 %collective-permute-start.21 = (s32[8,128]{1,0:T(8,128)S(1)}, s32[8,128]{1,0:T(8,128)S(1)}, u32[]{:S(2)}, u32[]{:S(2)}) collective-permute-start(s32[8,128]{1,0:T(8,128)S(1)} %bitcast.99), channel_id=1, source_target_pairs={{0,4},{1,5},{2,6},{3,7},{4,8},{5,9},{6,10},{7,11},{8,12},{9,13},{1... | collective-permute-start | bytes 12296 | tf_op jit(solution)/shard_map/ppermute | solution.py:31
  52.9 32.8 %collective-permute-start.13 = (bf16[32,64,256]{2,1,0:T(8,128)(2,1)S(1)}, bf16[32,64,256]{2,1,0:T(8,128)(2,1)}, u32[]{:S(2)}, u32[]{:S(2)}) collective-permute-start(bf16[32,64,256]{2,1,0:T(8,128)(2,1)S(1)} %pad_maximum_fusion.1.refs_3_), channel_id=1, source_target_pairs={{0,4},{1,5},{2,6},{3,7},{4,8},{5,9},{6,10},{7,11},{8,12},{9,13},{1... | collective-permute-start | bytes 3145736 | tf_op jit(solution)/shard_map/ppermute | solution.py:31
  57.8 30.4 %collective-permute-start.25 = (bf16[32,64,256]{2,1,0:T(8,128)(2,1)S(1)}, bf16[32,64,256]{2,1,0:T(8,128)(2,1)}, u32[]{:S(2)}, u32[]{:S(2)}) collective-permute-start(bf16[32,64,256]{2,1,0:T(8,128)(2,1)S(1)} %constant_dynamic-update-slice_fusion.refs_4_), channel_id=1, source_target_pairs={{0,4},{1,5},{2,6},{3,7},{4,8},{5,9},{6,10},{7,11},{8,12},{9,13},{1... | collective-permute-start | bytes 3145736 | tf_op jit(solution)/shard_map/ppermute | solution.py:31
  58.6 30.9 %collective-permute-start.19 = (bf16[32,64,256]{2,1,0:T(8,128)(2,1)S(1)}, bf16[32,64,256]{2,1,0:T(8,128)(2,1)}, u32[]{:S(2)}, u32[]{:S(2)}) collective-permute-start(bf16[32,64,256]{2,1,0:T(8,128)(2,1)S(1)} %constant_dynamic-update-slice_fusion.refs_4_), channel_id=1, source_target_pairs={{0,12},{1,13},{2,14},{3,15},{4,0},{5,1},{6,2},{7,3},{8,4},{9,5},{1... | collective-permute-start | bytes 3145736 | tf_op jit(solution)/shard_map/ppermute | solution.py:31
  64.2 13.8 %collective-permute-start.4 = (s32[8,128]{1,0:T(8,128)S(1)}, s32[8,128]{1,0:T(8,128)S(1)}, u32[]{:S(2)}, u32[]{:S(2)}) collective-permute-start(s32[8,128]{1,0:T(8,128)S(1)} %bitcast.100), channel_id=1, source_target_pairs={{0,8},{1,9},{2,10},{3,11},{4,12},{5,13},{6,14},{7,15},{8,0},{9,1},... | collective-permute-start | bytes 12296 | tf_op jit(solution)/shard_map/ppermute | solution.py:31
  78.0 24.8 %collective-permute-start.23 = (bf16[4,2,4,128,128]{4,3,2,1,0:T(8,128)(2,1)}, bf16[4,2,4,128,128]{4,3,2,1,0:T(8,128)(2,1)}, u32[]{:S(2)}, u32[]{:S(2)}) collective-permute-start(bf16[4,2,4,128,128]{4,3,2,1,0:T(8,128)(2,1)} %pad_maximum_fusion.2), channel_id=1, source_target_pairs={{0,4},{1,5},{2,6},{3,7},{4,8},{5,9},{6,10},{7,11},{8,12},{9,13},{1... | collective-permute-start | bytes 3145736 | tf_op jit(solution)/shard_map/ppermute | solution.py:31
  80.2 18.8 %collective-permute-start.6 = (bf16[2,2,4,128,128]{4,3,2,1,0:T(8,128)(2,1)}, bf16[2,2,4,128,128]{4,3,2,1,0:T(8,128)(2,1)}, u32[]{:S(2)}, u32[]{:S(2)}) collective-permute-start(bf16[2,2,4,128,128]{4,3,2,1,0:T(8,128)(2,1)} %get-tuple-element.15), channel_id=1, source_target_pairs={{0,4},{1,5},{2,6},{3,7},{4,8},{5,9},{6,10},{7,11},{8,12},{9,13},{1... | collective-permute-start | bytes 1572872 | tf_op jit(solution)/shard_map/ppermute | solution.py:31
  85.7 16.0 %collective-permute-start.8 = (bf16[2,2,4,128,128]{4,3,2,1,0:T(8,128)(2,1)}, bf16[2,2,4,128,128]{4,3,2,1,0:T(8,128)(2,1)}, u32[]{:S(2)}, u32[]{:S(2)}) collective-permute-start(bf16[2,2,4,128,128]{4,3,2,1,0:T(8,128)(2,1)} %get-tuple-element.16), channel_id=1, source_target_pairs={{0,12},{1,13},{2,14},{3,15},{4,0},{5,1},{6,2},{7,3},{8,4},{9,5},{1... | collective-permute-start | bytes 1572872 | tf_op jit(solution)/shard_map/ppermute | solution.py:31
  88.2 64.0 %collective-permute-start.14 = (bf16[32,64,256]{2,1,0:T(8,128)(2,1)}, bf16[32,64,256]{2,1,0:T(8,128)(2,1)}, u32[]{:S(2)}, u32[]{:S(2)}) collective-permute-start(bf16[32,64,256]{2,1,0:T(8,128)(2,1)} %collective-permute-done.13.refs_4_), channel_id=1, source_target_pairs={{0,4},{1,5},{2,6},{3,7},{4,8},{5,9},{6,10},{7,11},{8,12},{9,13},{1... | collective-permute-start | bytes 3145736 | tf_op jit(solution)/shard_map/ppermute | solution.py:31
  89.5 62.7 %collective-permute-start.20 = (bf16[32,64,256]{2,1,0:T(8,128)(2,1)}, bf16[32,64,256]{2,1,0:T(8,128)(2,1)}, u32[]{:S(2)}, u32[]{:S(2)}) collective-permute-start(bf16[32,64,256]{2,1,0:T(8,128)(2,1)} %collective-permute-done.19.refs_7_), channel_id=1, source_target_pairs={{0,12},{1,13},{2,14},{3,15},{4,0},{5,1},{6,2},{7,3},{8,4},{9,5},{1... | collective-permute-start | bytes 3145736 | tf_op jit(solution)/shard_map/ppermute | solution.py:31
  99.1 27.9 %collective-permute-start.24 = (bf16[4,2,4,128,128]{4,3,2,1,0:T(8,128)(2,1)}, bf16[4,2,4,128,128]{4,3,2,1,0:T(8,128)(2,1)}, u32[]{:S(2)}, u32[]{:S(2)}) collective-permute-start(bf16[4,2,4,128,128]{4,3,2,1,0:T(8,128)(2,1)} %pad_maximum_fusion.3), channel_id=1, source_target_pairs={{0,12},{1,13},{2,14},{3,15},{4,0},{5,1},{6,2},{7,3},{8,4},{9,5},{1... | collective-permute-start | bytes 3145736 | tf_op jit(solution)/shard_map/ppermute | solution.py:31
  101.7 49.2 %collective-permute-start.7 = (bf16[2,2,4,128,128]{4,3,2,1,0:T(8,128)(2,1)}, bf16[2,2,4,128,128]{4,3,2,1,0:T(8,128)(2,1)}, u32[]{:S(2)}, u32[]{:S(2)}) collective-permute-start(bf16[2,2,4,128,128]{4,3,2,1,0:T(8,128)(2,1)} %collective-permute-done.6), channel_id=1, source_target_pairs={{0,4},{1,5},{2,6},{3,7},{4,8},{5,9},{6,10},{7,11},{8,12},{9,13},{1... | collective-permute-start | bytes 1572872 | tf_op jit(solution)/shard_map/ppermute | solution.py:31
  102.8 48.1 %collective-permute-start.9 = (bf16[2,2,4,128,128]{4,3,2,1,0:T(8,128)(2,1)}, bf16[2,2,4,128,128]{4,3,2,1,0:T(8,128)(2,1)}, u32[]{:S(2)}, u32[]{:S(2)}) collective-permute-start(bf16[2,2,4,128,128]{4,3,2,1,0:T(8,128)(2,1)} %collective-permute-done.8), channel_id=1, source_target_pairs={{0,12},{1,13},{2,14},{3,15},{4,0},{5,1},{6,2},{7,3},{8,4},{9,5},{1... | collective-permute-start | bytes 1572872 | tf_op jit(solution)/shard_map/ppermute | solution.py:31
  172.0 17.1 %collective-permute-start.31 = (f32[4,32,16,128]{3,2,1,0:T(8,128)S(1)}, f32[4,32,16,128]{3,2,1,0:T(8,128)S(1)}, u32[]{:S(2)}, u32[]{:S(2)}) collective-permute-start(f32[4,32,16,128]{3,2,1,0:T(8,128)S(1)} %get-tuple-element.9), channel_id=1, source_target_pairs={{0,3},{1,0},{2,1},{3,2},{4,7},{5,4},{6,5},{7,6},{8,11},{9,8},{10,9... | collective-permute-start | bytes 3145736 | tf_op jit(solution)/shard_map/ppermute | solution.py:35
  177.3 15.2 %collective-permute-start.27 = (f32[4,32,16,128]{3,2,1,0:T(8,128)S(1)}, f32[4,32,16,128]{3,2,1,0:T(8,128)S(1)}, u32[]{:S(2)}, u32[]{:S(2)}) collective-permute-start(f32[4,32,16,128]{3,2,1,0:T(8,128)S(1)} %get-tuple-element.12), channel_id=1, source_target_pairs={{0,1},{1,2},{2,3},{3,0},{4,5},{5,6},{6,7},{7,4},{8,9},{9,10},{10,1... | collective-permute-start | bytes 3145736 | tf_op jit(solution)/shard_map/ppermute | solution.py:35
  177.3 26.4 %collective-permute-start.30 = (f32[4,32,16,128]{3,2,1,0:T(8,128)}, f32[4,32,16,128]{3,2,1,0:T(8,128)S(1)}, u32[]{:S(2)}, u32[]{:S(2)}) collective-permute-start(f32[4,32,16,128]{3,2,1,0:T(8,128)} %get-tuple-element.10), channel_id=1, source_target_pairs={{0,1},{1,2},{2,3},{3,0},{4,5},{5,6},{6,7},{7,4},{8,9},{9,10},{10,1... | collective-permute-start | bytes 3145736 | tf_op jit(solution)/shard_map/ppermute | solution.py:35
  177.3 26.4 %collective-permute-start.29 = (f32[4,32,16,128]{3,2,1,0:T(8,128)}, f32[4,32,16,128]{3,2,1,0:T(8,128)S(1)}, u32[]{:S(2)}, u32[]{:S(2)}) collective-permute-start(f32[4,32,16,128]{3,2,1,0:T(8,128)} %get-tuple-element.11), channel_id=1, source_target_pairs={{0,3},{1,0},{2,1},{3,2},{4,7},{5,4},{6,5},{7,6},{8,11},{9,8},{10,9... | collective-permute-start | bytes 3145736 | tf_op jit(solution)/shard_map/ppermute | solution.py:35
  194.2 17.4 %collective-permute-start.32 = (f32[4,32,16,128]{3,2,1,0:T(8,128)}, f32[4,32,16,128]{3,2,1,0:T(8,128)S(1)}, u32[]{:S(2)}, u32[]{:S(2)}) collective-permute-start(f32[4,32,16,128]{3,2,1,0:T(8,128)} %get-tuple-element.7), channel_id=1, source_target_pairs={{0,3},{1,0},{2,1},{3,2},{4,7},{5,4},{6,5},{7,6},{8,11},{9,8},{10,9... | collective-permute-start | bytes 3145736 | tf_op jit(solution)/shard_map/ppermute | solution.py:35
  194.3 20.8 %collective-permute-start.28 = (f32[4,32,16,128]{3,2,1,0:T(8,128)}, f32[4,32,16,128]{3,2,1,0:T(8,128)}, u32[]{:S(2)}, u32[]{:S(2)}) collective-permute-start(f32[4,32,16,128]{3,2,1,0:T(8,128)} %get-tuple-element.8), channel_id=1, source_target_pairs={{0,1},{1,2},{2,3},{3,0},{4,5},{5,6},{6,7},{7,4},{8,9},{9,10},{10,1... | collective-permute-start | bytes 3145736 | tf_op jit(solution)/shard_map/ppermute | solution.py:35
  (9 other events, 50.1 us)

commit v3 on v2

v3 whole, which is shorter than its diff:
```python
import jax
import jax.numpy as jnp
from jax import lax
from jax.experimental import pallas as pl
from jax.experimental.pallas import tpu as pltpu
from jax.sharding import Mesh, PartitionSpec as P

B = 64
HALF = 32
NCW = 32
SK = 4
SP = 8
X, C, Z, Y = 4, 2, 4, 4
ALL = ("x", "core", "z", "y")
PLANE = ("core", "z", "y")
TOP = 32766.0
MSG = 80


def lines(along):
    groups = []
    for c in range(C):
        for fixed in range(4):
            on_z = (c ^ along) == 0
            groups.append([(c * Z + (i if on_z else fixed)) * Y + (fixed if on_z else i) for i in range(4)])
    return groups


LINE, CROSS = lines(0), lines(1)


def over_line(v, step):
    pairs = [(group[i], group[(i + step) % 4]) for group in LINE for i in range(4)]
    return lax.ppermute(v, PLANE, pairs)


def over_x(v, step):
    return lax.ppermute(v, "x", [(i, (i + step) % X) for i in range(X)])


def over_core(v):
    return lax.ppermute(v, "core", [(0, 1), (1, 0)])


def regroup_kernel(core, mine, other, o_ref, sems):
    swapped = core[0] == 1
    copies = []
    for z in range(Z):
        for y in range(Y):
            t, o = jnp.where(swapped, y, z), jnp.where(swapped, z, y)
            for m, src in enumerate((mine, other)):
                copies.append(pltpu.make_async_copy(src.at[z * Y + y], o_ref.at[t, m, o], sems.at[len(copies)]))
    for copy in copies:
        copy.start()
    for copy in copies:
        copy.wait()


def regroup(core, mine, other):
    any_spec = pl.BlockSpec(memory_space=pl.ANY)
    return pl.pallas_call(
        regroup_kernel,
        grid_spec=pltpu.PrefetchScalarGridSpec(
            num_scalar_prefetch=1, grid=(1,), in_specs=[any_spec] * 2, out_specs=any_spec,
            scratch_shapes=[pltpu.SemaphoreType.DMA((32,))],
        ),
        out_shape=jax.ShapeDtypeStruct((4, 2, 4, 4, 128, 128), jnp.bfloat16),
        name="regroup",
    )(core, mine, other)


def encode(values, o_ref, at, write_code):
    top = jnp.zeros((16, 128), jnp.float32)
    for j in range(NCW):
        top = jnp.maximum(top, jnp.abs(values[j]))
    top = jnp.maximum(jnp.max(top, axis=0, keepdims=True), 2.0 ** -110)
    code = jnp.floor(jnp.log2(top) * 256.0) + 1.0
    scale = jnp.broadcast_to(jnp.exp2(code * (-1.0 / 256.0)) * TOP, (16, 128))
    write_code(jnp.broadcast_to(code.astype(jnp.int32), (16, 128)))
    for j in range(NCW):
        q = jnp.floor(values[j] * scale + 0.5).astype(jnp.int32).astype(jnp.int16)
        o_ref[at(j)] = q


def decoded_scale(code):
    return jnp.exp2(code.astype(jnp.int32).astype(jnp.float32) * (1.0 / 256.0)) * (1.0 / TOP)


def panel_kernel(n, first, kcol, jcol, place, *refs):
    kohn, panels, refs = refs[:n], refs[n], refs[n + 1:]
    if not first:
        p_ref, refs = refs[0], refs[1:]
    o_ref, dens, sems, acc = refs
    step = pl.program_id(0)

    @pl.when(step == 0)
    def _():
        copies = []
        for s in range(n):
            src = panels if first else panels.at[(place[0] + 1 + s) % 4]
            copies.append(pltpu.make_async_copy(src, dens.at[pl.ds(s * 64, 64)], sems.at[s]))
        for copy in copies:
            copy.start()
        for copy in copies:
            copy.wait()

    low = (lax.broadcasted_iota(jnp.int32, (32, 128), 1) < 64).astype(jnp.float32).astype(jnp.bfloat16)
    high = 1 - low
    zero = jnp.zeros((128, 128), jnp.bfloat16)

    def twice(blk):
        turned = jnp.concatenate([blk[:, B:], blk[:, :B]], axis=1)
        return jnp.concatenate([blk * low, turned * low, turned * high, blk * high], axis=0)

    def product(row, s, a):
        ks, weights = [], []
        for i in range(2):
            ks.append(kcol[((s * 4 + step) * 8 + row) * SK + a + i] + 64 * s)
            weights.append(twice(kohn[s][0, row // 4, 0, row % 4, (a + i) * 32:(a + i + 1) * 32, :]))
        left = jnp.concatenate([dens[ks[0]], dens[ks[1]]], axis=1)
        right = jnp.concatenate([
            jnp.concatenate([weights[0], zero], axis=1), jnp.concatenate([zero, weights[1]], axis=1)
        ], axis=0)
        r = lax.dot_general(left, right, (((1,), (1,)), ((), ())), preferred_element_type=jnp.float32)
        return ks, r

    def add(sums, ks, r):
        for i in range(2):
            js = [jcol[ks[i] * SP + b] for b in range(SP)]
            old = [sums[j] for j in js]
            for b in range(SP):
                sums[js[b]] = old[b] + r[b * 16:(b + 1) * 16, i * 128:(i + 1) * 128]

    todo = [(s, a) for s in range(n) for a in range(0, SK, 2)]

    def some_rows(row, _):
        rows = [row * 2, row * 2 + 1] if first else [row]
        work = [(q, r, s, a) for q, r in enumerate(rows) for s, a in todo]
        sums = []
        for q, r in enumerate(rows):
            if first:
                o_ref[0, r] = jnp.zeros((NCW, 16, 128), jnp.float32)
                sums.append(o_ref.at[0, r])
            else:
                acc[...] = p_ref[0, r]
                sums.append(acc)
        held = [product(*work[i][1:]) for i in range(2)]
        for i in range(len(work)):
            if i + 2 < len(work):
                held.append(product(*work[i + 2][1:]))
            add(sums[work[i][0]], *held[i])
        if not first:
            def write_code(code):
                o_ref[0, row, NCW] = code.astype(jnp.int16)

            encode(acc, o_ref, lambda j: (0, row, j), write_code)
        return 0

    lax.fori_loop(0, 4 if first else 8, some_rows, 0)


def panel_sums(kcol, jcol, place, kohn, panels, sums):
    first = sums is None
    n = 1 if first else 3
    offset = 0 if first else 1

    def k_spec(s):
        return pl.BlockSpec(
            (1, 2, 1, 4, 128, 128), lambda o, kcol, jcol, place: ((place[0] + s + offset) % 4, 0, o, 0, 0, 0)
        )

    s_spec = pl.BlockSpec((1, 8, NCW, 16, 128), lambda o, *_: (o, 0, 0, 0, 0))
    q_spec = pl.BlockSpec((1, 8, NCW + 1, 16, 128), lambda o, *_: (o, 0, 0, 0, 0))
    any_spec = pl.BlockSpec(memory_space=pl.ANY)
    if first:
        out_spec, out_shape = s_spec, jax.ShapeDtypeStruct((4, 8, NCW, 16, 128), jnp.float32)
    else:
        out_spec, out_shape = q_spec, jax.ShapeDtypeStruct((4, 8, NCW + 1, 16, 128), jnp.int16)
    return pl.pallas_call(
        lambda *refs: panel_kernel(n, first, *refs),
        grid_spec=pltpu.PrefetchScalarGridSpec(
            num_scalar_prefetch=3,
            grid=(4,),
            in_specs=[k_spec(s) for s in range(n)] + [any_spec] + [s_spec] * (not first),
            out_specs=out_spec,
            scratch_shapes=[
                pltpu.VMEM((n * 64, 128, 128), jnp.bfloat16),
                pltpu.SemaphoreType.DMA((n,)),
                pltpu.VMEM((NCW, 16, 128), jnp.float32),
            ],
        ),
        out_shape=out_shape,
        compiler_params=pltpu.CompilerParams(vmem_limit_bytes=40 << 20),
        cost_estimate=pl.CostEstimate(
            flops=2 * n * 128 * 128 * 128 * 128, bytes_accessed=(3 * n + 12) << 20, transcendentals=0
        ),
        name="own_panel" if first else "other_panels",
    )(kcol, jcol, place, *([kohn] * n), panels, *(() if first else (sums,)))


def pack_kernel(slots, r_ref, o_ref, total, codes):
    rows = lax.broadcasted_iota(jnp.int32, (16, 128), 0)
    lane = lax.broadcasted_iota(jnp.int32, (16, 128), 1)

    def clear(n, _):
        for m in range(4):
            o_ref[n * 4 + m] = jnp.zeros((MSG, 128), jnp.int16)
            codes[n * 4 + m] = jnp.zeros((16, 128), jnp.int32)
        return 0

    lax.fori_loop(0, 32, clear, 0)

    def one(row, _):
        scales = [decoded_scale(r_ref[src, row, NCW]) for src in range(4)]
        for group in range(NCW // 8):
            blocks = []
            for j in range(group * 8, group * 8 + 8):
                g = [r_ref[src, row, j].astype(jnp.int32).astype(jnp.float32) * scales[src] for src in range(4)]
                blocks.append((g[0] + g[1]) + (g[2] + g[3]))
            turned = jnp.concatenate(blocks, axis=0).T
            v = []
            for q in range(8):
                par, mh, zh = q // 4, (q // 2) % 2, q % 2
                at = (zh * 4 + par * 2 + mh) * 16
                v.append(turned[at:at + 16, :])
            for bit in (4, 2, 1):
                keep = (lane & (16 * bit)) == 0
                w = [None] * 8
                for i in range(8):
                    if not i & bit:
                        lo, hi = v[i], v[i | bit]
                        w[i] = jnp.where(keep, lo, pltpu.roll(hi, 16 * bit, 1))
                        w[i | bit] = jnp.where(keep, pltpu.roll(lo, 128 - 16 * bit, 1), hi)
                v = w
            for j in range(8):
                total[group * 8 + j] = v[j]

        def where_to(j):
            slot = slots[row * NCW + j]
            return slot // 4, pl.ds(pl.multiple_of((slot % 4) * 16, 16), 16), slice(None)

        def write_code(code):
            for j in range(NCW):
                slot = slots[row * NCW + j]
                codes[slot // 4] = jnp.where(rows == slot % 4, code, codes[slot // 4])

        encode(total, o_ref, where_to, write_code)
        return 0

    lax.fori_loop(0, 8, one, 0)

    def finish(n, _):
        for m in range(4):
            o_ref[n * 4 + m, 64:80, :] = codes[n * 4 + m].astype(jnp.int16)
        return 0

    lax.fori_loop(0, 32, finish, 0)


def pack(slots, parts):
    return pl.pallas_call(
        pack_kernel,
        grid_spec=pltpu.PrefetchScalarGridSpec(
            num_scalar_prefetch=1,
            grid=(1,),
            in_specs=[
                pl.BlockSpec((4, 8, NCW + 1, 16, 128), lambda i, *_: (0, 0, 0, 0, 0), pipeline_mode=pl.Buffered(1))
            ],
            out_specs=pl.BlockSpec((128, MSG, 128), lambda i, *_: (0, 0, 0), pipeline_mode=pl.Buffered(1)),
            scratch_shapes=[pltpu.VMEM((NCW, 16, 128), jnp.float32), pltpu.VMEM((128, 16, 128), jnp.int32)],
        ),
        out_shape=jax.ShapeDtypeStruct((128, MSG, 128), jnp.int16),
        compiler_params=pltpu.CompilerParams(vmem_limit_bytes=32 << 20),
        name="pack",
    )(slots, parts)


def unpack_kernel(r_ref, o_ref, full):
    low32 = (lax.broadcasted_iota(jnp.int32, (16, 128), 1) & 32) == 0
    for s in range(2):
        def one(n, _):
            scales = [decoded_scale(r_ref[0, c, n, 64:80, :]) for c in range(2)]
            for t in range(2):
                h = []
                for c in range(2):
                    at = (s * 2 + t) * 16
                    q = r_ref[0, c, n, at:at + 16, :].astype(jnp.int32).astype(jnp.float32)
                    h.append(q * scales[c][s * 2 + t:s * 2 + t + 1, :])
                base = pl.multiple_of(((s * 16 + n) * 2 + t) * 32, 32)
                full[pl.ds(base, 16), :] = jnp.where(low32, h[0], pltpu.roll(h[1], 32, 1))
                full[pl.ds(base + 16, 16), :] = jnp.where(low32, pltpu.roll(h[0], 96, 1), h[1])
            return 0

        lax.fori_loop(0, 16, one, 0, unroll=4)
    for p in range(32):
        o_ref[:, p * 128:(p + 1) * 128] = full[pl.ds(p, 64, stride=32), :]


def unpack(received):
    return pl.pallas_call(
        unpack_kernel,
        grid=(X,),
        in_specs=[pl.BlockSpec((1, C, 16, MSG, 128), lambda x: (x, 0, 0, 0, 0))],
        out_specs=pl.BlockSpec((64, 4096), lambda x: (x, 0)),
        out_shape=jax.ShapeDtypeStruct((256, 4096), jnp.float32),
        scratch_shapes=[pltpu.VMEM((64 * 32, 128), jnp.float32)],
        compiler_params=pltpu.CompilerParams(vmem_limit_bytes=32 << 20),
        name="unpack",
    )(received)


def local(kohn_blocks, kohn_columns, density_blocks, density_columns, owner_map):
    x, c = lax.axis_index("x"), lax.axis_index("core")
    z, y = lax.axis_index("z"), lax.axis_index("y")
    on_line = jnp.where(c == 0, z, y)
    place = on_line.reshape(1)
    four = jnp.arange(4, dtype=jnp.int32)

    halves = density_blocks.reshape(8, SP, B, C, 2, 16).transpose(3, 0, 1, 5, 4, 2).reshape(C, 8, 128, 128)
    mine = lax.dynamic_index_in_dim(halves, c, 0, keepdims=False)
    theirs = over_core(lax.dynamic_index_in_dim(halves, 1 - c, 0, keepdims=False))
    panel = lax.all_gather(jnp.concatenate([mine, theirs]), "x", axis=0, tiled=True)
    panels = lax.all_gather(panel, PLANE, axis_index_groups=LINE)

    ints = jnp.concatenate([kohn_columns.reshape(-1), density_columns.reshape(-1), owner_map.reshape(-1)])
    other = over_core(ints)
    columns = jnp.concatenate([ints[256:320], other[256:320]])
    columns = jnp.stack([columns, over_x(columns, -1), over_x(columns, 2), over_x(columns, 1)])
    columns = columns[(four - x) & 3].reshape(-1)
    words = jnp.concatenate([columns, ints[:256], other[:256]]).reshape(8, 128)
    words = [words, over_line(words, -1), over_line(words, 2), over_line(words, 1)]

    def indices(word):
        word = word.reshape(-1)
        rows = jnp.where(c == 0, on_line * Y + four, four * Y + on_line)
        k = word[512:].reshape(2, 16, 4, SK)[:, rows].transpose(1, 0, 2, 3).reshape(-1)
        return k ^ (8 * c), word[:512]

    kcols, jcols = zip(*[indices(word) for word in words])

    owners = jnp.stack([ints[320:], other[320:]])
    hit = (owners[..., None] == jnp.arange(128, dtype=jnp.int32)).astype(jnp.int32)
    ranks = jnp.sum(jnp.cumsum(hit, axis=1) * hit, axis=2) - 1
    source = jnp.arange(2, dtype=jnp.int32)[:, None] ^ c
    slots = (owners * 4 + source * 2 + ranks).reshape(-1)

    kohn = kohn_blocks.reshape(16, 4, SK * 32, 128)
    kohn = regroup(c.reshape(1), kohn, over_core(kohn))
    kohn_line = lax.all_to_all(kohn, PLANE, 0, 0, axis_index_groups=LINE, tiled=True)

    sums = panel_sums(kcols[0], jcols[0], place, kohn, panel, None)
    sums = panel_sums(jnp.concatenate(kcols[1:]), jnp.concatenate(jcols[1:]), place, kohn_line, panels, sums)
    parts = lax.all_to_all(sums, PLANE, 0, 0, axis_index_groups=CROSS, tiled=True)
    outgoing = pack(slots, parts)
    received = lax.all_to_all(outgoing, ALL, split_axis=0, concat_axis=0, tiled=True)
    return unpack(received.reshape(X, C, 16, MSG, 128))


def solution(mesh):
    grid = Mesh(mesh.devices.reshape(X, C, Z, Y), ALL)
    row, col = ("x", "core"), ("z", "y")
    return jax.shard_map(
        local,
        mesh=grid,
        in_specs=(
            P(row, col, None, None),
            P(row, col, None),
            P(col, row, None, None),
            P(col, row, None),
            P(ALL, None),
        ),
        out_specs=P(ALL, None),
        check_vma=False,
    )
```

time: 282 us -> 367 us (1.30)
  Pallas kernels: 75.5 us -> 180 us
  starting transfers between devices: 39.8 us -> 19.4 us
  waiting for transfers between devices: 62 us -> 82.2 us
  local copies, waits for them, and re-layouts: 47 us -> 29.1 us
  between operations: 0.37 us -> 13.7 us
  other arithmetic: 13.1 us -> 1.64 us
    pallas_call x0 -> x1, Pallas kernels: none -> 128 us  [regroup(): pl.pallas_call(regroup_kernel, grid_spec=pltpu.PrefetchScalarGridSpec(num...]
    ppermute x21 -> x3, waiting for transfers between devices: 50.5 us -> 13.4 us  [over_line(): return lax.ppermute(v, PLANE, pairs)]
    all_gather x0 -> x2, waiting for transfers between devices: none -> 33.1 us  [the longest x1 33.1 us: local(): lax.all_gather(jnp.concatenate([mine, theirs]), 'x', axis=0, tiled=True)]
    all_to_all x0 -> x2, waiting for transfers between devices: none -> 27 us  [the longest x1 27 us: local(): lax.all_to_all(sums, PLANE, 0, 0, axis_index_groups=CROSS, tiled=True)]
    gather x12 -> x5, local copies, waits for them, and re-layouts: 26.3 us -> 2.87 us  [the longest x4 2.31 us: indices(): word[512:].reshape(2, 16, 4, SK)[:, rows].transpose(1, 0, 2, 3).reshape(-1)]
    ppermute x21 -> x3, starting transfers between devices: 27.6 us -> 4.48 us  [over_line(): return lax.ppermute(v, PLANE, pairs)]
    pallas_call x3 -> x2, Pallas kernels: 56.2 us -> 34.2 us  [panel_sums(): pl.pallas_call(lambda *refs: panel_kernel(n, first, *refs), grid_spec=plt...]
    all_to_all x0 -> x2, starting transfers between devices: none -> 9.92 us  [the longest x1 5.03 us: local(): lax.all_to_all(kohn, PLANE, 0, 0, axis_index_groups=LINE, tiled=True)]
  transfers between devices with their start and end apart: 33 -> 13, of which waited for: 13 -> 9; matrix products, arithmetic and copies ran while one was open for 17% -> 2% of each run, Pallas kernels for 14% -> 37%
where the time goes in v3:
time: 367 us; the launch traced here: 366 us
  Pallas kernels  180 us (49%)
  waiting for transfers between devices  82.2 us (22%)
  blocking collectives  40.4 us (11%)
  local copies, waits for them, and re-layouts  29.1 us (8%)
  starting transfers between devices  19.4 us (5%)
  between operations  13.7 us (4%)
    pallas_call x1, Pallas kernels, regroup(): pl.pallas_call(regroup_kernel, grid_spec=pltpu.PrefetchScalarGridSpec(num...  128 us
    all_to_all x1, blocking collectives, local(): lax.all_to_all(outgoing, ALL, split_axis=0, concat_axis=0, tiled=True)  40.4 us
    pallas_call x2, Pallas kernels, panel_sums(): pl.pallas_call(lambda *refs: panel_kernel(n, first, *refs), grid_spec=plt...  34.2 us
    all_gather x1, waiting for transfers between devices, local(): lax.all_gather(jnp.concatenate([mine, theirs]), 'x', axis=0, tiled=True)  33.1 us
    all_to_all x1, waiting for transfers between devices, local(): lax.all_to_all(sums, PLANE, 0, 0, axis_index_groups=CROSS, tiled=True)  27 us
    ppermute x3, waiting for transfers between devices, over_line(): return lax.ppermute(v, PLANE, pairs)  13.4 us
    pallas_call x1, Pallas kernels, pack(): pl.pallas_call(pack_kernel, grid_spec=pltpu.PrefetchScalarGridSpec(num_sc...  10.1 us
    transpose x1, local copies, waits for them, and re-layouts, local(): density_blocks.reshape(8, SP, B, C, 2, 16).transpose(3, 0, 1, 5, 4, 2)  9.6 us
  transfers between devices with their start and end apart: 13, of which 9 were waited for; matrix products, arithmetic and copies ran while one was open for 2% of the time, Pallas kernels for 37%

profile of v3, /device:TPU:1, one launch (start us, length us, event | category | flops | bytes accessed | tf_op | source)
XLA Modules:
  0.0 366.4 jit_solution(9657426188040372307)
XLA Ops:
  6.5 5.4 %reshape.147 = bf16[8,8,64,2,2,16]{5,4,3,2,1,0:T(2,128)(2,1)} reshape(bf16[1,8,8,4096]{3,2,1,0:T(8,128)(2,1)} %param.7) | data formatting | bytes 1048576 | tf_op jit(solution)/shard_map/reshape | solution.py:319
  12.0 9.6 %copy.18 = bf16[2,8,8,16,2,64]{5,4,3,2,1,0:T(2,128)(2,1)S(1)} copy(bf16[2,8,8,16,2,64]{3,4,0,5,2,1:T(2,128)(2,1)} %bitcast.48) | data formatting | bytes 1048576 | tf_op jit(solution)/shard_map/transpose | solution.py:319
  22.1 1.5 collective-permute-start.8
  23.6 1.2 collective-permute-done.8
  24.8 0.8 pad_maximum_fusion
  25.7 33.1 %all-gather.4.cloned.1.call-done.refs_4_ = bf16[64,128,128]{2,1,0:T(8,128)(2,1)} async-done(((bf16[16,128,128]{2,1,0:T(8,128)(2,1)}), bf16[64,128,128]{2,1,0:T(8,128)(2,1)}) %all-gather.4.cloned.1.call-update) | async-done | bytes 2097168 | tf_op jit(solution)/shard_map/all_gather | solution.py:322
  58.8 3.8 %reshape.146.mine = bf16[16,4,128,128]{3,2,1,0:T(8,128)(2,1)S(1)} reshape(bf16[64,1,4,4096]{3,2,1,0:T(4,128)(2,1)} %param.5) | data formatting | bytes 4194304 | tf_op jit(solution)/shard_map/reshape | solution.py:347
  62.6 0.8 collective-permute-start.7
  63.4 3.8 %collective-permute-done.7.other = bf16[16,4,128,128]{3,2,1,0:T(8,128)(2,1)S(1)} collective-permute-done((bf16[16,4,128,128]{3,2,1,0:T(8,128)(2,1)S(1)}, bf16[16,4,128,128]{3,2,1,0:T(8,128)(2,1)S(1)}, u32[]{:S(2)}, u32[]{:S(2)}) %collective-permute-start.7) | collective-permute-done | bytes 2097184 | tf_op jit(solution)/shard_map/ppermute | solution.py:42
  67.1 1.3 copy-done.4
  68.5 128.4 %regroup.1.refs_3_ = bf16[4,2,4,4,128,128]{5,4,3,2,1,0:T(8,128)(2,1)} custom-call(s32[1]{0:T(128)} %bitcast.16.core, bf16[16,4,128,128]{3,2,1,0:T(8,128)(2,1)} %copy-done.3, bf16[16,4,128,128]{3,2,1,0:T(8,128)(2,1)} %copy-done.4), custom_call_target="tpu_custom_call" | custom-call | tf_op jit(solution)/shard_map/regroup/pallas_call | solution.py:61
  197.0 5.0 %all-to-all-start = ((bf16[4,2,4,4,128,128]{5,4,3,2,1,0:T(8,128)(2,1)}), bf16[4,2,4,4,128,128]{5,4,3,2,1,0:T(8,128)(2,1)}, u32[]{:S(2)}, u32[]{:S(2)}) async-start(bf16[4,2,4,4,128,128]{5,4,3,2,1,0:T(8,128)(2,1)} %regroup.1.refs_3_), calls=%async_computation | async-start | bytes 8388608 | tf_op jit(solution)/shard_map/all_to_all | solution.py:349
  202.8 0.8 collective-permute-done
  204.3 1.5 collective-permute-start.2
  206.8 1.4 collective-permute-done.2
  208.2 1.6 collective-permute-done.3
  210.3 1.4 collective-permute-start.6
  211.9 1.4 collective-permute-start.4
  213.3 1.7 collective-permute-start.5
  214.9 10.4 %collective-permute-done.6 = s32[8,128]{1,0:T(8,128)S(1)} collective-permute-done((s32[8,128]{1,0:T(8,128)S(1)}, s32[8,128]{1,0:T(8,128)S(1)}, u32[]{:S(2)}, u32[]{:S(2)}) %collective-permute-start.6) | collective-permute-done | bytes 4128 | tf_op jit(solution)/shard_map/ppermute | solution.py:34
  226.0 3.0 collective-permute-done.5
  229.2 0.6 gather_fusion.2
  230.2 0.6 gather_fusion.1
  230.9 2.2 copy-done
  233.1 8.8 %own_panel.1.refs_7_ = f32[4,8,32,16,128]{4,3,2,1,0:T(8,128)} custom-call(s32[128]{0:T(128)S(1)} %xor.65.refs_0_, s32[512]{0:T(512)S(1)} %bitcast.47, s32[1]{0:T(128)} %bitcast.15.refs_2_, bf16[4,2,4,4,128,128]{5,4,3,2,1,0:T(8,128)(2,1)S(1)} %copy-done, bf16[64,128,128]{2,1,0:T(8,128)(2,1)S(1)} %copy-done.2), custom_call_target="tpu_custom_call" | custom-call | flops 536870912 | bytes 15728640 | tf_op jit(solution)/shard_map/own_panel/pallas_call | solution.py:179
  241.9 25.4 %other_panels.1 = s16[4,8,33,16,128]{4,3,2,1,0:T(8,128)(2,1)S(1)} custom-call(s32[384]{0:T(512)S(1)} %pad_add_fusion.4.refs_0_, s32[1536]{0:T(1024)S(1)} %pad_add_fusion.1.refs_1_, s32[1]{0:T(128)} %bitcast.15.refs_2_, bf16[4,2,4,4,128,128]{5,4,3,2,1,0:T(8,128)(2,1)} %all-to-all-done.refs_3_.refs_4_.refs_5_, ...), custom_call_target="tpu_custom_call" | custom-call | flops 1610612736 | bytes 22020096 | tf_op jit(solution)/shard_map/other_panels/pallas_call | solution.py:179
  267.4 2.1 copy-done.1
  269.5 4.9 %all-to-all-start.1 = ((s16[4,8,33,16,128]{4,3,2,1,0:T(8,128)(2,1)}), s16[4,8,33,16,128]{4,3,2,1,0:T(8,128)(2,1)}, u32[]{:S(2)}, u32[]{:S(2)}) async-start(s16[4,8,33,16,128]{4,3,2,1,0:T(8,128)(2,1)} %copy-done.1), calls=%async_computation.1 | async-start | bytes 8650752 | tf_op jit(solution)/shard_map/all_to_all | solution.py:353
  275.0 27.0 %all-to-all-done.1.r_ref = s16[4,8,33,16,128]{4,3,2,1,0:T(8,128)(2,1)} async-done(((s16[4,8,33,16,128]{4,3,2,1,0:T(8,128)(2,1)}), s16[4,8,33,16,128]{4,3,2,1,0:T(8,128)(2,1)}, u32[]{:S(2)}, u32[]{:S(2)}) %all-to-all-start.1) | async-done | bytes 4325408 | tf_op jit(solution)/shard_map/all_to_all | solution.py:353
  302.0 10.1 %pack.1 = s16[128,80,128]{2,1,0:T(8,128)(2,1)S(1)} custom-call(s32[256]{0:T(256)S(1)} %add_bitcast_fusion.1.slots, s16[4,8,33,16,128]{4,3,2,1,0:T(8,128)(2,1)} %all-to-all-done.1.r_ref), custom_call_target="tpu_custom_call" | custom-call | tf_op jit(solution)/shard_map/pack/pallas_call | solution.py:261
  312.1 40.4 %all_to_all.15 = s16[128,80,128]{2,1,0:T(8,128)(2,1)S(1)} all-to-all(s16[128,80,128]{2,1,0:T(8,128)(2,1)S(1)} %pack.1), channel_id=1, replica_groups=mesh['x'=4,'core'=2,'z'=4,'y'=4] {'x','core','z','y'}, dimensions={0} | all-to-all | bytes 5242880 | tf_op jit(solution)/shard_map/all_to_all | solution.py:355
  352.5 7.1 %unpack.1 = f32[256,4096]{1,0:T(8,128)} custom-call(s16[4,2,16,80,128]{4,3,2,1,0:T(8,128)(2,1)S(1)} %bitcast.45), custom_call_target="tpu_custom_call" | custom-call | tf_op jit(solution)/shard_map/unpack/pallas_call | solution.py:300
  (66 shorter events, 5.8 us)
Async XLA Ops:
  6.5 52.2 %all-gather.4.cloned.1.call-start = ((), (), s32[]{:S(2)}) async-start(), calls=%async_computation.3 | async-start | bytes 2621440 | tf_op jit(solution)/shard_map/all_gather | solution.py:322
  22.1 2.7 collective-permute-start.8
  25.7 216.3 %all-gather.6.cloned.1.call-start = ((), (), s32[]{:S(2)}) async-start(), calls=%async_computation.4 | async-start | bytes 10485760 | tf_op jit(solution)/shard_map/all_gather | solution.py:323
  62.6 5.9 %copy-start.3 = (bf16[16,4,128,128]{3,2,1,0:T(8,128)(2,1)}, bf16[16,4,128,128]{3,2,1,0:T(8,128)(2,1)S(1)}, u32[]{:S(2)}) copy-start(bf16[16,4,128,128]{3,2,1,0:T(8,128)(2,1)S(1)} %reshape.146.mine) | copy-start | bytes 6291460
  62.6 4.5 %collective-permute-start.7 = (bf16[16,4,128,128]{3,2,1,0:T(8,128)(2,1)S(1)}, bf16[16,4,128,128]{3,2,1,0:T(8,128)(2,1)S(1)}, u32[]{:S(2)}, u32[]{:S(2)}) collective-permute-start(bf16[16,4,128,128]{3,2,1,0:T(8,128)(2,1)S(1)} %reshape.146.mine), channel_id=1, source_target_pairs={{0,16},{16,0},{1,17},{17,1},{2,18},{18,2},{3,19},{19,3},{4,20},{20... | collective-permute-start | bytes 6291464 | tf_op jit(solution)/shard_map/ppermute | solution.py:42
  67.1 1.3 copy-start.4
  196.9 5.1 %copy-start.7 = (s32[64,1,4]{0,2,1:T(4,128)S(1)}, s32[64,1,4]{0,2,1:T(4,128)}, u32[]{:S(2)}) copy-start(s32[64,1,4]{0,2,1:T(4,128)} %param.6) | copy-start | bytes 3076
  196.9 5.3 %copy-start.6 = (s32[1,8,8]{2,1,0:T(8,128)S(1)}, s32[1,8,8]{2,1,0:T(8,128)}, u32[]{:S(2)}) copy-start(s32[1,8,8]{2,1,0:T(8,128)} %param.8) | copy-start | bytes 772
  197.0 5.4 %copy-start.5 = (s32[128,1]{0,1:T(1,128)S(1)}, s32[128,1]{0,1:T(1,128)}, u32[]{:S(2)}) copy-start(s32[128,1]{0,1:T(1,128)} %param.9) | copy-start | bytes 1540
  197.0 33.9 %copy-start.2 = (bf16[64,128,128]{2,1,0:T(8,128)(2,1)S(1)}, bf16[64,128,128]{2,1,0:T(8,128)(2,1)}, u32[]{:S(2)}) copy-start(bf16[64,128,128]{2,1,0:T(8,128)(2,1)} %all-gather.4.cloned.1.call-done.refs_4_) | copy-start | bytes 6291460
  197.0 44.9 %all-to-all-start = ((bf16[4,2,4,4,128,128]{5,4,3,2,1,0:T(8,128)(2,1)}), bf16[4,2,4,4,128,128]{5,4,3,2,1,0:T(8,128)(2,1)}, u32[]{:S(2)}, u32[]{:S(2)}) async-start(bf16[4,2,4,4,128,128]{5,4,3,2,1,0:T(8,128)(2,1)} %regroup.1.refs_3_), calls=%async_computation | async-start | bytes 8388608 | tf_op jit(solution)/shard_map/all_to_all | solution.py:349
  202.4 1.2 collective-permute-start
  203.7 3.1 collective-permute-start.1
  204.3 3.9 %collective-permute-start.2 = (s32[128]{0:T(128)S(1)}, s32[128]{0:T(128)S(1)}, u32[]{:S(2)}, u32[]{:S(2)}) collective-permute-start(s32[128]{0:T(128)S(1)} %pad_add_fusion.6), channel_id=1, source_target_pairs={{0,64},{32,96},{64,0},{96,32},{1,65},{33,97},{65,1},{97,33},{2,66}... | collective-permute-start | bytes 1544 | tf_op jit(solution)/shard_map/ppermute | solution.py:38
  205.7 4.0 %collective-permute-start.3 = (s32[128]{0:T(128)S(1)}, s32[128]{0:T(128)S(1)}, u32[]{:S(2)}, u32[]{:S(2)}) collective-permute-start(s32[128]{0:T(128)S(1)} %pad_add_fusion.6), channel_id=1, source_target_pairs={{0,32},{32,64},{64,96},{96,0},{1,33},{33,65},{65,97},{97,1},{2,34}... | collective-permute-start | bytes 1544 | tf_op jit(solution)/shard_map/ppermute | solution.py:38
  210.3 15.0 %collective-permute-start.6 = (s32[8,128]{1,0:T(8,128)S(1)}, s32[8,128]{1,0:T(8,128)S(1)}, u32[]{:S(2)}, u32[]{:S(2)}) collective-permute-start(s32[8,128]{1,0:T(8,128)S(1)} %add_bitcast_fusion), channel_id=1, source_target_pairs={{0,4},{4,8},{8,12},{12,0},{1,5},{5,9},{9,13},{13,1},{2,6},{6,10},{... | collective-permute-start | bytes 12296 | tf_op jit(solution)/shard_map/ppermute | solution.py:34
  211.9 18.1 %collective-permute-start.4 = (s32[8,128]{1,0:T(8,128)S(1)}, s32[8,128]{1,0:T(8,128)S(1)}, u32[]{:S(2)}, u32[]{:S(2)}) collective-permute-start(s32[8,128]{1,0:T(8,128)S(1)} %add_bitcast_fusion), channel_id=1, source_target_pairs={{0,12},{4,0},{8,4},{12,8},{1,13},{5,1},{9,5},{13,9},{2,14},{6,2},{... | collective-permute-start | bytes 12296 | tf_op jit(solution)/shard_map/ppermute | solution.py:34
  213.3 15.8 %collective-permute-start.5 = (s32[8,128]{1,0:T(8,128)S(1)}, s32[8,128]{1,0:T(8,128)S(1)}, u32[]{:S(2)}, u32[]{:S(2)}) collective-permute-start(s32[8,128]{1,0:T(8,128)S(1)} %add_bitcast_fusion), channel_id=1, source_target_pairs={{0,8},{4,12},{8,0},{12,4},{1,9},{5,13},{9,1},{13,5},{2,10},{6,14},... | collective-permute-start | bytes 12296 | tf_op jit(solution)/shard_map/ppermute | solution.py:34
  230.9 2.2 copy-start
  267.4 2.1 copy-start.1
  269.5 32.6 %all-to-all-start.1 = ((s16[4,8,33,16,128]{4,3,2,1,0:T(8,128)(2,1)}), s16[4,8,33,16,128]{4,3,2,1,0:T(8,128)(2,1)}, u32[]{:S(2)}, u32[]{:S(2)}) async-start(s16[4,8,33,16,128]{4,3,2,1,0:T(8,128)(2,1)} %copy-done.1), calls=%async_computation.1 | async-start | bytes 8650752 | tf_op jit(solution)/shard_map/all_to_all | solution.py:353
Sparse Core Ops, SparseCore 0:
  25.8 32.9 all-gather.3
  60.4 49.6 all-gather.5

commit v4 on v3

v4 whole, which is shorter than its diff:
```python
import jax
import jax.numpy as jnp
from jax import lax
from jax.experimental import pallas as pl
from jax.experimental.pallas import tpu as pltpu
from jax.sharding import Mesh, PartitionSpec as P

B = 64
HALF = 32
NCW = 32
SK = 4
SP = 8
X, C, Z, Y = 4, 2, 4, 4
ALL = ("x", "core", "z", "y")
PLANE = ("core", "z", "y")
TOP = 32766.0
MSG = 80
ORDER = (2, 1, 3, 0)


def lines(along):
    groups = []
    for c in range(C):
        for fixed in range(4):
            on_z = (c ^ along) == 0
            groups.append([(c * Z + (i if on_z else fixed)) * Y + (fixed if on_z else i) for i in range(4)])
    return groups


LINE, CROSS = lines(0), lines(1)


def over(groups, v, step):
    return lax.ppermute(v, PLANE, [(group[i], group[(i + step) % 4]) for group in groups for i in range(4)])


def over_line(v, step):
    return over(LINE, v, step)


def over_cross(v, step):
    return over(CROSS, v, step)


def over_x(v, step):
    return lax.ppermute(v, "x", [(i, (i + step) % X) for i in range(X)])


def over_core(v):
    return lax.ppermute(v, "core", [(0, 1), (1, 0)])


def split_kernel(core, d_ref, mine, theirs, flat, wide):
    lane32 = lax.broadcasted_iota(jnp.int32, (32, 128), 1)
    lane64 = lax.broadcasted_iota(jnp.int32, (64, 128), 1)

    def one(k, _):
        rows = d_ref[k].astype(jnp.float32)
        for p in range(32):
            flat[p * 8:(p + 1) * 8, :] = rows[:, p * 128:(p + 1) * 128]
        v = []
        for b in range(4):
            lo, hi = flat[pl.ds(b, 32, stride=8), :], flat[pl.ds(b + 4, 32, stride=8), :]
            wide[b, pl.ds(0, 32, stride=2), :] = jnp.where(lane32 < 64, lo, pltpu.roll(hi, 64, 1))
            wide[b, pl.ds(1, 32, stride=2), :] = jnp.where(lane32 < 64, pltpu.roll(lo, 64, 1), hi)
        v = [wide[b] for b in range(4)]
        for bit in (2, 1):
            keep = (lane64 & (16 * bit)) == 0
            w = [None] * 4
            for i in range(4):
                if not i & bit:
                    lo, hi = v[i], v[i | bit]
                    w[i] = jnp.where(keep, lo, pltpu.roll(hi, 16 * bit, 1))
                    w[i | bit] = jnp.where(keep, pltpu.roll(lo, 128 - 16 * bit, 1), hi)
            v = w
        first = jnp.concatenate([v[0], v[1]], axis=0).T
        second = jnp.concatenate([v[2], v[3]], axis=0).T
        swapped = core[0] == 1
        mine[k] = jnp.where(swapped, second, first).astype(jnp.bfloat16)
        theirs[k] = jnp.where(swapped, first, second).astype(jnp.bfloat16)
        return 0

    lax.fori_loop(0, 8, one, 0)


def split(core, dens):
    half = jax.ShapeDtypeStruct((8, 128, 128), jnp.bfloat16)
    whole = pl.BlockSpec((8, 128, 128), lambda i, *_: (0, 0, 0))
    return pl.pallas_call(
        split_kernel,
        grid_spec=pltpu.PrefetchScalarGridSpec(
            num_scalar_prefetch=1, grid=(1,),
            in_specs=[pl.BlockSpec((8, SP, B * B), lambda i, *_: (0, 0, 0))],
            out_specs=[whole, whole],
            scratch_shapes=[pltpu.VMEM((256, 128), jnp.float32), pltpu.VMEM((4, B, 128), jnp.float32)],
        ),
        out_shape=[half, half],
        name="split",
    )(core, dens)


def regroup_kernel(at, mine, other, own, after, before, far0, far1, sems):
    swapped, line, cross = at[0] == 1, at[1], at[2]
    copies = []
    for step, dst in enumerate((own, after, None, before)):
        t = (line + step) % 4
        for i, rel in enumerate(ORDER):
            o = (cross + rel) % 4
            row = jnp.where(swapped, o * 4 + t, t * 4 + o)
            for m, src in enumerate((mine, other)):
                to = (far0, far1)[m].at[i] if dst is None else dst.at[m, i]
                copies.append(pltpu.make_async_copy(src.at[row], to, sems.at[len(copies)]))
    for copy in copies:
        copy.start()
    for copy in copies:
        copy.wait()


def regroup(at, mine, other):
    two, one = (2, 4, 4, 128, 128), (4, 4, 128, 128)
    shapes = [two, two, two, one, one]
    return pl.pallas_call(
        regroup_kernel,
        grid_spec=pltpu.PrefetchScalarGridSpec(
            num_scalar_prefetch=1, grid=(1,), in_specs=[pl.BlockSpec(memory_space=pl.ANY)] * 2,
            out_specs=[pl.BlockSpec(shape, lambda i, *_, n=len(shape): (0,) * n) for shape in shapes],
            scratch_shapes=[pltpu.SemaphoreType.DMA((32,))],
        ),
        out_shape=[jax.ShapeDtypeStruct(shape, jnp.bfloat16) for shape in shapes],
        compiler_params=pltpu.CompilerParams(vmem_limit_bytes=24 << 20),
        name="regroup",
    )(at, mine, other)


def encode(values, put, write_code):
    top = jnp.zeros((16, 128), jnp.float32)
    for j in range(NCW):
        top = jnp.maximum(top, jnp.abs(values[j]))
    top = jnp.maximum(jnp.max(top, axis=0, keepdims=True), 2.0 ** -110)
    code = jnp.floor(jnp.log2(top) * 256.0) + 1.0
    scale = jnp.broadcast_to(jnp.exp2(code * (-1.0 / 256.0)) * TOP, (16, 128))
    write_code(jnp.broadcast_to(code.astype(jnp.int32), (16, 128)))
    for j in range(NCW):
        put(j, jnp.floor(values[j] * scale + 0.5).astype(jnp.int32).astype(jnp.int16))


def decoded_scale(code):
    return jnp.exp2(code.astype(jnp.int32).astype(jnp.float32) * (1.0 / 256.0)) * (1.0 / TOP)


def panel_kernel(n, rows_of_block, has_sums, coded, kcol, jcol, *refs):
    kohn, refs = refs[:2 * n], refs[2 * n:]
    panels, refs = refs[:2 * n], refs[2 * n:]
    if has_sums:
        p_ref, refs = refs[0], refs[1:]
    outs, (dens, sems, acc) = refs[:-3], refs[-3:]
    step = pl.program_id(0) + rows_of_block

    @pl.when(pl.program_id(0) == 0)
    def _():
        copies = [pltpu.make_async_copy(panels[s], dens.at[pl.ds(s * 32, 32)], sems.at[s]) for s in range(2 * n)]
        for copy in copies:
            copy.start()
        for copy in copies:
            copy.wait()

    low = (lax.broadcasted_iota(jnp.int32, (32, 128), 1) < 64).astype(jnp.float32).astype(jnp.bfloat16)
    high = 1 - low
    zero = jnp.zeros((128, 128), jnp.bfloat16)

    def twice(blk):
        turned = jnp.concatenate([blk[:, B:], blk[:, :B]], axis=1)
        return jnp.concatenate([blk * low, turned * low, turned * high, blk * high], axis=0)

    def product(m, r, s, a):
        ks, weights = [], []
        for i in range(2):
            ks.append(kcol[(((s * 4 + step) * 2 + m) * 4 + r) * SK + a + i] + 64 * s)
            weights.append(twice(kohn[2 * s + m][0, 0, r, (a + i) * 32:(a + i + 1) * 32, :]))
        left = jnp.concatenate([dens[ks[0]], dens[ks[1]]], axis=1)
        right = jnp.concatenate([
            jnp.concatenate([weights[0], zero], axis=1), jnp.concatenate([zero, weights[1]], axis=1)
        ], axis=0)
        r = lax.dot_general(left, right, (((1,), (1,)), ((), ())), preferred_element_type=jnp.float32)
        return ks, r

    def add(sums, ks, r):
        for i in range(2):
            js = [jcol[ks[i] * SP + b] for b in range(SP)]
            old = [sums[j] for j in js]
            for b in range(SP):
                sums[js[b]] = old[b] + r[b * 16:(b + 1) * 16, i * 128:(i + 1) * 128]

    def two_rows(m, pair):
        work, sums = [], []
        for q in range(2):
            r = pair * 2 + q
            work += [(q, r, s, a) for s in range(n) for a in range(0, SK, 2)]
            place = acc.at[q] if coded else outs[0].at[0, m * 4 + r]
            place[...] = p_ref[0, m * 4 + r] if has_sums else jnp.zeros((NCW, 16, 128), jnp.float32)
            sums.append(place)
        held = [product(m, *work[i][1:]) for i in range(2)]
        for i in range(len(work)):
            if i + 2 < len(work):
                held.append(product(m, *work[i + 2][1:]))
            add(sums[work[i][0]], *held[i])
        if coded:
            for q in range(2):
                r = pair * 2 + q
                out, row = (outs[m], r) if len(outs) == 2 else (outs[0], m * 4 + r)

                def put(j, value, out=out, row=row):
                    out[row, j] = value

                encode(sums[q], put, lambda code, put=put: put(NCW, code.astype(jnp.int16)))

    for m in range(2):
        lax.fori_loop(0, 2, lambda pair, _, m=m: (two_rows(m, pair), 0)[1], 0)


def panel_sums(name, kcol, jcol, kohn, panels, sums, target=None, coded=False):
    n = len(panels) // 2
    base = 0 if target is None else target
    k_specs = [
        pl.BlockSpec((1, 1, 4, 128, 128), lambda o, *_, m=m: (m, o + base, 0, 0, 0)) for _, m in kohn
    ]
    s_shape = (1, 8, NCW, 16, 128)
    s_spec = pl.BlockSpec(s_shape, lambda o, *_: (o + base, 0, 0, 0, 0))
    o_specs = [pl.BlockSpec(s_shape, lambda o, *_: (o, 0, 0, 0, 0))]
    shapes = [jax.ShapeDtypeStruct((4 if target is None else 1,) + s_shape[1:], jnp.float32)]
    if coded:
        parts = 2 if target == 0 else 1
        o_specs = [pl.BlockSpec((8 // parts, NCW + 1, 16, 128), lambda o, *_: (0, 0, 0, 0))] * parts
        shapes = [jax.ShapeDtypeStruct((8 // parts, NCW + 1, 16, 128), jnp.int16)] * parts
    any_spec = pl.BlockSpec(memory_space=pl.ANY)
    steps = 4 if target is None else 1
    return pl.pallas_call(
        lambda *refs: panel_kernel(n, base, sums is not None, coded, *refs),
        grid_spec=pltpu.PrefetchScalarGridSpec(
            num_scalar_prefetch=2,
            grid=(steps,),
            in_specs=k_specs + [any_spec] * (2 * n) + [s_spec] * (sums is not None),
            out_specs=o_specs,
            scratch_shapes=[
                pltpu.VMEM((n * 64, 128, 128), jnp.bfloat16),
                pltpu.SemaphoreType.DMA((2 * n,)),
                pltpu.VMEM((2, NCW, 16, 128), jnp.float32),
            ],
        ),
        out_shape=shapes,
        compiler_params=pltpu.CompilerParams(vmem_limit_bytes=40 << 20),
        cost_estimate=pl.CostEstimate(
            flops=2 * n * 32 * steps * 128 * 128 * 128, bytes_accessed=(2 * n + 5 * steps) << 20, transcendentals=0
        ),
        name=name,
    )(kcol, jcol, *[array for array, _ in kohn], *panels, *(() if sums is None else (sums,)))


def pack_kernel(slots, own, after, before, far0, far1, o_ref, total, codes):
    rows = lax.broadcasted_iota(jnp.int32, (16, 128), 0)
    lane = lax.broadcasted_iota(jnp.int32, (16, 128), 1)

    def clear(n, _):
        for m in range(4):
            o_ref[n * 4 + m] = jnp.zeros((MSG, 128), jnp.int16)
            codes[n * 4 + m] = jnp.zeros((16, 128), jnp.int32)
        return 0

    lax.fori_loop(0, 32, clear, 0)

    def one(m, r):
        row = m * 4 + r
        coded = [(before, row), (after, row), ((far0, far1)[m], r)]
        scales = [decoded_scale(ref[at, NCW]) for ref, at in coded]
        for group in range(NCW // 8):
            blocks = []
            for j in range(group * 8, group * 8 + 8):
                g = [ref[at, j].astype(jnp.int32).astype(jnp.float32) * scale for (ref, at), scale in zip(coded, scales)]
                blocks.append((own[0, row, j] + g[0]) + (g[1] + g[2]))
            turned = jnp.concatenate(blocks, axis=0).T
            v = []
            for q in range(8):
                par, mh, zh = q // 4, (q // 2) % 2, q % 2
                at = (zh * 4 + par * 2 + mh) * 16
                v.append(turned[at:at + 16, :])
            for bit in (4, 2, 1):
                keep = (lane & (16 * bit)) == 0
                w = [None] * 8
                for i in range(8):
                    if not i & bit:
                        lo, hi = v[i], v[i | bit]
                        w[i] = jnp.where(keep, lo, pltpu.roll(hi, 16 * bit, 1))
                        w[i | bit] = jnp.where(keep, pltpu.roll(lo, 128 - 16 * bit, 1), hi)
                v = w
            for j in range(8):
                total[group * 8 + j] = v[j]

        def put(j, value):
            slot = slots[row * NCW + j]
            o_ref[slot // 4, pl.ds(pl.multiple_of((slot % 4) * 16, 16), 16), :] = value

        def write_code(code):
            for j in range(NCW):
                slot = slots[row * NCW + j]
                codes[slot // 4] = jnp.where(rows == slot % 4, code, codes[slot // 4])

        encode(total, put, write_code)

    for m in range(2):
        lax.fori_loop(0, 4, lambda r, _, m=m: (one(m, r), 0)[1], 0)

    def finish(n, _):
        for m in range(4):
            o_ref[n * 4 + m, 64:80, :] = codes[n * 4 + m].astype(jnp.int16)
        return 0

    lax.fori_loop(0, 32, finish, 0)


def pack(slots, own, after, before, far0, far1):
    def whole(array):
        return pl.BlockSpec(
            array.shape, lambda i, *_, n=array.ndim: (0,) * n, pipeline_mode=pl.Buffered(1)
        )

    return pl.pallas_call(
        pack_kernel,
        grid_spec=pltpu.PrefetchScalarGridSpec(
            num_scalar_prefetch=1,
            grid=(1,),
            in_specs=[whole(array) for array in (own, after, before, far0, far1)],
            out_specs=pl.BlockSpec((128, MSG, 128), lambda i, *_: (0, 0, 0), pipeline_mode=pl.Buffered(1)),
            scratch_shapes=[pltpu.VMEM((NCW, 16, 128), jnp.float32), pltpu.VMEM((128, 16, 128), jnp.int32)],
        ),
        out_shape=jax.ShapeDtypeStruct((128, MSG, 128), jnp.int16),
        compiler_params=pltpu.CompilerParams(vmem_limit_bytes=32 << 20),
        name="pack",
    )(slots, own, after, before, far0, far1)


def unpack_kernel(r_ref, o_ref, full):
    low32 = (lax.broadcasted_iota(jnp.int32, (16, 128), 1) & 32) == 0
    for s in range(2):
        def one(n, _):
            scales = [decoded_scale(r_ref[0, c, n, 64:80, :]) for c in range(2)]
            for t in range(2):
                h = []
                for c in range(2):
                    at = (s * 2 + t) * 16
                    q = r_ref[0, c, n, at:at + 16, :].astype(jnp.int32).astype(jnp.float32)
                    h.append(q * scales[c][s * 2 + t:s * 2 + t + 1, :])
                base = pl.multiple_of(((s * 16 + n) * 2 + t) * 32, 32)
                full[pl.ds(base, 16), :] = jnp.where(low32, h[0], pltpu.roll(h[1], 32, 1))
                full[pl.ds(base + 16, 16), :] = jnp.where(low32, pltpu.roll(h[0], 96, 1), h[1])
            return 0

        lax.fori_loop(0, 16, one, 0, unroll=4)
    for p in range(32):
        o_ref[:, p * 128:(p + 1) * 128] = full[pl.ds(p, 64, stride=32), :]


def unpack(received):
    return pl.pallas_call(
        unpack_kernel,
        grid=(X,),
        in_specs=[pl.BlockSpec((1, C, 16, MSG, 128), lambda x: (x, 0, 0, 0, 0))],
        out_specs=pl.BlockSpec((64, 4096), lambda x: (x, 0)),
        out_shape=jax.ShapeDtypeStruct((256, 4096), jnp.float32),
        scratch_shapes=[pltpu.VMEM((64 * 32, 128), jnp.float32)],
        compiler_params=pltpu.CompilerParams(vmem_limit_bytes=32 << 20),
        name="unpack",
    )(received)


def local(kohn_blocks, kohn_columns, density_blocks, density_columns, owner_map):
    x, c = lax.axis_index("x"), lax.axis_index("core")
    z, y = lax.axis_index("z"), lax.axis_index("y")
    on_line, on_cross = jnp.where(c == 0, z, y), jnp.where(c == 0, y, z)
    four = jnp.arange(4, dtype=jnp.int32)

    mine, theirs = split(c.reshape(1), density_blocks[0])
    theirs = over_core(theirs)
    left0, right0 = over_x(mine, 1), over_x(mine, -1)
    left1, right1 = over_x(theirs, 1), over_x(theirs, -1)
    far0, far1 = over_x(left0, 1), over_x(right1, -1)
    low = jnp.concatenate([mine, theirs, left0, left1])
    high = jnp.concatenate([right0, right1, far0, far1])

    prev_low, prev_high = over_line(low, 1), over_line(high, 1)
    next_high, next_low = over_line(high, -1), over_line(low, -1)
    far_low, far_high = over_line(prev_low, 1), over_line(next_high, -1)

    ints = jnp.concatenate([kohn_columns.reshape(-1), density_columns.reshape(-1), owner_map.reshape(-1)])
    other = over_core(ints)
    columns = jnp.concatenate([ints[256:320], other[256:320]])
    columns = jnp.concatenate([columns, over_x(columns, 1), over_x(columns, -1), over_x(columns, 2)])
    words = jnp.concatenate([columns, ints[:256], other[:256]]).reshape(8, 128)
    words = [words, over_line(words, 1), over_line(words, -1), over_line(words, 2)]

    def indices(word):
        word = word.reshape(-1)
        targets = (on_cross + jnp.array(ORDER, jnp.int32)) % 4
        rows = jnp.where(c == 0, on_line * Y + targets, targets * Y + on_line)
        k = word[512:].reshape(2, 16, 4, SK)[:, rows].transpose(1, 0, 2, 3).reshape(-1)
        away = ((k >> 4) - x) & 3
        slot = jnp.where(away == 0, 0, jnp.where(away == 3, 1, away + 1))
        return slot * 16 + ((k & 15) ^ (8 * c)), word[:512]

    kcols, jcols = zip(*[indices(word) for word in words])

    owners = jnp.stack([ints[320:], other[320:]])
    hit = (owners[..., None] == jnp.arange(128, dtype=jnp.int32)).astype(jnp.int32)
    ranks = jnp.sum(jnp.cumsum(hit, axis=1) * hit, axis=2) - 1
    source = jnp.arange(2, dtype=jnp.int32)[:, None] ^ c
    slots = (owners * 4 + source * 2 + ranks).reshape(-1)

    kohn = kohn_blocks.reshape(16, 4, SK * 32, 128)
    kohn, after, before, opposite0, opposite1 = regroup(
        jnp.stack([c, on_line, on_cross]), kohn, over_core(kohn)
    )
    before, after = over_line(after, 1), over_line(before, -1)
    opposite0 = over_line(over_line(opposite0, 1), 1)
    opposite1 = over_line(over_line(opposite1, -1), -1)

    def both(array):
        return [(array, 0), (array, 1)]

    sums, = panel_sums("own_panel", kcols[0], jcols[0], both(kohn), [low, high], None)
    sums, = panel_sums(
        "near_panels", jnp.concatenate(kcols[1:3]), jnp.concatenate(jcols[1:3]), both(before) + both(after),
        [prev_low, prev_high, next_low, next_high], sums,
    )
    opposite = [(opposite0[None], 0), (opposite1[None], 0)]

    def last(target, coded):
        return panel_sums(
            "last_panel", kcols[3], jcols[3], opposite, [far_low, far_high], sums, target=target, coded=coded
        )

    sums0, sums1 = last(0, True)
    sums0, sums1 = over_cross(sums0, 1), over_cross(sums1, -1)
    to_next, = last(1, True)
    from_prev = over_cross(to_next, 1)
    to_prev, = last(2, True)
    from_next = over_cross(to_prev, -1)
    sums0, sums1 = over_cross(sums0, 1), over_cross(sums1, -1)
    own, = last(3, False)

    outgoing = pack(slots, own, from_next, from_prev, sums0, sums1)
    received = lax.all_to_all(outgoing, ALL, split_axis=0, concat_axis=0, tiled=True)
    return unpack(received.reshape(X, C, 16, MSG, 128))


def solution(mesh):
    grid = Mesh(mesh.devices.reshape(X, C, Z, Y), ALL)
    row, col = ("x", "core"), ("z", "y")
    return jax.shard_map(
        local,
        mesh=grid,
        in_specs=(
            P(row, col, None, None),
            P(row, col, None),
            P(col, row, None, None),
            P(col, row, None),
            P(ALL, None),
        ),
        out_specs=P(ALL, None),
        check_vma=False,
    )
```

time: 367 us -> 232 us (0.63)
  Pallas kernels: 180 us -> 63.2 us
  waiting for transfers between devices: 82.2 us -> 49.6 us
  starting transfers between devices: 19.4 us -> 39 us
  between operations: 13.7 us -> 0.41 us
  blocking collectives: 40.4 us -> 49.4 us
    pallas_call x1, Pallas kernels: 128 us -> 5.84 us  [regroup(): pl.pallas_call(regroup_kernel, grid_spec=pltpu.PrefetchScalarGridSpec(num...]
    all_gather x2 -> x0, waiting for transfers between devices: 33.1 us -> none  [the longest x1 33.1 us: local(): lax.all_gather(jnp.concatenate([mine, theirs]), 'x', axis=0, tiled=True)]
    all_to_all x2 -> x0, waiting for transfers between devices: 27 us -> none  [the longest x1 27 us: local(): lax.all_to_all(sums, PLANE, 0, 0, axis_index_groups=CROSS, tiled=True)]
    ppermute x3 -> x21, waiting for transfers between devices: 13.4 us -> 35.7 us  [over(): lax.ppermute(v, PLANE, [(group[i], group[(i + step) % 4]) for group in gr...]
    ppermute x3 -> x21, starting transfers between devices: 4.48 us -> 26.4 us  [over(): lax.ppermute(v, PLANE, [(group[i], group[(i + step) % 4]) for group in gr...]
    unnamed x17 -> x33, local copies, waits for them, and re-layouts: 5.71 us -> 20.5 us
    ppermute x3 -> x9, waiting for transfers between devices: 2.98 us -> 13.9 us  [over_x(): return lax.ppermute(v, 'x', [(i, (i + step) % X) for i in range(X)])]
    all_to_all x2 -> x0, starting transfers between devices: 9.92 us -> none  [the longest x1 5.03 us: local(): lax.all_to_all(kohn, PLANE, 0, 0, axis_index_groups=LINE, tiled=True)]
  transfers between devices with their start and end apart: 13 -> 33, of which waited for: 9 -> 11; matrix products, arithmetic and copies ran while one was open for 2% -> 5% of each run, Pallas kernels for 37% -> 20%
where the time goes in v4:
time: 232 us; the launch traced here: 231 us
  Pallas kernels  63.2 us (27%)
  waiting for transfers between devices  49.6 us (21%)
  blocking collectives  49.4 us (21%)
  starting transfers between devices  39 us (17%)
  local copies, waits for them, and re-layouts  28.7 us (12%)
    all_to_all x1, blocking collectives, local(): lax.all_to_all(outgoing, ALL, split_axis=0, concat_axis=0, tiled=True)  49.4 us
    pallas_call x6, Pallas kernels, panel_sums(): pl.pallas_call(lambda *refs: panel_kernel(n, base, sums is not None, code...  37.8 us
    ppermute x21, waiting for transfers between devices, over(): lax.ppermute(v, PLANE, [(group[i], group[(i + step) % 4]) for group in gr...  35.7 us
    ppermute x21, starting transfers between devices, over(): lax.ppermute(v, PLANE, [(group[i], group[(i + step) % 4]) for group in gr...  26.4 us
    unnamed x33, local copies, waits for them, and re-layouts  20.5 us
    ppermute x9, waiting for transfers between devices, over_x(): return lax.ppermute(v, 'x', [(i, (i + step) % X) for i in range(X)])  13.9 us
    ppermute x9, starting transfers between devices, over_x(): return lax.ppermute(v, 'x', [(i, (i + step) % X) for i in range(X)])  10 us
    pallas_call x1, Pallas kernels, pack(): pl.pallas_call(pack_kernel, grid_spec=pltpu.PrefetchScalarGridSpec(num_sc...  7.94 us
  transfers between devices with their start and end apart: 33, of which 11 were waited for; matrix products, arithmetic and copies ran while one was open for 5% of the time, Pallas kernels for 20%

profile of v4, /device:TPU:1, one launch (start us, length us, event | category | flops | bytes accessed | tf_op | source)
XLA Modules:
  0.0 231.2 jit_solution(8719949972352029636)
XLA Ops:
  0.0 3.8 %reshape.136.mine = bf16[16,4,128,128]{3,2,1,0:T(8,128)(2,1)S(1)} reshape(bf16[64,1,4,4096]{3,2,1,0:T(4,128)(2,1)} %param.9) | data formatting | bytes 4194304 | tf_op jit(solution)/shard_map/reshape | solution.py:417
  5.3 4.5 %split.1 = (bf16[8,128,128]{2,1,0:T(8,128)(2,1)}, bf16[8,128,128]{2,1,0:T(8,128)(2,1)}) custom-call(s32[1]{0:T(128)} %bitcast.9.core, bf16[8,8,4096]{2,1,0:T(8,128)(2,1)} %bitcast.64), custom_call_target="tpu_custom_call" | custom-call | tf_op jit(solution)/shard_map/split/pallas_call | solution.py:89
  15.1 2.7 %collective-permute-start.16 = (bf16[8,128,128]{2,1,0:T(8,128)(2,1)}, bf16[8,128,128]{2,1,0:T(8,128)(2,1)S(1)}, u32[]{:S(2)}, u32[]{:S(2)}) collective-permute-start(bf16[8,128,128]{2,1,0:T(8,128)(2,1)} %collective-permute-done.10), channel_id=1, source_target_pairs={{0,96},{32,0},{64,32},{96,64},{1,97},{33,1},{65,33},{97,65},{2,98}... | collective-permute-start | bytes 786440 | tf_op jit(solution)/shard_map/ppermute | solution.py:46
  19.9 4.4 %collective-permute-done.12 = bf16[8,128,128]{2,1,0:T(8,128)(2,1)S(1)} collective-permute-done((bf16[8,128,128]{2,1,0:T(8,128)(2,1)}, bf16[8,128,128]{2,1,0:T(8,128)(2,1)S(1)}, u32[]{:S(2)}, u32[]{:S(2)}) %collective-permute-start.12) | collective-permute-done | bytes 262176 | tf_op jit(solution)/shard_map/ppermute | solution.py:46
  25.8 1.7 collective-permute-start.18
  29.2 2.8 %collective-permute-start.26 = (bf16[32,128,128]{2,1,0:T(8,128)(2,1)S(1)}, bf16[32,128,128]{2,1,0:T(8,128)(2,1)}, u32[]{:S(2)}, u32[]{:S(2)}) collective-permute-start(bf16[32,128,128]{2,1,0:T(8,128)(2,1)S(1)} %constant_dynamic-update-slice_fusion.refs_4_), channel_id=1, source_target_pairs={{0,12},{4,0},{8,4},{12,8},{1,13},{5,1},{9,5},{13,9},{2,14},{6,2},{... | collective-permute-start | bytes 3145736 | tf_op jit(solution)/shard_map/ppermute | solution.py:34
  34.8 4.6 %collective-permute-done.1 = s32[128]{0:T(128)S(1)} collective-permute-done((s32[128]{0:T(128)S(1)}, s32[128]{0:T(128)S(1)}, u32[]{:S(2)}, u32[]{:S(2)}) %collective-permute-start.1) | collective-permute-done | bytes 544 | tf_op jit(solution)/shard_map/ppermute | solution.py:46
  43.3 2.7 %collective-permute-done.3 = s32[128]{0:T(128)S(1)} collective-permute-done((s32[128]{0:T(128)S(1)}, s32[128]{0:T(128)S(1)}, u32[]{:S(2)}, u32[]{:S(2)}) %collective-permute-start.3) | collective-permute-done | bytes 544 | tf_op jit(solution)/shard_map/ppermute | solution.py:46
  46.5 3.2 %collective-permute-done.21 = s32[8,128]{1,0:T(8,128)S(1)} collective-permute-done((s32[8,128]{1,0:T(8,128)S(1)}, s32[8,128]{1,0:T(8,128)S(1)}, u32[]{:S(2)}, u32[]{:S(2)}) %collective-permute-start.21) | collective-permute-done | bytes 4128 | tf_op jit(solution)/shard_map/ppermute | solution.py:34
  49.8 5.4 %collective-permute-done.22 = s32[8,128]{1,0:T(8,128)S(1)} collective-permute-done((s32[8,128]{1,0:T(8,128)S(1)}, s32[8,128]{1,0:T(8,128)S(1)}, u32[]{:S(2)}, u32[]{:S(2)}) %collective-permute-start.22) | collective-permute-done | bytes 4128 | tf_op jit(solution)/shard_map/ppermute | solution.py:34
  56.2 3.6 %collective-permute-start.4 = (s32[8,128]{1,0:T(8,128)S(1)}, s32[8,128]{1,0:T(8,128)S(1)}, u32[]{:S(2)}, u32[]{:S(2)}) collective-permute-start(s32[8,128]{1,0:T(8,128)S(1)} %bitcast.71), channel_id=1, source_target_pairs={{0,8},{4,12},{8,0},{12,4},{1,9},{5,13},{9,1},{13,5},{2,10},{6,14},... | collective-permute-start | bytes 12296 | tf_op jit(solution)/shard_map/ppermute | solution.py:34
  60.4 5.8 %regroup.1 = (bf16[2,4,4,128,128]{4,3,2,1,0:T(8,128)(2,1)S(1)}, bf16[2,4,4,128,128]{4,3,2,1,0:T(8,128)(2,1)}, bf16[2,4,4,128,128]{4,3,2,1,0:T(8,128)(2,1)S(1)}, ...) custom-call(s32[3]{0:T(128)S(1)} %pad_add_fusion.6.at, bf16[16,4,128,128]{3,2,1,0:T(8,128)(2,1)S(1)} %reshape.136.mine, ...), custom_call_target="tpu_custom_call" | custom-call | tf_op jit(solution)/shard_map/regroup/pallas_call | solution.py:122
  69.0 2.8 %collective-permute-done.4 = s32[8,128]{1,0:T(8,128)S(1)} collective-permute-done((s32[8,128]{1,0:T(8,128)S(1)}, s32[8,128]{1,0:T(8,128)S(1)}, u32[]{:S(2)}, u32[]{:S(2)}) %collective-permute-start.4) | collective-permute-done | bytes 4128 | tf_op jit(solution)/shard_map/ppermute | solution.py:34
  72.1 2.7 %collective-permute-start.24 = (bf16[2,4,4,128,128]{4,3,2,1,0:T(8,128)(2,1)}, bf16[2,4,4,128,128]{4,3,2,1,0:T(8,128)(2,1)}, u32[]{:S(2)}, u32[]{:S(2)}) collective-permute-start(bf16[2,4,4,128,128]{4,3,2,1,0:T(8,128)(2,1)} %copy-done.7), channel_id=1, source_target_pairs={{0,12},{4,0},{8,4},{12,8},{1,13},{5,1},{9,5},{13,9},{2,14},{6,2},{... | collective-permute-start | bytes 3145736 | tf_op jit(solution)/shard_map/ppermute | solution.py:34
  77.8 15.1 %collective-permute-done.6 = bf16[4,4,128,128]{3,2,1,0:T(8,128)(2,1)} collective-permute-done((bf16[4,4,128,128]{3,2,1,0:T(8,128)(2,1)}, bf16[4,4,128,128]{3,2,1,0:T(8,128)(2,1)}, u32[]{:S(2)}, u32[]{:S(2)}) %collective-permute-start.6) | collective-permute-done | bytes 524320 | tf_op jit(solution)/shard_map/ppermute | solution.py:34
  99.3 8.4 %own_panel.1.refs_10_ = f32[4,8,32,16,128]{4,3,2,1,0:T(8,128)S(1)} custom-call(s32[128]{0:T(128)S(1)} %reshape.167.refs_0_, s32[512]{0:T(512)S(1)} %concatenate.44.refs_1_, bf16[2,4,4,128,128]{4,3,2,1,0:T(8,128)(2,1)S(1)} %copy-done.4, bf16[2,4,4,128,128]{4,3,2,1,0:T(8,128)(2,1)S(1)} %copy-done.4, bf16[32,128,128]{2,1,0:T(8,128)(2,1)S(1)} %copy-done.6, ...), custom_call_target="tpu_custom_call" | custom-call | flops 536870912 | bytes 23068672 | tf_op jit(solution)/shard_map/own_panel/pallas_call | solution.py:237
  107.8 3.3 %copy-done.2 = f32[4,8,32,16,128]{4,3,2,1,0:T(8,128)} copy-done((f32[4,8,32,16,128]{4,3,2,1,0:T(8,128)}, f32[4,8,32,16,128]{4,3,2,1,0:T(8,128)S(1)}, u32[]{:S(2)}) %copy-start.2) | copy-done | bytes 8388632
  111.0 15.9 %near_panels.1.refs_6_ = f32[4,8,32,16,128]{4,3,2,1,0:T(8,128)} custom-call(s32[256]{0:T(256)S(1)} %pad_add_fusion.4.refs_0_, s32[1024]{0:T(1024)S(1)} %pad_add_fusion.1.refs_1_, bf16[2,4,4,128,128]{4,3,2,1,0:T(8,128)(2,1)} %collective-permute-done.23.refs_2_.refs_3_, bf16[2,4,4,128,128]{4,3,2,1,0:T(8,128)(2,1)} %collective-permute-done.23.refs_2_.refs_3_, ...), custom_call_target="tpu_custom_call" | custom-call | flops 1073741824 | bytes 25165824 | tf_op jit(solution)/shard_map/near_panels/pallas_call | solution.py:237
  126.9 3.4 %copy-done = f32[4,8,32,16,128]{4,3,2,1,0:T(8,128)S(1)} copy-done((f32[4,8,32,16,128]{4,3,2,1,0:T(8,128)S(1)}, f32[4,8,32,16,128]{4,3,2,1,0:T(8,128)}, u32[]{:S(2)}) %copy-start) | copy-done | bytes 8388632
  130.3 3.1 %last_panel.7 = (s16[4,33,16,128]{3,2,1,0:T(8,128)(2,1)S(1)}, s16[4,33,16,128]{3,2,1,0:T(8,128)(2,1)S(1)}) custom-call(s32[128]{0:T(128)S(1)} %reshape.164.refs_0_, s32[512]{0:T(512)S(1)} %get-tuple-element.27.refs_1_, bf16[1,4,4,128,128]{4,3,2,1,0:T(8,128)(2,1)S(1)} %bitcast.56, bf16[1,4,4,128,128]{4,3,2,1,0:T(8,128)(2,1)S(1)} %bitcast.60, ...), custom_call_target="tpu_custom_call" | custom-call | flops 134217728 | bytes 7340032 | tf_op jit(solution)/shard_map/last_panel/pallas_call | solution.py:237
  134.8 2.9 %collective-permute-start.31 = (s16[4,33,16,128]{3,2,1,0:T(8,128)(2,1)S(1)}, s16[4,33,16,128]{3,2,1,0:T(8,128)(2,1)}, u32[]{:S(2)}, u32[]{:S(2)}) collective-permute-start(s16[4,33,16,128]{3,2,1,0:T(8,128)(2,1)S(1)} %get-tuple-element.22), channel_id=1, source_target_pairs={{0,3},{1,0},{2,1},{3,2},{4,7},{5,4},{6,5},{7,6},{8,11},{9,8},{10,9... | collective-permute-start | bytes 1622024 | tf_op jit(solution)/shard_map/ppermute | solution.py:34
  137.7 4.0 %last_panel.6 = s16[8,33,16,128]{3,2,1,0:T(8,128)(2,1)} custom-call(s32[128]{0:T(128)S(1)} %reshape.164.refs_0_, s32[512]{0:T(512)S(1)} %get-tuple-element.27.refs_1_, bf16[1,4,4,128,128]{4,3,2,1,0:T(8,128)(2,1)S(1)} %bitcast.57, bf16[1,4,4,128,128]{4,3,2,1,0:T(8,128)(2,1)S(1)} %bitcast.61, bf16[32,128,128]{2,1,0:T(8,128)(2,1)S(1)} %collective-permute-done.14.refs_4_, ...), custom_call_target="tpu_custom_call" | custom-call | flops 134217728 | bytes 7340032 | tf_op jit(solution)/shard_map/last_panel/pallas_call | solution.py:237
  141.8 4.1 %last_panel.5 = s16[8,33,16,128]{3,2,1,0:T(8,128)(2,1)} custom-call(s32[128]{0:T(128)S(1)} %reshape.164.refs_0_, s32[512]{0:T(512)S(1)} %get-tuple-element.27.refs_1_, bf16[1,4,4,128,128]{4,3,2,1,0:T(8,128)(2,1)S(1)} %bitcast.58, bf16[1,4,4,128,128]{4,3,2,1,0:T(8,128)(2,1)S(1)} %bitcast.62, bf16[32,128,128]{2,1,0:T(8,128)(2,1)S(1)} %collective-permute-done.14.refs_4_, ...), custom_call_target="tpu_custom_call" | custom-call | flops 134217728 | bytes 7340032 | tf_op jit(solution)/shard_map/last_panel/pallas_call | solution.py:237
  145.9 2.7 %collective-permute-start.27 = (s16[8,33,16,128]{3,2,1,0:T(8,128)(2,1)}, s16[8,33,16,128]{3,2,1,0:T(8,128)(2,1)}, u32[]{:S(2)}, u32[]{:S(2)}) collective-permute-start(s16[8,33,16,128]{3,2,1,0:T(8,128)(2,1)} %last_panel.5), channel_id=1, source_target_pairs={{0,3},{1,0},{2,1},{3,2},{4,7},{5,4},{6,5},{7,6},{8,11},{9,8},{10,9... | collective-permute-start | bytes 3244040 | tf_op jit(solution)/shard_map/ppermute | solution.py:34
  148.8 2.7 %collective-permute-start.32 = (s16[4,33,16,128]{3,2,1,0:T(8,128)(2,1)}, s16[4,33,16,128]{3,2,1,0:T(8,128)(2,1)}, u32[]{:S(2)}, u32[]{:S(2)}) collective-permute-start(s16[4,33,16,128]{3,2,1,0:T(8,128)(2,1)} %collective-permute-done.31), channel_id=1, source_target_pairs={{0,3},{1,0},{2,1},{3,2},{4,7},{5,4},{6,5},{7,6},{8,11},{9,8},{10,9... | collective-permute-start | bytes 1622024 | tf_op jit(solution)/shard_map/ppermute | solution.py:34
  152.0 3.4 %copy-done.1 = f32[4,8,32,16,128]{4,3,2,1,0:T(8,128)S(1)} copy-done((f32[4,8,32,16,128]{4,3,2,1,0:T(8,128)S(1)}, f32[4,8,32,16,128]{4,3,2,1,0:T(8,128)}, u32[]{:S(2)}) %copy-start.1) | copy-done | bytes 8388632
  155.4 2.4 %last_panel.4.own = f32[1,8,32,16,128]{4,3,2,1,0:T(8,128)S(1)} custom-call(s32[128]{0:T(128)S(1)} %reshape.164.refs_0_, s32[512]{0:T(512)S(1)} %get-tuple-element.27.refs_1_, bf16[1,4,4,128,128]{4,3,2,1,0:T(8,128)(2,1)S(1)} %bitcast.59, bf16[1,4,4,128,128]{4,3,2,1,0:T(8,128)(2,1)S(1)} %bitcast.63, bf16[32,128,128]{2,1,0:T(8,128)(2,1)S(1)} %collective-permute-done.14.refs_4_, ...), custom_call_target="tpu_custom_call" | custom-call | flops 134217728 | bytes 7340032 | tf_op jit(solution)/shard_map/last_panel/pallas_call | solution.py:237
  157.7 5.7 %collective-permute-done.30.far0 = s16[4,33,16,128]{3,2,1,0:T(8,128)(2,1)} collective-permute-done((s16[4,33,16,128]{3,2,1,0:T(8,128)(2,1)}, s16[4,33,16,128]{3,2,1,0:T(8,128)(2,1)}, u32[]{:S(2)}, u32[]{:S(2)}) %collective-permute-start.30) | collective-permute-done | bytes 540704 | tf_op jit(solution)/shard_map/ppermute | solution.py:34
  163.4 3.4 %collective-permute-done.32.far1 = s16[4,33,16,128]{3,2,1,0:T(8,128)(2,1)} collective-permute-done((s16[4,33,16,128]{3,2,1,0:T(8,128)(2,1)}, s16[4,33,16,128]{3,2,1,0:T(8,128)(2,1)}, u32[]{:S(2)}, u32[]{:S(2)}) %collective-permute-start.32) | collective-permute-done | bytes 540704 | tf_op jit(solution)/shard_map/ppermute | solution.py:34
  166.8 7.9 %pack.1 = s16[128,80,128]{2,1,0:T(8,128)(2,1)S(1)} custom-call(s32[256]{0:T(256)S(1)} %add_bitcast_fusion.slots, f32[1,8,32,16,128]{4,3,2,1,0:T(8,128)S(1)} %last_panel.4.own, s16[8,33,16,128]{3,2,1,0:T(8,128)(2,1)} %collective-permute-done.27.after, s16[8,33,16,128]{3,2,1,0:T(8,128)(2,1)} %collective-permute-done.28.before, ...), custom_call_target="tpu_custom_call" | custom-call | tf_op jit(solution)/shard_map/pack/pallas_call | solution.py:326
  174.8 49.4 %all_to_all.5 = s16[128,80,128]{2,1,0:T(8,128)(2,1)S(1)} all-to-all(s16[128,80,128]{2,1,0:T(8,128)(2,1)S(1)} %pack.1), channel_id=1, replica_groups=mesh['x'=4,'core'=2,'z'=4,'y'=4] {'x','core','z','y'}, dimensions={0} | all-to-all | bytes 5242880 | tf_op jit(solution)/shard_map/all_to_all | solution.py:450
  224.2 7.1 %unpack.1 = f32[256,4096]{1,0:T(8,128)} custom-call(s16[4,2,16,80,128]{4,3,2,1,0:T(8,128)(2,1)S(1)} %bitcast.55), custom_call_target="tpu_custom_call" | custom-call | tf_op jit(solution)/shard_map/unpack/pallas_call | solution.py:363
  (120 shorter events, 35.3 us)
Async XLA Ops:
  3.8 52.4 %collective-permute-start.5 = (bf16[16,4,128,128]{3,2,1,0:T(8,128)(2,1)S(1)}, bf16[16,4,128,128]{3,2,1,0:T(8,128)(2,1)}, u32[]{:S(2)}, u32[]{:S(2)}) collective-permute-start(bf16[16,4,128,128]{3,2,1,0:T(8,128)(2,1)S(1)} %reshape.136.mine), channel_id=1, source_target_pairs={{0,16},{16,0},{1,17},{17,1},{2,18},{18,2},{3,19},{19,3},{4,20},{20... | collective-permute-start | bytes 6291464 | tf_op jit(solution)/shard_map/ppermute | solution.py:50
  9.9 4.2 %collective-permute-start.10 = (bf16[8,128,128]{2,1,0:T(8,128)(2,1)}, bf16[8,128,128]{2,1,0:T(8,128)(2,1)}, u32[]{:S(2)}, u32[]{:S(2)}) collective-permute-start(bf16[8,128,128]{2,1,0:T(8,128)(2,1)} %get-tuple-element.17), channel_id=1, source_target_pairs={{0,16},{16,0},{1,17},{17,1},{2,18},{18,2},{3,19},{19,3},{4,20},{20... | collective-permute-start | bytes 786440 | tf_op jit(solution)/shard_map/ppermute | solution.py:50
  9.9 8.8 %collective-permute-start.11 = (bf16[8,128,128]{2,1,0:T(8,128)(2,1)}, bf16[8,128,128]{2,1,0:T(8,128)(2,1)S(1)}, u32[]{:S(2)}, u32[]{:S(2)}) collective-permute-start(bf16[8,128,128]{2,1,0:T(8,128)(2,1)} %get-tuple-element.16), channel_id=1, source_target_pairs={{0,32},{32,64},{64,96},{96,0},{1,33},{33,65},{65,97},{97,1},{2,34}... | collective-permute-start | bytes 786440 | tf_op jit(solution)/shard_map/ppermute | solution.py:46
  11.2 16.4 %collective-permute-start.15 = (bf16[8,128,128]{2,1,0:T(8,128)(2,1)}, bf16[8,128,128]{2,1,0:T(8,128)(2,1)}, u32[]{:S(2)}, u32[]{:S(2)}) collective-permute-start(bf16[8,128,128]{2,1,0:T(8,128)(2,1)} %get-tuple-element.16), channel_id=1, source_target_pairs={{0,96},{32,0},{64,32},{96,64},{1,97},{33,1},{65,33},{97,65},{2,98}... | collective-permute-start | bytes 786440 | tf_op jit(solution)/shard_map/ppermute | solution.py:46
  14.0 10.3 %collective-permute-start.12 = (bf16[8,128,128]{2,1,0:T(8,128)(2,1)}, bf16[8,128,128]{2,1,0:T(8,128)(2,1)S(1)}, u32[]{:S(2)}, u32[]{:S(2)}) collective-permute-start(bf16[8,128,128]{2,1,0:T(8,128)(2,1)} %collective-permute-done.10), channel_id=1, source_target_pairs={{0,32},{32,64},{64,96},{96,0},{1,33},{33,65},{65,97},{97,1},{2,34}... | collective-permute-start | bytes 786440 | tf_op jit(solution)/shard_map/ppermute | solution.py:46
  15.1 10.7 %collective-permute-start.16 = (bf16[8,128,128]{2,1,0:T(8,128)(2,1)}, bf16[8,128,128]{2,1,0:T(8,128)(2,1)S(1)}, u32[]{:S(2)}, u32[]{:S(2)}) collective-permute-start(bf16[8,128,128]{2,1,0:T(8,128)(2,1)} %collective-permute-done.10), channel_id=1, source_target_pairs={{0,96},{32,0},{64,32},{96,64},{1,97},{33,1},{65,33},{97,65},{2,98}... | collective-permute-start | bytes 786440 | tf_op jit(solution)/shard_map/ppermute | solution.py:46
  18.7 14.1 %collective-permute-start.17 = (bf16[8,128,128]{2,1,0:T(8,128)(2,1)S(1)}, bf16[8,128,128]{2,1,0:T(8,128)(2,1)S(1)}, u32[]{:S(2)}, u32[]{:S(2)}) collective-permute-start(bf16[8,128,128]{2,1,0:T(8,128)(2,1)S(1)} %collective-permute-done.11), channel_id=1, source_target_pairs={{0,32},{32,64},{64,96},{96,0},{1,33},{33,65},{65,97},{97,1},{2,34}... | collective-permute-start | bytes 786440 | tf_op jit(solution)/shard_map/ppermute | solution.py:46
  24.4 47.5 %collective-permute-start.13 = (bf16[32,128,128]{2,1,0:T(8,128)(2,1)S(1)}, bf16[32,128,128]{2,1,0:T(8,128)(2,1)}, u32[]{:S(2)}, u32[]{:S(2)}) collective-permute-start(bf16[32,128,128]{2,1,0:T(8,128)(2,1)S(1)} %constant_dynamic-update-slice_fusion.refs_4_), channel_id=1, source_target_pairs={{0,4},{4,8},{8,12},{12,0},{1,5},{5,9},{9,13},{13,1},{2,6},{6,10},{... | collective-permute-start | bytes 3145736 | tf_op jit(solution)/shard_map/ppermute | solution.py:34
  25.8 7.7 %collective-permute-start.18 = (bf16[8,128,128]{2,1,0:T(8,128)(2,1)S(1)}, bf16[8,128,128]{2,1,0:T(8,128)(2,1)S(1)}, u32[]{:S(2)}, u32[]{:S(2)}) collective-permute-start(bf16[8,128,128]{2,1,0:T(8,128)(2,1)S(1)} %collective-permute-done.16), channel_id=1, source_target_pairs={{0,96},{32,0},{64,32},{96,64},{1,97},{33,1},{65,33},{97,65},{2,98}... | collective-permute-start | bytes 786440 | tf_op jit(solution)/shard_map/ppermute | solution.py:46
  29.2 42.9 %collective-permute-start.26 = (bf16[32,128,128]{2,1,0:T(8,128)(2,1)S(1)}, bf16[32,128,128]{2,1,0:T(8,128)(2,1)}, u32[]{:S(2)}, u32[]{:S(2)}) collective-permute-start(bf16[32,128,128]{2,1,0:T(8,128)(2,1)S(1)} %constant_dynamic-update-slice_fusion.refs_4_), channel_id=1, source_target_pairs={{0,12},{4,0},{8,4},{12,8},{1,13},{5,1},{9,5},{13,9},{2,14},{6,2},{... | collective-permute-start | bytes 3145736 | tf_op jit(solution)/shard_map/ppermute | solution.py:34
  34.2 40.6 %collective-permute-start.19 = (bf16[32,128,128]{2,1,0:T(8,128)(2,1)}, bf16[32,128,128]{2,1,0:T(8,128)(2,1)}, u32[]{:S(2)}, u32[]{:S(2)}) collective-permute-start(bf16[32,128,128]{2,1,0:T(8,128)(2,1)} %constant_dynamic-update-slice_fusion.4.refs_5_), channel_id=1, source_target_pairs={{0,12},{4,0},{8,4},{12,8},{1,13},{5,1},{9,5},{13,9},{2,14},{6,2},{... | collective-permute-start | bytes 3145736 | tf_op jit(solution)/shard_map/ppermute | solution.py:34
  34.8 4.6 %collective-permute-start.1 = (s32[128]{0:T(128)S(1)}, s32[128]{0:T(128)S(1)}, u32[]{:S(2)}, u32[]{:S(2)}) collective-permute-start(s32[128]{0:T(128)S(1)} %pad_add_fusion.5), channel_id=1, source_target_pairs={{0,32},{32,64},{64,96},{96,0},{1,33},{33,65},{65,97},{97,1},{2,34}... | collective-permute-start | bytes 1544 | tf_op jit(solution)/shard_map/ppermute | solution.py:46
  39.3 2.8 %collective-permute-start.2 = (s32[128]{0:T(128)S(1)}, s32[128]{0:T(128)S(1)}, u32[]{:S(2)}, u32[]{:S(2)}) collective-permute-start(s32[128]{0:T(128)S(1)} %pad_add_fusion.5), channel_id=1, source_target_pairs={{0,96},{32,0},{64,32},{96,64},{1,97},{33,1},{65,33},{97,65},{2,98}... | collective-permute-start | bytes 1544 | tf_op jit(solution)/shard_map/ppermute | solution.py:46
  42.1 3.9 %collective-permute-start.3 = (s32[128]{0:T(128)S(1)}, s32[128]{0:T(128)S(1)}, u32[]{:S(2)}, u32[]{:S(2)}) collective-permute-start(s32[128]{0:T(128)S(1)} %pad_add_fusion.5), channel_id=1, source_target_pairs={{0,64},{32,96},{64,0},{96,32},{1,65},{33,97},{65,1},{97,33},{2,66}... | collective-permute-start | bytes 1544 | tf_op jit(solution)/shard_map/ppermute | solution.py:46
  46.1 3.7 %collective-permute-start.21 = (s32[8,128]{1,0:T(8,128)S(1)}, s32[8,128]{1,0:T(8,128)S(1)}, u32[]{:S(2)}, u32[]{:S(2)}) collective-permute-start(s32[8,128]{1,0:T(8,128)S(1)} %bitcast.69), channel_id=1, source_target_pairs={{0,4},{4,8},{8,12},{12,0},{1,5},{5,9},{9,13},{13,1},{2,6},{6,10},{... | collective-permute-start | bytes 12296 | tf_op jit(solution)/shard_map/ppermute | solution.py:34
  49.8 5.4 %collective-permute-start.22 = (s32[8,128]{1,0:T(8,128)S(1)}, s32[8,128]{1,0:T(8,128)S(1)}, u32[]{:S(2)}, u32[]{:S(2)}) collective-permute-start(s32[8,128]{1,0:T(8,128)S(1)} %bitcast.70), channel_id=1, source_target_pairs={{0,12},{4,0},{8,4},{12,8},{1,13},{5,1},{9,5},{13,9},{2,14},{6,2},{... | collective-permute-start | bytes 12296 | tf_op jit(solution)/shard_map/ppermute | solution.py:34
  55.1 22.6 %collective-permute-start.25 = (bf16[32,128,128]{2,1,0:T(8,128)(2,1)}, bf16[32,128,128]{2,1,0:T(8,128)(2,1)}, u32[]{:S(2)}, u32[]{:S(2)}) collective-permute-start(bf16[32,128,128]{2,1,0:T(8,128)(2,1)} %constant_dynamic-update-slice_fusion.4.refs_5_), channel_id=1, source_target_pairs={{0,4},{4,8},{8,12},{12,0},{1,5},{5,9},{9,13},{13,1},{2,6},{6,10},{... | collective-permute-start | bytes 3145736 | tf_op jit(solution)/shard_map/ppermute | solution.py:34
  56.2 15.7 %collective-permute-start.4 = (s32[8,128]{1,0:T(8,128)S(1)}, s32[8,128]{1,0:T(8,128)S(1)}, u32[]{:S(2)}, u32[]{:S(2)}) collective-permute-start(s32[8,128]{1,0:T(8,128)S(1)} %bitcast.71), channel_id=1, source_target_pairs={{0,8},{4,12},{8,0},{12,4},{1,9},{5,13},{9,1},{13,5},{2,10},{6,14},... | collective-permute-start | bytes 12296 | tf_op jit(solution)/shard_map/ppermute | solution.py:34
  71.9 23.6 %collective-permute-start.23 = (bf16[2,4,4,128,128]{4,3,2,1,0:T(8,128)(2,1)}, bf16[2,4,4,128,128]{4,3,2,1,0:T(8,128)(2,1)}, u32[]{:S(2)}, u32[]{:S(2)}) collective-permute-start(bf16[2,4,4,128,128]{4,3,2,1,0:T(8,128)(2,1)} %get-tuple-element.18), channel_id=1, source_target_pairs={{0,4},{4,8},{8,12},{12,0},{1,5},{5,9},{9,13},{13,1},{2,6},{6,10},{... | collective-permute-start | bytes 3145736 | tf_op jit(solution)/shard_map/ppermute | solution.py:34
  71.9 21.1 %collective-permute-start.6 = (bf16[4,4,128,128]{3,2,1,0:T(8,128)(2,1)}, bf16[4,4,128,128]{3,2,1,0:T(8,128)(2,1)}, u32[]{:S(2)}, u32[]{:S(2)}) collective-permute-start(bf16[4,4,128,128]{3,2,1,0:T(8,128)(2,1)} %get-tuple-element.14), channel_id=1, source_target_pairs={{0,4},{4,8},{8,12},{12,0},{1,5},{5,9},{9,13},{13,1},{2,6},{6,10},{... | collective-permute-start | bytes 1572872 | tf_op jit(solution)/shard_map/ppermute | solution.py:34
  72.1 38.9 %collective-permute-start.24 = (bf16[2,4,4,128,128]{4,3,2,1,0:T(8,128)(2,1)}, bf16[2,4,4,128,128]{4,3,2,1,0:T(8,128)(2,1)}, u32[]{:S(2)}, u32[]{:S(2)}) collective-permute-start(bf16[2,4,4,128,128]{4,3,2,1,0:T(8,128)(2,1)} %copy-done.7), channel_id=1, source_target_pairs={{0,12},{4,0},{8,4},{12,8},{1,13},{5,1},{9,5},{13,9},{2,14},{6,2},{... | collective-permute-start | bytes 3145736 | tf_op jit(solution)/shard_map/ppermute | solution.py:34
  74.9 19.1 %collective-permute-start.8 = (bf16[4,4,128,128]{3,2,1,0:T(8,128)(2,1)}, bf16[4,4,128,128]{3,2,1,0:T(8,128)(2,1)}, u32[]{:S(2)}, u32[]{:S(2)}) collective-permute-start(bf16[4,4,128,128]{3,2,1,0:T(8,128)(2,1)} %copy-done.8), channel_id=1, source_target_pairs={{0,12},{4,0},{8,4},{12,8},{1,13},{5,1},{9,5},{13,9},{2,14},{6,2},{... | collective-permute-start | bytes 1572872 | tf_op jit(solution)/shard_map/ppermute | solution.py:34
  77.7 49.1 %collective-permute-start.14 = (bf16[32,128,128]{2,1,0:T(8,128)(2,1)}, bf16[32,128,128]{2,1,0:T(8,128)(2,1)S(1)}, u32[]{:S(2)}, u32[]{:S(2)}) collective-permute-start(bf16[32,128,128]{2,1,0:T(8,128)(2,1)} %collective-permute-done.13.refs_6_), channel_id=1, source_target_pairs={{0,4},{4,8},{8,12},{12,0},{1,5},{5,9},{9,13},{13,1},{2,6},{6,10},{... | collective-permute-start | bytes 3145736 | tf_op jit(solution)/shard_map/ppermute | solution.py:34
  93.0 33.9 %collective-permute-start.20 = (bf16[32,128,128]{2,1,0:T(8,128)(2,1)}, bf16[32,128,128]{2,1,0:T(8,128)(2,1)S(1)}, u32[]{:S(2)}, u32[]{:S(2)}) collective-permute-start(bf16[32,128,128]{2,1,0:T(8,128)(2,1)} %collective-permute-done.19.refs_9_), channel_id=1, source_target_pairs={{0,12},{4,0},{8,4},{12,8},{1,13},{5,1},{9,5},{13,9},{2,14},{6,2},{... | collective-permute-start | bytes 3145736 | tf_op jit(solution)/shard_map/ppermute | solution.py:34
  94.0 32.9 %collective-permute-start.7 = (bf16[4,4,128,128]{3,2,1,0:T(8,128)(2,1)}, bf16[4,4,128,128]{3,2,1,0:T(8,128)(2,1)S(1)}, u32[]{:S(2)}, u32[]{:S(2)}) collective-permute-start(bf16[4,4,128,128]{3,2,1,0:T(8,128)(2,1)} %collective-permute-done.6), channel_id=1, source_target_pairs={{0,4},{4,8},{8,12},{12,0},{1,5},{5,9},{9,13},{13,1},{2,6},{6,10},{... | collective-permute-start | bytes 1572872 | tf_op jit(solution)/shard_map/ppermute | solution.py:34
  95.5 31.4 %collective-permute-start.9 = (bf16[4,4,128,128]{3,2,1,0:T(8,128)(2,1)}, bf16[4,4,128,128]{3,2,1,0:T(8,128)(2,1)S(1)}, u32[]{:S(2)}, u32[]{:S(2)}) collective-permute-start(bf16[4,4,128,128]{3,2,1,0:T(8,128)(2,1)} %collective-permute-done.8), channel_id=1, source_target_pairs={{0,12},{4,0},{8,4},{12,8},{1,13},{5,1},{9,5},{13,9},{2,14},{6,2},{... | collective-permute-start | bytes 1572872 | tf_op jit(solution)/shard_map/ppermute | solution.py:34
  133.4 15.3 %collective-permute-start.29 = (s16[4,33,16,128]{3,2,1,0:T(8,128)(2,1)S(1)}, s16[4,33,16,128]{3,2,1,0:T(8,128)(2,1)}, u32[]{:S(2)}, u32[]{:S(2)}) collective-permute-start(s16[4,33,16,128]{3,2,1,0:T(8,128)(2,1)S(1)} %get-tuple-element.21), channel_id=1, source_target_pairs={{0,1},{1,2},{2,3},{3,0},{4,5},{5,6},{6,7},{7,4},{8,9},{9,10},{10,1... | collective-permute-start | bytes 1622024 | tf_op jit(solution)/shard_map/ppermute | solution.py:34
  134.8 14.0 %collective-permute-start.31 = (s16[4,33,16,128]{3,2,1,0:T(8,128)(2,1)S(1)}, s16[4,33,16,128]{3,2,1,0:T(8,128)(2,1)}, u32[]{:S(2)}, u32[]{:S(2)}) collective-permute-start(s16[4,33,16,128]{3,2,1,0:T(8,128)(2,1)S(1)} %get-tuple-element.22), channel_id=1, source_target_pairs={{0,3},{1,0},{2,1},{3,2},{4,7},{5,4},{6,5},{7,6},{8,11},{9,8},{10,9... | collective-permute-start | bytes 1622024 | tf_op jit(solution)/shard_map/ppermute | solution.py:34
  141.7 25.1 %collective-permute-start.28 = (s16[8,33,16,128]{3,2,1,0:T(8,128)(2,1)}, s16[8,33,16,128]{3,2,1,0:T(8,128)(2,1)}, u32[]{:S(2)}, u32[]{:S(2)}) collective-permute-start(s16[8,33,16,128]{3,2,1,0:T(8,128)(2,1)} %last_panel.6), channel_id=1, source_target_pairs={{0,1},{1,2},{2,3},{3,0},{4,5},{5,6},{6,7},{7,4},{8,9},{9,10},{10,1... | collective-permute-start | bytes 3244040 | tf_op jit(solution)/shard_map/ppermute | solution.py:34
  145.9 20.9 %collective-permute-start.27 = (s16[8,33,16,128]{3,2,1,0:T(8,128)(2,1)}, s16[8,33,16,128]{3,2,1,0:T(8,128)(2,1)}, u32[]{:S(2)}, u32[]{:S(2)}) collective-permute-start(s16[8,33,16,128]{3,2,1,0:T(8,128)(2,1)} %last_panel.5), channel_id=1, source_target_pairs={{0,3},{1,0},{2,1},{3,2},{4,7},{5,4},{6,5},{7,6},{8,11},{9,8},{10,9... | collective-permute-start | bytes 3244040 | tf_op jit(solution)/shard_map/ppermute | solution.py:34
  148.7 14.7 %collective-permute-start.30 = (s16[4,33,16,128]{3,2,1,0:T(8,128)(2,1)}, s16[4,33,16,128]{3,2,1,0:T(8,128)(2,1)}, u32[]{:S(2)}, u32[]{:S(2)}) collective-permute-start(s16[4,33,16,128]{3,2,1,0:T(8,128)(2,1)} %collective-permute-done.29), channel_id=1, source_target_pairs={{0,1},{1,2},{2,3},{3,0},{4,5},{5,6},{6,7},{7,4},{8,9},{9,10},{10,1... | collective-permute-start | bytes 1622024 | tf_op jit(solution)/shard_map/ppermute | solution.py:34
  148.8 18.0 %collective-permute-start.32 = (s16[4,33,16,128]{3,2,1,0:T(8,128)(2,1)}, s16[4,33,16,128]{3,2,1,0:T(8,128)(2,1)}, u32[]{:S(2)}, u32[]{:S(2)}) collective-permute-start(s16[4,33,16,128]{3,2,1,0:T(8,128)(2,1)} %collective-permute-done.31), channel_id=1, source_target_pairs={{0,3},{1,0},{2,1},{3,2},{4,7},{5,4},{6,5},{7,6},{8,11},{9,8},{10,9... | collective-permute-start | bytes 1622024 | tf_op jit(solution)/shard_map/ppermute | solution.py:34
  (14 other events, 140.4 us)

commit v5 on v4

--- a/solution.py
+++ b/solution.py
@@ -15,6 +15,7 @@
 PLANE = ("core", "z", "y")
 TOP = 32766.0
 MSG = 80
+PART = 8 * 128 + 16
 ORDER = (2, 1, 3, 0)
 
 
@@ -50,7 +51,7 @@
     return lax.ppermute(v, "core", [(0, 1), (1, 0)])
 
 
-def split_kernel(core, d_ref, mine, theirs, flat, wide):
+def split_kernel(core, d_ref, i_ref, mine, theirs, flat, wide):
     lane32 = lax.broadcasted_iota(jnp.int32, (32, 128), 1)
     lane64 = lax.broadcasted_iota(jnp.int32, (64, 128), 1)
 
@@ -76,27 +77,33 @@
         first = jnp.concatenate([v[0], v[1]], axis=0).T
         second = jnp.concatenate([v[2], v[3]], axis=0).T
         swapped = core[0] == 1
-        mine[k] = jnp.where(swapped, second, first).astype(jnp.bfloat16)
-        theirs[k] = jnp.where(swapped, first, second).astype(jnp.bfloat16)
+        at = pl.ds(pl.multiple_of(k * 128, 128), 128)
+        mine[at, :] = jnp.where(swapped, second, first).astype(jnp.bfloat16)
+        theirs[at, :] = jnp.where(swapped, first, second).astype(jnp.bfloat16)
         return 0
 
     lax.fori_loop(0, 8, one, 0)
-
-
-def split(core, dens):
-    half = jax.ShapeDtypeStruct((8, 128, 128), jnp.bfloat16)
-    whole = pl.BlockSpec((8, 128, 128), lambda i, *_: (0, 0, 0))
+    ints = i_ref[...].astype(jnp.float32).astype(jnp.bfloat16)
+    mine[8 * 128:, :] = ints
+    theirs[8 * 128:, :] = ints
+
+
+def split(core, dens, ints):
+    half = jax.ShapeDtypeStruct((PART, 128), jnp.bfloat16)
+    whole = pl.BlockSpec((PART, 128), lambda i, *_: (0, 0))
     return pl.pallas_call(
         split_kernel,
         grid_spec=pltpu.PrefetchScalarGridSpec(
             num_scalar_prefetch=1, grid=(1,),
-            in_specs=[pl.BlockSpec((8, SP, B * B), lambda i, *_: (0, 0, 0))],
+            in_specs=[
+                pl.BlockSpec((8, SP, B * B), lambda i, *_: (0, 0, 0)), pl.BlockSpec((16, 128), lambda i, *_: (0, 0))
+            ],
             out_specs=[whole, whole],
             scratch_shapes=[pltpu.VMEM((256, 128), jnp.float32), pltpu.VMEM((4, B, 128), jnp.float32)],
         ),
         out_shape=[half, half],
         name="split",
-    )(core, dens)
+    )(core, dens, ints)
 
 
 def regroup_kernel(at, mine, other, own, after, before, far0, far1, sems):
@@ -148,17 +155,27 @@
     return jnp.exp2(code.astype(jnp.int32).astype(jnp.float32) * (1.0 / 256.0)) * (1.0 / TOP)
 
 
-def panel_kernel(n, rows_of_block, has_sums, coded, kcol, jcol, *refs):
+def panel_kernel(n, pieces, target, has_sums, coded, ints, at, *refs):
     kohn, refs = refs[:2 * n], refs[2 * n:]
-    panels, refs = refs[:2 * n], refs[2 * n:]
+    panels, refs = refs[:pieces], refs[pieces:]
     if has_sums:
         p_ref, refs = refs[0], refs[1:]
     outs, (dens, sems, acc) = refs[:-3], refs[-3:]
-    step = pl.program_id(0) + rows_of_block
+    size = n * 8 * PART // pieces
+    core, line, cross, x = at[0], at[1], at[2], at[3]
+    if target is None:
+        step = pl.program_id(0)
+        ahead = jnp.where(step == 0, ORDER[0], jnp.where(step == 1, ORDER[1], jnp.where(step == 2, ORDER[2], ORDER[3])))
+    else:
+        ahead = ORDER[target]
+    goal = (cross + ahead) & 3
+    block_row = jnp.where(core == 1, goal * 4 + line, line * 4 + goal)
 
     @pl.when(pl.program_id(0) == 0)
     def _():
-        copies = [pltpu.make_async_copy(panels[s], dens.at[pl.ds(s * 32, 32)], sems.at[s]) for s in range(2 * n)]
+        copies = [
+            pltpu.make_async_copy(panels[s], dens.at[pl.ds(s * size, size)], sems.at[s]) for s in range(pieces)
+        ]
         for copy in copies:
             copy.start()
         for copy in copies:
@@ -166,43 +183,39 @@
 
     low = (lax.broadcasted_iota(jnp.int32, (32, 128), 1) < 64).astype(jnp.float32).astype(jnp.bfloat16)
     high = 1 - low
-    zero = jnp.zeros((128, 128), jnp.bfloat16)
 
     def twice(blk):
         turned = jnp.concatenate([blk[:, B:], blk[:, :B]], axis=1)
         return jnp.concatenate([blk * low, turned * low, turned * high, blk * high], axis=0)
 
     def product(m, r, s, a):
-        ks, weights = [], []
-        for i in range(2):
-            ks.append(kcol[(((s * 4 + step) * 2 + m) * 4 + r) * SK + a + i] + 64 * s)
-            weights.append(twice(kohn[2 * s + m][0, 0, r, (a + i) * 32:(a + i + 1) * 32, :]))
-        left = jnp.concatenate([dens[ks[0]], dens[ks[1]]], axis=1)
-        right = jnp.concatenate([
-            jnp.concatenate([weights[0], zero], axis=1), jnp.concatenate([zero, weights[1]], axis=1)
-        ], axis=0)
+        k = ints[(s * 8 + m) * 8 + (block_row >> 3), (block_row & 7) * 16 + r * 4 + a]
+        slot = (120 >> (2 * (((k >> 4) - x) & 3))) & 3
+        k = slot * 16 + ((k & 15) ^ (8 * core))
+        part = s * 8 + (k >> 3)
+        left = dens[pl.ds(pl.multiple_of(part * PART + (k & 7) * 128, 16), 128), :]
+        right = twice(kohn[2 * s + m][0, 0, r, a * 32:(a + 1) * 32, :])
         r = lax.dot_general(left, right, (((1,), (1,)), ((), ())), preferred_element_type=jnp.float32)
-        return ks, r
-
-    def add(sums, ks, r):
-        for i in range(2):
-            js = [jcol[ks[i] * SP + b] for b in range(SP)]
-            old = [sums[j] for j in js]
-            for b in range(SP):
-                sums[js[b]] = old[b] + r[b * 16:(b + 1) * 16, i * 128:(i + 1) * 128]
+        return part, (k & 7) * SP, r
+
+    def add(sums, part, first, r):
+        js = [ints[part * 8 + 2, first + b] for b in range(SP)]
+        old = [sums[j] for j in js]
+        for b in range(SP):
+            sums[js[b]] = old[b] + r[b * 16:(b + 1) * 16, :]
 
     def two_rows(m, pair):
         work, sums = [], []
         for q in range(2):
             r = pair * 2 + q
-            work += [(q, r, s, a) for s in range(n) for a in range(0, SK, 2)]
+            work += [(q, r, s, a) for s in range(n) for a in range(SK)]
             place = acc.at[q] if coded else outs[0].at[0, m * 4 + r]
             place[...] = p_ref[0, m * 4 + r] if has_sums else jnp.zeros((NCW, 16, 128), jnp.float32)
             sums.append(place)
-        held = [product(m, *work[i][1:]) for i in range(2)]
+        held = [product(m, *work[i][1:]) for i in range(3)]
         for i in range(len(work)):
-            if i + 2 < len(work):
-                held.append(product(m, *work[i + 2][1:]))
+            if i + 3 < len(work):
+                held.append(product(m, *work[i + 3][1:]))
             add(sums[work[i][0]], *held[i])
         if coded:
             for q in range(2):
@@ -218,8 +231,8 @@
         lax.fori_loop(0, 2, lambda pair, _, m=m: (two_rows(m, pair), 0)[1], 0)
 
 
-def panel_sums(name, kcol, jcol, kohn, panels, sums, target=None, coded=False):
-    n = len(panels) // 2
+def panel_sums(name, ints, at, kohn, panels, sums, target=None, coded=False):
+    n, pieces = len(kohn) // 2, len(panels)
     base = 0 if target is None else target
     k_specs = [
         pl.BlockSpec((1, 1, 4, 128, 128), lambda o, *_, m=m: (m, o + base, 0, 0, 0)) for _, m in kohn
@@ -235,25 +248,25 @@
     any_spec = pl.BlockSpec(memory_space=pl.ANY)
     steps = 4 if target is None else 1
     return pl.pallas_call(
-        lambda *refs: panel_kernel(n, base, sums is not None, coded, *refs),
+        lambda *refs: panel_kernel(n, pieces, target, sums is not None, coded, *refs),
         grid_spec=pltpu.PrefetchScalarGridSpec(
             num_scalar_prefetch=2,
             grid=(steps,),
-            in_specs=k_specs + [any_spec] * (2 * n) + [s_spec] * (sums is not None),
+            in_specs=k_specs + [any_spec] * pieces + [s_spec] * (sums is not None),
             out_specs=o_specs,
             scratch_shapes=[
-                pltpu.VMEM((n * 64, 128, 128), jnp.bfloat16),
-                pltpu.SemaphoreType.DMA((2 * n,)),
+                pltpu.VMEM((n * 8 * PART, 128), jnp.bfloat16),
+                pltpu.SemaphoreType.DMA((pieces,)),
                 pltpu.VMEM((2, NCW, 16, 128), jnp.float32),
             ],
         ),
         out_shape=shapes,
-        compiler_params=pltpu.CompilerParams(vmem_limit_bytes=40 << 20),
+        compiler_params=pltpu.CompilerParams(vmem_limit_bytes=44 << 20),
         cost_estimate=pl.CostEstimate(
             flops=2 * n * 32 * steps * 128 * 128 * 128, bytes_accessed=(2 * n + 5 * steps) << 20, transcendentals=0
         ),
         name=name,
-    )(kcol, jcol, *[array for array, _ in kohn], *panels, *(() if sums is None else (sums,)))
+    )(ints, at, *[array for array, _ in kohn], *panels, *(() if sums is None else (sums,)))
 
 
 def pack_kernel(slots, own, after, before, far0, far1, o_ref, total, codes):
@@ -376,65 +389,55 @@
     x, c = lax.axis_index("x"), lax.axis_index("core")
     z, y = lax.axis_index("z"), lax.axis_index("y")
     on_line, on_cross = jnp.where(c == 0, z, y), jnp.where(c == 0, y, z)
-    four = jnp.arange(4, dtype=jnp.int32)
-
-    mine, theirs = split(c.reshape(1), density_blocks[0])
-    theirs = over_core(theirs)
-    left0, right0 = over_x(mine, 1), over_x(mine, -1)
-    left1, right1 = over_x(theirs, 1), over_x(theirs, -1)
-    far0, far1 = over_x(left0, 1), over_x(right1, -1)
-    low = jnp.concatenate([mine, theirs, left0, left1])
-    high = jnp.concatenate([right0, right1, far0, far1])
-
-    prev_low, prev_high = over_line(low, 1), over_line(high, 1)
-    next_high, next_low = over_line(high, -1), over_line(low, -1)
-    far_low, far_high = over_line(prev_low, 1), over_line(next_high, -1)
-
-    ints = jnp.concatenate([kohn_columns.reshape(-1), density_columns.reshape(-1), owner_map.reshape(-1)])
-    other = over_core(ints)
-    columns = jnp.concatenate([ints[256:320], other[256:320]])
-    columns = jnp.concatenate([columns, over_x(columns, 1), over_x(columns, -1), over_x(columns, 2)])
-    words = jnp.concatenate([columns, ints[:256], other[:256]]).reshape(8, 128)
-    words = [words, over_line(words, 1), over_line(words, -1), over_line(words, 2)]
-
-    def indices(word):
-        word = word.reshape(-1)
-        targets = (on_cross + jnp.array(ORDER, jnp.int32)) % 4
-        rows = jnp.where(c == 0, on_line * Y + targets, targets * Y + on_line)
-        k = word[512:].reshape(2, 16, 4, SK)[:, rows].transpose(1, 0, 2, 3).reshape(-1)
-        away = ((k >> 4) - x) & 3
-        slot = jnp.where(away == 0, 0, jnp.where(away == 3, 1, away + 1))
-        return slot * 16 + ((k & 15) ^ (8 * c)), word[:512]
-
-    kcols, jcols = zip(*[indices(word) for word in words])
-
-    owners = jnp.stack([ints[320:], other[320:]])
+    at = jnp.stack([c, on_line, on_cross, x])
+
+    kohn = kohn_blocks.reshape(16, 4, SK * 32, 128)
+    kohn_other = over_core(kohn)
+
+    ints = jnp.concatenate([
+        kohn_columns.reshape(2, 128), jnp.pad(density_columns.reshape(1, 64), ((0, 0), (0, 64))),
+        owner_map.reshape(1, 128), jnp.zeros((12, 128), jnp.int32),
+    ])
+    dens, kohn = lax.optimization_barrier((density_blocks[0], kohn))
+
+    mine, theirs = split(at, dens, ints)
+    shard = jnp.concatenate([mine, over_core(theirs)])
+    left, right = over_x(shard, 1), over_x(shard, -1)
+
+    kohn, after, before, opposite0, opposite1 = regroup(at, kohn, kohn_other)
+    left, right, _ = lax.optimization_barrier((left, right, opposite0))
+    kohn_before, kohn_after = over_line(after, 1), over_line(before, -1)
+    opposite0, opposite1 = over_line(opposite0, 1), over_line(opposite1, -1)
+
+    panel = jnp.concatenate([shard, left, right, over_x(left[:PART], 1), over_x(right[PART:], -1)])
+    sent, kohn_before, kohn_after = lax.optimization_barrier((panel, kohn_before, kohn_after))
+    prev, after = over_line(sent, 1), over_line(sent, -1)
+    opposite0, opposite1 = over_line(opposite0, 1), over_line(opposite1, -1)
+    far_low, far_high = over_line(prev[:4 * PART], 1), over_line(after[4 * PART:], -1)
+
+    def words(*arrays):
+        parts = jnp.concatenate([array.reshape(-1, PART, 128)[:, 8 * 128:8 * 128 + 8] for array in arrays])
+        return parts.astype(jnp.int32).reshape(-1, 128)
+
+    owners = jnp.stack([owner_map.reshape(128), shard[PART + 8 * 128 + 3].astype(jnp.int32)])
     hit = (owners[..., None] == jnp.arange(128, dtype=jnp.int32)).astype(jnp.int32)
     ranks = jnp.sum(jnp.cumsum(hit, axis=1) * hit, axis=2) - 1
     source = jnp.arange(2, dtype=jnp.int32)[:, None] ^ c
     slots = (owners * 4 + source * 2 + ranks).reshape(-1)
 
-    kohn = kohn_blocks.reshape(16, 4, SK * 32, 128)
-    kohn, after, before, opposite0, opposite1 = regroup(
-        jnp.stack([c, on_line, on_cross]), kohn, over_core(kohn)
-    )
-    before, after = over_line(after, 1), over_line(before, -1)
-    opposite0 = over_line(over_line(opposite0, 1), 1)
-    opposite1 = over_line(over_line(opposite1, -1), -1)
-
     def both(array):
         return [(array, 0), (array, 1)]
 
-    sums, = panel_sums("own_panel", kcols[0], jcols[0], both(kohn), [low, high], None)
+    sums, = panel_sums("own_panel", words(panel), at, both(kohn), [panel], None)
     sums, = panel_sums(
-        "near_panels", jnp.concatenate(kcols[1:3]), jnp.concatenate(jcols[1:3]), both(before) + both(after),
-        [prev_low, prev_high, next_low, next_high], sums,
+        "near_panels", words(prev, after), at, both(kohn_before) + both(kohn_after), [prev, after], sums
     )
     opposite = [(opposite0[None], 0), (opposite1[None], 0)]
+    far_words = words(far_low, far_high)
 
     def last(target, coded):
         return panel_sums(
-            "last_panel", kcols[3], jcols[3], opposite, [far_low, far_high], sums, target=target, coded=coded
+            "last_panel", far_words, at, opposite, [far_low, far_high], sums, target=target, coded=coded
         )
 
     sums0, sums1 = last(0, True)

time: 232 us -> 227 us (0.978)
  local copies, waits for them, and re-layouts: 28.7 us -> 5.68 us
  waiting for transfers between devices: 49.6 us -> 70.1 us
  Pallas kernels: 63.2 us -> 72.1 us
  starting transfers between devices: 39 us -> 30.5 us
  blocking collectives: 49.4 us -> 45.9 us
    ppermute x21 -> x16, waiting for transfers between devices: 35.7 us -> 59.9 us  [over(): lax.ppermute(v, PLANE, [(group[i], group[(i + step) % 4]) for group in gr...]
    unnamed x33 -> x13, local copies, waits for them, and re-layouts: 20.5 us -> 1.31 us
    pallas_call x6, Pallas kernels: 37.8 us -> 46.9 us  [panel_sums(): pl.pallas_call(lambda *refs: panel_kernel(n, pieces, target, sums is not...]
    ppermute x9 -> x4, waiting for transfers between devices: 13.9 us -> 9.44 us  [over_x(): return lax.ppermute(v, 'x', [(i, (i + step) % X) for i in range(X)])]
    ppermute x9 -> x4, starting transfers between devices: 10 us -> 5.56 us  [over_x(): return lax.ppermute(v, 'x', [(i, (i + step) % X) for i in range(X)])]
    all_to_all x1, blocking collectives: 49.4 us -> 45.9 us  [local(): lax.all_to_all(outgoing, ALL, split_axis=0, concat_axis=0, tiled=True)]
    ppermute x21 -> x16, starting transfers between devices: 26.4 us -> 23.4 us  [over(): lax.ppermute(v, PLANE, [(group[i], group[(i + step) % 4]) for group in gr...]
  transfers between devices with their start and end apart: 33 -> 22, of which waited for: 11 -> 8; matrix products, arithmetic and copies ran while one was open for 5% -> 2% of each run, Pallas kernels for 20% -> 23%
where the time goes in v5:
time: 227 us; the launch traced here: 226 us
  Pallas kernels  72.1 us (32%)
  waiting for transfers between devices  70.1 us (31%)
  blocking collectives  45.9 us (20%)
  starting transfers between devices  30.5 us (13%)
  local copies, waits for them, and re-layouts  5.68 us (3%)
    ppermute x16, waiting for transfers between devices, over(): lax.ppermute(v, PLANE, [(group[i], group[(i + step) % 4]) for group in gr...  59.9 us
    pallas_call x6, Pallas kernels, panel_sums(): pl.pallas_call(lambda *refs: panel_kernel(n, pieces, target, sums is not...  46.9 us
    all_to_all x1, blocking collectives, local(): lax.all_to_all(outgoing, ALL, split_axis=0, concat_axis=0, tiled=True)  45.9 us
    ppermute x16, starting transfers between devices, over(): lax.ppermute(v, PLANE, [(group[i], group[(i + step) % 4]) for group in gr...  23.4 us
    ppermute x4, waiting for transfers between devices, over_x(): return lax.ppermute(v, 'x', [(i, (i + step) % X) for i in range(X)])  9.44 us
    pallas_call x1, Pallas kernels, pack(): pl.pallas_call(pack_kernel, grid_spec=pltpu.PrefetchScalarGridSpec(num_sc...  7.94 us
    pallas_call x1, Pallas kernels, unpack(): pl.pallas_call(unpack_kernel, grid=(X,), in_specs=[pl.BlockSpec((1, C, 16...  7.07 us
    ppermute x4, starting transfers between devices, over_x(): return lax.ppermute(v, 'x', [(i, (i + step) % X) for i in range(X)])  5.56 us
  transfers between devices with their start and end apart: 22, of which 8 were waited for; matrix products, arithmetic and copies ran while one was open for 2% of the time, Pallas kernels for 23%

profile of v5, /device:TPU:1, one launch (start us, length us, event | category | flops | bytes accessed | tf_op | source)
XLA Modules:
  0.0 226.5 jit_solution(17369401224650083902)
XLA Ops:
  0.0 3.8 %reshape.59.mine = bf16[16,4,128,128]{3,2,1,0:T(8,128)(2,1)S(1)} reshape(bf16[64,1,4,4096]{3,2,1,0:T(4,128)(2,1)} %param.5) | data formatting | bytes 4194304 | tf_op jit(solution)/shard_map/reshape | solution.py:394
  3.8 1.5 collective-permute-start.3
  7.0 5.2 %split.1 = (bf16[1040,128]{1,0:T(8,128)(2,1)}, bf16[1040,128]{1,0:T(8,128)(2,1)}) custom-call(s32[4]{0:T(128)} %pad_add_fusion.2.core.at.refs_1_, bf16[8,8,4096]{2,1,0:T(8,128)(2,1)} %bitcast.47, s32[16,128]{1,0:T(8,128)} %fusion.5.i_ref), custom_call_target="tpu_custom_call" | custom-call | tf_op jit(solution)/shard_map/split/pallas_call | solution.py:94
  14.0 1.4 collective-permute-start.1
  15.4 1.4 collective-permute-start.2
  16.8 5.0 %regroup.1 = (bf16[2,4,4,128,128]{4,3,2,1,0:T(8,128)(2,1)S(1)}, bf16[2,4,4,128,128]{4,3,2,1,0:T(8,128)(2,1)S(1)}, bf16[2,4,4,128,128]{4,3,2,1,0:T(8,128)(2,1)S(1...) custom-call(s32[4]{0:T(128)S(1)} %copy-done, bf16[16,4,128,128]{3,2,1,0:T(8,128)(2,1)S(1)} %reshape.59.mine, ...), custom_call_target="tpu_custom_call" | custom-call | tf_op jit(solution)/shard_map/regroup/pallas_call | solution.py:129
  21.8 7.1 %collective-permute-done.1 = bf16[2080,128]{1,0:T(8,128)(2,1)S(1)} collective-permute-done((bf16[2080,128]{1,0:T(8,128)(2,1)S(1)}, bf16[2080,128]{1,0:T(8,128)(2,1)S(1)}, u32[]{:S(2)}, u32[]{:S(2)}) %collective-permute-start.1) | collective-permute-done | bytes 532512 | tf_op jit(solution)/shard_map/ppermute | solution.py:47
  30.0 1.8 collective-permute-start.5
  31.8 1.4 collective-permute-start.6
  33.1 1.4 collective-permute-start.7
  34.7 2.3 %collective-permute-done.4 = bf16[1040,128]{1,0:T(8,128)(2,1)S(1)} collective-permute-done((bf16[1040,128]{1,0:T(8,128)(2,1)S(1)}, bf16[1040,128]{1,0:T(8,128)(2,1)S(1)}, u32[]{:S(2)}, u32[]{:S(2)}) %collective-permute-start.4) | collective-permute-done | bytes 266272 | tf_op jit(solution)/shard_map/ppermute | solution.py:47
  37.1 9.9 %collective-permute-done.6.refs_2_.refs_3_ = bf16[2,4,4,128,128]{4,3,2,1,0:T(8,128)(2,1)S(1)} collective-permute-done((bf16[2,4,4,128,128]{4,3,2,1,0:T(8,128)(2,1)S(1)}, bf16[2,4,4,128,128]{4,3,2,1,0:T(8,128)(2,1)S(1)}, u32[]{:S(2)}, u32[]{:S(2)}) %collective-permute-start.6) | collective-permute-done | bytes 1048608 | tf_op jit(solution)/shard_map/ppermute | solution.py:35
  48.4 1.4 collective-permute-start.10
  49.8 24.1 %collective-permute-done.8.refs_6_ = bf16[8320,128]{1,0:T(8,128)(2,1)S(1)} collective-permute-done((bf16[8320,128]{1,0:T(8,128)(2,1)S(1)}, bf16[8320,128]{1,0:T(8,128)(2,1)S(1)}, u32[]{:S(2)}, u32[]{:S(2)}) %collective-permute-start.8) | collective-permute-done | bytes 2129952 | tf_op jit(solution)/shard_map/ppermute | solution.py:35
  74.1 2.7 %collective-permute-start.11 = (bf16[4160,128]{1,0:T(8,128)(2,1)S(1)}, bf16[4160,128]{1,0:T(8,128)(2,1)S(1)}, u32[]{:S(2)}, u32[]{:S(2)}) collective-permute-start(bf16[4160,128]{1,0:T(8,128)(2,1)S(1)} %slice.43), channel_id=1, source_target_pairs={{0,12},{4,0},{8,4},{12,8},{1,13},{5,1},{9,5},{13,9},{2,14},{6,2},{... | collective-permute-start | bytes 3194888 | tf_op jit(solution)/shard_map/ppermute | solution.py:35
  76.8 2.7 %collective-permute-start.14 = (bf16[4,4,128,128]{3,2,1,0:T(8,128)(2,1)S(1)}, bf16[4,4,128,128]{3,2,1,0:T(8,128)(2,1)S(1)}, u32[]{:S(2)}, u32[]{:S(2)}) collective-permute-start(bf16[4,4,128,128]{3,2,1,0:T(8,128)(2,1)S(1)} %get-tuple-element.31), channel_id=1, source_target_pairs={{0,12},{4,0},{8,4},{12,8},{1,13},{5,1},{9,5},{13,9},{2,14},{6,2},{... | collective-permute-start | bytes 1572872 | tf_op jit(solution)/shard_map/ppermute | solution.py:35
  79.5 15.4 %collective-permute-done.12 = bf16[4,4,128,128]{3,2,1,0:T(8,128)(2,1)S(1)} collective-permute-done((bf16[4,4,128,128]{3,2,1,0:T(8,128)(2,1)S(1)}, bf16[4,4,128,128]{3,2,1,0:T(8,128)(2,1)S(1)}, u32[]{:S(2)}, u32[]{:S(2)}) %collective-permute-start.12) | collective-permute-done | bytes 524320 | tf_op jit(solution)/shard_map/ppermute | solution.py:35
  94.9 2.8 %collective-permute-start.15 = (bf16[4,4,128,128]{3,2,1,0:T(8,128)(2,1)S(1)}, bf16[4,4,128,128]{3,2,1,0:T(8,128)(2,1)S(1)}, u32[]{:S(2)}, u32[]{:S(2)}) collective-permute-start(bf16[4,4,128,128]{3,2,1,0:T(8,128)(2,1)S(1)} %collective-permute-done.14), channel_id=1, source_target_pairs={{0,12},{4,0},{8,4},{12,8},{1,13},{5,1},{9,5},{13,9},{2,14},{6,2},{... | collective-permute-start | bytes 1572872 | tf_op jit(solution)/shard_map/ppermute | solution.py:35
  97.7 8.8 %own_panel.1.refs_8_ = f32[4,8,32,16,128]{4,3,2,1,0:T(8,128)} custom-call(s32[64,128]{1,0:T(8,128)S(1)} %fusion.2.refs_0_, s32[4]{0:T(128)S(1)} %copy-done, bf16[2,4,4,128,128]{4,3,2,1,0:T(8,128)(2,1)S(1)} %get-tuple-element.34.refs_2_.refs_3_, bf16[2,4,4,128,128]{4,3,2,1,0:T(8,128)(2,1)S(1)} %get-tuple-element.34.refs_2_.refs_3_, ...), custom_call_target="tpu_custom_call" | custom-call | flops 536870912 | bytes 23068672 | tf_op jit(solution)/shard_map/own_panel/pallas_call | solution.py:250
  106.6 16.4 %near_panels.1.refs_6_ = f32[4,8,32,16,128]{4,3,2,1,0:T(8,128)} custom-call(s32[128,128]{1,0:T(8,128)S(1)} %fusion.1.refs_0_, s32[4]{0:T(128)S(1)} %copy-done, bf16[2,4,4,128,128]{4,3,2,1,0:T(8,128)(2,1)S(1)} %collective-permute-done.6.refs_2_.refs_3_, bf16[2,4,4,128,128]{4,3,2,1,0:T(8,128)(2,1)S(1)} %collective-permute-done.6.refs_2_.refs_3_, ...), custom_call_target="tpu_custom_call" | custom-call | flops 1073741824 | bytes 25165824 | tf_op jit(solution)/shard_map/near_panels/pallas_call | solution.py:250
  123.1 5.1 %last_panel.7 = (s16[4,33,16,128]{3,2,1,0:T(8,128)(2,1)S(1)}, s16[4,33,16,128]{3,2,1,0:T(8,128)(2,1)S(1)}) custom-call(s32[64,128]{1,0:T(8,128)S(1)} %fusion.3.refs_0_, s32[4]{0:T(128)S(1)} %copy-done, bf16[1,4,4,128,128]{4,3,2,1,0:T(8,128)(2,1)S(1)} %bitcast.36, bf16[1,4,4,128,128]{4,3,2,1,0:T(8,128)(2,1)S(1)} %bitcast.40, ...), custom_call_target="tpu_custom_call" | custom-call | flops 134217728 | bytes 7340032 | tf_op jit(solution)/shard_map/last_panel/pallas_call | solution.py:250
  129.3 3.0 %collective-permute-start.20 = (s16[4,33,16,128]{3,2,1,0:T(8,128)(2,1)S(1)}, s16[4,33,16,128]{3,2,1,0:T(8,128)(2,1)}, u32[]{:S(2)}, u32[]{:S(2)}) collective-permute-start(s16[4,33,16,128]{3,2,1,0:T(8,128)(2,1)S(1)} %get-tuple-element.36), channel_id=1, source_target_pairs={{0,3},{1,0},{2,1},{3,2},{4,7},{5,4},{6,5},{7,6},{8,11},{9,8},{10,9... | collective-permute-start | bytes 1622024 | tf_op jit(solution)/shard_map/ppermute | solution.py:35
  132.3 6.1 %last_panel.6 = s16[8,33,16,128]{3,2,1,0:T(8,128)(2,1)} custom-call(s32[64,128]{1,0:T(8,128)S(1)} %fusion.3.refs_0_, s32[4]{0:T(128)S(1)} %copy-done, bf16[1,4,4,128,128]{4,3,2,1,0:T(8,128)(2,1)S(1)} %bitcast.37, bf16[1,4,4,128,128]{4,3,2,1,0:T(8,128)(2,1)S(1)} %bitcast.41, bf16[4160,128]{1,0:T(8,128)(2,1)S(1)} %collective-permute-done.9.refs_4_, ...), custom_call_target="tpu_custom_call" | custom-call | flops 134217728 | bytes 7340032 | tf_op jit(solution)/shard_map/last_panel/pallas_call | solution.py:250
  138.5 6.1 %last_panel.5 = s16[8,33,16,128]{3,2,1,0:T(8,128)(2,1)} custom-call(s32[64,128]{1,0:T(8,128)S(1)} %fusion.3.refs_0_, s32[4]{0:T(128)S(1)} %copy-done, bf16[1,4,4,128,128]{4,3,2,1,0:T(8,128)(2,1)S(1)} %bitcast.38, bf16[1,4,4,128,128]{4,3,2,1,0:T(8,128)(2,1)S(1)} %bitcast.42, bf16[4160,128]{1,0:T(8,128)(2,1)S(1)} %collective-permute-done.9.refs_4_, ...), custom_call_target="tpu_custom_call" | custom-call | flops 134217728 | bytes 7340032 | tf_op jit(solution)/shard_map/last_panel/pallas_call | solution.py:250
  144.6 2.7 %collective-permute-start.16 = (s16[8,33,16,128]{3,2,1,0:T(8,128)(2,1)}, s16[8,33,16,128]{3,2,1,0:T(8,128)(2,1)}, u32[]{:S(2)}, u32[]{:S(2)}) collective-permute-start(s16[8,33,16,128]{3,2,1,0:T(8,128)(2,1)} %last_panel.5), channel_id=1, source_target_pairs={{0,3},{1,0},{2,1},{3,2},{4,7},{5,4},{6,5},{7,6},{8,11},{9,8},{10,9... | collective-permute-start | bytes 3244040 | tf_op jit(solution)/shard_map/ppermute | solution.py:35
  147.4 2.7 %collective-permute-start.21 = (s16[4,33,16,128]{3,2,1,0:T(8,128)(2,1)}, s16[4,33,16,128]{3,2,1,0:T(8,128)(2,1)}, u32[]{:S(2)}, u32[]{:S(2)}) collective-permute-start(s16[4,33,16,128]{3,2,1,0:T(8,128)(2,1)} %collective-permute-done.20), channel_id=1, source_target_pairs={{0,3},{1,0},{2,1},{3,2},{4,7},{5,4},{6,5},{7,6},{8,11},{9,8},{10,9... | collective-permute-start | bytes 1622024 | tf_op jit(solution)/shard_map/ppermute | solution.py:35
  150.6 4.4 %last_panel.4.own = f32[1,8,32,16,128]{4,3,2,1,0:T(8,128)S(1)} custom-call(s32[64,128]{1,0:T(8,128)S(1)} %fusion.3.refs_0_, s32[4]{0:T(128)S(1)} %copy-done, bf16[1,4,4,128,128]{4,3,2,1,0:T(8,128)(2,1)S(1)} %bitcast.39, bf16[1,4,4,128,128]{4,3,2,1,0:T(8,128)(2,1)S(1)} %bitcast.43, bf16[4160,128]{1,0:T(8,128)(2,1)S(1)} %collective-permute-done.9.refs_4_, ...), custom_call_target="tpu_custom_call" | custom-call | flops 134217728 | bytes 7340032 | tf_op jit(solution)/shard_map/last_panel/pallas_call | solution.py:250
  155.0 5.0 %collective-permute-done.19.far0 = s16[4,33,16,128]{3,2,1,0:T(8,128)(2,1)} collective-permute-done((s16[4,33,16,128]{3,2,1,0:T(8,128)(2,1)}, s16[4,33,16,128]{3,2,1,0:T(8,128)(2,1)}, u32[]{:S(2)}, u32[]{:S(2)}) %collective-permute-start.19) | collective-permute-done | bytes 540704 | tf_op jit(solution)/shard_map/ppermute | solution.py:35
  160.1 5.4 %collective-permute-done.21.far1 = s16[4,33,16,128]{3,2,1,0:T(8,128)(2,1)} collective-permute-done((s16[4,33,16,128]{3,2,1,0:T(8,128)(2,1)}, s16[4,33,16,128]{3,2,1,0:T(8,128)(2,1)}, u32[]{:S(2)}, u32[]{:S(2)}) %collective-permute-start.21) | collective-permute-done | bytes 540704 | tf_op jit(solution)/shard_map/ppermute | solution.py:35
  165.5 7.9 %pack.1 = s16[128,80,128]{2,1,0:T(8,128)(2,1)S(1)} custom-call(s32[256]{0:T(256)S(1)} %add_bitcast_fusion.slots, f32[1,8,32,16,128]{4,3,2,1,0:T(8,128)S(1)} %last_panel.4.own, s16[8,33,16,128]{3,2,1,0:T(8,128)(2,1)} %collective-permute-done.16.after, s16[8,33,16,128]{3,2,1,0:T(8,128)(2,1)} %collective-permute-done.17.before, ...), custom_call_target="tpu_custom_call" | custom-call | tf_op jit(solution)/shard_map/pack/pallas_call | solution.py:339
  173.5 45.9 %all_to_all.5 = s16[128,80,128]{2,1,0:T(8,128)(2,1)S(1)} all-to-all(s16[128,80,128]{2,1,0:T(8,128)(2,1)S(1)} %pack.1), channel_id=1, replica_groups=mesh['x'=4,'core'=2,'z'=4,'y'=4] {'x','core','z','y'}, dimensions={0} | all-to-all | bytes 5242880 | tf_op jit(solution)/shard_map/all_to_all | solution.py:453
  219.4 7.1 %unpack.1 = f32[256,4096]{1,0:T(8,128)} custom-call(s16[4,2,16,80,128]{4,3,2,1,0:T(8,128)(2,1)S(1)} %bitcast.35), custom_call_target="tpu_custom_call" | custom-call | tf_op jit(solution)/shard_map/unpack/pallas_call | solution.py:376
  (63 shorter events, 8.3 us)
Async XLA Ops:
  0.0 5.3 %copy-start.3 = (s32[64,1,4]{0,2,1:T(4,128)S(1)}, s32[64,1,4]{0,2,1:T(4,128)}, u32[]{:S(2)}) copy-start(s32[64,1,4]{0,2,1:T(4,128)} %param.6) | copy-start | bytes 3076
  0.0 5.6 %copy-start.2 = (s32[1,8,8]{2,1,0:T(8,128)S(1)}, s32[1,8,8]{2,1,0:T(8,128)}, u32[]{:S(2)}) copy-start(s32[1,8,8]{2,1,0:T(8,128)} %param.8) | copy-start | bytes 772
  0.0 6.3 %copy-start.1 = (s32[128,1]{0,1:T(1,128)S(1)}, s32[128,1]{0,1:T(1,128)}, u32[]{:S(2)}) copy-start(s32[128,1]{0,1:T(1,128)} %param.9) | copy-start | bytes 1540
  3.8 13.0 %collective-permute-start.3 = (bf16[16,4,128,128]{3,2,1,0:T(8,128)(2,1)S(1)}, bf16[16,4,128,128]{3,2,1,0:T(8,128)(2,1)}, u32[]{:S(2)}, u32[]{:S(2)}) collective-permute-start(bf16[16,4,128,128]{3,2,1,0:T(8,128)(2,1)S(1)} %reshape.59.mine), channel_id=1, source_target_pairs={{0,16},{16,0},{1,17},{17,1},{2,18},{18,2},{3,19},{19,3},{4,20},{20... | collective-permute-start | bytes 6291464 | tf_op jit(solution)/shard_map/ppermute | solution.py:51
  6.3 10.5 %copy-start = (s32[4]{0:T(128)S(1)}, s32[4]{0:T(128)}, u32[]{:S(2)}) copy-start(s32[4]{0:T(128)} %pad_add_fusion.2.core.at.refs_1_) | copy-start | bytes 52
  12.2 1.8 collective-permute-start
  14.0 14.8 %collective-permute-start.1 = (bf16[2080,128]{1,0:T(8,128)(2,1)S(1)}, bf16[2080,128]{1,0:T(8,128)(2,1)S(1)}, u32[]{:S(2)}, u32[]{:S(2)}) collective-permute-start(bf16[2080,128]{1,0:T(8,128)(2,1)S(1)} %get-tuple-element.37), channel_id=1, source_target_pairs={{0,32},{32,64},{64,96},{96,0},{1,33},{33,65},{65,97},{97,1},{2,34}... | collective-permute-start | bytes 1597448 | tf_op jit(solution)/shard_map/ppermute | solution.py:47
  15.4 13.5 %collective-permute-start.2 = (bf16[2080,128]{1,0:T(8,128)(2,1)S(1)}, bf16[2080,128]{1,0:T(8,128)(2,1)S(1)}, u32[]{:S(2)}, u32[]{:S(2)}) collective-permute-start(bf16[2080,128]{1,0:T(8,128)(2,1)S(1)} %get-tuple-element.37), channel_id=1, source_target_pairs={{0,96},{32,0},{64,32},{96,64},{1,97},{33,1},{65,33},{97,65},{2,98}... | collective-permute-start | bytes 1597448 | tf_op jit(solution)/shard_map/ppermute | solution.py:47
  28.9 8.1 %collective-permute-start.4 = (bf16[1040,128]{1,0:T(8,128)(2,1)S(1)}, bf16[1040,128]{1,0:T(8,128)(2,1)S(1)}, u32[]{:S(2)}, u32[]{:S(2)}) collective-permute-start(bf16[1040,128]{1,0:T(8,128)(2,1)S(1)} %slice.31), channel_id=1, source_target_pairs={{0,32},{32,64},{64,96},{96,0},{1,33},{33,65},{65,97},{97,1},{2,34}... | collective-permute-start | bytes 798728 | tf_op jit(solution)/shard_map/ppermute | solution.py:47
  30.0 7.1 %collective-permute-start.5 = (bf16[1040,128]{1,0:T(8,128)(2,1)S(1)}, bf16[1040,128]{1,0:T(8,128)(2,1)S(1)}, u32[]{:S(2)}, u32[]{:S(2)}) collective-permute-start(bf16[1040,128]{1,0:T(8,128)(2,1)S(1)} %slice.32), channel_id=1, source_target_pairs={{0,96},{32,0},{64,32},{96,64},{1,97},{33,1},{65,33},{97,65},{2,98}... | collective-permute-start | bytes 798728 | tf_op jit(solution)/shard_map/ppermute | solution.py:47
  31.8 15.3 %collective-permute-start.6 = (bf16[2,4,4,128,128]{4,3,2,1,0:T(8,128)(2,1)S(1)}, bf16[2,4,4,128,128]{4,3,2,1,0:T(8,128)(2,1)S(1)}, u32[]{:S(2)}, u32[]{:S(2)}) collective-permute-start(bf16[2,4,4,128,128]{4,3,2,1,0:T(8,128)(2,1)S(1)} %get-tuple-element.28), channel_id=1, source_target_pairs={{0,4},{4,8},{8,12},{12,0},{1,5},{5,9},{9,13},{13,1},{2,6},{6,10},{... | collective-permute-start | bytes 3145736 | tf_op jit(solution)/shard_map/ppermute | solution.py:35
  33.1 13.9 %collective-permute-start.7 = (bf16[2,4,4,128,128]{4,3,2,1,0:T(8,128)(2,1)S(1)}, bf16[2,4,4,128,128]{4,3,2,1,0:T(8,128)(2,1)S(1)}, u32[]{:S(2)}, u32[]{:S(2)}) collective-permute-start(bf16[2,4,4,128,128]{4,3,2,1,0:T(8,128)(2,1)S(1)} %get-tuple-element.29), channel_id=1, source_target_pairs={{0,12},{4,0},{8,4},{12,8},{1,13},{5,1},{9,5},{13,9},{2,14},{6,2},{... | collective-permute-start | bytes 3145736 | tf_op jit(solution)/shard_map/ppermute | solution.py:35
  47.1 26.7 %collective-permute-start.8 = (bf16[8320,128]{1,0:T(8,128)(2,1)S(1)}, bf16[8320,128]{1,0:T(8,128)(2,1)S(1)}, u32[]{:S(2)}, u32[]{:S(2)}) collective-permute-start(bf16[8320,128]{1,0:T(8,128)(2,1)S(1)} %constant_dynamic-update-slice_fusion.2.refs_4_), channel_id=1, source_target_pairs={{0,4},{4,8},{8,12},{12,0},{1,5},{5,9},{9,13},{13,1},{2,6},{6,10},{... | collective-permute-start | bytes 6389768 | tf_op jit(solution)/shard_map/ppermute | solution.py:35
  48.4 25.7 %collective-permute-start.10 = (bf16[8320,128]{1,0:T(8,128)(2,1)S(1)}, bf16[8320,128]{1,0:T(8,128)(2,1)S(1)}, u32[]{:S(2)}, u32[]{:S(2)}) collective-permute-start(bf16[8320,128]{1,0:T(8,128)(2,1)S(1)} %constant_dynamic-update-slice_fusion.2.refs_4_), channel_id=1, source_target_pairs={{0,12},{4,0},{8,4},{12,8},{1,13},{5,1},{9,5},{13,9},{2,14},{6,2},{... | collective-permute-start | bytes 6389768 | tf_op jit(solution)/shard_map/ppermute | solution.py:35
  73.9 49.1 %collective-permute-start.9 = (bf16[4160,128]{1,0:T(8,128)(2,1)S(1)}, bf16[4160,128]{1,0:T(8,128)(2,1)S(1)}, u32[]{:S(2)}, u32[]{:S(2)}) collective-permute-start(bf16[4160,128]{1,0:T(8,128)(2,1)S(1)} %slice.41), channel_id=1, source_target_pairs={{0,4},{4,8},{8,12},{12,0},{1,5},{5,9},{9,13},{13,1},{2,6},{6,10},{... | collective-permute-start | bytes 3194888 | tf_op jit(solution)/shard_map/ppermute | solution.py:35
  74.1 48.9 %collective-permute-start.11 = (bf16[4160,128]{1,0:T(8,128)(2,1)S(1)}, bf16[4160,128]{1,0:T(8,128)(2,1)S(1)}, u32[]{:S(2)}, u32[]{:S(2)}) collective-permute-start(bf16[4160,128]{1,0:T(8,128)(2,1)S(1)} %slice.43), channel_id=1, source_target_pairs={{0,12},{4,0},{8,4},{12,8},{1,13},{5,1},{9,5},{13,9},{2,14},{6,2},{... | collective-permute-start | bytes 3194888 | tf_op jit(solution)/shard_map/ppermute | solution.py:35
  76.8 18.1 %collective-permute-start.12 = (bf16[4,4,128,128]{3,2,1,0:T(8,128)(2,1)S(1)}, bf16[4,4,128,128]{3,2,1,0:T(8,128)(2,1)S(1)}, u32[]{:S(2)}, u32[]{:S(2)}) collective-permute-start(bf16[4,4,128,128]{3,2,1,0:T(8,128)(2,1)S(1)} %get-tuple-element.25), channel_id=1, source_target_pairs={{0,4},{4,8},{8,12},{12,0},{1,5},{5,9},{9,13},{13,1},{2,6},{6,10},{... | collective-permute-start | bytes 1572872 | tf_op jit(solution)/shard_map/ppermute | solution.py:35
  76.8 18.1 %collective-permute-start.14 = (bf16[4,4,128,128]{3,2,1,0:T(8,128)(2,1)S(1)}, bf16[4,4,128,128]{3,2,1,0:T(8,128)(2,1)S(1)}, u32[]{:S(2)}, u32[]{:S(2)}) collective-permute-start(bf16[4,4,128,128]{3,2,1,0:T(8,128)(2,1)S(1)} %get-tuple-element.31), channel_id=1, source_target_pairs={{0,12},{4,0},{8,4},{12,8},{1,13},{5,1},{9,5},{13,9},{2,14},{6,2},{... | collective-permute-start | bytes 1572872 | tf_op jit(solution)/shard_map/ppermute | solution.py:35
  94.9 28.1 %collective-permute-start.13 = (bf16[4,4,128,128]{3,2,1,0:T(8,128)(2,1)S(1)}, bf16[4,4,128,128]{3,2,1,0:T(8,128)(2,1)S(1)}, u32[]{:S(2)}, u32[]{:S(2)}) collective-permute-start(bf16[4,4,128,128]{3,2,1,0:T(8,128)(2,1)S(1)} %collective-permute-done.12), channel_id=1, source_target_pairs={{0,4},{4,8},{8,12},{12,0},{1,5},{5,9},{9,13},{13,1},{2,6},{6,10},{... | collective-permute-start | bytes 1572872 | tf_op jit(solution)/shard_map/ppermute | solution.py:35
  94.9 28.1 %collective-permute-start.15 = (bf16[4,4,128,128]{3,2,1,0:T(8,128)(2,1)S(1)}, bf16[4,4,128,128]{3,2,1,0:T(8,128)(2,1)S(1)}, u32[]{:S(2)}, u32[]{:S(2)}) collective-permute-start(bf16[4,4,128,128]{3,2,1,0:T(8,128)(2,1)S(1)} %collective-permute-done.14), channel_id=1, source_target_pairs={{0,12},{4,0},{8,4},{12,8},{1,13},{5,1},{9,5},{13,9},{2,14},{6,2},{... | collective-permute-start | bytes 1572872 | tf_op jit(solution)/shard_map/ppermute | solution.py:35
  128.2 19.1 %collective-permute-start.18 = (s16[4,33,16,128]{3,2,1,0:T(8,128)(2,1)S(1)}, s16[4,33,16,128]{3,2,1,0:T(8,128)(2,1)}, u32[]{:S(2)}, u32[]{:S(2)}) collective-permute-start(s16[4,33,16,128]{3,2,1,0:T(8,128)(2,1)S(1)} %get-tuple-element.35), channel_id=1, source_target_pairs={{0,1},{1,2},{2,3},{3,0},{4,5},{5,6},{6,7},{7,4},{8,9},{9,10},{10,1... | collective-permute-start | bytes 1622024 | tf_op jit(solution)/shard_map/ppermute | solution.py:35
  129.3 18.1 %collective-permute-start.20 = (s16[4,33,16,128]{3,2,1,0:T(8,128)(2,1)S(1)}, s16[4,33,16,128]{3,2,1,0:T(8,128)(2,1)}, u32[]{:S(2)}, u32[]{:S(2)}) collective-permute-start(s16[4,33,16,128]{3,2,1,0:T(8,128)(2,1)S(1)} %get-tuple-element.36), channel_id=1, source_target_pairs={{0,3},{1,0},{2,1},{3,2},{4,7},{5,4},{6,5},{7,6},{8,11},{9,8},{10,9... | collective-permute-start | bytes 1622024 | tf_op jit(solution)/shard_map/ppermute | solution.py:35
  138.4 27.1 %collective-permute-start.17 = (s16[8,33,16,128]{3,2,1,0:T(8,128)(2,1)}, s16[8,33,16,128]{3,2,1,0:T(8,128)(2,1)}, u32[]{:S(2)}, u32[]{:S(2)}) collective-permute-start(s16[8,33,16,128]{3,2,1,0:T(8,128)(2,1)} %last_panel.6), channel_id=1, source_target_pairs={{0,1},{1,2},{2,3},{3,0},{4,5},{5,6},{6,7},{7,4},{8,9},{9,10},{10,1... | collective-permute-start | bytes 3244040 | tf_op jit(solution)/shard_map/ppermute | solution.py:35
  144.6 20.9 %collective-permute-start.16 = (s16[8,33,16,128]{3,2,1,0:T(8,128)(2,1)}, s16[8,33,16,128]{3,2,1,0:T(8,128)(2,1)}, u32[]{:S(2)}, u32[]{:S(2)}) collective-permute-start(s16[8,33,16,128]{3,2,1,0:T(8,128)(2,1)} %last_panel.5), channel_id=1, source_target_pairs={{0,3},{1,0},{2,1},{3,2},{4,7},{5,4},{6,5},{7,6},{8,11},{9,8},{10,9... | collective-permute-start | bytes 3244040 | tf_op jit(solution)/shard_map/ppermute | solution.py:35
  147.3 12.7 %collective-permute-start.19 = (s16[4,33,16,128]{3,2,1,0:T(8,128)(2,1)}, s16[4,33,16,128]{3,2,1,0:T(8,128)(2,1)}, u32[]{:S(2)}, u32[]{:S(2)}) collective-permute-start(s16[4,33,16,128]{3,2,1,0:T(8,128)(2,1)} %collective-permute-done.18), channel_id=1, source_target_pairs={{0,1},{1,2},{2,3},{3,0},{4,5},{5,6},{6,7},{7,4},{8,9},{9,10},{10,1... | collective-permute-start | bytes 1622024 | tf_op jit(solution)/shard_map/ppermute | solution.py:35
  147.4 18.1 %collective-permute-start.21 = (s16[4,33,16,128]{3,2,1,0:T(8,128)(2,1)}, s16[4,33,16,128]{3,2,1,0:T(8,128)(2,1)}, u32[]{:S(2)}, u32[]{:S(2)}) collective-permute-start(s16[4,33,16,128]{3,2,1,0:T(8,128)(2,1)} %collective-permute-done.20), channel_id=1, source_target_pairs={{0,3},{1,0},{2,1},{3,2},{4,7},{5,4},{6,5},{7,6},{8,11},{9,8},{10,9... | collective-permute-start | bytes 1622024 | tf_op jit(solution)/shard_map/ppermute | solution.py:35

commit v6 on v5

--- a/solution.py
+++ b/solution.py
@@ -106,17 +106,17 @@
     )(core, dens, ints)
 
 
-def regroup_kernel(at, mine, other, own, after, before, far0, far1, sems):
+def regroup_kernel(at, mine, other, own, ahead, back, sems):
     swapped, line, cross = at[0] == 1, at[1], at[2]
     copies = []
-    for step, dst in enumerate((own, after, None, before)):
+    for step in range(4):
         t = (line + step) % 4
         for i, rel in enumerate(ORDER):
             o = (cross + rel) % 4
             row = jnp.where(swapped, o * 4 + t, t * 4 + o)
             for m, src in enumerate((mine, other)):
-                to = (far0, far1)[m].at[i] if dst is None else dst.at[m, i]
-                copies.append(pltpu.make_async_copy(src.at[row], to, sems.at[len(copies)]))
+                dst = (own.at[m, i], ahead.at[m, i], (ahead, back)[m].at[2, i], back.at[m, i])[step]
+                copies.append(pltpu.make_async_copy(src.at[row], dst, sems.at[len(copies)]))
     for copy in copies:
         copy.start()
     for copy in copies:
@@ -124,8 +124,7 @@
 
 
 def regroup(at, mine, other):
-    two, one = (2, 4, 4, 128, 128), (4, 4, 128, 128)
-    shapes = [two, two, two, one, one]
+    shapes = [(2, 4, 4, 128, 128), (3, 4, 4, 128, 128), (3, 4, 4, 128, 128)]
     return pl.pallas_call(
         regroup_kernel,
         grid_spec=pltpu.PrefetchScalarGridSpec(
@@ -155,21 +154,16 @@
     return jnp.exp2(code.astype(jnp.int32).astype(jnp.float32) * (1.0 / 256.0)) * (1.0 / TOP)
 
 
-def panel_kernel(n, pieces, target, has_sums, coded, ints, at, *refs):
+def panel_kernel(n, pieces, halves, form, at, *refs):
     kohn, refs = refs[:2 * n], refs[2 * n:]
     panels, refs = refs[:pieces], refs[pieces:]
-    if has_sums:
-        p_ref, refs = refs[0], refs[1:]
-    outs, (dens, sems, acc) = refs[:-3], refs[-3:]
+    if form != "first":
+        sums_in, refs = refs[:2], refs[2:]
+    if form == "sent":
+        received, refs = refs[:2], refs[2:]
+    outs, (dens, sems, acc, staged, ints) = refs[:-5], refs[-5:]
     size = n * 8 * PART // pieces
     core, line, cross, x = at[0], at[1], at[2], at[3]
-    if target is None:
-        step = pl.program_id(0)
-        ahead = jnp.where(step == 0, ORDER[0], jnp.where(step == 1, ORDER[1], jnp.where(step == 2, ORDER[2], ORDER[3])))
-    else:
-        ahead = ORDER[target]
-    goal = (cross + ahead) & 3
-    block_row = jnp.where(core == 1, goal * 4 + line, line * 4 + goal)
 
     @pl.when(pl.program_id(0) == 0)
     def _():
@@ -180,6 +174,22 @@
             copy.start()
         for copy in copies:
             copy.wait()
+        for s in range(n):
+            rows = [dens[pl.ds((s * 8 + p) * PART + 8 * 128, 16), :].astype(jnp.float32) for p in range(8)]
+            rows = [row[2:3] for row in rows] + [rows[0][0:2], rows[1][0:2], jnp.zeros((4, 128), jnp.float32)]
+            staged[s * 16:(s + 1) * 16, :] = jnp.concatenate(rows, axis=0).astype(jnp.int32)
+        copy = pltpu.make_async_copy(staged, ints, sems.at[pieces])
+        copy.start()
+        copy.wait()
+
+    def place_of(target):
+        if target is None:
+            step = pl.program_id(0)
+            ahead = jnp.where(step < 2, ORDER[0] - step, ORDER[2] * (3 - step))
+        else:
+            ahead = ORDER[target]
+        goal = (cross + ahead) & 3
+        return jnp.where(core == 1, goal * 4 + line, line * 4 + goal)
 
     low = (lax.broadcasted_iota(jnp.int32, (32, 128), 1) < 64).astype(jnp.float32).astype(jnp.bfloat16)
     high = 1 - low
@@ -188,88 +198,103 @@
         turned = jnp.concatenate([blk[:, B:], blk[:, :B]], axis=1)
         return jnp.concatenate([blk * low, turned * low, turned * high, blk * high], axis=0)
 
-    def product(m, r, s, a):
-        k = ints[(s * 8 + m) * 8 + (block_row >> 3), (block_row & 7) * 16 + r * 4 + a]
+    def product(h, place, r, s, a):
+        k = ints[s * 16 + 8 + halves[h][1] * 2 + (place >> 3), (place & 7) * 16 + r * 4 + a]
         slot = (120 >> (2 * (((k >> 4) - x) & 3))) & 3
         k = slot * 16 + ((k & 15) ^ (8 * core))
         part = s * 8 + (k >> 3)
         left = dens[pl.ds(pl.multiple_of(part * PART + (k & 7) * 128, 16), 128), :]
-        right = twice(kohn[2 * s + m][0, 0, r, a * 32:(a + 1) * 32, :])
+        right = twice(kohn[2 * s + h][0, 0, r, a * 32:(a + 1) * 32, :])
         r = lax.dot_general(left, right, (((1,), (1,)), ((), ())), preferred_element_type=jnp.float32)
-        return part, (k & 7) * SP, r
-
-    def add(sums, part, first, r):
-        js = [ints[part * 8 + 2, first + b] for b in range(SP)]
+        return s * 16 + (k >> 3), (k & 7) * SP, r
+
+    def add(sums, word, first, r):
+        js = [ints[word, first + b] for b in range(SP)]
         old = [sums[j] for j in js]
         for b in range(SP):
             sums[js[b]] = old[b] + r[b * 16:(b + 1) * 16, :]
 
-    def two_rows(m, pair):
+    def two_rows(h, place, pair):
         work, sums = [], []
         for q in range(2):
             r = pair * 2 + q
             work += [(q, r, s, a) for s in range(n) for a in range(SK)]
-            place = acc.at[q] if coded else outs[0].at[0, m * 4 + r]
-            place[...] = p_ref[0, m * 4 + r] if has_sums else jnp.zeros((NCW, 16, 128), jnp.float32)
-            sums.append(place)
-        held = [product(m, *work[i][1:]) for i in range(3)]
+            total = acc.at[q] if form in ("coded", "sent") else outs[0].at[0, h * 4 + r]
+            if form == "first":
+                total[...] = jnp.zeros((NCW, 16, 128), jnp.float32)
+            elif form == "sent":
+                scale = decoded_scale(received[h][r, NCW])
+                for j in range(NCW):
+                    total[j] = sums_in[h][0, r, j] + received[h][r, j].astype(jnp.int32).astype(jnp.float32) * scale
+            else:
+                total[...] = sums_in[h][0, r]
+            sums.append(total)
+        held = [product(h, place, *work[i][1:]) for i in range(3)]
         for i in range(len(work)):
             if i + 3 < len(work):
-                held.append(product(m, *work[i + 3][1:]))
+                held.append(product(h, place, *work[i + 3][1:]))
             add(sums[work[i][0]], *held[i])
-        if coded:
+        if form in ("coded", "sent"):
             for q in range(2):
                 r = pair * 2 + q
-                out, row = (outs[m], r) if len(outs) == 2 else (outs[0], m * 4 + r)
-
-                def put(j, value, out=out, row=row):
-                    out[row, j] = value
+
+                def put(j, value, r=r):
+                    outs[h][r, j] = value
 
                 encode(sums[q], put, lambda code, put=put: put(NCW, code.astype(jnp.int16)))
 
-    for m in range(2):
-        lax.fori_loop(0, 2, lambda pair, _, m=m: (two_rows(m, pair), 0)[1], 0)
-
-
-def panel_sums(name, ints, at, kohn, panels, sums, target=None, coded=False):
+    for h in range(2):
+        place = place_of(halves[h][0])
+        lax.fori_loop(0, 2, lambda pair, _, h=h, place=place: (two_rows(h, place, pair), 0)[1], 0)
+
+
+def panel_sums(name, form, at, kohn, panels, halves, sums=None, received=(), us=4.0):
     n, pieces = len(kohn) // 2, len(panels)
-    base = 0 if target is None else target
-    k_specs = [
-        pl.BlockSpec((1, 1, 4, 128, 128), lambda o, *_, m=m: (m, o + base, 0, 0, 0)) for _, m in kohn
-    ]
-    s_shape = (1, 8, NCW, 16, 128)
-    s_spec = pl.BlockSpec(s_shape, lambda o, *_: (o + base, 0, 0, 0, 0))
-    o_specs = [pl.BlockSpec(s_shape, lambda o, *_: (o, 0, 0, 0, 0))]
-    shapes = [jax.ShapeDtypeStruct((4 if target is None else 1,) + s_shape[1:], jnp.float32)]
-    if coded:
-        parts = 2 if target == 0 else 1
-        o_specs = [pl.BlockSpec((8 // parts, NCW + 1, 16, 128), lambda o, *_: (0, 0, 0, 0))] * parts
-        shapes = [jax.ShapeDtypeStruct((8 // parts, NCW + 1, 16, 128), jnp.int16)] * parts
+    steps = 4 if halves[0][0] is None else 1
+
+    def at_target(h, lead):
+        target = halves[h][0]
+        return lambda o, *_: (lead, o if target is None else target, 0, 0, 0)
+
+    k_specs = [pl.BlockSpec((1, 1, 4, 128, 128), at_target(i % 2, place)) for i, (_, place) in enumerate(kohn)]
+
+    def s_spec(h):
+        target, m = halves[h]
+        return pl.BlockSpec((1, 4, NCW, 16, 128), lambda o, *_: (o if target is None else target, m, 0, 0, 0))
+
+    coded = pl.BlockSpec((4, NCW + 1, 16, 128), lambda o, *_: (0, 0, 0, 0))
+    if form in ("coded", "sent"):
+        o_specs = [coded] * 2
+        shapes = [jax.ShapeDtypeStruct((4, NCW + 1, 16, 128), jnp.int16)] * 2
+    else:
+        o_specs = [pl.BlockSpec((1, 8, NCW, 16, 128), lambda o, *_: (o, 0, 0, 0, 0))]
+        shapes = [jax.ShapeDtypeStruct((steps, 8, NCW, 16, 128), jnp.float32)]
     any_spec = pl.BlockSpec(memory_space=pl.ANY)
-    steps = 4 if target is None else 1
     return pl.pallas_call(
-        lambda *refs: panel_kernel(n, pieces, target, sums is not None, coded, *refs),
+        lambda *refs: panel_kernel(n, pieces, halves, form, *refs),
         grid_spec=pltpu.PrefetchScalarGridSpec(
-            num_scalar_prefetch=2,
+            num_scalar_prefetch=1,
             grid=(steps,),
-            in_specs=k_specs + [any_spec] * pieces + [s_spec] * (sums is not None),
+            in_specs=(
+                k_specs + [any_spec] * pieces + ([] if sums is None else [s_spec(0), s_spec(1)]) + [coded] * len(received)
+            ),
             out_specs=o_specs,
             scratch_shapes=[
                 pltpu.VMEM((n * 8 * PART, 128), jnp.bfloat16),
-                pltpu.SemaphoreType.DMA((pieces,)),
+                pltpu.SemaphoreType.DMA((pieces + 1,)),
                 pltpu.VMEM((2, NCW, 16, 128), jnp.float32),
+                pltpu.VMEM((n * 16, 128), jnp.int32),
+                pltpu.SMEM((n * 16, 128), jnp.int32),
             ],
         ),
         out_shape=shapes,
         compiler_params=pltpu.CompilerParams(vmem_limit_bytes=44 << 20),
-        cost_estimate=pl.CostEstimate(
-            flops=2 * n * 32 * steps * 128 * 128 * 128, bytes_accessed=(2 * n + 5 * steps) << 20, transcendentals=0
-        ),
+        cost_estimate=pl.CostEstimate(flops=int(us * 1.1e9), bytes_accessed=int(us * 2e6), transcendentals=0),
         name=name,
-    )(ints, at, *[array for array, _ in kohn], *panels, *(() if sums is None else (sums,)))
-
-
-def pack_kernel(slots, own, after, before, far0, far1, o_ref, total, codes):
+    )(at, *[array for array, _ in kohn], *panels, *([] if sums is None else [sums, sums]), *received)
+
+
+def pack_kernel(slots, own, prev0, prev1, next0, next1, o_ref, total, codes):
     rows = lax.broadcasted_iota(jnp.int32, (16, 128), 0)
     lane = lax.broadcasted_iota(jnp.int32, (16, 128), 1)
 
@@ -283,13 +308,13 @@
 
     def one(m, r):
         row = m * 4 + r
-        coded = [(before, row), (after, row), ((far0, far1)[m], r)]
+        coded = [((prev0, prev1)[m], r), ((next0, next1)[m], r)]
         scales = [decoded_scale(ref[at, NCW]) for ref, at in coded]
         for group in range(NCW // 8):
             blocks = []
             for j in range(group * 8, group * 8 + 8):
                 g = [ref[at, j].astype(jnp.int32).astype(jnp.float32) * scale for (ref, at), scale in zip(coded, scales)]
-                blocks.append((own[0, row, j] + g[0]) + (g[1] + g[2]))
+                blocks.append(own[0, row, j] + g[0] + g[1])
             turned = jnp.concatenate(blocks, axis=0).T
             v = []
             for q in range(8):
@@ -330,7 +355,7 @@
     lax.fori_loop(0, 32, finish, 0)
 
 
-def pack(slots, own, after, before, far0, far1):
+def pack(slots, *parts):
     def whole(array):
         return pl.BlockSpec(
             array.shape, lambda i, *_, n=array.ndim: (0,) * n, pipeline_mode=pl.Buffered(1)
@@ -341,14 +366,14 @@
         grid_spec=pltpu.PrefetchScalarGridSpec(
             num_scalar_prefetch=1,
             grid=(1,),
-            in_specs=[whole(array) for array in (own, after, before, far0, far1)],
+            in_specs=[whole(array) for array in parts],
             out_specs=pl.BlockSpec((128, MSG, 128), lambda i, *_: (0, 0, 0), pipeline_mode=pl.Buffered(1)),
             scratch_shapes=[pltpu.VMEM((NCW, 16, 128), jnp.float32), pltpu.VMEM((128, 16, 128), jnp.int32)],
         ),
         out_shape=jax.ShapeDtypeStruct((128, MSG, 128), jnp.int16),
         compiler_params=pltpu.CompilerParams(vmem_limit_bytes=32 << 20),
         name="pack",
-    )(slots, own, after, before, far0, far1)
+    )(slots, *parts)
 
 
 def unpack_kernel(r_ref, o_ref, full):
@@ -402,22 +427,17 @@
 
     mine, theirs = split(at, dens, ints)
     shard = jnp.concatenate([mine, over_core(theirs)])
+    shard, kohn, kohn_other = lax.optimization_barrier((shard, kohn, kohn_other))
     left, right = over_x(shard, 1), over_x(shard, -1)
 
-    kohn, after, before, opposite0, opposite1 = regroup(at, kohn, kohn_other)
-    left, right, _ = lax.optimization_barrier((left, right, opposite0))
-    kohn_before, kohn_after = over_line(after, 1), over_line(before, -1)
-    opposite0, opposite1 = over_line(opposite0, 1), over_line(opposite1, -1)
+    kohn, ahead, back = regroup(at, kohn, kohn_other)
+    kohn_prev, kohn_next = over_line(ahead, 1), over_line(back, -1)
+    left, right, kohn_prev, kohn_next = lax.optimization_barrier((left, right, kohn_prev, kohn_next))
+    opposite0, opposite1 = over_line(kohn_prev[2:], 1), over_line(kohn_next[2:], -1)
 
     panel = jnp.concatenate([shard, left, right, over_x(left[:PART], 1), over_x(right[PART:], -1)])
-    sent, kohn_before, kohn_after = lax.optimization_barrier((panel, kohn_before, kohn_after))
+    sent, opposite0, opposite1 = lax.optimization_barrier((panel, opposite0, opposite1))
     prev, after = over_line(sent, 1), over_line(sent, -1)
-    opposite0, opposite1 = over_line(opposite0, 1), over_line(opposite1, -1)
-    far_low, far_high = over_line(prev[:4 * PART], 1), over_line(after[4 * PART:], -1)
-
-    def words(*arrays):
-        parts = jnp.concatenate([array.reshape(-1, PART, 128)[:, 8 * 128:8 * 128 + 8] for array in arrays])
-        return parts.astype(jnp.int32).reshape(-1, 128)
 
     owners = jnp.stack([owner_map.reshape(128), shard[PART + 8 * 128 + 3].astype(jnp.int32)])
     hit = (owners[..., None] == jnp.arange(128, dtype=jnp.int32)).astype(jnp.int32)
@@ -428,28 +448,27 @@
     def both(array):
         return [(array, 0), (array, 1)]
 
-    sums, = panel_sums("own_panel", words(panel), at, both(kohn), [panel], None)
+    everything = ((None, 0), (None, 1))
+    sums, = panel_sums("own_panel", "first", at, both(kohn), [panel], everything, us=9.0)
+    prev, after, sums = lax.optimization_barrier((prev, after, sums))
+    far_low, far_high = over_line(prev[:4 * PART], 1), over_line(after[4 * PART:], -1)
     sums, = panel_sums(
-        "near_panels", words(prev, after), at, both(kohn_before) + both(kohn_after), [prev, after], sums
+        "near_panels", "more", at, both(kohn_prev) + both(kohn_next), [prev, after], everything, sums, us=16.0
     )
-    opposite = [(opposite0[None], 0), (opposite1[None], 0)]
-    far_words = words(far_low, far_high)
-
-    def last(target, coded):
-        return panel_sums(
-            "last_panel", far_words, at, opposite, [far_low, far_high], sums, target=target, coded=coded
-        )
-
-    sums0, sums1 = last(0, True)
-    sums0, sums1 = over_cross(sums0, 1), over_cross(sums1, -1)
-    to_next, = last(1, True)
-    from_prev = over_cross(to_next, 1)
-    to_prev, = last(2, True)
-    from_next = over_cross(to_prev, -1)
-    sums0, sums1 = over_cross(sums0, 1), over_cross(sums1, -1)
-    own, = last(3, False)
-
-    outgoing = pack(slots, own, from_next, from_prev, sums0, sums1)
+
+    def last(form, halves, received=()):
+        kohn = [((opposite0, opposite1)[m], 0) for _, m in halves]
+        return panel_sums("last_" + form, form, at, kohn, [far_low, far_high], halves, sums, received)
+
+    via_next, via_prev = last("coded", ((0, 0), (0, 1)))
+    via_next, via_prev = over_cross(via_next, 1), over_cross(via_prev, -1)
+    next1, prev0 = last("coded", ((1, 1), (2, 0)))
+    prev_1, next_0 = over_cross(next1, 1), over_cross(prev0, -1)
+    next0, prev1 = last("sent", ((1, 0), (2, 1)), (via_next, via_prev))
+    prev_0, next_1 = over_cross(next0, 1), over_cross(prev1, -1)
+    own, = last("more", ((3, 0), (3, 1)))
+
+    outgoing = pack(slots, own, prev_0, prev_1, next_0, next_1)
     received = lax.all_to_all(outgoing, ALL, split_axis=0, concat_axis=0, tiled=True)
     return unpack(received.reshape(X, C, 16, MSG, 128))
 

time: 227 us -> 196 us (0.86)
  waiting for transfers between devices: 70.1 us -> 45.2 us
  starting transfers between devices: 30.5 us -> 26 us
  Pallas kernels: 72.1 us -> 69.4 us
    ppermute x16 -> x14, waiting for transfers between devices: 59.9 us -> 26.4 us  [over(): lax.ppermute(v, PLANE, [(group[i], group[(i + step) % 4]) for group in gr...]
    ppermute x4, waiting for transfers between devices: 9.44 us -> 17.1 us  [over_x(): return lax.ppermute(v, 'x', [(i, (i + step) % X) for i in range(X)])]
    ppermute x16 -> x14, starting transfers between devices: 23.4 us -> 19.4 us  [over(): lax.ppermute(v, PLANE, [(group[i], group[(i + step) % 4]) for group in gr...]
  transfers between devices with their start and end apart: 22 -> 20, of which waited for: 8 -> 10; matrix products, arithmetic and copies ran while one was open for 2% -> 2% of each run, Pallas kernels for 23% -> 23%
where the time goes in v6:
time: 196 us
  Pallas kernels  69.4 us (35%)
  blocking collectives  46.9 us (24%)
  waiting for transfers between devices  45.2 us (23%)
  starting transfers between devices  26 us (13%)
  local copies, waits for them, and re-layouts  5.31 us (3%)
  other arithmetic  2.84 us (1%)
    all_to_all x1, blocking collectives, local(): lax.all_to_all(outgoing, ALL, split_axis=0, concat_axis=0, tiled=True)  46.9 us
    pallas_call x6, Pallas kernels, panel_sums(): pl.pallas_call(lambda *refs: panel_kernel(n, pieces, halves, form, *refs)...  46.3 us
    ppermute x14, waiting for transfers between devices, over(): lax.ppermute(v, PLANE, [(group[i], group[(i + step) % 4]) for group in gr...  26.4 us
    ppermute x14, starting transfers between devices, over(): lax.ppermute(v, PLANE, [(group[i], group[(i + step) % 4]) for group in gr...  19.4 us
    ppermute x4, waiting for transfers between devices, over_x(): return lax.ppermute(v, 'x', [(i, (i + step) % X) for i in range(X)])  17.1 us
    pallas_call x1, Pallas kernels, unpack(): pl.pallas_call(unpack_kernel, grid=(X,), in_specs=[pl.BlockSpec((1, C, 16...  7.07 us
    pallas_call x1, Pallas kernels, pack(): pl.pallas_call(pack_kernel, grid_spec=pltpu.PrefetchScalarGridSpec(num_sc...  5.86 us
    pallas_call x1, Pallas kernels, split(): pl.pallas_call(split_kernel, grid_spec=pltpu.PrefetchScalarGridSpec(num_s...  5.22 us
  transfers between devices with their start and end apart: 20, of which 10 were waited for; matrix products, arithmetic and copies ran while one was open for 2% of the time, Pallas kernels for 23%

profile of v6, /device:TPU:1, one launch (start us, length us, event | category | flops | bytes accessed | tf_op | source)
XLA Modules:
  0.0 195.9 jit_solution(10121905321547946799)
XLA Ops:
  0.0 3.8 %reshape.31.mine = bf16[16,4,128,128]{3,2,1,0:T(8,128)(2,1)S(1)} reshape(bf16[64,1,4,4096]{3,2,1,0:T(4,128)(2,1)} %param.5) | data formatting | bytes 4194304 | tf_op jit(solution)/shard_map/reshape | solution.py:419
  3.8 1.5 collective-permute-start.1
  7.0 5.2 %split.1 = (bf16[1040,128]{1,0:T(8,128)(2,1)}, bf16[1040,128]{1,0:T(8,128)(2,1)}) custom-call(s32[4]{0:T(128)} %pad_add_fusion.2.core.at.refs_0_, bf16[8,8,4096]{2,1,0:T(8,128)(2,1)} %bitcast.12, s32[16,128]{1,0:T(8,128)} %fusion.2.i_ref), custom_call_target="tpu_custom_call" | custom-call | tf_op jit(solution)/shard_map/split/pallas_call | solution.py:94
  12.3 1.7 collective-permute-done
  15.6 5.0 %regroup.1 = (bf16[2,4,4,128,128]{4,3,2,1,0:T(8,128)(2,1)S(1)}, bf16[3,4,4,128,128]{4,3,2,1,0:T(8,128)(2,1)S(1)}, bf16[3,4,4,128,128]{4,3,2,1,0:T(8,128)(2,1)S(1)}) custom-call(s32[4]{0:T(128)S(1)} %copy-done, bf16[16,4,128,128]{3,2,1,0:T(8,128)(2,1)S(1)} %reshape.31.mine, bf16[16,4,128,128]{3,2,1,0:T(8,128)(2,1)} %collective-permute-done.1.other), custom_call_target="tpu_custom_call" | custom-call | tf_op jit(solution)/shard_map/regroup/pallas_call | solution.py:128
  20.6 1.4 collective-permute-start.4
  22.0 1.5 collective-permute-start.5
  23.6 2.5 %collective-permute-start.3 = (bf16[2080,128]{1,0:T(8,128)(2,1)S(1)}, bf16[2080,128]{1,0:T(8,128)(2,1)S(1)}, u32[]{:S(2)}, u32[]{:S(2)}) collective-permute-start(bf16[2080,128]{1,0:T(8,128)(2,1)S(1)} %pad_maximum_fusion), channel_id=1, source_target_pairs={{0,96},{32,0},{64,32},{96,64},{1,97},{33,1},{65,33},{97,65},{2,98}... | collective-permute-start | bytes 1597448 | tf_op jit(solution)/shard_map/ppermute | solution.py:47
  26.1 9.9 %collective-permute-done.3 = bf16[2080,128]{1,0:T(8,128)(2,1)S(1)} collective-permute-done((bf16[2080,128]{1,0:T(8,128)(2,1)S(1)}, bf16[2080,128]{1,0:T(8,128)(2,1)S(1)}, u32[]{:S(2)}, u32[]{:S(2)}) %collective-permute-start.3) | collective-permute-done | bytes 532512 | tf_op jit(solution)/shard_map/ppermute | solution.py:47
  36.0 3.1 %collective-permute-done.2 = bf16[2080,128]{1,0:T(8,128)(2,1)S(1)} collective-permute-done((bf16[2080,128]{1,0:T(8,128)(2,1)S(1)}, bf16[2080,128]{1,0:T(8,128)(2,1)S(1)}, u32[]{:S(2)}, u32[]{:S(2)}) %collective-permute-start.2) | collective-permute-done | bytes 532512 | tf_op jit(solution)/shard_map/ppermute | solution.py:47
  39.1 2.5 %collective-permute-done.4.refs_1_.refs_2_ = bf16[3,4,4,128,128]{4,3,2,1,0:T(8,128)(2,1)S(1)} collective-permute-done((bf16[3,4,4,128,128]{4,3,2,1,0:T(8,128)(2,1)S(1)}, bf16[3,4,4,128,128]{4,3,2,1,0:T(8,128)(2,1)S(1)}, u32[]{:S(2)}, u32[]{:S(2)}) %collective-permute-start.4) | collective-permute-done | bytes 1572896 | tf_op jit(solution)/shard_map/ppermute | solution.py:35
  41.6 2.5 %collective-permute-start.7 = (bf16[1040,128]{1,0:T(8,128)(2,1)S(1)}, bf16[1040,128]{1,0:T(8,128)(2,1)S(1)}, u32[]{:S(2)}, u32[]{:S(2)}) collective-permute-start(bf16[1040,128]{1,0:T(8,128)(2,1)S(1)} %slice.23), channel_id=1, source_target_pairs={{0,96},{32,0},{64,32},{96,64},{1,97},{33,1},{65,33},{97,65},{2,98}... | collective-permute-start | bytes 798728 | tf_op jit(solution)/shard_map/ppermute | solution.py:47
  44.3 2.8 %collective-permute-start.9 = (bf16[1,4,4,128,128]{4,3,2,1,0:T(8,128)(2,1)S(1)}, bf16[1,4,4,128,128]{4,3,2,1,0:T(8,128)(2,1)S(1)}, u32[]{:S(2)}, u32[]{:S(2)}) collective-permute-start(bf16[1,4,4,128,128]{4,3,2,1,0:T(8,128)(2,1)S(1)} %slice.25), channel_id=1, source_target_pairs={{0,12},{4,0},{8,4},{12,8},{1,13},{5,1},{9,5},{13,9},{2,14},{6,2},{... | collective-permute-start | bytes 1572872 | tf_op jit(solution)/shard_map/ppermute | solution.py:35
  47.2 4.0 %collective-permute-done.6 = bf16[1040,128]{1,0:T(8,128)(2,1)S(1)} collective-permute-done((bf16[1040,128]{1,0:T(8,128)(2,1)S(1)}, bf16[1040,128]{1,0:T(8,128)(2,1)S(1)}, u32[]{:S(2)}, u32[]{:S(2)}) %collective-permute-start.6) | collective-permute-done | bytes 266272 | tf_op jit(solution)/shard_map/ppermute | solution.py:47
  51.4 1.8 collective-permute-done.9.refs_2_.refs_1_
  53.2 3.4 %collective-permute-done.8.refs_1_.refs_2_ = bf16[1,4,4,128,128]{4,3,2,1,0:T(8,128)(2,1)S(1)} collective-permute-done((bf16[1,4,4,128,128]{4,3,2,1,0:T(8,128)(2,1)S(1)}, bf16[1,4,4,128,128]{4,3,2,1,0:T(8,128)(2,1)S(1)}, u32[]{:S(2)}, u32[]{:S(2)}) %collective-permute-start.8) | collective-permute-done | bytes 524320 | tf_op jit(solution)/shard_map/ppermute | solution.py:35
  56.6 1.5 collective-permute-start.10
  58.1 9.0 %own_panel.1.refs_7_.refs_8_ = f32[4,8,32,16,128]{4,3,2,1,0:T(8,128)} custom-call(s32[4]{0:T(128)S(1)} %copy-done.1, bf16[2,4,4,128,128]{4,3,2,1,0:T(8,128)(2,1)S(1)} %get-tuple-element.47.refs_1_.refs_2_, bf16[2,4,4,128,128]{4,3,2,1,0:T(8,128)(2,1)S(1)} %get-tuple-element.47.refs_1_.refs_2_, bf16[8320,128]{1,0:T(8,128)(2,1)S(1)} %constant_dynamic-update-slice_fusion.refs_3_), custom_call_target="tpu_custom_call" | custom-call | flops 9900000256 | bytes 18000000 | tf_op jit(solution)/shard_map/own_panel/pallas_call | solution.py:273
  67.2 15.0 %collective-permute-done.11.refs_6_ = bf16[8320,128]{1,0:T(8,128)(2,1)S(1)} collective-permute-done((bf16[8320,128]{1,0:T(8,128)(2,1)S(1)}, bf16[8320,128]{1,0:T(8,128)(2,1)S(1)}, u32[]{:S(2)}, u32[]{:S(2)}) %collective-permute-start.11) | collective-permute-done | bytes 2129952 | tf_op jit(solution)/shard_map/ppermute | solution.py:35
  83.8 2.4 %collective-permute-start.13 = (bf16[4160,128]{1,0:T(8,128)(2,1)S(1)}, bf16[4160,128]{1,0:T(8,128)(2,1)S(1)}, u32[]{:S(2)}, u32[]{:S(2)}) collective-permute-start(bf16[4160,128]{1,0:T(8,128)(2,1)S(1)} %slice.27), channel_id=1, source_target_pairs={{0,12},{4,0},{8,4},{12,8},{1,13},{5,1},{9,5},{13,9},{2,14},{6,2},{... | collective-permute-start | bytes 3194888 | tf_op jit(solution)/shard_map/ppermute | solution.py:35
  86.3 15.9 %near_panels.1.refs_5_.refs_6_ = f32[4,8,32,16,128]{4,3,2,1,0:T(8,128)} custom-call(s32[4]{0:T(128)S(1)} %copy-done.1, bf16[3,4,4,128,128]{4,3,2,1,0:T(8,128)(2,1)S(1)} %collective-permute-done.4.refs_1_.refs_2_, bf16[3,4,4,128,128]{4,3,2,1,0:T(8,128)(2,1)S(1)} %collective-permute-done.4.refs_1_.refs_2_, ...), custom_call_target="tpu_custom_call" | custom-call | flops 17600000000 | bytes 32000000 | tf_op jit(solution)/shard_map/near_panels/pallas_call | solution.py:273
  102.2 6.1 %last_coded.2 = (s16[4,33,16,128]{3,2,1,0:T(8,128)(2,1)}, s16[4,33,16,128]{3,2,1,0:T(8,128)(2,1)}) custom-call(s32[4]{0:T(128)S(1)} %copy-done.1, bf16[1,4,4,128,128]{4,3,2,1,0:T(8,128)(2,1)S(1)} %collective-permute-done.8.refs_1_.refs_2_, bf16[1,4,4,128,128]{4,3,2,1,0:T(8,128)(2,1)S(1)} %collective-permute-done.9.refs_2_.refs_1_, ...), custom_call_target="tpu_custom_call" | custom-call | flops 4400000000 | bytes 8000000 | tf_op jit(solution)/shard_map/last_coded/pallas_call | solution.py:273
  109.4 2.9 %collective-permute-start.15 = (s16[4,33,16,128]{3,2,1,0:T(8,128)(2,1)}, s16[4,33,16,128]{3,2,1,0:T(8,128)(2,1)}, u32[]{:S(2)}, u32[]{:S(2)}) collective-permute-start(s16[4,33,16,128]{3,2,1,0:T(8,128)(2,1)} %get-tuple-element.52), channel_id=1, source_target_pairs={{0,3},{1,0},{2,1},{3,2},{4,7},{5,4},{6,5},{7,6},{8,11},{9,8},{10,9... | collective-permute-start | bytes 1622024 | tf_op jit(solution)/shard_map/ppermute | solution.py:35
  112.7 5.2 %last_coded.3 = (s16[4,33,16,128]{3,2,1,0:T(8,128)(2,1)S(1)}, s16[4,33,16,128]{3,2,1,0:T(8,128)(2,1)S(1)}) custom-call(s32[4]{0:T(128)S(1)} %copy-done.1, bf16[1,4,4,128,128]{4,3,2,1,0:T(8,128)(2,1)S(1)} %collective-permute-done.9.refs_2_.refs_1_, bf16[1,4,4,128,128]{4,3,2,1,0:T(8,128)(2,1)S(1)} %collective-permute-done.8.refs_1_.refs_2_, ...), custom_call_target="tpu_custom_call" | custom-call | flops 4400000000 | bytes 8000000 | tf_op jit(solution)/shard_map/last_coded/pallas_call | solution.py:273
  118.1 2.7 %collective-permute-start.18 = (s16[4,33,16,128]{3,2,1,0:T(8,128)(2,1)S(1)}, s16[4,33,16,128]{3,2,1,0:T(8,128)(2,1)S(1)}, u32[]{:S(2)}, u32[]{:S(2)}) collective-permute-start(s16[4,33,16,128]{3,2,1,0:T(8,128)(2,1)S(1)} %get-tuple-element.55), channel_id=1, source_target_pairs={{0,3},{1,0},{2,1},{3,2},{4,7},{5,4},{6,5},{7,6},{8,11},{9,8},{10,9... | collective-permute-start | bytes 1622024 | tf_op jit(solution)/shard_map/ppermute | solution.py:35
  120.7 5.5 %last_sent.1 = (s16[4,33,16,128]{3,2,1,0:T(8,128)(2,1)S(1)}, s16[4,33,16,128]{3,2,1,0:T(8,128)(2,1)S(1)}) custom-call(s32[4]{0:T(128)S(1)} %copy-done.1, bf16[1,4,4,128,128]{4,3,2,1,0:T(8,128)(2,1)S(1)} %collective-permute-done.8.refs_1_.refs_2_, bf16[1,4,4,128,128]{4,3,2,1,0:T(8,128)(2,1)S(1)} %collective-permute-done.9.refs_2_.refs_1_, ...), custom_call_target="tpu_custom_call" | custom-call | flops 4400000000 | bytes 8000000 | tf_op jit(solution)/shard_map/last_sent/pallas_call | solution.py:273
  126.3 2.7 %collective-permute-start.19 = (s16[4,33,16,128]{3,2,1,0:T(8,128)(2,1)S(1)}, s16[4,33,16,128]{3,2,1,0:T(8,128)(2,1)S(1)}, u32[]{:S(2)}, u32[]{:S(2)}) collective-permute-start(s16[4,33,16,128]{3,2,1,0:T(8,128)(2,1)S(1)} %get-tuple-element.56), channel_id=1, source_target_pairs={{0,3},{1,0},{2,1},{3,2},{4,7},{5,4},{6,5},{7,6},{8,11},{9,8},{10,9... | collective-permute-start | bytes 1622024 | tf_op jit(solution)/shard_map/ppermute | solution.py:35
  129.1 4.5 %last_more.1.own = f32[1,8,32,16,128]{4,3,2,1,0:T(8,128)S(1)} custom-call(s32[4]{0:T(128)S(1)} %copy-done.1, bf16[1,4,4,128,128]{4,3,2,1,0:T(8,128)(2,1)S(1)} %collective-permute-done.8.refs_1_.refs_2_, bf16[1,4,4,128,128]{4,3,2,1,0:T(8,128)(2,1)S(1)} %collective-permute-done.9.refs_2_.refs_1_, bf16[4160,128]{1,0:T(8,128)(2,1)S(1)} %collective-permute-done.12.refs_3_, ...), custom_call_target="tpu_custom_call" | custom-call | flops 4400000000 | bytes 8000000 | tf_op jit(solution)/shard_map/last_more/pallas_call | solution.py:273
  133.6 2.4 %collective-permute-done.16.prev0 = s16[4,33,16,128]{3,2,1,0:T(8,128)(2,1)S(1)} collective-permute-done((s16[4,33,16,128]{3,2,1,0:T(8,128)(2,1)S(1)}, s16[4,33,16,128]{3,2,1,0:T(8,128)(2,1)S(1)}, u32[]{:S(2)}, u32[]{:S(2)}) %collective-permute-start.16) | collective-permute-done | bytes 540704 | tf_op jit(solution)/shard_map/ppermute | solution.py:35
  136.0 5.9 %pack.1 = s16[128,80,128]{2,1,0:T(8,128)(2,1)S(1)} custom-call(s32[256]{0:T(256)S(1)} %add_bitcast_fusion.slots, f32[1,8,32,16,128]{4,3,2,1,0:T(8,128)S(1)} %last_more.1.own, s16[4,33,16,128]{3,2,1,0:T(8,128)(2,1)S(1)} %collective-permute-done.16.prev0, s16[4,33,16,128]{3,2,1,0:T(8,128)(2,1)S(1)} %collective-permute-done.17.prev1, ...), custom_call_target="tpu_custom_call" | custom-call | tf_op jit(solution)/shard_map/pack/pallas_call | solution.py:364
  141.9 46.9 %all_to_all.5 = s16[128,80,128]{2,1,0:T(8,128)(2,1)S(1)} all-to-all(s16[128,80,128]{2,1,0:T(8,128)(2,1)S(1)} %pack.1), channel_id=1, replica_groups=mesh['x'=4,'core'=2,'z'=4,'y'=4] {'x','core','z','y'}, dimensions={0} | all-to-all | bytes 5242880 | tf_op jit(solution)/shard_map/all_to_all | solution.py:472
  188.8 7.1 %unpack.1 = f32[256,4096]{1,0:T(8,128)} custom-call(s16[4,2,16,80,128]{4,3,2,1,0:T(8,128)(2,1)S(1)} %bitcast.11), custom_call_target="tpu_custom_call" | custom-call | tf_op jit(solution)/shard_map/unpack/pallas_call | solution.py:401
  (56 shorter events, 7.1 us)
Async XLA Ops:
  0.0 5.3 %copy-start.3 = (s32[1,8,8]{2,1,0:T(8,128)S(1)}, s32[1,8,8]{2,1,0:T(8,128)}, u32[]{:S(2)}) copy-start(s32[1,8,8]{2,1,0:T(8,128)} %param.8) | copy-start | bytes 772
  0.0 5.5 %copy-start.4 = (s32[64,1,4]{0,2,1:T(4,128)S(1)}, s32[64,1,4]{0,2,1:T(4,128)}, u32[]{:S(2)}) copy-start(s32[64,1,4]{0,2,1:T(4,128)} %param.6) | copy-start | bytes 3076
  0.0 6.3 %copy-start.2 = (s32[128,1]{0,1:T(1,128)S(1)}, s32[128,1]{0,1:T(1,128)}, u32[]{:S(2)}) copy-start(s32[128,1]{0,1:T(1,128)} %param.9) | copy-start | bytes 1540
  3.8 11.1 %collective-permute-start.1 = (bf16[16,4,128,128]{3,2,1,0:T(8,128)(2,1)S(1)}, bf16[16,4,128,128]{3,2,1,0:T(8,128)(2,1)}, u32[]{:S(2)}, u32[]{:S(2)}) collective-permute-start(bf16[16,4,128,128]{3,2,1,0:T(8,128)(2,1)S(1)} %reshape.31.mine), channel_id=1, source_target_pairs={{0,16},{16,0},{1,17},{17,1},{2,18},{18,2},{3,19},{19,3},{4,20},{20... | collective-permute-start | bytes 6291464 | tf_op jit(solution)/shard_map/ppermute | solution.py:51
  12.2 1.8 collective-permute-start
  15.0 0.6 copy-start
  20.6 21.0 %collective-permute-start.4 = (bf16[3,4,4,128,128]{4,3,2,1,0:T(8,128)(2,1)S(1)}, bf16[3,4,4,128,128]{4,3,2,1,0:T(8,128)(2,1)S(1)}, u32[]{:S(2)}, u32[]{:S(2)}) collective-permute-start(bf16[3,4,4,128,128]{4,3,2,1,0:T(8,128)(2,1)S(1)} %get-tuple-element.38), channel_id=1, source_target_pairs={{0,4},{4,8},{8,12},{12,0},{1,5},{5,9},{9,13},{13,1},{2,6},{6,10},{... | collective-permute-start | bytes 4718600 | tf_op jit(solution)/shard_map/ppermute | solution.py:35
  22.0 19.6 %collective-permute-start.5 = (bf16[3,4,4,128,128]{4,3,2,1,0:T(8,128)(2,1)S(1)}, bf16[3,4,4,128,128]{4,3,2,1,0:T(8,128)(2,1)S(1)}, u32[]{:S(2)}, u32[]{:S(2)}) collective-permute-start(bf16[3,4,4,128,128]{4,3,2,1,0:T(8,128)(2,1)S(1)} %get-tuple-element.39), channel_id=1, source_target_pairs={{0,12},{4,0},{8,4},{12,8},{1,13},{5,1},{9,5},{13,9},{2,14},{6,2},{... | collective-permute-start | bytes 4718600 | tf_op jit(solution)/shard_map/ppermute | solution.py:35
  23.6 12.4 %collective-permute-start.3 = (bf16[2080,128]{1,0:T(8,128)(2,1)S(1)}, bf16[2080,128]{1,0:T(8,128)(2,1)S(1)}, u32[]{:S(2)}, u32[]{:S(2)}) collective-permute-start(bf16[2080,128]{1,0:T(8,128)(2,1)S(1)} %pad_maximum_fusion), channel_id=1, source_target_pairs={{0,96},{32,0},{64,32},{96,64},{1,97},{33,1},{65,33},{97,65},{2,98}... | collective-permute-start | bytes 1597448 | tf_op jit(solution)/shard_map/ppermute | solution.py:47
  26.0 13.1 %collective-permute-start.2 = (bf16[2080,128]{1,0:T(8,128)(2,1)S(1)}, bf16[2080,128]{1,0:T(8,128)(2,1)S(1)}, u32[]{:S(2)}, u32[]{:S(2)}) collective-permute-start(bf16[2080,128]{1,0:T(8,128)(2,1)S(1)} %pad_maximum_fusion), channel_id=1, source_target_pairs={{0,32},{32,64},{64,96},{96,0},{1,33},{33,65},{65,97},{97,1},{2,34}... | collective-permute-start | bytes 1597448 | tf_op jit(solution)/shard_map/ppermute | solution.py:47
  41.6 9.7 %collective-permute-start.7 = (bf16[1040,128]{1,0:T(8,128)(2,1)S(1)}, bf16[1040,128]{1,0:T(8,128)(2,1)S(1)}, u32[]{:S(2)}, u32[]{:S(2)}) collective-permute-start(bf16[1040,128]{1,0:T(8,128)(2,1)S(1)} %slice.23), channel_id=1, source_target_pairs={{0,96},{32,0},{64,32},{96,64},{1,97},{33,1},{65,33},{97,65},{2,98}... | collective-permute-start | bytes 798728 | tf_op jit(solution)/shard_map/ppermute | solution.py:47
  44.2 7.1 %collective-permute-start.6 = (bf16[1040,128]{1,0:T(8,128)(2,1)S(1)}, bf16[1040,128]{1,0:T(8,128)(2,1)S(1)}, u32[]{:S(2)}, u32[]{:S(2)}) collective-permute-start(bf16[1040,128]{1,0:T(8,128)(2,1)S(1)} %slice.22), channel_id=1, source_target_pairs={{0,32},{32,64},{64,96},{96,0},{1,33},{33,65},{65,97},{97,1},{2,34}... | collective-permute-start | bytes 798728 | tf_op jit(solution)/shard_map/ppermute | solution.py:47
  44.2 13.9 %copy-start.1 = (s32[4]{0:T(128)S(1)}, s32[4]{0:T(128)}, u32[]{:S(2)}) copy-start(s32[4]{0:T(128)} %pad_add_fusion.2.core.at.refs_0_) | copy-start | bytes 52
  44.3 8.9 %collective-permute-start.9 = (bf16[1,4,4,128,128]{4,3,2,1,0:T(8,128)(2,1)S(1)}, bf16[1,4,4,128,128]{4,3,2,1,0:T(8,128)(2,1)S(1)}, u32[]{:S(2)}, u32[]{:S(2)}) collective-permute-start(bf16[1,4,4,128,128]{4,3,2,1,0:T(8,128)(2,1)S(1)} %slice.25), channel_id=1, source_target_pairs={{0,12},{4,0},{8,4},{12,8},{1,13},{5,1},{9,5},{13,9},{2,14},{6,2},{... | collective-permute-start | bytes 1572872 | tf_op jit(solution)/shard_map/ppermute | solution.py:35
  47.1 9.5 %collective-permute-start.8 = (bf16[1,4,4,128,128]{4,3,2,1,0:T(8,128)(2,1)S(1)}, bf16[1,4,4,128,128]{4,3,2,1,0:T(8,128)(2,1)S(1)}, u32[]{:S(2)}, u32[]{:S(2)}) collective-permute-start(bf16[1,4,4,128,128]{4,3,2,1,0:T(8,128)(2,1)S(1)} %slice.24), channel_id=1, source_target_pairs={{0,4},{4,8},{8,12},{12,0},{1,5},{5,9},{9,13},{13,1},{2,6},{6,10},{... | collective-permute-start | bytes 1572872 | tf_op jit(solution)/shard_map/ppermute | solution.py:35
  56.6 25.5 %collective-permute-start.11 = (bf16[8320,128]{1,0:T(8,128)(2,1)S(1)}, bf16[8320,128]{1,0:T(8,128)(2,1)S(1)}, u32[]{:S(2)}, u32[]{:S(2)}) collective-permute-start(bf16[8320,128]{1,0:T(8,128)(2,1)S(1)} %constant_dynamic-update-slice_fusion.refs_3_), channel_id=1, source_target_pairs={{0,12},{4,0},{8,4},{12,8},{1,13},{5,1},{9,5},{13,9},{2,14},{6,2},{... | collective-permute-start | bytes 6389768 | tf_op jit(solution)/shard_map/ppermute | solution.py:35
  56.6 26.7 %collective-permute-start.10 = (bf16[8320,128]{1,0:T(8,128)(2,1)S(1)}, bf16[8320,128]{1,0:T(8,128)(2,1)S(1)}, u32[]{:S(2)}, u32[]{:S(2)}) collective-permute-start(bf16[8320,128]{1,0:T(8,128)(2,1)S(1)} %constant_dynamic-update-slice_fusion.refs_3_), channel_id=1, source_target_pairs={{0,4},{4,8},{8,12},{12,0},{1,5},{5,9},{9,13},{13,1},{2,6},{6,10},{... | collective-permute-start | bytes 6389768 | tf_op jit(solution)/shard_map/ppermute | solution.py:35
  83.5 18.7 %collective-permute-start.12 = (bf16[4160,128]{1,0:T(8,128)(2,1)S(1)}, bf16[4160,128]{1,0:T(8,128)(2,1)S(1)}, u32[]{:S(2)}, u32[]{:S(2)}) collective-permute-start(bf16[4160,128]{1,0:T(8,128)(2,1)S(1)} %slice.26), channel_id=1, source_target_pairs={{0,4},{4,8},{8,12},{12,0},{1,5},{5,9},{9,13},{13,1},{2,6},{6,10},{... | collective-permute-start | bytes 3194888 | tf_op jit(solution)/shard_map/ppermute | solution.py:35
  83.8 18.4 %collective-permute-start.13 = (bf16[4160,128]{1,0:T(8,128)(2,1)S(1)}, bf16[4160,128]{1,0:T(8,128)(2,1)S(1)}, u32[]{:S(2)}, u32[]{:S(2)}) collective-permute-start(bf16[4160,128]{1,0:T(8,128)(2,1)S(1)} %slice.27), channel_id=1, source_target_pairs={{0,12},{4,0},{8,4},{12,8},{1,13},{5,1},{9,5},{13,9},{2,14},{6,2},{... | collective-permute-start | bytes 3194888 | tf_op jit(solution)/shard_map/ppermute | solution.py:35
  108.3 12.4 %collective-permute-start.14 = (s16[4,33,16,128]{3,2,1,0:T(8,128)(2,1)}, s16[4,33,16,128]{3,2,1,0:T(8,128)(2,1)}, u32[]{:S(2)}, u32[]{:S(2)}) collective-permute-start(s16[4,33,16,128]{3,2,1,0:T(8,128)(2,1)} %get-tuple-element.51), channel_id=1, source_target_pairs={{0,1},{1,2},{2,3},{3,0},{4,5},{5,6},{6,7},{7,4},{8,9},{9,10},{10,1... | collective-permute-start | bytes 1622024 | tf_op jit(solution)/shard_map/ppermute | solution.py:35
  109.4 11.4 %collective-permute-start.15 = (s16[4,33,16,128]{3,2,1,0:T(8,128)(2,1)}, s16[4,33,16,128]{3,2,1,0:T(8,128)(2,1)}, u32[]{:S(2)}, u32[]{:S(2)}) collective-permute-start(s16[4,33,16,128]{3,2,1,0:T(8,128)(2,1)} %get-tuple-element.52), channel_id=1, source_target_pairs={{0,3},{1,0},{2,1},{3,2},{4,7},{5,4},{6,5},{7,6},{8,11},{9,8},{10,9... | collective-permute-start | bytes 1622024 | tf_op jit(solution)/shard_map/ppermute | solution.py:35
  118.0 15.6 %collective-permute-start.17 = (s16[4,33,16,128]{3,2,1,0:T(8,128)(2,1)S(1)}, s16[4,33,16,128]{3,2,1,0:T(8,128)(2,1)S(1)}, u32[]{:S(2)}, u32[]{:S(2)}) collective-permute-start(s16[4,33,16,128]{3,2,1,0:T(8,128)(2,1)S(1)} %get-tuple-element.54), channel_id=1, source_target_pairs={{0,1},{1,2},{2,3},{3,0},{4,5},{5,6},{6,7},{7,4},{8,9},{9,10},{10,1... | collective-permute-start | bytes 1622024 | tf_op jit(solution)/shard_map/ppermute | solution.py:35
  118.1 15.5 %collective-permute-start.18 = (s16[4,33,16,128]{3,2,1,0:T(8,128)(2,1)S(1)}, s16[4,33,16,128]{3,2,1,0:T(8,128)(2,1)S(1)}, u32[]{:S(2)}, u32[]{:S(2)}) collective-permute-start(s16[4,33,16,128]{3,2,1,0:T(8,128)(2,1)S(1)} %get-tuple-element.55), channel_id=1, source_target_pairs={{0,3},{1,0},{2,1},{3,2},{4,7},{5,4},{6,5},{7,6},{8,11},{9,8},{10,9... | collective-permute-start | bytes 1622024 | tf_op jit(solution)/shard_map/ppermute | solution.py:35
  126.3 9.8 %collective-permute-start.16 = (s16[4,33,16,128]{3,2,1,0:T(8,128)(2,1)S(1)}, s16[4,33,16,128]{3,2,1,0:T(8,128)(2,1)S(1)}, u32[]{:S(2)}, u32[]{:S(2)}) collective-permute-start(s16[4,33,16,128]{3,2,1,0:T(8,128)(2,1)S(1)} %get-tuple-element.53), channel_id=1, source_target_pairs={{0,1},{1,2},{2,3},{3,0},{4,5},{5,6},{6,7},{7,4},{8,9},{9,10},{10,1... | collective-permute-start | bytes 1622024 | tf_op jit(solution)/shard_map/ppermute | solution.py:35
  126.3 9.7 %collective-permute-start.19 = (s16[4,33,16,128]{3,2,1,0:T(8,128)(2,1)S(1)}, s16[4,33,16,128]{3,2,1,0:T(8,128)(2,1)S(1)}, u32[]{:S(2)}, u32[]{:S(2)}) collective-permute-start(s16[4,33,16,128]{3,2,1,0:T(8,128)(2,1)S(1)} %get-tuple-element.56), channel_id=1, source_target_pairs={{0,3},{1,0},{2,1},{3,2},{4,7},{5,4},{6,5},{7,6},{8,11},{9,8},{10,9... | collective-permute-start | bytes 1622024 | tf_op jit(solution)/shard_map/ppermute | solution.py:35

commit v7 on v6

--- a/solution.py
+++ b/solution.py
@@ -154,42 +154,32 @@
     return jnp.exp2(code.astype(jnp.int32).astype(jnp.float32) * (1.0 / 256.0)) * (1.0 / TOP)
 
 
-def panel_kernel(n, pieces, halves, form, at, *refs):
+def panel_kernel(n, pieces, halves, form, kcol, jcol, *refs):
+    whole = halves[0][0] is None
     kohn, refs = refs[:2 * n], refs[2 * n:]
     panels, refs = refs[:pieces], refs[pieces:]
     if form != "first":
-        sums_in, refs = refs[:2], refs[2:]
+        sums_in, refs = refs[0], refs[1:]
     if form == "sent":
         received, refs = refs[:2], refs[2:]
-    outs, (dens, sems, acc, staged, ints) = refs[:-5], refs[-5:]
+    outs, (dens, sems, acc) = refs[:-3], refs[-3:]
     size = n * 8 * PART // pieces
-    core, line, cross, x = at[0], at[1], at[2], at[3]
 
     @pl.when(pl.program_id(0) == 0)
     def _():
         copies = [
             pltpu.make_async_copy(panels[s], dens.at[pl.ds(s * size, size)], sems.at[s]) for s in range(pieces)
         ]
+        if not whole:
+            for h, (target, m) in enumerate(halves):
+                into = outs[0].at[0] if form == "own" else acc
+                copies.append(pltpu.make_async_copy(
+                    sums_in.at[target, pl.ds(m * 4, 4)], into.at[pl.ds(h * 4, 4)], sems.at[pieces + h]
+                ))
         for copy in copies:
             copy.start()
         for copy in copies:
             copy.wait()
-        for s in range(n):
-            rows = [dens[pl.ds((s * 8 + p) * PART + 8 * 128, 16), :].astype(jnp.float32) for p in range(8)]
-            rows = [row[2:3] for row in rows] + [rows[0][0:2], rows[1][0:2], jnp.zeros((4, 128), jnp.float32)]
-            staged[s * 16:(s + 1) * 16, :] = jnp.concatenate(rows, axis=0).astype(jnp.int32)
-        copy = pltpu.make_async_copy(staged, ints, sems.at[pieces])
-        copy.start()
-        copy.wait()
-
-    def place_of(target):
-        if target is None:
-            step = pl.program_id(0)
-            ahead = jnp.where(step < 2, ORDER[0] - step, ORDER[2] * (3 - step))
-        else:
-            ahead = ORDER[target]
-        goal = (cross + ahead) & 3
-        return jnp.where(core == 1, goal * 4 + line, line * 4 + goal)
 
     low = (lax.broadcasted_iota(jnp.int32, (32, 128), 1) < 64).astype(jnp.float32).astype(jnp.bfloat16)
     high = 1 - low
@@ -198,41 +188,41 @@
         turned = jnp.concatenate([blk[:, B:], blk[:, :B]], axis=1)
         return jnp.concatenate([blk * low, turned * low, turned * high, blk * high], axis=0)
 
-    def product(h, place, r, s, a):
-        k = ints[s * 16 + 8 + halves[h][1] * 2 + (place >> 3), (place & 7) * 16 + r * 4 + a]
-        slot = (120 >> (2 * (((k >> 4) - x) & 3))) & 3
-        k = slot * 16 + ((k & 15) ^ (8 * core))
-        part = s * 8 + (k >> 3)
-        left = dens[pl.ds(pl.multiple_of(part * PART + (k & 7) * 128, 16), 128), :]
+    def product(h, r, s, a):
+        target, m = halves[h]
+        step = pl.program_id(0) if whole else target
+        k = kcol[(((s * 4 + step) * 2 + m) * 4 + r) * SK + a]
+        at = s * 8 * PART + k * 128 + (k >> 3) * 16
+        left = dens[pl.ds(pl.multiple_of(at, 16), 128), :]
         right = twice(kohn[2 * s + h][0, 0, r, a * 32:(a + 1) * 32, :])
         r = lax.dot_general(left, right, (((1,), (1,)), ((), ())), preferred_element_type=jnp.float32)
-        return s * 16 + (k >> 3), (k & 7) * SP, r
-
-    def add(sums, word, first, r):
-        js = [ints[word, first + b] for b in range(SP)]
+        return s * 512 + k * SP, r
+
+    def add(sums, first, r):
+        js = [jcol[first + b] for b in range(SP)]
         old = [sums[j] for j in js]
         for b in range(SP):
             sums[js[b]] = old[b] + r[b * 16:(b + 1) * 16, :]
 
-    def two_rows(h, place, pair):
+    def two_rows(h, pair):
         work, sums = [], []
         for q in range(2):
             r = pair * 2 + q
             work += [(q, r, s, a) for s in range(n) for a in range(SK)]
-            total = acc.at[q] if form in ("coded", "sent") else outs[0].at[0, h * 4 + r]
+            total = acc.at[h * 4 + r] if form in ("coded", "sent") else outs[0].at[0, h * 4 + r]
             if form == "first":
                 total[...] = jnp.zeros((NCW, 16, 128), jnp.float32)
+            elif form == "more":
+                total[...] = sums_in[0, h * 4 + r]
             elif form == "sent":
                 scale = decoded_scale(received[h][r, NCW])
                 for j in range(NCW):
-                    total[j] = sums_in[h][0, r, j] + received[h][r, j].astype(jnp.int32).astype(jnp.float32) * scale
-            else:
-                total[...] = sums_in[h][0, r]
+                    total[j] = total[j] + received[h][r, j].astype(jnp.int32).astype(jnp.float32) * scale
             sums.append(total)
-        held = [product(h, place, *work[i][1:]) for i in range(3)]
+        held = [product(h, *work[i][1:]) for i in range(3)]
         for i in range(len(work)):
             if i + 3 < len(work):
-                held.append(product(h, place, *work[i + 3][1:]))
+                held.append(product(h, *work[i + 3][1:]))
             add(sums[work[i][0]], *held[i])
         if form in ("coded", "sent"):
             for q in range(2):
@@ -244,54 +234,49 @@
                 encode(sums[q], put, lambda code, put=put: put(NCW, code.astype(jnp.int16)))
 
     for h in range(2):
-        place = place_of(halves[h][0])
-        lax.fori_loop(0, 2, lambda pair, _, h=h, place=place: (two_rows(h, place, pair), 0)[1], 0)
-
-
-def panel_sums(name, form, at, kohn, panels, halves, sums=None, received=(), us=4.0):
+        lax.fori_loop(0, 2, lambda pair, _, h=h: (two_rows(h, pair), 0)[1], 0)
+
+
+def panel_sums(name, form, kcol, jcol, kohn, panels, halves, sums=None, received=(), us=3.0):
     n, pieces = len(kohn) // 2, len(panels)
-    steps = 4 if halves[0][0] is None else 1
+    whole = halves[0][0] is None
+    steps = 4 if whole else 1
 
     def at_target(h, lead):
         target = halves[h][0]
         return lambda o, *_: (lead, o if target is None else target, 0, 0, 0)
 
     k_specs = [pl.BlockSpec((1, 1, 4, 128, 128), at_target(i % 2, place)) for i, (_, place) in enumerate(kohn)]
-
-    def s_spec(h):
-        target, m = halves[h]
-        return pl.BlockSpec((1, 4, NCW, 16, 128), lambda o, *_: (o if target is None else target, m, 0, 0, 0))
-
+    any_spec = pl.BlockSpec(memory_space=pl.ANY)
+    s_spec = pl.BlockSpec((1, 8, NCW, 16, 128), lambda o, *_: (o, 0, 0, 0, 0))
     coded = pl.BlockSpec((4, NCW + 1, 16, 128), lambda o, *_: (0, 0, 0, 0))
     if form in ("coded", "sent"):
         o_specs = [coded] * 2
         shapes = [jax.ShapeDtypeStruct((4, NCW + 1, 16, 128), jnp.int16)] * 2
     else:
-        o_specs = [pl.BlockSpec((1, 8, NCW, 16, 128), lambda o, *_: (o, 0, 0, 0, 0))]
+        o_specs = [s_spec]
         shapes = [jax.ShapeDtypeStruct((steps, 8, NCW, 16, 128), jnp.float32)]
-    any_spec = pl.BlockSpec(memory_space=pl.ANY)
     return pl.pallas_call(
         lambda *refs: panel_kernel(n, pieces, halves, form, *refs),
         grid_spec=pltpu.PrefetchScalarGridSpec(
-            num_scalar_prefetch=1,
+            num_scalar_prefetch=2,
             grid=(steps,),
             in_specs=(
-                k_specs + [any_spec] * pieces + ([] if sums is None else [s_spec(0), s_spec(1)]) + [coded] * len(received)
+                k_specs + [any_spec] * pieces + ([] if sums is None else [s_spec if whole else any_spec])
+                + [coded] * len(received)
             ),
             out_specs=o_specs,
             scratch_shapes=[
                 pltpu.VMEM((n * 8 * PART, 128), jnp.bfloat16),
-                pltpu.SemaphoreType.DMA((pieces + 1,)),
-                pltpu.VMEM((2, NCW, 16, 128), jnp.float32),
-                pltpu.VMEM((n * 16, 128), jnp.int32),
-                pltpu.SMEM((n * 16, 128), jnp.int32),
+                pltpu.SemaphoreType.DMA((pieces + 2,)),
+                pltpu.VMEM((8 if form in ("coded", "sent") else 1, NCW, 16, 128), jnp.float32),
             ],
         ),
         out_shape=shapes,
         compiler_params=pltpu.CompilerParams(vmem_limit_bytes=44 << 20),
         cost_estimate=pl.CostEstimate(flops=int(us * 1.1e9), bytes_accessed=int(us * 2e6), transcendentals=0),
         name=name,
-    )(at, *[array for array, _ in kohn], *panels, *([] if sums is None else [sums, sums]), *received)
+    )(kcol, jcol, *[array for array, _ in kohn], *panels, *([] if sums is None else [sums]), *received)
 
 
 def pack_kernel(slots, own, prev0, prev1, next0, next1, o_ref, total, codes):
@@ -432,12 +417,32 @@
 
     kohn, ahead, back = regroup(at, kohn, kohn_other)
     kohn_prev, kohn_next = over_line(ahead, 1), over_line(back, -1)
-    left, right, kohn_prev, kohn_next = lax.optimization_barrier((left, right, kohn_prev, kohn_next))
     opposite0, opposite1 = over_line(kohn_prev[2:], 1), over_line(kohn_next[2:], -1)
 
-    panel = jnp.concatenate([shard, left, right, over_x(left[:PART], 1), over_x(right[PART:], -1)])
-    sent, opposite0, opposite1 = lax.optimization_barrier((panel, opposite0, opposite1))
+    far0, far1 = over_x(left[:PART], 1), over_x(right[PART:], -1)
+    panel = jnp.concatenate([shard, left, right, far0, far1])
+    sent, kohn_prev, kohn_next = lax.optimization_barrier((panel, kohn_prev, kohn_next))
     prev, after = over_line(sent, 1), over_line(sent, -1)
+
+    rows = panel.reshape(8, PART, 128)[:, 8 * 128:8 * 128 + 8].astype(jnp.int32)
+    words = jnp.concatenate([rows[:, 2, :64].reshape(4, 128), rows[:2, :2].reshape(4, 128)])
+
+    def indices(word):
+        targets = (on_cross + jnp.array(ORDER, jnp.int32)) % 4
+        places = jnp.where(c == 0, on_line * Y + targets, targets * Y + on_line)
+        k = word[4:].reshape(2, 16, 4, SK)[:, places].transpose(1, 0, 2, 3).reshape(-1)
+        away = ((k >> 4) - x) & 3
+        slot = jnp.where(away == 0, 0, jnp.where(away == 3, 1, away + 1))
+        return slot * 16 + ((k & 15) ^ (8 * c)), word[:4].reshape(-1)
+
+    def both(array):
+        return [(array, 0), (array, 1)]
+
+    everything = ((None, 0), (None, 1))
+    sums, = panel_sums("own_panel", "first", *indices(words), both(kohn), [panel], everything, us=9.0)
+    words, sums = lax.optimization_barrier((words, sums))
+    near = tuple(jnp.concatenate(pair) for pair in zip(indices(over_line(words, 1)), indices(over_line(words, -1))))
+    far = indices(over_line(words, 2))
 
     owners = jnp.stack([owner_map.reshape(128), shard[PART + 8 * 128 + 3].astype(jnp.int32)])
     hit = (owners[..., None] == jnp.arange(128, dtype=jnp.int32)).astype(jnp.int32)
@@ -445,20 +450,17 @@
     source = jnp.arange(2, dtype=jnp.int32)[:, None] ^ c
     slots = (owners * 4 + source * 2 + ranks).reshape(-1)
 
-    def both(array):
-        return [(array, 0), (array, 1)]
-
-    everything = ((None, 0), (None, 1))
-    sums, = panel_sums("own_panel", "first", at, both(kohn), [panel], everything, us=9.0)
-    prev, after, sums = lax.optimization_barrier((prev, after, sums))
+    prev, after, sums, near, far, opposite0, opposite1 = lax.optimization_barrier(
+        (prev, after, sums, near, far, opposite0, opposite1)
+    )
     far_low, far_high = over_line(prev[:4 * PART], 1), over_line(after[4 * PART:], -1)
     sums, = panel_sums(
-        "near_panels", "more", at, both(kohn_prev) + both(kohn_next), [prev, after], everything, sums, us=16.0
+        "near_panels", "more", *near, both(kohn_prev) + both(kohn_next), [prev, after], everything, sums, us=16.0
     )
 
     def last(form, halves, received=()):
         kohn = [((opposite0, opposite1)[m], 0) for _, m in halves]
-        return panel_sums("last_" + form, form, at, kohn, [far_low, far_high], halves, sums, received)
+        return panel_sums("last_" + form, form, *far, kohn, [far_low, far_high], halves, sums, received)
 
     via_next, via_prev = last("coded", ((0, 0), (0, 1)))
     via_next, via_prev = over_cross(via_next, 1), over_cross(via_prev, -1)
@@ -466,7 +468,7 @@
     prev_1, next_0 = over_cross(next1, 1), over_cross(prev0, -1)
     next0, prev1 = last("sent", ((1, 0), (2, 1)), (via_next, via_prev))
     prev_0, next_1 = over_cross(next0, 1), over_cross(prev1, -1)
-    own, = last("more", ((3, 0), (3, 1)))
+    own, = last("own", ((3, 0), (3, 1)))
 
     outgoing = pack(slots, own, prev_0, prev_1, next_0, next_1)
     received = lax.all_to_all(outgoing, ALL, split_axis=0, concat_axis=0, tiled=True)

time: 196 us -> 207 us (1.056)
  local copies, waits for them, and re-layouts: 5.31 us -> 22 us
  waiting for transfers between devices: 45.2 us -> 33.3 us
  starting transfers between devices: 26 us -> 31.5 us
  Pallas kernels: 69.4 us -> 67.1 us
    unnamed x15 -> x33, local copies, waits for them, and re-layouts: 0.95 us -> 9.2 us
    ppermute x4, waiting for transfers between devices: 17.1 us -> 9.26 us  [over_x(): return lax.ppermute(v, 'x', [(i, (i + step) % X) for i in range(X)])]
    ppermute x14 -> x17, starting transfers between devices: 19.4 us -> 23.8 us  [over(): lax.ppermute(v, PLANE, [(group[i], group[(i + step) % 4]) for group in gr...]
    ppermute x14 -> x17, waiting for transfers between devices: 26.4 us -> 22.3 us  [over(): lax.ppermute(v, PLANE, [(group[i], group[(i + step) % 4]) for group in gr...]
    pallas_call x6, Pallas kernels: 46.3 us -> 42.7 us  [panel_sums(): pl.pallas_call(lambda *refs: panel_kernel(n, pieces, halves, form, *refs)...]
    gather x0 -> x4, local copies, waits for them, and re-layouts: none -> 2.31 us  [indices(): word[4:].reshape(2, 16, 4, SK)[:, places].transpose(1, 0, 2, 3).reshape(-1)]
  transfers between devices with their start and end apart: 20 -> 23, of which waited for: 10 -> 8; matrix products, arithmetic and copies ran while one was open for 2% -> 6% of each run, Pallas kernels for 23% -> 24%
where the time goes in v7:
time: 207 us; the launch traced here: 206 us
  Pallas kernels  67.1 us (32%)
  blocking collectives  48.4 us (23%)
  waiting for transfers between devices  33.3 us (16%)
  starting transfers between devices  31.5 us (15%)
  local copies, waits for them, and re-layouts  22 us (11%)
  other arithmetic  3.59 us (2%)
    all_to_all x1, blocking collectives, local(): lax.all_to_all(outgoing, ALL, split_axis=0, concat_axis=0, tiled=True)  48.4 us
    pallas_call x6, Pallas kernels, panel_sums(): pl.pallas_call(lambda *refs: panel_kernel(n, pieces, halves, form, *refs)...  42.7 us
    ppermute x17, starting transfers between devices, over(): lax.ppermute(v, PLANE, [(group[i], group[(i + step) % 4]) for group in gr...  23.8 us
    ppermute x17, waiting for transfers between devices, over(): lax.ppermute(v, PLANE, [(group[i], group[(i + step) % 4]) for group in gr...  22.3 us
    ppermute x4, waiting for transfers between devices, over_x(): return lax.ppermute(v, 'x', [(i, (i + step) % X) for i in range(X)])  9.26 us
    unnamed x33, local copies, waits for them, and re-layouts  9.2 us
    pallas_call x1, Pallas kernels, unpack(): pl.pallas_call(unpack_kernel, grid=(X,), in_specs=[pl.BlockSpec((1, C, 16...  7.07 us
    pallas_call x1, Pallas kernels, regroup(): pl.pallas_call(regroup_kernel, grid_spec=pltpu.PrefetchScalarGridSpec(num...  6.22 us
  transfers between devices with their start and end apart: 23, of which 8 were waited for; matrix products, arithmetic and copies ran while one was open for 6% of the time, Pallas kernels for 24%

profile of v7, /device:TPU:1, one launch (start us, length us, event | category | flops | bytes accessed | tf_op | source)
XLA Modules:
  0.0 206.4 jit_solution(16937492460206677559)
XLA Ops:
  0.0 3.8 %reshape.123.mine = bf16[16,4,128,128]{3,2,1,0:T(8,128)(2,1)S(1)} reshape(bf16[64,1,4,4096]{3,2,1,0:T(4,128)(2,1)} %param.9) | data formatting | bytes 4194304 | tf_op jit(solution)/shard_map/reshape | solution.py:404
  7.0 5.2 %split.1 = (bf16[1040,128]{1,0:T(8,128)(2,1)}, bf16[1040,128]{1,0:T(8,128)(2,1)}) custom-call(s32[4]{0:T(128)} %pad_add_fusion.5.core.at, bf16[8,8,4096]{2,1,0:T(8,128)(2,1)} %bitcast.54, s32[16,128]{1,0:T(8,128)} %fusion.10.i_ref), custom_call_target="tpu_custom_call" | custom-call | tf_op jit(solution)/shard_map/split/pallas_call | solution.py:94
  12.2 1.7 collective-permute-done
  14.9 2.6 %collective-permute-start.3 = (bf16[2080,128]{1,0:T(8,128)(2,1)S(1)}, bf16[2080,128]{1,0:T(8,128)(2,1)S(1)}, u32[]{:S(2)}, u32[]{:S(2)}) collective-permute-start(bf16[2080,128]{1,0:T(8,128)(2,1)S(1)} %pad_maximum_fusion), channel_id=1, source_target_pairs={{0,96},{32,0},{64,32},{96,64},{1,97},{33,1},{65,33},{97,65},{2,98}... | collective-permute-start | bytes 1597448 | tf_op jit(solution)/shard_map/ppermute | solution.py:47
  18.2 6.2 %regroup.1 = (bf16[2,4,4,128,128]{4,3,2,1,0:T(8,128)(2,1)S(1)}, bf16[3,4,4,128,128]{4,3,2,1,0:T(8,128)(2,1)}, bf16[3,4,4,128,128]{4,3,2,1,0:T(8,128)(2,1)}) custom-call(s32[4]{0:T(128)S(1)} %copy-done.6, bf16[16,4,128,128]{3,2,1,0:T(8,128)(2,1)S(1)} %reshape.123.mine, bf16[16,4,128,128]{3,2,1,0:T(8,128)(2,1)} %collective-permute-done.1.other), custom_call_target="tpu_custom_call" | custom-call | tf_op jit(solution)/shard_map/regroup/pallas_call | solution.py:128
  27.4 1.6 collective-permute-done.3
  29.0 3.5 %collective-permute-start.5 = (bf16[1040,128]{1,0:T(8,128)(2,1)S(1)}, bf16[1040,128]{1,0:T(8,128)(2,1)S(1)}, u32[]{:S(2)}, u32[]{:S(2)}) collective-permute-start(bf16[1040,128]{1,0:T(8,128)(2,1)S(1)} %slice.73), channel_id=1, source_target_pairs={{0,96},{32,0},{64,32},{96,64},{1,97},{33,1},{65,33},{97,65},{2,98}... | collective-permute-start | bytes 798728 | tf_op jit(solution)/shard_map/ppermute | solution.py:47
  32.7 7.7 %collective-permute-done.4 = bf16[1040,128]{1,0:T(8,128)(2,1)S(1)} collective-permute-done((bf16[1040,128]{1,0:T(8,128)(2,1)S(1)}, bf16[1040,128]{1,0:T(8,128)(2,1)S(1)}, u32[]{:S(2)}, u32[]{:S(2)}) %collective-permute-start.4) | collective-permute-done | bytes 266272 | tf_op jit(solution)/shard_map/ppermute | solution.py:47
  42.9 2.7 %collective-permute-done.6.refs_2_.refs_3_ = bf16[3,4,4,128,128]{4,3,2,1,0:T(8,128)(2,1)S(1)} collective-permute-done((bf16[3,4,4,128,128]{4,3,2,1,0:T(8,128)(2,1)}, bf16[3,4,4,128,128]{4,3,2,1,0:T(8,128)(2,1)S(1)}, u32[]{:S(2)}, u32[]{:S(2)}) %collective-permute-start.6) | collective-permute-done | bytes 1572896 | tf_op jit(solution)/shard_map/ppermute | solution.py:35
  46.7 1.6 collective-permute-start.9
  48.3 1.7 copy-done.5
  51.2 8.3 %own_panel.1.refs_8_ = f32[4,8,32,16,128]{4,3,2,1,0:T(8,128)} custom-call(s32[128]{0:T(128)S(1)} %reshape.159.refs_0_, s32[512]{0:T(512)S(1)} %reshape_reshape_squeeze.3.refs_1_, bf16[2,4,4,128,128]{4,3,2,1,0:T(8,128)(2,1)S(1)} %copy-done.8, bf16[2,4,4,128,128]{4,3,2,1,0:T(8,128)(2,1)S(1)} %copy-done.8, bf16[8320,128]{1,0:T(8,128)(2,1)S(1)} %copy-done.5), custom_call_target="tpu_custom_call" | custom-call | flops 9900000256 | bytes 18000000 | tf_op jit(solution)/shard_map/own_panel/pallas_call | solution.py:259
  60.3 3.7 %collective-permute-start.12 = (s32[8,128]{1,0:T(8,128)S(1)}, s32[8,128]{1,0:T(8,128)S(1)}, u32[]{:S(2)}, u32[]{:S(2)}) collective-permute-start(s32[8,128]{1,0:T(8,128)S(1)} %pad_add_fusion.1), channel_id=1, source_target_pairs={{0,8},{4,12},{8,0},{12,4},{1,9},{5,13},{9,1},{13,5},{2,10},{6,14},... | collective-permute-start | bytes 12296 | tf_op jit(solution)/shard_map/ppermute | solution.py:35
  64.1 11.4 %collective-permute-done.10 = s32[8,128]{1,0:T(8,128)S(1)} collective-permute-done((s32[8,128]{1,0:T(8,128)S(1)}, s32[8,128]{1,0:T(8,128)S(1)}, u32[]{:S(2)}, u32[]{:S(2)}) %collective-permute-start.10) | collective-permute-done | bytes 4128 | tf_op jit(solution)/shard_map/ppermute | solution.py:35
  76.9 1.9 slice.77
  78.9 1.9 slice.78
  80.8 2.7 %collective-permute-start.14 = (bf16[1,4,4,128,128]{4,3,2,1,0:T(8,128)(2,1)}, bf16[1,4,4,128,128]{4,3,2,1,0:T(8,128)(2,1)S(1)}, u32[]{:S(2)}, u32[]{:S(2)}) collective-permute-start(bf16[1,4,4,128,128]{4,3,2,1,0:T(8,128)(2,1)} %slice.78), channel_id=1, source_target_pairs={{0,12},{4,0},{8,4},{12,8},{1,13},{5,1},{9,5},{13,9},{2,14},{6,2},{... | collective-permute-start | bytes 1572872 | tf_op jit(solution)/shard_map/ppermute | solution.py:35
  84.6 4.1 %collective-permute-done.13.refs_2_.refs_3_ = bf16[1,4,4,128,128]{4,3,2,1,0:T(8,128)(2,1)S(1)} collective-permute-done((bf16[1,4,4,128,128]{4,3,2,1,0:T(8,128)(2,1)}, bf16[1,4,4,128,128]{4,3,2,1,0:T(8,128)(2,1)S(1)}, u32[]{:S(2)}, u32[]{:S(2)}) %collective-permute-start.13) | collective-permute-done | bytes 524320 | tf_op jit(solution)/shard_map/ppermute | solution.py:35
  92.7 3.4 %collective-permute-start.16 = (bf16[4160,128]{1,0:T(8,128)(2,1)S(1)}, bf16[4160,128]{1,0:T(8,128)(2,1)S(1)}, u32[]{:S(2)}, u32[]{:S(2)}) collective-permute-start(bf16[4160,128]{1,0:T(8,128)(2,1)S(1)} %slice.63), channel_id=1, source_target_pairs={{0,12},{4,0},{8,4},{12,8},{1,13},{5,1},{9,5},{13,9},{2,14},{6,2},{... | collective-permute-start | bytes 3194888 | tf_op jit(solution)/shard_map/ppermute | solution.py:35
  96.0 1.6 copy-done.1
  97.6 14.8 %near_panels.1.refs_6_ = f32[4,8,32,16,128]{4,3,2,1,0:T(8,128)} custom-call(s32[256]{0:T(256)S(1)} %pad_add_fusion.4.refs_0_, s32[1024]{0:T(1024)S(1)} %pad_add_fusion.2.refs_1_, bf16[3,4,4,128,128]{4,3,2,1,0:T(8,128)(2,1)S(1)} %copy-done.3, bf16[3,4,4,128,128]{4,3,2,1,0:T(8,128)(2,1)S(1)} %copy-done.3, ...), custom_call_target="tpu_custom_call" | custom-call | flops 17600000000 | bytes 32000000 | tf_op jit(solution)/shard_map/near_panels/pallas_call | solution.py:259
  112.5 5.5 %last_coded.2 = (s16[4,33,16,128]{3,2,1,0:T(8,128)(2,1)}, s16[4,33,16,128]{3,2,1,0:T(8,128)(2,1)}) custom-call(s32[128]{0:T(128)S(1)} %reshape.162.refs_0_, s32[512]{0:T(512)S(1)} %get-tuple-element.49.refs_1_, bf16[1,4,4,128,128]{4,3,2,1,0:T(8,128)(2,1)S(1)} %collective-permute-done.13.refs_2_.refs_3_, ...), custom_call_target="tpu_custom_call" | custom-call | flops 3300000000 | bytes 6000000 | tf_op jit(solution)/shard_map/last_coded/pallas_call | solution.py:259
  119.1 2.8 %collective-permute-start.18 = (s16[4,33,16,128]{3,2,1,0:T(8,128)(2,1)}, s16[4,33,16,128]{3,2,1,0:T(8,128)(2,1)}, u32[]{:S(2)}, u32[]{:S(2)}) collective-permute-start(s16[4,33,16,128]{3,2,1,0:T(8,128)(2,1)} %get-tuple-element.60), channel_id=1, source_target_pairs={{0,3},{1,0},{2,1},{3,2},{4,7},{5,4},{6,5},{7,6},{8,11},{9,8},{10,9... | collective-permute-start | bytes 1622024 | tf_op jit(solution)/shard_map/ppermute | solution.py:35
  122.2 4.5 %last_coded.3 = (s16[4,33,16,128]{3,2,1,0:T(8,128)(2,1)S(1)}, s16[4,33,16,128]{3,2,1,0:T(8,128)(2,1)S(1)}) custom-call(s32[128]{0:T(128)S(1)} %reshape.162.refs_0_, s32[512]{0:T(512)S(1)} %get-tuple-element.49.refs_1_, bf16[1,4,4,128,128]{4,3,2,1,0:T(8,128)(2,1)S(1)} %collective-permute-done.14.refs_3_.refs_2_, ...), custom_call_target="tpu_custom_call" | custom-call | flops 3300000000 | bytes 6000000 | tf_op jit(solution)/shard_map/last_coded/pallas_call | solution.py:259
  126.8 2.7 %collective-permute-start.21 = (s16[4,33,16,128]{3,2,1,0:T(8,128)(2,1)S(1)}, s16[4,33,16,128]{3,2,1,0:T(8,128)(2,1)S(1)}, u32[]{:S(2)}, u32[]{:S(2)}) collective-permute-start(s16[4,33,16,128]{3,2,1,0:T(8,128)(2,1)S(1)} %get-tuple-element.63), channel_id=1, source_target_pairs={{0,3},{1,0},{2,1},{3,2},{4,7},{5,4},{6,5},{7,6},{8,11},{9,8},{10,9... | collective-permute-start | bytes 1622024 | tf_op jit(solution)/shard_map/ppermute | solution.py:35
  129.4 5.8 %last_sent.1 = (s16[4,33,16,128]{3,2,1,0:T(8,128)(2,1)S(1)}, s16[4,33,16,128]{3,2,1,0:T(8,128)(2,1)S(1)}) custom-call(s32[128]{0:T(128)S(1)} %reshape.162.refs_0_, s32[512]{0:T(512)S(1)} %get-tuple-element.49.refs_1_, bf16[1,4,4,128,128]{4,3,2,1,0:T(8,128)(2,1)S(1)} %collective-permute-done.13.refs_2_.refs_3_, ...), custom_call_target="tpu_custom_call" | custom-call | flops 3300000000 | bytes 6000000 | tf_op jit(solution)/shard_map/last_sent/pallas_call | solution.py:259
  135.6 2.3 %collective-permute-start.22 = (s16[4,33,16,128]{3,2,1,0:T(8,128)(2,1)S(1)}, s16[4,33,16,128]{3,2,1,0:T(8,128)(2,1)S(1)}, u32[]{:S(2)}, u32[]{:S(2)}) collective-permute-start(s16[4,33,16,128]{3,2,1,0:T(8,128)(2,1)S(1)} %get-tuple-element.64), channel_id=1, source_target_pairs={{0,3},{1,0},{2,1},{3,2},{4,7},{5,4},{6,5},{7,6},{8,11},{9,8},{10,9... | collective-permute-start | bytes 1622024 | tf_op jit(solution)/shard_map/ppermute | solution.py:35
  138.2 3.8 %last_own.1.own = f32[1,8,32,16,128]{4,3,2,1,0:T(8,128)S(1)} custom-call(s32[128]{0:T(128)S(1)} %reshape.162.refs_0_, s32[512]{0:T(512)S(1)} %get-tuple-element.49.refs_1_, bf16[1,4,4,128,128]{4,3,2,1,0:T(8,128)(2,1)S(1)} %collective-permute-done.13.refs_2_.refs_3_, bf16[1,4,4,128,128]{4,3,2,1,0:T(8,128)(2,1)S(1)} %collective-permute-done.14.refs_3_.refs_2_, ...), custom_call_target="tpu_custom_call" | custom-call | flops 3300000000 | bytes 6000000 | tf_op jit(solution)/shard_map/last_own/pallas_call | solution.py:259
  142.1 2.9 %collective-permute-done.19.prev0 = s16[4,33,16,128]{3,2,1,0:T(8,128)(2,1)S(1)} collective-permute-done((s16[4,33,16,128]{3,2,1,0:T(8,128)(2,1)S(1)}, s16[4,33,16,128]{3,2,1,0:T(8,128)(2,1)S(1)}, u32[]{:S(2)}, u32[]{:S(2)}) %collective-permute-start.19) | collective-permute-done | bytes 540704 | tf_op jit(solution)/shard_map/ppermute | solution.py:35
  145.0 5.9 %pack.1 = s16[128,80,128]{2,1,0:T(8,128)(2,1)S(1)} custom-call(s32[256]{0:T(256)S(1)} %add_bitcast_fusion.slots, f32[1,8,32,16,128]{4,3,2,1,0:T(8,128)S(1)} %last_own.1.own, s16[4,33,16,128]{3,2,1,0:T(8,128)(2,1)S(1)} %collective-permute-done.19.prev0, s16[4,33,16,128]{3,2,1,0:T(8,128)(2,1)S(1)} %collective-permute-done.20.prev1, ...), custom_call_target="tpu_custom_call" | custom-call | tf_op jit(solution)/shard_map/pack/pallas_call | solution.py:349
  150.9 48.4 %all_to_all.5 = s16[128,80,128]{2,1,0:T(8,128)(2,1)S(1)} all-to-all(s16[128,80,128]{2,1,0:T(8,128)(2,1)S(1)} %pack.1), channel_id=1, replica_groups=mesh['x'=4,'core'=2,'z'=4,'y'=4] {'x','core','z','y'}, dimensions={0} | all-to-all | bytes 5242880 | tf_op jit(solution)/shard_map/all_to_all | solution.py:474
  199.3 7.1 %unpack.1 = f32[256,4096]{1,0:T(8,128)} custom-call(s16[4,2,16,80,128]{4,3,2,1,0:T(8,128)(2,1)S(1)} %bitcast.52), custom_call_target="tpu_custom_call" | custom-call | tf_op jit(solution)/shard_map/unpack/pallas_call | solution.py:386
  (108 shorter events, 22.3 us)
Async XLA Ops:
  0.0 12.2 %copy-start.13 = (s32[4]{0:T(128)S(1)}, s32[4]{0:T(128)}, u32[]{:S(2)}) copy-start(s32[4]{0:T(128)} %constant.76.clone) | copy-start | bytes 52
  0.0 5.3 %copy-start.11 = (s32[1,8,8]{2,1,0:T(8,128)S(1)}, s32[1,8,8]{2,1,0:T(8,128)}, u32[]{:S(2)}) copy-start(s32[1,8,8]{2,1,0:T(8,128)} %param.12) | copy-start | bytes 772
  0.0 5.5 %copy-start.12 = (s32[64,1,4]{0,2,1:T(4,128)S(1)}, s32[64,1,4]{0,2,1:T(4,128)}, u32[]{:S(2)}) copy-start(s32[64,1,4]{0,2,1:T(4,128)} %param.10) | copy-start | bytes 3076
  0.0 6.3 %copy-start.10 = (s32[128,1]{0,1:T(1,128)S(1)}, s32[128,1]{0,1:T(1,128)}, u32[]{:S(2)}) copy-start(s32[128,1]{0,1:T(1,128)} %param.13) | copy-start | bytes 1540
  3.8 11.1 %collective-permute-start.1 = (bf16[16,4,128,128]{3,2,1,0:T(8,128)(2,1)S(1)}, bf16[16,4,128,128]{3,2,1,0:T(8,128)(2,1)}, u32[]{:S(2)}, u32[]{:S(2)}) collective-permute-start(bf16[16,4,128,128]{3,2,1,0:T(8,128)(2,1)S(1)} %reshape.123.mine), channel_id=1, source_target_pairs={{0,16},{16,0},{1,17},{17,1},{2,18},{18,2},{3,19},{19,3},{4,20},{20... | collective-permute-start | bytes 6291464 | tf_op jit(solution)/shard_map/ppermute | solution.py:51
  12.2 1.8 collective-permute-start
  14.9 12.4 %copy-start.9 = (bf16[2080,128]{1,0:T(8,128)(2,1)}, bf16[2080,128]{1,0:T(8,128)(2,1)S(1)}, u32[]{:S(2)}) copy-start(bf16[2080,128]{1,0:T(8,128)(2,1)S(1)} %pad_maximum_fusion) | copy-start | bytes 1597444
  14.9 14.0 %collective-permute-start.3 = (bf16[2080,128]{1,0:T(8,128)(2,1)S(1)}, bf16[2080,128]{1,0:T(8,128)(2,1)S(1)}, u32[]{:S(2)}, u32[]{:S(2)}) collective-permute-start(bf16[2080,128]{1,0:T(8,128)(2,1)S(1)} %pad_maximum_fusion), channel_id=1, source_target_pairs={{0,96},{32,0},{64,32},{96,64},{1,97},{33,1},{65,33},{97,65},{2,98}... | collective-permute-start | bytes 1597448 | tf_op jit(solution)/shard_map/ppermute | solution.py:47
  17.6 14.9 %collective-permute-start.2 = (bf16[2080,128]{1,0:T(8,128)(2,1)S(1)}, bf16[2080,128]{1,0:T(8,128)(2,1)S(1)}, u32[]{:S(2)}, u32[]{:S(2)}) collective-permute-start(bf16[2080,128]{1,0:T(8,128)(2,1)S(1)} %pad_maximum_fusion), channel_id=1, source_target_pairs={{0,32},{32,64},{64,96},{96,0},{1,33},{33,65},{65,97},{97,1},{2,34}... | collective-permute-start | bytes 1597448 | tf_op jit(solution)/shard_map/ppermute | solution.py:47
  24.4 8.3 %copy-start.7 = (bf16[2,4,4,128,128]{4,3,2,1,0:T(8,128)(2,1)}, bf16[2,4,4,128,128]{4,3,2,1,0:T(8,128)(2,1)S(1)}, u32[]{:S(2)}) copy-start(bf16[2,4,4,128,128]{4,3,2,1,0:T(8,128)(2,1)S(1)} %get-tuple-element.45.refs_2_.refs_3_) | copy-start | bytes 3145732
  24.4 21.1 %collective-permute-start.6 = (bf16[3,4,4,128,128]{4,3,2,1,0:T(8,128)(2,1)}, bf16[3,4,4,128,128]{4,3,2,1,0:T(8,128)(2,1)S(1)}, u32[]{:S(2)}, u32[]{:S(2)}) collective-permute-start(bf16[3,4,4,128,128]{4,3,2,1,0:T(8,128)(2,1)} %get-tuple-element.42), channel_id=1, source_target_pairs={{0,4},{4,8},{8,12},{12,0},{1,5},{5,9},{9,13},{13,1},{2,6},{6,10},{... | collective-permute-start | bytes 4718600 | tf_op jit(solution)/shard_map/ppermute | solution.py:35
  25.8 20.9 %collective-permute-start.7 = (bf16[3,4,4,128,128]{4,3,2,1,0:T(8,128)(2,1)}, bf16[3,4,4,128,128]{4,3,2,1,0:T(8,128)(2,1)}, u32[]{:S(2)}, u32[]{:S(2)}) collective-permute-start(bf16[3,4,4,128,128]{4,3,2,1,0:T(8,128)(2,1)} %get-tuple-element.43), channel_id=1, source_target_pairs={{0,12},{4,0},{8,4},{12,8},{1,13},{5,1},{9,5},{13,9},{2,14},{6,2},{... | collective-permute-start | bytes 4718600 | tf_op jit(solution)/shard_map/ppermute | solution.py:35
  29.0 11.5 %collective-permute-start.5 = (bf16[1040,128]{1,0:T(8,128)(2,1)S(1)}, bf16[1040,128]{1,0:T(8,128)(2,1)S(1)}, u32[]{:S(2)}, u32[]{:S(2)}) collective-permute-start(bf16[1040,128]{1,0:T(8,128)(2,1)S(1)} %slice.73), channel_id=1, source_target_pairs={{0,96},{32,0},{64,32},{96,64},{1,97},{33,1},{65,33},{97,65},{2,98}... | collective-permute-start | bytes 798728 | tf_op jit(solution)/shard_map/ppermute | solution.py:47
  32.5 7.9 %collective-permute-start.4 = (bf16[1040,128]{1,0:T(8,128)(2,1)S(1)}, bf16[1040,128]{1,0:T(8,128)(2,1)S(1)}, u32[]{:S(2)}, u32[]{:S(2)}) collective-permute-start(bf16[1040,128]{1,0:T(8,128)(2,1)S(1)} %slice.72), channel_id=1, source_target_pairs={{0,32},{32,64},{64,96},{96,0},{1,33},{33,65},{65,97},{97,1},{2,34}... | collective-permute-start | bytes 798728 | tf_op jit(solution)/shard_map/ppermute | solution.py:47
  46.7 43.2 %collective-permute-start.9 = (bf16[8320,128]{1,0:T(8,128)(2,1)}, bf16[8320,128]{1,0:T(8,128)(2,1)S(1)}, u32[]{:S(2)}, u32[]{:S(2)}) collective-permute-start(bf16[8320,128]{1,0:T(8,128)(2,1)} %copy-done.4), channel_id=1, source_target_pairs={{0,12},{4,0},{8,4},{12,8},{1,13},{5,1},{9,5},{13,9},{2,14},{6,2},{... | collective-permute-start | bytes 6389768 | tf_op jit(solution)/shard_map/ppermute | solution.py:35
  48.3 41.6 %collective-permute-start.8 = (bf16[8320,128]{1,0:T(8,128)(2,1)}, bf16[8320,128]{1,0:T(8,128)(2,1)}, u32[]{:S(2)}, u32[]{:S(2)}) collective-permute-start(bf16[8320,128]{1,0:T(8,128)(2,1)} %copy-done.4), channel_id=1, source_target_pairs={{0,4},{4,8},{8,12},{12,0},{1,5},{5,9},{9,13},{13,1},{2,6},{6,10},{... | collective-permute-start | bytes 6389768 | tf_op jit(solution)/shard_map/ppermute | solution.py:35
  48.3 1.7 copy-start.5
  59.5 16.0 %collective-permute-start.10 = (s32[8,128]{1,0:T(8,128)S(1)}, s32[8,128]{1,0:T(8,128)S(1)}, u32[]{:S(2)}, u32[]{:S(2)}) collective-permute-start(s32[8,128]{1,0:T(8,128)S(1)} %pad_add_fusion.1), channel_id=1, source_target_pairs={{0,4},{4,8},{8,12},{12,0},{1,5},{5,9},{9,13},{13,1},{2,6},{6,10},{... | collective-permute-start | bytes 12296 | tf_op jit(solution)/shard_map/ppermute | solution.py:35
  60.3 23.1 %collective-permute-start.12 = (s32[8,128]{1,0:T(8,128)S(1)}, s32[8,128]{1,0:T(8,128)S(1)}, u32[]{:S(2)}, u32[]{:S(2)}) collective-permute-start(s32[8,128]{1,0:T(8,128)S(1)} %pad_add_fusion.1), channel_id=1, source_target_pairs={{0,8},{4,12},{8,0},{12,4},{1,9},{5,13},{9,1},{13,5},{2,10},{6,14},... | collective-permute-start | bytes 12296 | tf_op jit(solution)/shard_map/ppermute | solution.py:35
  64.1 12.1 %collective-permute-start.11 = (s32[8,128]{1,0:T(8,128)S(1)}, s32[8,128]{1,0:T(8,128)S(1)}, u32[]{:S(2)}, u32[]{:S(2)}) collective-permute-start(s32[8,128]{1,0:T(8,128)S(1)} %pad_add_fusion.1), channel_id=1, source_target_pairs={{0,12},{4,0},{8,4},{12,8},{1,13},{5,1},{9,5},{13,9},{2,14},{6,2},{... | collective-permute-start | bytes 12296 | tf_op jit(solution)/shard_map/ppermute | solution.py:35
  78.9 9.7 %collective-permute-start.13 = (bf16[1,4,4,128,128]{4,3,2,1,0:T(8,128)(2,1)}, bf16[1,4,4,128,128]{4,3,2,1,0:T(8,128)(2,1)S(1)}, u32[]{:S(2)}, u32[]{:S(2)}) collective-permute-start(bf16[1,4,4,128,128]{4,3,2,1,0:T(8,128)(2,1)} %slice.77), channel_id=1, source_target_pairs={{0,4},{4,8},{8,12},{12,0},{1,5},{5,9},{9,13},{13,1},{2,6},{6,10},{... | collective-permute-start | bytes 1572872 | tf_op jit(solution)/shard_map/ppermute | solution.py:35
  80.8 9.1 %collective-permute-start.14 = (bf16[1,4,4,128,128]{4,3,2,1,0:T(8,128)(2,1)}, bf16[1,4,4,128,128]{4,3,2,1,0:T(8,128)(2,1)S(1)}, u32[]{:S(2)}, u32[]{:S(2)}) collective-permute-start(bf16[1,4,4,128,128]{4,3,2,1,0:T(8,128)(2,1)} %slice.78), channel_id=1, source_target_pairs={{0,12},{4,0},{8,4},{12,8},{1,13},{5,1},{9,5},{13,9},{2,14},{6,2},{... | collective-permute-start | bytes 1572872 | tf_op jit(solution)/shard_map/ppermute | solution.py:35
  89.9 6.1 %copy-start.3 = (bf16[3,4,4,128,128]{4,3,2,1,0:T(8,128)(2,1)S(1)}, bf16[3,4,4,128,128]{4,3,2,1,0:T(8,128)(2,1)}, u32[]{:S(2)}) copy-start(bf16[3,4,4,128,128]{4,3,2,1,0:T(8,128)(2,1)} %copy-done.2) | copy-start | bytes 4718596
  92.6 19.9 %collective-permute-start.15 = (bf16[4160,128]{1,0:T(8,128)(2,1)S(1)}, bf16[4160,128]{1,0:T(8,128)(2,1)S(1)}, u32[]{:S(2)}, u32[]{:S(2)}) collective-permute-start(bf16[4160,128]{1,0:T(8,128)(2,1)S(1)} %slice.62), channel_id=1, source_target_pairs={{0,4},{4,8},{8,12},{12,0},{1,5},{5,9},{9,13},{13,1},{2,6},{6,10},{... | collective-permute-start | bytes 3194888 | tf_op jit(solution)/shard_map/ppermute | solution.py:35
  92.7 19.8 %collective-permute-start.16 = (bf16[4160,128]{1,0:T(8,128)(2,1)S(1)}, bf16[4160,128]{1,0:T(8,128)(2,1)S(1)}, u32[]{:S(2)}, u32[]{:S(2)}) collective-permute-start(bf16[4160,128]{1,0:T(8,128)(2,1)S(1)} %slice.63), channel_id=1, source_target_pairs={{0,12},{4,0},{8,4},{12,8},{1,13},{5,1},{9,5},{13,9},{2,14},{6,2},{... | collective-permute-start | bytes 3194888 | tf_op jit(solution)/shard_map/ppermute | solution.py:35
  96.0 1.6 copy-start.1
  118.0 11.4 %collective-permute-start.17 = (s16[4,33,16,128]{3,2,1,0:T(8,128)(2,1)}, s16[4,33,16,128]{3,2,1,0:T(8,128)(2,1)}, u32[]{:S(2)}, u32[]{:S(2)}) collective-permute-start(s16[4,33,16,128]{3,2,1,0:T(8,128)(2,1)} %get-tuple-element.59), channel_id=1, source_target_pairs={{0,1},{1,2},{2,3},{3,0},{4,5},{5,6},{6,7},{7,4},{8,9},{9,10},{10,1... | collective-permute-start | bytes 1622024 | tf_op jit(solution)/shard_map/ppermute | solution.py:35
  119.1 10.4 %collective-permute-start.18 = (s16[4,33,16,128]{3,2,1,0:T(8,128)(2,1)}, s16[4,33,16,128]{3,2,1,0:T(8,128)(2,1)}, u32[]{:S(2)}, u32[]{:S(2)}) collective-permute-start(s16[4,33,16,128]{3,2,1,0:T(8,128)(2,1)} %get-tuple-element.60), channel_id=1, source_target_pairs={{0,3},{1,0},{2,1},{3,2},{4,7},{5,4},{6,5},{7,6},{8,11},{9,8},{10,9... | collective-permute-start | bytes 1622024 | tf_op jit(solution)/shard_map/ppermute | solution.py:35
  126.7 15.4 %collective-permute-start.20 = (s16[4,33,16,128]{3,2,1,0:T(8,128)(2,1)S(1)}, s16[4,33,16,128]{3,2,1,0:T(8,128)(2,1)S(1)}, u32[]{:S(2)}, u32[]{:S(2)}) collective-permute-start(s16[4,33,16,128]{3,2,1,0:T(8,128)(2,1)S(1)} %get-tuple-element.62), channel_id=1, source_target_pairs={{0,1},{1,2},{2,3},{3,0},{4,5},{5,6},{6,7},{7,4},{8,9},{9,10},{10,1... | collective-permute-start | bytes 1622024 | tf_op jit(solution)/shard_map/ppermute | solution.py:35
  126.8 15.3 %collective-permute-start.21 = (s16[4,33,16,128]{3,2,1,0:T(8,128)(2,1)S(1)}, s16[4,33,16,128]{3,2,1,0:T(8,128)(2,1)S(1)}, u32[]{:S(2)}, u32[]{:S(2)}) collective-permute-start(s16[4,33,16,128]{3,2,1,0:T(8,128)(2,1)S(1)} %get-tuple-element.63), channel_id=1, source_target_pairs={{0,3},{1,0},{2,1},{3,2},{4,7},{5,4},{6,5},{7,6},{8,11},{9,8},{10,9... | collective-permute-start | bytes 1622024 | tf_op jit(solution)/shard_map/ppermute | solution.py:35
  135.2 9.8 %collective-permute-start.19 = (s16[4,33,16,128]{3,2,1,0:T(8,128)(2,1)S(1)}, s16[4,33,16,128]{3,2,1,0:T(8,128)(2,1)S(1)}, u32[]{:S(2)}, u32[]{:S(2)}) collective-permute-start(s16[4,33,16,128]{3,2,1,0:T(8,128)(2,1)S(1)} %get-tuple-element.61), channel_id=1, source_target_pairs={{0,1},{1,2},{2,3},{3,0},{4,5},{5,6},{6,7},{7,4},{8,9},{9,10},{10,1... | collective-permute-start | bytes 1622024 | tf_op jit(solution)/shard_map/ppermute | solution.py:35
  135.6 9.4 %collective-permute-start.22 = (s16[4,33,16,128]{3,2,1,0:T(8,128)(2,1)S(1)}, s16[4,33,16,128]{3,2,1,0:T(8,128)(2,1)S(1)}, u32[]{:S(2)}, u32[]{:S(2)}) collective-permute-start(s16[4,33,16,128]{3,2,1,0:T(8,128)(2,1)S(1)} %get-tuple-element.64), channel_id=1, source_target_pairs={{0,3},{1,0},{2,1},{3,2},{4,7},{5,4},{6,5},{7,6},{8,11},{9,8},{10,9... | collective-permute-start | bytes 1622024 | tf_op jit(solution)/shard_map/ppermute | solution.py:35
  (5 other events, 5.7 us)

commit v8 on v6

--- a/solution.py
+++ b/solution.py
@@ -15,6 +15,7 @@
 PLANE = ("core", "z", "y")
 TOP = 32766.0
 MSG = 80
+LIMIT = 16
 PART = 8 * 128 + 16
 ORDER = (2, 1, 3, 0)
 
@@ -106,7 +107,7 @@
     )(core, dens, ints)
 
 
-def regroup_kernel(at, mine, other, own, ahead, back, sems):
+def regroup_kernel(at, mine, other, own, ahead, back, far0, far1, sems):
     swapped, line, cross = at[0] == 1, at[1], at[2]
     copies = []
     for step in range(4):
@@ -115,7 +116,7 @@
             o = (cross + rel) % 4
             row = jnp.where(swapped, o * 4 + t, t * 4 + o)
             for m, src in enumerate((mine, other)):
-                dst = (own.at[m, i], ahead.at[m, i], (ahead, back)[m].at[2, i], back.at[m, i])[step]
+                dst = (own.at[m, i], ahead.at[m, i], (far0, far1)[m].at[0, i], back.at[m, i])[step]
                 copies.append(pltpu.make_async_copy(src.at[row], dst, sems.at[len(copies)]))
     for copy in copies:
         copy.start()
@@ -124,16 +125,17 @@
 
 
 def regroup(at, mine, other):
-    shapes = [(2, 4, 4, 128, 128), (3, 4, 4, 128, 128), (3, 4, 4, 128, 128)]
+    shapes = [(2, 4, 4, 128, 128)] * 3 + [(1, 4, 4, 128, 128)] * 2
     return pl.pallas_call(
         regroup_kernel,
         grid_spec=pltpu.PrefetchScalarGridSpec(
-            num_scalar_prefetch=1, grid=(1,), in_specs=[pl.BlockSpec(memory_space=pl.ANY)] * 2,
-            out_specs=[pl.BlockSpec(shape, lambda i, *_, n=len(shape): (0,) * n) for shape in shapes],
+            num_scalar_prefetch=1, grid=(1,),
+            in_specs=[pl.BlockSpec((16, 4, 128, 128), lambda i, *_: (0, 0, 0, 0), pipeline_mode=pl.Buffered(1))] * 2,
+            out_specs=[pl.BlockSpec(memory_space=pl.ANY)] * 5,
             scratch_shapes=[pltpu.SemaphoreType.DMA((32,))],
         ),
         out_shape=[jax.ShapeDtypeStruct(shape, jnp.bfloat16) for shape in shapes],
-        compiler_params=pltpu.CompilerParams(vmem_limit_bytes=24 << 20),
+        compiler_params=pltpu.CompilerParams(vmem_limit_bytes=12 << 20),
         name="regroup",
     )(at, mine, other)
 
@@ -158,38 +160,35 @@
     kohn, refs = refs[:2 * n], refs[2 * n:]
     panels, refs = refs[:pieces], refs[pieces:]
     if form != "first":
-        sums_in, refs = refs[:2], refs[2:]
+        sums_in, refs = refs[0], refs[1:]
     if form == "sent":
         received, refs = refs[:2], refs[2:]
-    outs, (dens, sems, acc, staged, ints) = refs[:-5], refs[-5:]
+    outs, (dens, sems, acc, in_sems, out_sems, staged, ints) = refs[:-7], refs[-7:]
     size = n * 8 * PART // pieces
     core, line, cross, x = at[0], at[1], at[2], at[3]
 
-    @pl.when(pl.program_id(0) == 0)
-    def _():
-        copies = [
-            pltpu.make_async_copy(panels[s], dens.at[pl.ds(s * size, size)], sems.at[s]) for s in range(pieces)
-        ]
-        for copy in copies:
-            copy.start()
-        for copy in copies:
-            copy.wait()
-        for s in range(n):
-            rows = [dens[pl.ds((s * 8 + p) * PART + 8 * 128, 16), :].astype(jnp.float32) for p in range(8)]
-            rows = [row[2:3] for row in rows] + [rows[0][0:2], rows[1][0:2], jnp.zeros((4, 128), jnp.float32)]
-            staged[s * 16:(s + 1) * 16, :] = jnp.concatenate(rows, axis=0).astype(jnp.int32)
-        copy = pltpu.make_async_copy(staged, ints, sems.at[pieces])
+    loads = [pltpu.make_async_copy(panels[s], dens.at[pl.ds(s * size, size)], sems.at[s]) for s in range(pieces)]
+    sums = []
+    if form != "first":
+        for h, (target, m) in enumerate(halves):
+            src = sums_in.at[target, pl.ds(m * 4, 4)]
+            sums.append(pltpu.make_async_copy(src, acc.at[h], in_sems.at[h]))
+    stores = []
+    if form in ("first", "more"):
+        for h, (target, m) in enumerate(halves):
+            dst = outs[0].at[target if len(halves) > 2 else 0, pl.ds(m * 4, 4)]
+            stores.append(pltpu.make_async_copy(acc.at[h], dst, out_sems.at[h]))
+    for copy in loads + sums:
         copy.start()
+    for copy in loads:
         copy.wait()
-
-    def place_of(target):
-        if target is None:
-            step = pl.program_id(0)
-            ahead = jnp.where(step < 2, ORDER[0] - step, ORDER[2] * (3 - step))
-        else:
-            ahead = ORDER[target]
-        goal = (cross + ahead) & 3
-        return jnp.where(core == 1, goal * 4 + line, line * 4 + goal)
+    for s in range(n):
+        rows = [dens[pl.ds((s * 8 + p) * PART + 8 * 128, 16), :].astype(jnp.float32) for p in range(8)]
+        rows = [row[2:3] for row in rows] + [rows[0][0:2], rows[1][0:2], jnp.zeros((4, 128), jnp.float32)]
+        staged[s * 16:(s + 1) * 16, :] = jnp.concatenate(rows, axis=0).astype(jnp.int32)
+    copy = pltpu.make_async_copy(staged, ints, sems.at[pieces])
+    copy.start()
+    copy.wait()
 
     low = (lax.broadcasted_iota(jnp.int32, (32, 128), 1) < 64).astype(jnp.float32).astype(jnp.bfloat16)
     high = 1 - low
@@ -198,42 +197,44 @@
         turned = jnp.concatenate([blk[:, B:], blk[:, :B]], axis=1)
         return jnp.concatenate([blk * low, turned * low, turned * high, blk * high], axis=0)
 
-    def product(h, place, r, s, a):
-        k = ints[s * 16 + 8 + halves[h][1] * 2 + (place >> 3), (place & 7) * 16 + r * 4 + a]
+    def product(h, r, s, a):
+        target, m = halves[h]
+        goal = (cross + ORDER[target]) & 3
+        place = jnp.where(core == 1, goal * 4 + line, line * 4 + goal)
+        k = ints[s * 16 + 8 + m * 2 + (place >> 3), (place & 7) * 16 + r * 4 + a]
         slot = (120 >> (2 * (((k >> 4) - x) & 3))) & 3
         k = slot * 16 + ((k & 15) ^ (8 * core))
         part = s * 8 + (k >> 3)
         left = dens[pl.ds(pl.multiple_of(part * PART + (k & 7) * 128, 16), 128), :]
-        right = twice(kohn[2 * s + h][0, 0, r, a * 32:(a + 1) * 32, :])
+        ref, index = kohn[2 * s + m], target if kohn[2 * s + m].shape[1] == 4 else 0
+        right = twice(ref[0, index, r, a * 32:(a + 1) * 32, :])
         r = lax.dot_general(left, right, (((1,), (1,)), ((), ())), preferred_element_type=jnp.float32)
         return s * 16 + (k >> 3), (k & 7) * SP, r
 
-    def add(sums, word, first, r):
+    def add(total, word, first, r):
         js = [ints[word, first + b] for b in range(SP)]
-        old = [sums[j] for j in js]
+        old = [total[j] for j in js]
         for b in range(SP):
-            sums[js[b]] = old[b] + r[b * 16:(b + 1) * 16, :]
-
-    def two_rows(h, place, pair):
-        work, sums = [], []
+            total[js[b]] = old[b] + r[b * 16:(b + 1) * 16, :]
+
+    def two_rows(h, pair):
+        work, totals = [], []
         for q in range(2):
             r = pair * 2 + q
             work += [(q, r, s, a) for s in range(n) for a in range(SK)]
-            total = acc.at[q] if form in ("coded", "sent") else outs[0].at[0, h * 4 + r]
+            total = acc.at[h, r]
             if form == "first":
                 total[...] = jnp.zeros((NCW, 16, 128), jnp.float32)
             elif form == "sent":
                 scale = decoded_scale(received[h][r, NCW])
                 for j in range(NCW):
-                    total[j] = sums_in[h][0, r, j] + received[h][r, j].astype(jnp.int32).astype(jnp.float32) * scale
-            else:
-                total[...] = sums_in[h][0, r]
-            sums.append(total)
-        held = [product(h, place, *work[i][1:]) for i in range(3)]
+                    total[j] = total[j] + received[h][r, j].astype(jnp.int32).astype(jnp.float32) * scale
+            totals.append(total)
+        held = [product(h, *work[i][1:]) for i in range(3)]
         for i in range(len(work)):
             if i + 3 < len(work):
-                held.append(product(h, place, *work[i + 3][1:]))
-            add(sums[work[i][0]], *held[i])
+                held.append(product(h, *work[i + 3][1:]))
+            add(totals[work[i][0]], *held[i])
         if form in ("coded", "sent"):
             for q in range(2):
                 r = pair * 2 + q
@@ -241,57 +242,61 @@
                 def put(j, value, r=r):
                     outs[h][r, j] = value
 
-                encode(sums[q], put, lambda code, put=put: put(NCW, code.astype(jnp.int16)))
-
-    for h in range(2):
-        place = place_of(halves[h][0])
-        lax.fori_loop(0, 2, lambda pair, _, h=h, place=place: (two_rows(h, place, pair), 0)[1], 0)
+                encode(totals[q], put, lambda code, put=put: put(NCW, code.astype(jnp.int16)))
+
+    for h in range(len(halves)):
+        if sums:
+            sums[h].wait()
+        lax.fori_loop(0, 2, lambda pair, _, h=h: (two_rows(h, pair), 0)[1], 0)
+        if stores:
+            stores[h].start()
+    for copy in stores:
+        copy.wait()
 
 
 def panel_sums(name, form, at, kohn, panels, halves, sums=None, received=(), us=4.0):
-    n, pieces = len(kohn) // 2, len(panels)
-    steps = 4 if halves[0][0] is None else 1
-
-    def at_target(h, lead):
-        target = halves[h][0]
-        return lambda o, *_: (lead, o if target is None else target, 0, 0, 0)
-
-    k_specs = [pl.BlockSpec((1, 1, 4, 128, 128), at_target(i % 2, place)) for i, (_, place) in enumerate(kohn)]
-
-    def s_spec(h):
-        target, m = halves[h]
-        return pl.BlockSpec((1, 4, NCW, 16, 128), lambda o, *_: (o if target is None else target, m, 0, 0, 0))
-
-    coded = pl.BlockSpec((4, NCW + 1, 16, 128), lambda o, *_: (0, 0, 0, 0))
+    n, pieces, groups = len(kohn) // 2, len(panels), len(halves)
+
+    def k_spec(i, place):
+        if groups > 2:
+            return pl.BlockSpec((1, 4, 4, 128, 128), lambda *_: (place, 0, 0, 0, 0), pipeline_mode=pl.Buffered(1))
+        target = {m: t for t, m in halves}[i % 2]
+        return pl.BlockSpec((1, 1, 4, 128, 128), lambda *_: (place, target, 0, 0, 0), pipeline_mode=pl.Buffered(1))
+
+    any_spec = pl.BlockSpec(memory_space=pl.ANY)
+    sums_spec = pl.BlockSpec(memory_space=pltpu.HBM)
+    coded = pl.BlockSpec((4, NCW + 1, 16, 128), lambda *_: (0, 0, 0, 0), pipeline_mode=pl.Buffered(1))
     if form in ("coded", "sent"):
         o_specs = [coded] * 2
         shapes = [jax.ShapeDtypeStruct((4, NCW + 1, 16, 128), jnp.int16)] * 2
     else:
-        o_specs = [pl.BlockSpec((1, 8, NCW, 16, 128), lambda o, *_: (o, 0, 0, 0, 0))]
-        shapes = [jax.ShapeDtypeStruct((steps, 8, NCW, 16, 128), jnp.float32)]
-    any_spec = pl.BlockSpec(memory_space=pl.ANY)
+        o_specs = [sums_spec if groups > 2 else any_spec]
+        shapes = [jax.ShapeDtypeStruct((max(groups // 2, 1), 8, NCW, 16, 128), jnp.float32)]
     return pl.pallas_call(
         lambda *refs: panel_kernel(n, pieces, halves, form, *refs),
         grid_spec=pltpu.PrefetchScalarGridSpec(
             num_scalar_prefetch=1,
-            grid=(steps,),
+            grid=(1,),
             in_specs=(
-                k_specs + [any_spec] * pieces + ([] if sums is None else [s_spec(0), s_spec(1)]) + [coded] * len(received)
+                [k_spec(i, place) for i, (_, place) in enumerate(kohn)] + [any_spec] * pieces
+                + ([] if sums is None else [sums_spec]) + [coded] * len(received)
             ),
             out_specs=o_specs,
             scratch_shapes=[
                 pltpu.VMEM((n * 8 * PART, 128), jnp.bfloat16),
                 pltpu.SemaphoreType.DMA((pieces + 1,)),
-                pltpu.VMEM((2, NCW, 16, 128), jnp.float32),
+                pltpu.VMEM((groups, 4, NCW, 16, 128), jnp.float32),
+                pltpu.SemaphoreType.DMA((groups,)),
+                pltpu.SemaphoreType.DMA((groups,)),
                 pltpu.VMEM((n * 16, 128), jnp.int32),
                 pltpu.SMEM((n * 16, 128), jnp.int32),
             ],
         ),
         out_shape=shapes,
-        compiler_params=pltpu.CompilerParams(vmem_limit_bytes=44 << 20),
+        compiler_params=pltpu.CompilerParams(vmem_limit_bytes=LIMIT << 20),
         cost_estimate=pl.CostEstimate(flops=int(us * 1.1e9), bytes_accessed=int(us * 2e6), transcendentals=0),
         name=name,
-    )(at, *[array for array, _ in kohn], *panels, *([] if sums is None else [sums, sums]), *received)
+    )(at, *[array for array, _ in kohn], *panels, *([] if sums is None else [sums]), *received)
 
 
 def pack_kernel(slots, own, prev0, prev1, next0, next1, o_ref, total, codes):
@@ -430,13 +435,15 @@
     shard, kohn, kohn_other = lax.optimization_barrier((shard, kohn, kohn_other))
     left, right = over_x(shard, 1), over_x(shard, -1)
 
-    kohn, ahead, back = regroup(at, kohn, kohn_other)
+    kohn, ahead, back, opposite0, opposite1 = regroup(at, kohn, kohn_other)
+    opposite0, opposite1 = over_line(opposite0, 1), over_line(opposite1, -1)
     kohn_prev, kohn_next = over_line(ahead, 1), over_line(back, -1)
-    left, right, kohn_prev, kohn_next = lax.optimization_barrier((left, right, kohn_prev, kohn_next))
-    opposite0, opposite1 = over_line(kohn_prev[2:], 1), over_line(kohn_next[2:], -1)
+    opposite0, opposite1 = over_line(opposite0, 1), over_line(opposite1, -1)
 
     panel = jnp.concatenate([shard, left, right, over_x(left[:PART], 1), over_x(right[PART:], -1)])
-    sent, opposite0, opposite1 = lax.optimization_barrier((panel, opposite0, opposite1))
+    sent, kohn_prev, kohn_next, opposite0, opposite1 = lax.optimization_barrier(
+        (panel, kohn_prev, kohn_next, opposite0, opposite1)
+    )
     prev, after = over_line(sent, 1), over_line(sent, -1)
 
     owners = jnp.stack([owner_map.reshape(128), shard[PART + 8 * 128 + 3].astype(jnp.int32)])
@@ -448,7 +455,7 @@
     def both(array):
         return [(array, 0), (array, 1)]
 
-    everything = ((None, 0), (None, 1))
+    everything = tuple((target, m) for target in range(4) for m in range(2))
     sums, = panel_sums("own_panel", "first", at, both(kohn), [panel], everything, us=9.0)
     prev, after, sums = lax.optimization_barrier((prev, after, sums))
     far_low, far_high = over_line(prev[:4 * PART], 1), over_line(after[4 * PART:], -1)
@@ -457,7 +464,7 @@
     )
 
     def last(form, halves, received=()):
-        kohn = [((opposite0, opposite1)[m], 0) for _, m in halves]
+        kohn = [(opposite0, 0), (opposite1, 0)]
         return panel_sums("last_" + form, form, at, kohn, [far_low, far_high], halves, sums, received)
 
     via_next, via_prev = last("coded", ((0, 0), (0, 1)))

time: 196 us -> 199 us (1.015)
  local copies, waits for them, and re-layouts: 5.31 us -> 10.7 us
  Pallas kernels: 69.4 us -> 65.8 us
    pallas_call x6, Pallas kernels: 46.3 us -> 39.2 us  [panel_sums(): pl.pallas_call(lambda *refs: panel_kernel(n, pieces, halves, form, *refs)...]
    unnamed x15 -> x27, local copies, waits for them, and re-layouts: 0.95 us -> 6.39 us
    ppermute x4, waiting for transfers between devices: 17.1 us -> 12 us  [over_x(): return lax.ppermute(v, 'x', [(i, (i + step) % X) for i in range(X)])]
    ppermute x14 -> x16, waiting for transfers between devices: 26.4 us -> 31.4 us  [over(): lax.ppermute(v, PLANE, [(group[i], group[(i + step) % 4]) for group in gr...]
    pallas_call x1, Pallas kernels: 4.96 us -> 8.42 us  [regroup(): pl.pallas_call(regroup_kernel, grid_spec=pltpu.PrefetchScalarGridSpec(num...]
    ppermute x14 -> x16, starting transfers between devices: 19.4 us -> 21.9 us  [over(): lax.ppermute(v, PLANE, [(group[i], group[(i + step) % 4]) for group in gr...]
    ppermute x4, starting transfers between devices: 5.03 us -> 2.88 us  [over_x(): return lax.ppermute(v, 'x', [(i, (i + step) % X) for i in range(X)])]
  transfers between devices with their start and end apart: 20 -> 22, of which waited for: 10 -> 9; matrix products, arithmetic and copies ran while one was open for 2% -> 2% of each run, Pallas kernels for 23% -> 24%
where the time goes in v8:
time: 199 us
  Pallas kernels  65.8 us (33%)
  blocking collectives  48 us (24%)
  waiting for transfers between devices  45.2 us (23%)
  starting transfers between devices  26.3 us (13%)
  local copies, waits for them, and re-layouts  10.7 us (5%)
  other arithmetic  2.8 us (1%)
    all_to_all x1, blocking collectives, local(): lax.all_to_all(outgoing, ALL, split_axis=0, concat_axis=0, tiled=True)  48 us
    pallas_call x6, Pallas kernels, panel_sums(): pl.pallas_call(lambda *refs: panel_kernel(n, pieces, halves, form, *refs)...  39.2 us
    ppermute x16, waiting for transfers between devices, over(): lax.ppermute(v, PLANE, [(group[i], group[(i + step) % 4]) for group in gr...  31.4 us
    ppermute x16, starting transfers between devices, over(): lax.ppermute(v, PLANE, [(group[i], group[(i + step) % 4]) for group in gr...  21.9 us
    ppermute x4, waiting for transfers between devices, over_x(): return lax.ppermute(v, 'x', [(i, (i + step) % X) for i in range(X)])  12 us
    pallas_call x1, Pallas kernels, regroup(): pl.pallas_call(regroup_kernel, grid_spec=pltpu.PrefetchScalarGridSpec(num...  8.42 us
    pallas_call x1, Pallas kernels, unpack(): pl.pallas_call(unpack_kernel, grid=(X,), in_specs=[pl.BlockSpec((1, C, 16...  7.07 us
    unnamed x27, local copies, waits for them, and re-layouts  6.39 us
  transfers between devices with their start and end apart: 22, of which 9 were waited for; matrix products, arithmetic and copies ran while one was open for 2% of the time, Pallas kernels for 24%

profile of v8, /device:TPU:1, one launch (start us, length us, event | category | flops | bytes accessed | tf_op | source)
XLA Modules:
  0.0 199.0 jit_solution(14925892403262963421)
XLA Ops:
  0.0 3.8 %reshape.31.mine = bf16[16,4,128,128]{3,2,1,0:T(8,128)(2,1)S(1)} reshape(bf16[64,1,4,4096]{3,2,1,0:T(4,128)(2,1)} %param.5) | data formatting | bytes 4194304 | tf_op jit(solution)/shard_map/reshape | solution.py:424
  3.8 1.5 collective-permute-start.1
  7.0 5.2 %split.1 = (bf16[1040,128]{1,0:T(8,128)(2,1)}, bf16[1040,128]{1,0:T(8,128)(2,1)}) custom-call(s32[4]{0:T(128)} %pad_add_fusion.2.core.at.refs_0_, bf16[8,8,4096]{2,1,0:T(8,128)(2,1)} %bitcast.12, s32[16,128]{1,0:T(8,128)} %fusion.2.i_ref), custom_call_target="tpu_custom_call" | custom-call | tf_op jit(solution)/shard_map/split/pallas_call | solution.py:95
  12.2 1.7 collective-permute-done
  18.3 8.4 %regroup.1 = (bf16[2,4,4,128,128]{4,3,2,1,0:T(8,128)(2,1)S(1)}, bf16[2,4,4,128,128]{4,3,2,1,0:T(8,128)(2,1)S(1)}, bf16[2,4,4,128,128]{4,3,2,1,0:T(8,128)(2,1)S(1...) custom-call(s32[4]{0:T(128)S(1)} %copy-done, bf16[16,4,128,128]{3,2,1,0:T(8,128)(2,1)S(1)} %reshape.31.mine, ...), custom_call_target="tpu_custom_call" | custom-call | tf_op jit(solution)/shard_map/regroup/pallas_call | solution.py:129
  26.7 1.4 collective-permute-start.8
  28.2 1.5 collective-permute-start.10
  29.7 6.7 %collective-permute-done.8 = bf16[1,4,4,128,128]{4,3,2,1,0:T(8,128)(2,1)S(1)} collective-permute-done((bf16[1,4,4,128,128]{4,3,2,1,0:T(8,128)(2,1)S(1)}, bf16[1,4,4,128,128]{4,3,2,1,0:T(8,128)(2,1)S(1)}, u32[]{:S(2)}, u32[]{:S(2)}) %collective-permute-start.8) | collective-permute-done | bytes 524320 | tf_op jit(solution)/shard_map/ppermute | solution.py:36
  36.5 1.5 collective-permute-start.7
  37.9 2.7 %collective-permute-start.11 = (bf16[1,4,4,128,128]{4,3,2,1,0:T(8,128)(2,1)S(1)}, bf16[1,4,4,128,128]{4,3,2,1,0:T(8,128)(2,1)S(1)}, u32[]{:S(2)}, u32[]{:S(2)}) collective-permute-start(bf16[1,4,4,128,128]{4,3,2,1,0:T(8,128)(2,1)S(1)} %collective-permute-done.10), channel_id=1, source_target_pairs={{0,12},{4,0},{8,4},{12,8},{1,13},{5,1},{9,5},{13,9},{2,14},{6,2},{... | collective-permute-start | bytes 1572872 | tf_op jit(solution)/shard_map/ppermute | solution.py:36
  40.8 6.7 %collective-permute-done.4 = bf16[1040,128]{1,0:T(8,128)(2,1)S(1)} collective-permute-done((bf16[1040,128]{1,0:T(8,128)(2,1)S(1)}, bf16[1040,128]{1,0:T(8,128)(2,1)S(1)}, u32[]{:S(2)}, u32[]{:S(2)}) %collective-permute-start.4) | collective-permute-done | bytes 266272 | tf_op jit(solution)/shard_map/ppermute | solution.py:48
  47.7 5.4 %collective-permute-done.5 = bf16[1040,128]{1,0:T(8,128)(2,1)S(1)} collective-permute-done((bf16[1040,128]{1,0:T(8,128)(2,1)S(1)}, bf16[1040,128]{1,0:T(8,128)(2,1)S(1)}, u32[]{:S(2)}, u32[]{:S(2)}) %collective-permute-start.5) | collective-permute-done | bytes 266272 | tf_op jit(solution)/shard_map/ppermute | solution.py:48
  53.3 2.7 %collective-permute-done.11.refs_2_ = bf16[1,4,4,128,128]{4,3,2,1,0:T(8,128)(2,1)S(1)} collective-permute-done((bf16[1,4,4,128,128]{4,3,2,1,0:T(8,128)(2,1)S(1)}, bf16[1,4,4,128,128]{4,3,2,1,0:T(8,128)(2,1)S(1)}, u32[]{:S(2)}, u32[]{:S(2)}) %collective-permute-start.11) | collective-permute-done | bytes 524320 | tf_op jit(solution)/shard_map/ppermute | solution.py:36
  56.0 2.4 %collective-permute-start.13 = (bf16[8320,128]{1,0:T(8,128)(2,1)S(1)}, bf16[8320,128]{1,0:T(8,128)(2,1)S(1)}, u32[]{:S(2)}, u32[]{:S(2)}) collective-permute-start(bf16[8320,128]{1,0:T(8,128)(2,1)S(1)} %constant_dynamic-update-slice_fusion.refs_3_), channel_id=1, source_target_pairs={{0,12},{4,0},{8,4},{12,8},{1,13},{5,1},{9,5},{13,9},{2,14},{6,2},{... | collective-permute-start | bytes 6389768 | tf_op jit(solution)/shard_map/ppermute | solution.py:36
  58.4 8.3 %own_panel.1.refs_7_ = f32[4,8,32,16,128]{4,3,2,1,0:T(8,128)S(1)} custom-call(s32[4]{0:T(128)S(1)} %copy-done.1, bf16[2,4,4,128,128]{4,3,2,1,0:T(8,128)(2,1)S(1)} %get-tuple-element.45.refs_1_.refs_2_, bf16[2,4,4,128,128]{4,3,2,1,0:T(8,128)(2,1)S(1)} %get-tuple-element.45.refs_1_.refs_2_, bf16[8320,128]{1,0:T(8,128)(2,1)S(1)} %constant_dynamic-update-slice_fusion.refs_3_), custom_call_target="tpu_custom_call" | custom-call | flops 9900000256 | bytes 18000000 | tf_op jit(solution)/shard_map/own_panel/pallas_call | solution.py:275
  66.8 15.0 %collective-permute-done.13.refs_6_ = bf16[8320,128]{1,0:T(8,128)(2,1)S(1)} collective-permute-done((bf16[8320,128]{1,0:T(8,128)(2,1)S(1)}, bf16[8320,128]{1,0:T(8,128)(2,1)S(1)}, u32[]{:S(2)}, u32[]{:S(2)}) %collective-permute-start.13) | collective-permute-done | bytes 2129952 | tf_op jit(solution)/shard_map/ppermute | solution.py:36
  81.7 3.4 %collective-permute-done.12.refs_5_ = bf16[8320,128]{1,0:T(8,128)(2,1)S(1)} collective-permute-done((bf16[8320,128]{1,0:T(8,128)(2,1)S(1)}, bf16[8320,128]{1,0:T(8,128)(2,1)S(1)}, u32[]{:S(2)}, u32[]{:S(2)}) %collective-permute-start.12) | collective-permute-done | bytes 2129952 | tf_op jit(solution)/shard_map/ppermute | solution.py:36
  85.4 2.7 %collective-permute-start.15 = (bf16[4160,128]{1,0:T(8,128)(2,1)S(1)}, bf16[4160,128]{1,0:T(8,128)(2,1)S(1)}, u32[]{:S(2)}, u32[]{:S(2)}) collective-permute-start(bf16[4160,128]{1,0:T(8,128)(2,1)S(1)} %slice.19), channel_id=1, source_target_pairs={{0,12},{4,0},{8,4},{12,8},{1,13},{5,1},{9,5},{13,9},{2,14},{6,2},{... | collective-permute-start | bytes 3194888 | tf_op jit(solution)/shard_map/ppermute | solution.py:36
  88.0 14.2 %near_panels.1.refs_5_ = f32[4,8,32,16,128]{4,3,2,1,0:T(8,128)S(1)} custom-call(s32[4]{0:T(128)S(1)} %copy-done.1, bf16[2,4,4,128,128]{4,3,2,1,0:T(8,128)(2,1)S(1)} %collective-permute-done.6.refs_1_.refs_2_, bf16[2,4,4,128,128]{4,3,2,1,0:T(8,128)(2,1)S(1)} %collective-permute-done.6.refs_1_.refs_2_, ...), custom_call_target="tpu_custom_call" | custom-call | flops 17600000000 | bytes 32000000 | tf_op jit(solution)/shard_map/near_panels/pallas_call | solution.py:275
  102.3 4.6 %last_coded.2 = (s16[4,33,16,128]{3,2,1,0:T(8,128)(2,1)}, s16[4,33,16,128]{3,2,1,0:T(8,128)(2,1)S(1)}) custom-call(s32[4]{0:T(128)S(1)} %copy-done.1, bf16[1,4,4,128,128]{4,3,2,1,0:T(8,128)(2,1)S(1)} %collective-permute-done.9.refs_1_, bf16[1,4,4,128,128]{4,3,2,1,0:T(8,128)(2,1)S(1)} %collective-permute-done.11.refs_2_, ...), custom_call_target="tpu_custom_call" | custom-call | flops 4400000000 | bytes 8000000 | tf_op jit(solution)/shard_map/last_coded/pallas_call | solution.py:275
  107.0 1.4 collective-permute-start.16
  108.4 2.8 %collective-permute-start.17 = (s16[4,33,16,128]{3,2,1,0:T(8,128)(2,1)S(1)}, s16[4,33,16,128]{3,2,1,0:T(8,128)(2,1)}, u32[]{:S(2)}, u32[]{:S(2)}) collective-permute-start(s16[4,33,16,128]{3,2,1,0:T(8,128)(2,1)S(1)} %get-tuple-element.52), channel_id=1, source_target_pairs={{0,3},{1,0},{2,1},{3,2},{4,7},{5,4},{6,5},{7,6},{8,11},{9,8},{10,9... | collective-permute-start | bytes 1622024 | tf_op jit(solution)/shard_map/ppermute | solution.py:36
  113.8 3.4 %copy-done.7 = f32[4,8,32,16,128]{4,3,2,1,0:T(8,128)S(1)} copy-done((f32[4,8,32,16,128]{4,3,2,1,0:T(8,128)S(1)}, f32[4,8,32,16,128]{4,3,2,1,0:T(8,128)}, u32[]{:S(2)}) %copy-start.7) | copy-done | bytes 8388632
  117.1 3.8 %last_coded.3 = (s16[4,33,16,128]{3,2,1,0:T(8,128)(2,1)S(1)}, s16[4,33,16,128]{3,2,1,0:T(8,128)(2,1)S(1)}) custom-call(s32[4]{0:T(128)S(1)} %copy-done.1, bf16[1,4,4,128,128]{4,3,2,1,0:T(8,128)(2,1)S(1)} %copy-done.3, bf16[1,4,4,128,128]{4,3,2,1,0:T(8,128)(2,1)S(1)} %copy-done.5, bf16[4160,128]{1,0:T(8,128)(2,1)S(1)} %collective-permute-done.14.refs_3_, ...), custom_call_target="tpu_custom_call" | custom-call | flops 4400000000 | bytes 8000000 | tf_op jit(solution)/shard_map/last_coded/pallas_call | solution.py:275
  121.1 2.7 %collective-permute-start.20 = (s16[4,33,16,128]{3,2,1,0:T(8,128)(2,1)S(1)}, s16[4,33,16,128]{3,2,1,0:T(8,128)(2,1)S(1)}, u32[]{:S(2)}, u32[]{:S(2)}) collective-permute-start(s16[4,33,16,128]{3,2,1,0:T(8,128)(2,1)S(1)} %get-tuple-element.55), channel_id=1, source_target_pairs={{0,3},{1,0},{2,1},{3,2},{4,7},{5,4},{6,5},{7,6},{8,11},{9,8},{10,9... | collective-permute-start | bytes 1622024 | tf_op jit(solution)/shard_map/ppermute | solution.py:36
  123.7 4.9 %last_sent.1 = (s16[4,33,16,128]{3,2,1,0:T(8,128)(2,1)S(1)}, s16[4,33,16,128]{3,2,1,0:T(8,128)(2,1)S(1)}) custom-call(s32[4]{0:T(128)S(1)} %copy-done.1, bf16[1,4,4,128,128]{4,3,2,1,0:T(8,128)(2,1)S(1)} %copy-done.3, bf16[1,4,4,128,128]{4,3,2,1,0:T(8,128)(2,1)S(1)} %copy-done.5, bf16[4160,128]{1,0:T(8,128)(2,1)S(1)} %collective-permute-done.14.refs_3_, ...), custom_call_target="tpu_custom_call" | custom-call | flops 4400000000 | bytes 8000000 | tf_op jit(solution)/shard_map/last_sent/pallas_call | solution.py:275
  128.7 2.7 %collective-permute-start.21 = (s16[4,33,16,128]{3,2,1,0:T(8,128)(2,1)S(1)}, s16[4,33,16,128]{3,2,1,0:T(8,128)(2,1)S(1)}, u32[]{:S(2)}, u32[]{:S(2)}) collective-permute-start(s16[4,33,16,128]{3,2,1,0:T(8,128)(2,1)S(1)} %get-tuple-element.56), channel_id=1, source_target_pairs={{0,3},{1,0},{2,1},{3,2},{4,7},{5,4},{6,5},{7,6},{8,11},{9,8},{10,9... | collective-permute-start | bytes 1622024 | tf_op jit(solution)/shard_map/ppermute | solution.py:36
  131.5 3.3 %last_more.1.own = f32[1,8,32,16,128]{4,3,2,1,0:T(8,128)S(1)} custom-call(s32[4]{0:T(128)S(1)} %copy-done.1, bf16[1,4,4,128,128]{4,3,2,1,0:T(8,128)(2,1)S(1)} %copy-done.3, bf16[1,4,4,128,128]{4,3,2,1,0:T(8,128)(2,1)S(1)} %copy-done.5, bf16[4160,128]{1,0:T(8,128)(2,1)S(1)} %collective-permute-done.14.refs_3_, ...), custom_call_target="tpu_custom_call" | custom-call | flops 4400000000 | bytes 8000000 | tf_op jit(solution)/shard_map/last_more/pallas_call | solution.py:275
  134.8 3.3 %collective-permute-done.18.prev0 = s16[4,33,16,128]{3,2,1,0:T(8,128)(2,1)S(1)} collective-permute-done((s16[4,33,16,128]{3,2,1,0:T(8,128)(2,1)S(1)}, s16[4,33,16,128]{3,2,1,0:T(8,128)(2,1)S(1)}, u32[]{:S(2)}, u32[]{:S(2)}) %collective-permute-start.18) | collective-permute-done | bytes 540704 | tf_op jit(solution)/shard_map/ppermute | solution.py:36
  138.1 5.9 %pack.1 = s16[128,80,128]{2,1,0:T(8,128)(2,1)S(1)} custom-call(s32[256]{0:T(256)S(1)} %add_bitcast_fusion.slots, f32[1,8,32,16,128]{4,3,2,1,0:T(8,128)S(1)} %last_more.1.own, s16[4,33,16,128]{3,2,1,0:T(8,128)(2,1)S(1)} %collective-permute-done.18.prev0, s16[4,33,16,128]{3,2,1,0:T(8,128)(2,1)S(1)} %collective-permute-done.19.prev1, ...), custom_call_target="tpu_custom_call" | custom-call | tf_op jit(solution)/shard_map/pack/pallas_call | solution.py:369
  144.0 48.0 %all_to_all.5 = s16[128,80,128]{2,1,0:T(8,128)(2,1)S(1)} all-to-all(s16[128,80,128]{2,1,0:T(8,128)(2,1)S(1)} %pack.1), channel_id=1, replica_groups=mesh['x'=4,'core'=2,'z'=4,'y'=4] {'x','core','z','y'}, dimensions={0} | all-to-all | bytes 5242880 | tf_op jit(solution)/shard_map/all_to_all | solution.py:479
  192.0 7.1 %unpack.1 = f32[256,4096]{1,0:T(8,128)} custom-call(s16[4,2,16,80,128]{4,3,2,1,0:T(8,128)(2,1)S(1)} %bitcast.11), custom_call_target="tpu_custom_call" | custom-call | tf_op jit(solution)/shard_map/unpack/pallas_call | solution.py:406
  (70 shorter events, 9.7 us)
Async XLA Ops:
  0.0 5.3 %copy-start.9 = (s32[1,8,8]{2,1,0:T(8,128)S(1)}, s32[1,8,8]{2,1,0:T(8,128)}, u32[]{:S(2)}) copy-start(s32[1,8,8]{2,1,0:T(8,128)} %param.8) | copy-start | bytes 772
  0.0 5.5 %copy-start.10 = (s32[64,1,4]{0,2,1:T(4,128)S(1)}, s32[64,1,4]{0,2,1:T(4,128)}, u32[]{:S(2)}) copy-start(s32[64,1,4]{0,2,1:T(4,128)} %param.6) | copy-start | bytes 3076
  0.0 6.3 %copy-start.8 = (s32[128,1]{0,1:T(1,128)S(1)}, s32[128,1]{0,1:T(1,128)}, u32[]{:S(2)}) copy-start(s32[128,1]{0,1:T(1,128)} %param.9) | copy-start | bytes 1540
  3.8 11.1 %collective-permute-start.1 = (bf16[16,4,128,128]{3,2,1,0:T(8,128)(2,1)S(1)}, bf16[16,4,128,128]{3,2,1,0:T(8,128)(2,1)}, u32[]{:S(2)}, u32[]{:S(2)}) collective-permute-start(bf16[16,4,128,128]{3,2,1,0:T(8,128)(2,1)S(1)} %reshape.31.mine), channel_id=1, source_target_pairs={{0,16},{16,0},{1,17},{17,1},{2,18},{18,2},{3,19},{19,3},{4,20},{20... | collective-permute-start | bytes 6291464 | tf_op jit(solution)/shard_map/ppermute | solution.py:52
  12.2 1.8 collective-permute-start
  14.9 23.0 %collective-permute-start.2 = (bf16[2080,128]{1,0:T(8,128)(2,1)S(1)}, bf16[2080,128]{1,0:T(8,128)(2,1)S(1)}, u32[]{:S(2)}, u32[]{:S(2)}) collective-permute-start(bf16[2080,128]{1,0:T(8,128)(2,1)S(1)} %pad_maximum_fusion), channel_id=1, source_target_pairs={{0,32},{32,64},{64,96},{96,0},{1,33},{33,65},{65,97},{97,1},{2,34}... | collective-permute-start | bytes 1597448 | tf_op jit(solution)/shard_map/ppermute | solution.py:48
  16.3 24.3 %collective-permute-start.3 = (bf16[2080,128]{1,0:T(8,128)(2,1)S(1)}, bf16[2080,128]{1,0:T(8,128)(2,1)S(1)}, u32[]{:S(2)}, u32[]{:S(2)}) collective-permute-start(bf16[2080,128]{1,0:T(8,128)(2,1)S(1)} %pad_maximum_fusion), channel_id=1, source_target_pairs={{0,96},{32,0},{64,32},{96,64},{1,97},{33,1},{65,33},{97,65},{2,98}... | collective-permute-start | bytes 1597448 | tf_op jit(solution)/shard_map/ppermute | solution.py:48
  26.7 9.8 %collective-permute-start.8 = (bf16[1,4,4,128,128]{4,3,2,1,0:T(8,128)(2,1)S(1)}, bf16[1,4,4,128,128]{4,3,2,1,0:T(8,128)(2,1)S(1)}, u32[]{:S(2)}, u32[]{:S(2)}) collective-permute-start(bf16[1,4,4,128,128]{4,3,2,1,0:T(8,128)(2,1)S(1)} %get-tuple-element.40), channel_id=1, source_target_pairs={{0,4},{4,8},{8,12},{12,0},{1,5},{5,9},{9,13},{13,1},{2,6},{6,10},{... | collective-permute-start | bytes 1572872 | tf_op jit(solution)/shard_map/ppermute | solution.py:36
  28.2 9.8 %collective-permute-start.10 = (bf16[1,4,4,128,128]{4,3,2,1,0:T(8,128)(2,1)S(1)}, bf16[1,4,4,128,128]{4,3,2,1,0:T(8,128)(2,1)S(1)}, u32[]{:S(2)}, u32[]{:S(2)}) collective-permute-start(bf16[1,4,4,128,128]{4,3,2,1,0:T(8,128)(2,1)S(1)} %get-tuple-element.41), channel_id=1, source_target_pairs={{0,12},{4,0},{8,4},{12,8},{1,13},{5,1},{9,5},{13,9},{2,14},{6,2},{... | collective-permute-start | bytes 1572872 | tf_op jit(solution)/shard_map/ppermute | solution.py:36
  29.7 23.4 %collective-permute-start.6 = (bf16[2,4,4,128,128]{4,3,2,1,0:T(8,128)(2,1)S(1)}, bf16[2,4,4,128,128]{4,3,2,1,0:T(8,128)(2,1)S(1)}, u32[]{:S(2)}, u32[]{:S(2)}) collective-permute-start(bf16[2,4,4,128,128]{4,3,2,1,0:T(8,128)(2,1)S(1)} %get-tuple-element.38), channel_id=1, source_target_pairs={{0,4},{4,8},{8,12},{12,0},{1,5},{5,9},{9,13},{13,1},{2,6},{6,10},{... | collective-permute-start | bytes 3145736 | tf_op jit(solution)/shard_map/ppermute | solution.py:36
  36.5 22.0 %copy-start.1 = (s32[4]{0:T(128)S(1)}, s32[4]{0:T(128)}, u32[]{:S(2)}) copy-start(s32[4]{0:T(128)} %pad_add_fusion.2.core.at.refs_0_) | copy-start | bytes 52
  36.5 16.6 %collective-permute-start.7 = (bf16[2,4,4,128,128]{4,3,2,1,0:T(8,128)(2,1)S(1)}, bf16[2,4,4,128,128]{4,3,2,1,0:T(8,128)(2,1)S(1)}, u32[]{:S(2)}, u32[]{:S(2)}) collective-permute-start(bf16[2,4,4,128,128]{4,3,2,1,0:T(8,128)(2,1)S(1)} %get-tuple-element.39), channel_id=1, source_target_pairs={{0,12},{4,0},{8,4},{12,8},{1,13},{5,1},{9,5},{13,9},{2,14},{6,2},{... | collective-permute-start | bytes 3145736 | tf_op jit(solution)/shard_map/ppermute | solution.py:36
  37.9 15.4 %collective-permute-start.9 = (bf16[1,4,4,128,128]{4,3,2,1,0:T(8,128)(2,1)S(1)}, bf16[1,4,4,128,128]{4,3,2,1,0:T(8,128)(2,1)S(1)}, u32[]{:S(2)}, u32[]{:S(2)}) collective-permute-start(bf16[1,4,4,128,128]{4,3,2,1,0:T(8,128)(2,1)S(1)} %collective-permute-done.8), channel_id=1, source_target_pairs={{0,4},{4,8},{8,12},{12,0},{1,5},{5,9},{9,13},{13,1},{2,6},{6,10},{... | collective-permute-start | bytes 1572872 | tf_op jit(solution)/shard_map/ppermute | solution.py:36
  37.9 18.1 %collective-permute-start.11 = (bf16[1,4,4,128,128]{4,3,2,1,0:T(8,128)(2,1)S(1)}, bf16[1,4,4,128,128]{4,3,2,1,0:T(8,128)(2,1)S(1)}, u32[]{:S(2)}, u32[]{:S(2)}) collective-permute-start(bf16[1,4,4,128,128]{4,3,2,1,0:T(8,128)(2,1)S(1)} %collective-permute-done.10), channel_id=1, source_target_pairs={{0,12},{4,0},{8,4},{12,8},{1,13},{5,1},{9,5},{13,9},{2,14},{6,2},{... | collective-permute-start | bytes 1572872 | tf_op jit(solution)/shard_map/ppermute | solution.py:36
  40.6 6.8 %collective-permute-start.4 = (bf16[1040,128]{1,0:T(8,128)(2,1)S(1)}, bf16[1040,128]{1,0:T(8,128)(2,1)S(1)}, u32[]{:S(2)}, u32[]{:S(2)}) collective-permute-start(bf16[1040,128]{1,0:T(8,128)(2,1)S(1)} %slice.20), channel_id=1, source_target_pairs={{0,32},{32,64},{64,96},{96,0},{1,33},{33,65},{65,97},{97,1},{2,34}... | collective-permute-start | bytes 798728 | tf_op jit(solution)/shard_map/ppermute | solution.py:48
  47.5 5.6 %collective-permute-start.5 = (bf16[1040,128]{1,0:T(8,128)(2,1)S(1)}, bf16[1040,128]{1,0:T(8,128)(2,1)S(1)}, u32[]{:S(2)}, u32[]{:S(2)}) collective-permute-start(bf16[1040,128]{1,0:T(8,128)(2,1)S(1)} %slice.21), channel_id=1, source_target_pairs={{0,96},{32,0},{64,32},{96,64},{1,97},{33,1},{65,33},{97,65},{2,98}... | collective-permute-start | bytes 798728 | tf_op jit(solution)/shard_map/ppermute | solution.py:48
  53.3 49.0 %copy-start.2 = (bf16[1,4,4,128,128]{4,3,2,1,0:T(8,128)(2,1)}, bf16[1,4,4,128,128]{4,3,2,1,0:T(8,128)(2,1)S(1)}, u32[]{:S(2)}) copy-start(bf16[1,4,4,128,128]{4,3,2,1,0:T(8,128)(2,1)S(1)} %collective-permute-done.9.refs_1_) | copy-start | bytes 1572868
  56.0 46.3 %copy-start.4 = (bf16[1,4,4,128,128]{4,3,2,1,0:T(8,128)(2,1)}, bf16[1,4,4,128,128]{4,3,2,1,0:T(8,128)(2,1)S(1)}, u32[]{:S(2)}) copy-start(bf16[1,4,4,128,128]{4,3,2,1,0:T(8,128)(2,1)S(1)} %collective-permute-done.11.refs_2_) | copy-start | bytes 1572868
  56.0 25.7 %collective-permute-start.13 = (bf16[8320,128]{1,0:T(8,128)(2,1)S(1)}, bf16[8320,128]{1,0:T(8,128)(2,1)S(1)}, u32[]{:S(2)}, u32[]{:S(2)}) collective-permute-start(bf16[8320,128]{1,0:T(8,128)(2,1)S(1)} %constant_dynamic-update-slice_fusion.refs_3_), channel_id=1, source_target_pairs={{0,12},{4,0},{8,4},{12,8},{1,13},{5,1},{9,5},{13,9},{2,14},{6,2},{... | collective-permute-start | bytes 6389768 | tf_op jit(solution)/shard_map/ppermute | solution.py:36
  58.4 26.7 %collective-permute-start.12 = (bf16[8320,128]{1,0:T(8,128)(2,1)S(1)}, bf16[8320,128]{1,0:T(8,128)(2,1)S(1)}, u32[]{:S(2)}, u32[]{:S(2)}) collective-permute-start(bf16[8320,128]{1,0:T(8,128)(2,1)S(1)} %constant_dynamic-update-slice_fusion.refs_3_), channel_id=1, source_target_pairs={{0,4},{4,8},{8,12},{12,0},{1,5},{5,9},{9,13},{13,1},{2,6},{6,10},{... | collective-permute-start | bytes 6389768 | tf_op jit(solution)/shard_map/ppermute | solution.py:36
  85.3 17.0 %collective-permute-start.14 = (bf16[4160,128]{1,0:T(8,128)(2,1)S(1)}, bf16[4160,128]{1,0:T(8,128)(2,1)S(1)}, u32[]{:S(2)}, u32[]{:S(2)}) collective-permute-start(bf16[4160,128]{1,0:T(8,128)(2,1)S(1)} %slice.18), channel_id=1, source_target_pairs={{0,4},{4,8},{8,12},{12,0},{1,5},{5,9},{9,13},{13,1},{2,6},{6,10},{... | collective-permute-start | bytes 3194888 | tf_op jit(solution)/shard_map/ppermute | solution.py:36
  85.4 16.9 %collective-permute-start.15 = (bf16[4160,128]{1,0:T(8,128)(2,1)S(1)}, bf16[4160,128]{1,0:T(8,128)(2,1)S(1)}, u32[]{:S(2)}, u32[]{:S(2)}) collective-permute-start(bf16[4160,128]{1,0:T(8,128)(2,1)S(1)} %slice.19), channel_id=1, source_target_pairs={{0,12},{4,0},{8,4},{12,8},{1,13},{5,1},{9,5},{13,9},{2,14},{6,2},{... | collective-permute-start | bytes 3194888 | tf_op jit(solution)/shard_map/ppermute | solution.py:36
  102.3 4.7 %copy-start.6 = (f32[4,8,32,16,128]{4,3,2,1,0:T(8,128)}, f32[4,8,32,16,128]{4,3,2,1,0:T(8,128)S(1)}, u32[]{:S(2)}) copy-start(f32[4,8,32,16,128]{4,3,2,1,0:T(8,128)S(1)} %near_panels.1.refs_5_) | copy-start | bytes 25165828
  107.0 16.7 %collective-permute-start.16 = (s16[4,33,16,128]{3,2,1,0:T(8,128)(2,1)}, s16[4,33,16,128]{3,2,1,0:T(8,128)(2,1)S(1)}, u32[]{:S(2)}, u32[]{:S(2)}) collective-permute-start(s16[4,33,16,128]{3,2,1,0:T(8,128)(2,1)} %get-tuple-element.51), channel_id=1, source_target_pairs={{0,1},{1,2},{2,3},{3,0},{4,5},{5,6},{6,7},{7,4},{8,9},{9,10},{10,1... | collective-permute-start | bytes 1622024 | tf_op jit(solution)/shard_map/ppermute | solution.py:36
  108.4 15.3 %collective-permute-start.17 = (s16[4,33,16,128]{3,2,1,0:T(8,128)(2,1)S(1)}, s16[4,33,16,128]{3,2,1,0:T(8,128)(2,1)}, u32[]{:S(2)}, u32[]{:S(2)}) collective-permute-start(s16[4,33,16,128]{3,2,1,0:T(8,128)(2,1)S(1)} %get-tuple-element.52), channel_id=1, source_target_pairs={{0,3},{1,0},{2,1},{3,2},{4,7},{5,4},{6,5},{7,6},{8,11},{9,8},{10,9... | collective-permute-start | bytes 1622024 | tf_op jit(solution)/shard_map/ppermute | solution.py:36
  111.7 1.1 copy-start.3
  112.7 1.0 copy-start.5
  113.8 3.4 %copy-start.7 = (f32[4,8,32,16,128]{4,3,2,1,0:T(8,128)S(1)}, f32[4,8,32,16,128]{4,3,2,1,0:T(8,128)}, u32[]{:S(2)}) copy-start(f32[4,8,32,16,128]{4,3,2,1,0:T(8,128)} %copy-done.6) | copy-start | bytes 25165828
  121.0 13.8 %collective-permute-start.19 = (s16[4,33,16,128]{3,2,1,0:T(8,128)(2,1)S(1)}, s16[4,33,16,128]{3,2,1,0:T(8,128)(2,1)S(1)}, u32[]{:S(2)}, u32[]{:S(2)}) collective-permute-start(s16[4,33,16,128]{3,2,1,0:T(8,128)(2,1)S(1)} %get-tuple-element.54), channel_id=1, source_target_pairs={{0,1},{1,2},{2,3},{3,0},{4,5},{5,6},{6,7},{7,4},{8,9},{9,10},{10,1... | collective-permute-start | bytes 1622024 | tf_op jit(solution)/shard_map/ppermute | solution.py:36
  121.1 13.7 %collective-permute-start.20 = (s16[4,33,16,128]{3,2,1,0:T(8,128)(2,1)S(1)}, s16[4,33,16,128]{3,2,1,0:T(8,128)(2,1)S(1)}, u32[]{:S(2)}, u32[]{:S(2)}) collective-permute-start(s16[4,33,16,128]{3,2,1,0:T(8,128)(2,1)S(1)} %get-tuple-element.55), channel_id=1, source_target_pairs={{0,3},{1,0},{2,1},{3,2},{4,7},{5,4},{6,5},{7,6},{8,11},{9,8},{10,9... | collective-permute-start | bytes 1622024 | tf_op jit(solution)/shard_map/ppermute | solution.py:36
  128.7 9.5 %collective-permute-start.18 = (s16[4,33,16,128]{3,2,1,0:T(8,128)(2,1)S(1)}, s16[4,33,16,128]{3,2,1,0:T(8,128)(2,1)S(1)}, u32[]{:S(2)}, u32[]{:S(2)}) collective-permute-start(s16[4,33,16,128]{3,2,1,0:T(8,128)(2,1)S(1)} %get-tuple-element.53), channel_id=1, source_target_pairs={{0,1},{1,2},{2,3},{3,0},{4,5},{5,6},{6,7},{7,4},{8,9},{9,10},{10,1... | collective-permute-start | bytes 1622024 | tf_op jit(solution)/shard_map/ppermute | solution.py:36
  128.7 9.4 %collective-permute-start.21 = (s16[4,33,16,128]{3,2,1,0:T(8,128)(2,1)S(1)}, s16[4,33,16,128]{3,2,1,0:T(8,128)(2,1)S(1)}, u32[]{:S(2)}, u32[]{:S(2)}) collective-permute-start(s16[4,33,16,128]{3,2,1,0:T(8,128)(2,1)S(1)} %get-tuple-element.56), channel_id=1, source_target_pairs={{0,3},{1,0},{2,1},{3,2},{4,7},{5,4},{6,5},{7,6},{8,11},{9,8},{10,9... | collective-permute-start | bytes 1622024 | tf_op jit(solution)/shard_map/ppermute | solution.py:36
  (1 other events, 0.6 us)

commit v9 on v8

--- a/solution.py
+++ b/solution.py
@@ -130,8 +130,8 @@
         regroup_kernel,
         grid_spec=pltpu.PrefetchScalarGridSpec(
             num_scalar_prefetch=1, grid=(1,),
-            in_specs=[pl.BlockSpec((16, 4, 128, 128), lambda i, *_: (0, 0, 0, 0), pipeline_mode=pl.Buffered(1))] * 2,
-            out_specs=[pl.BlockSpec(memory_space=pl.ANY)] * 5,
+            in_specs=[pl.BlockSpec(memory_space=pl.ANY)] * 2,
+            out_specs=[pl.BlockSpec(s, lambda i, *_: (0,) * 5, pipeline_mode=pl.Buffered(1)) for s in shapes],
             scratch_shapes=[pltpu.SemaphoreType.DMA((32,))],
         ),
         out_shape=[jax.ShapeDtypeStruct(shape, jnp.bfloat16) for shape in shapes],
@@ -381,23 +381,26 @@
     )(slots, *parts)
 
 
-def unpack_kernel(r_ref, o_ref, full):
+def unpack_kernel(r_ref, o_ref, full, scales):
     low32 = (lax.broadcasted_iota(jnp.int32, (16, 128), 1) & 32) == 0
-    for s in range(2):
-        def one(n, _):
-            scales = [decoded_scale(r_ref[0, c, n, 64:80, :]) for c in range(2)]
+    for n in range(16):
+        for c in range(2):
+            scales[n * 2 + c] = decoded_scale(r_ref[0, c, n, 64:80, :])[:8]
+
+    def one(n, _):
+        for s in range(2):
             for t in range(2):
                 h = []
                 for c in range(2):
                     at = (s * 2 + t) * 16
                     q = r_ref[0, c, n, at:at + 16, :].astype(jnp.int32).astype(jnp.float32)
-                    h.append(q * scales[c][s * 2 + t:s * 2 + t + 1, :])
+                    h.append(q * scales[n * 2 + c, s * 2 + t:s * 2 + t + 1, :])
                 base = pl.multiple_of(((s * 16 + n) * 2 + t) * 32, 32)
                 full[pl.ds(base, 16), :] = jnp.where(low32, h[0], pltpu.roll(h[1], 32, 1))
                 full[pl.ds(base + 16, 16), :] = jnp.where(low32, pltpu.roll(h[0], 96, 1), h[1])
-            return 0
-
-        lax.fori_loop(0, 16, one, 0, unroll=4)
+        return 0
+
+    lax.fori_loop(0, 16, one, 0, unroll=4)
     for p in range(32):
         o_ref[:, p * 128:(p + 1) * 128] = full[pl.ds(p, 64, stride=32), :]
 
@@ -409,7 +412,7 @@
         in_specs=[pl.BlockSpec((1, C, 16, MSG, 128), lambda x: (x, 0, 0, 0, 0))],
         out_specs=pl.BlockSpec((64, 4096), lambda x: (x, 0)),
         out_shape=jax.ShapeDtypeStruct((256, 4096), jnp.float32),
-        scratch_shapes=[pltpu.VMEM((64 * 32, 128), jnp.float32)],
+        scratch_shapes=[pltpu.VMEM((64 * 32, 128), jnp.float32), pltpu.VMEM((32, 8, 128), jnp.float32)],
         compiler_params=pltpu.CompilerParams(vmem_limit_bytes=32 << 20),
         name="unpack",
     )(received)
@@ -433,18 +436,12 @@
     mine, theirs = split(at, dens, ints)
     shard = jnp.concatenate([mine, over_core(theirs)])
     shard, kohn, kohn_other = lax.optimization_barrier((shard, kohn, kohn_other))
-    left, right = over_x(shard, 1), over_x(shard, -1)
+    left, right, far = over_x(shard, 1), over_x(shard, -1), over_x(shard, 2)
 
     kohn, ahead, back, opposite0, opposite1 = regroup(at, kohn, kohn_other)
     opposite0, opposite1 = over_line(opposite0, 1), over_line(opposite1, -1)
     kohn_prev, kohn_next = over_line(ahead, 1), over_line(back, -1)
     opposite0, opposite1 = over_line(opposite0, 1), over_line(opposite1, -1)
-
-    panel = jnp.concatenate([shard, left, right, over_x(left[:PART], 1), over_x(right[PART:], -1)])
-    sent, kohn_prev, kohn_next, opposite0, opposite1 = lax.optimization_barrier(
-        (panel, kohn_prev, kohn_next, opposite0, opposite1)
-    )
-    prev, after = over_line(sent, 1), over_line(sent, -1)
 
     owners = jnp.stack([owner_map.reshape(128), shard[PART + 8 * 128 + 3].astype(jnp.int32)])
     hit = (owners[..., None] == jnp.arange(128, dtype=jnp.int32)).astype(jnp.int32)
@@ -452,15 +449,23 @@
     source = jnp.arange(2, dtype=jnp.int32)[:, None] ^ c
     slots = (owners * 4 + source * 2 + ranks).reshape(-1)
 
+    low, high = jnp.concatenate([shard, left]), jnp.concatenate([right, far])
+    low_sent, high_sent, kohn_prev, kohn_next, slots = lax.optimization_barrier((low, high, kohn_prev, kohn_next, slots))
+    prev_low, next_high = over_line(low_sent, 1), over_line(high_sent, -1)
+    prev_high, next_low = over_line(high_sent, 1), over_line(low_sent, -1)
+
     def both(array):
         return [(array, 0), (array, 1)]
 
     everything = tuple((target, m) for target in range(4) for m in range(2))
-    sums, = panel_sums("own_panel", "first", at, both(kohn), [panel], everything, us=9.0)
-    prev, after, sums = lax.optimization_barrier((prev, after, sums))
-    far_low, far_high = over_line(prev[:4 * PART], 1), over_line(after[4 * PART:], -1)
+    sums, = panel_sums("own_panel", "first", at, both(kohn), [low, high], everything, us=9.0)
+    prev_low, next_high, opposite0, opposite1, sums = lax.optimization_barrier(
+        (prev_low, next_high, opposite0, opposite1, sums)
+    )
+    far_low, far_high = over_line(prev_low, 1), over_line(next_high, -1)
     sums, = panel_sums(
-        "near_panels", "more", at, both(kohn_prev) + both(kohn_next), [prev, after], everything, sums, us=16.0
+        "near_panels", "more", at, both(kohn_prev) + both(kohn_next), [prev_low, prev_high, next_low, next_high],
+        everything, sums, us=16.0,
     )
 
     def last(form, halves, received=()):

time: 199 us -> 195 us (0.980)
  starting transfers between devices: 26.3 us -> 34.3 us
  Pallas kernels: 65.8 us -> 59.4 us
  local copies, waits for them, and re-layouts: 10.7 us -> 6.48 us
  blocking collectives: 48 us -> 45.9 us
    ppermute x16 -> x18, starting transfers between devices: 21.9 us -> 28.4 us  [over(): lax.ppermute(v, PLANE, [(group[i], group[(i + step) % 4]) for group in gr...]
    unnamed x27 -> x11, local copies, waits for them, and re-layouts: 6.39 us -> 1.22 us
    pallas_call x1, Pallas kernels: 8.42 us -> 4.97 us  [regroup(): pl.pallas_call(regroup_kernel, grid_spec=pltpu.PrefetchScalarGridSpec(num...]
    ppermute x4 -> x3, waiting for transfers between devices: 12 us -> 14.3 us  [over_x(): return lax.ppermute(v, 'x', [(i, (i + step) % X) for i in range(X)])]
    all_to_all x1, blocking collectives: 48 us -> 45.9 us  [local(): lax.all_to_all(outgoing, ALL, split_axis=0, concat_axis=0, tiled=True)]
    ppermute x16 -> x18, waiting for transfers between devices: 31.4 us -> 29.4 us  [over(): lax.ppermute(v, PLANE, [(group[i], group[(i + step) % 4]) for group in gr...]
    ppermute x4 -> x3, starting transfers between devices: 2.88 us -> 4.37 us  [over_x(): return lax.ppermute(v, 'x', [(i, (i + step) % X) for i in range(X)])]
  transfers between devices with their start and end apart: 22 -> 23, of which waited for: 9 -> 7; matrix products, arithmetic and copies ran while one was open for 2% -> 3% of each run, Pallas kernels for 24% -> 23%
where the time goes in v9:
time: 195 us
  Pallas kernels  59.4 us (30%)
  blocking collectives  45.9 us (24%)
  waiting for transfers between devices  45.4 us (23%)
  starting transfers between devices  34.3 us (18%)
  local copies, waits for them, and re-layouts  6.48 us (3%)
  other arithmetic  2.87 us (1%)
    all_to_all x1, blocking collectives, local(): lax.all_to_all(outgoing, ALL, split_axis=0, concat_axis=0, tiled=True)  45.9 us
    pallas_call x6, Pallas kernels, panel_sums(): pl.pallas_call(lambda *refs: panel_kernel(n, pieces, halves, form, *refs)...  37.4 us
    ppermute x18, waiting for transfers between devices, over(): lax.ppermute(v, PLANE, [(group[i], group[(i + step) % 4]) for group in gr...  29.4 us
    ppermute x18, starting transfers between devices, over(): lax.ppermute(v, PLANE, [(group[i], group[(i + step) % 4]) for group in gr...  28.4 us
    ppermute x3, waiting for transfers between devices, over_x(): return lax.ppermute(v, 'x', [(i, (i + step) % X) for i in range(X)])  14.3 us
    pallas_call x1, Pallas kernels, pack(): pl.pallas_call(pack_kernel, grid_spec=pltpu.PrefetchScalarGridSpec(num_sc...  5.87 us
    pallas_call x1, Pallas kernels, unpack(): pl.pallas_call(unpack_kernel, grid=(X,), in_specs=[pl.BlockSpec((1, C, 16...  5.77 us
    pallas_call x1, Pallas kernels, split(): pl.pallas_call(split_kernel, grid_spec=pltpu.PrefetchScalarGridSpec(num_s...  5.36 us
  transfers between devices with their start and end apart: 23, of which 7 were waited for; matrix products, arithmetic and copies ran while one was open for 3% of the time, Pallas kernels for 23%

profile of v9, /device:TPU:1, one launch (start us, length us, event | category | flops | bytes accessed | tf_op | source)
XLA Modules:
  0.0 194.6 jit_solution(7100532617727929001)
XLA Ops:
  0.0 3.8 %reshape.33.mine = bf16[16,4,128,128]{3,2,1,0:T(8,128)(2,1)S(1)} reshape(bf16[64,1,4,4096]{3,2,1,0:T(4,128)(2,1)} %param.5) | data formatting | bytes 4194304 | tf_op jit(solution)/shard_map/reshape | solution.py:427
  3.8 1.5 collective-permute-start.1
  7.0 5.4 %split.1 = (bf16[1040,128]{1,0:T(8,128)(2,1)}, bf16[1040,128]{1,0:T(8,128)(2,1)}) custom-call(s32[4]{0:T(128)} %pad_add_fusion.2.core.at.refs_0_, bf16[8,8,4096]{2,1,0:T(8,128)(2,1)} %bitcast.12, s32[16,128]{1,0:T(8,128)} %fusion.2.i_ref), custom_call_target="tpu_custom_call" | custom-call | tf_op jit(solution)/shard_map/split/pallas_call | solution.py:95
  12.4 1.7 collective-permute-done
  15.2 2.9 %collective-permute-start.4 = (bf16[2080,128]{1,0:T(8,128)(2,1)S(1)}, bf16[2080,128]{1,0:T(8,128)(2,1)S(1)}, u32[]{:S(2)}, u32[]{:S(2)}) collective-permute-start(bf16[2080,128]{1,0:T(8,128)(2,1)S(1)} %pad_maximum_fusion), channel_id=1, source_target_pairs={{0,64},{32,96},{64,0},{96,32},{1,65},{33,97},{65,1},{97,33},{2,66}... | collective-permute-start | bytes 1597448 | tf_op jit(solution)/shard_map/ppermute | solution.py:48
  20.0 5.0 %regroup.1 = (bf16[2,4,4,128,128]{4,3,2,1,0:T(8,128)(2,1)S(1)}, bf16[2,4,4,128,128]{4,3,2,1,0:T(8,128)(2,1)S(1)}, bf16[2,4,4,128,128]{4,3,2,1,0:T(8,128)(2,1)S(1...) custom-call(s32[4]{0:T(128)S(1)} %copy-done, bf16[16,4,128,128]{3,2,1,0:T(8,128)(2,1)S(1)} %reshape.33.mine, ...), custom_call_target="tpu_custom_call" | custom-call | tf_op jit(solution)/shard_map/regroup/pallas_call | solution.py:129
  25.0 1.4 collective-permute-start.9
  26.4 1.3 collective-permute-start.5
  27.8 14.3 %collective-permute-done.3 = bf16[2080,128]{1,0:T(8,128)(2,1)} collective-permute-done((bf16[2080,128]{1,0:T(8,128)(2,1)S(1)}, bf16[2080,128]{1,0:T(8,128)(2,1)}, u32[]{:S(2)}, u32[]{:S(2)}) %collective-permute-start.3) | collective-permute-done | bytes 532512 | tf_op jit(solution)/shard_map/ppermute | solution.py:48
  42.0 2.7 %collective-permute-start.6 = (bf16[2,4,4,128,128]{4,3,2,1,0:T(8,128)(2,1)S(1)}, bf16[2,4,4,128,128]{4,3,2,1,0:T(8,128)(2,1)S(1)}, u32[]{:S(2)}, u32[]{:S(2)}) collective-permute-start(bf16[2,4,4,128,128]{4,3,2,1,0:T(8,128)(2,1)S(1)} %get-tuple-element.41), channel_id=1, source_target_pairs={{0,12},{4,0},{8,4},{12,8},{1,13},{5,1},{9,5},{13,9},{2,14},{6,2},{... | collective-permute-start | bytes 3145736 | tf_op jit(solution)/shard_map/ppermute | solution.py:36
  44.8 1.1 constant_dynamic-update-slice_fusion.3
  47.5 1.1 constant_dynamic-update-slice_fusion.refs_3_
  48.6 7.9 %collective-permute-done.6.refs_3_.refs_4_ = bf16[2,4,4,128,128]{4,3,2,1,0:T(8,128)(2,1)S(1)} collective-permute-done((bf16[2,4,4,128,128]{4,3,2,1,0:T(8,128)(2,1)S(1)}, bf16[2,4,4,128,128]{4,3,2,1,0:T(8,128)(2,1)S(1)}, u32[]{:S(2)}, u32[]{:S(2)}) %collective-permute-start.6) | collective-permute-done | bytes 1048608 | tf_op jit(solution)/shard_map/ppermute | solution.py:36
  57.3 2.7 %collective-permute-start.8 = (bf16[4160,128]{1,0:T(8,128)(2,1)S(1)}, bf16[4160,128]{1,0:T(8,128)(2,1)S(1)}, u32[]{:S(2)}, u32[]{:S(2)}) collective-permute-start(bf16[4160,128]{1,0:T(8,128)(2,1)S(1)} %constant_dynamic-update-slice_fusion.2.refs_4_), channel_id=1, source_target_pairs={{0,12},{4,0},{8,4},{12,8},{1,13},{5,1},{9,5},{13,9},{2,14},{6,2},{... | collective-permute-start | bytes 3194888 | tf_op jit(solution)/shard_map/ppermute | solution.py:36
  59.9 1.5 collective-permute-start.16
  62.9 2.4 %collective-permute-start.12 = (bf16[1,4,4,128,128]{4,3,2,1,0:T(8,128)(2,1)S(1)}, bf16[1,4,4,128,128]{4,3,2,1,0:T(8,128)(2,1)S(1)}, u32[]{:S(2)}, u32[]{:S(2)}) collective-permute-start(bf16[1,4,4,128,128]{4,3,2,1,0:T(8,128)(2,1)S(1)} %collective-permute-done.11), channel_id=1, source_target_pairs={{0,12},{4,0},{8,4},{12,8},{1,13},{5,1},{9,5},{13,9},{2,14},{6,2},{... | collective-permute-start | bytes 1572872 | tf_op jit(solution)/shard_map/ppermute | solution.py:36
  65.2 8.3 %own_panel.1.refs_9_ = f32[4,8,32,16,128]{4,3,2,1,0:T(8,128)S(1)} custom-call(s32[4]{0:T(128)S(1)} %copy-done, bf16[2,4,4,128,128]{4,3,2,1,0:T(8,128)(2,1)S(1)} %get-tuple-element.47.refs_1_.refs_2_, bf16[2,4,4,128,128]{4,3,2,1,0:T(8,128)(2,1)S(1)} %get-tuple-element.47.refs_1_.refs_2_, bf16[4160,128]{1,0:T(8,128)(2,1)S(1)} %constant_dynamic-update-slice_fusion.refs_3_, ...), custom_call_target="tpu_custom_call" | custom-call | flops 9900000256 | bytes 18000000 | tf_op jit(solution)/shard_map/own_panel/pallas_call | solution.py:275
  73.6 17.0 %collective-permute-done.12.refs_2_ = bf16[1,4,4,128,128]{4,3,2,1,0:T(8,128)(2,1)S(1)} collective-permute-done((bf16[1,4,4,128,128]{4,3,2,1,0:T(8,128)(2,1)S(1)}, bf16[1,4,4,128,128]{4,3,2,1,0:T(8,128)(2,1)S(1)}, u32[]{:S(2)}, u32[]{:S(2)}) %collective-permute-start.12) | collective-permute-done | bytes 524320 | tf_op jit(solution)/shard_map/ppermute | solution.py:36
  91.3 2.6 %collective-permute-start.14 = (bf16[4160,128]{1,0:T(8,128)(2,1)S(1)}, bf16[4160,128]{1,0:T(8,128)(2,1)S(1)}, u32[]{:S(2)}, u32[]{:S(2)}) collective-permute-start(bf16[4160,128]{1,0:T(8,128)(2,1)S(1)} %collective-permute-done.8.refs_8_), channel_id=1, source_target_pairs={{0,12},{4,0},{8,4},{12,8},{1,13},{5,1},{9,5},{13,9},{2,14},{6,2},{... | collective-permute-start | bytes 3194888 | tf_op jit(solution)/shard_map/ppermute | solution.py:36
  93.9 14.2 %near_panels.1.refs_5_ = f32[4,8,32,16,128]{4,3,2,1,0:T(8,128)S(1)} custom-call(s32[4]{0:T(128)S(1)} %copy-done, bf16[2,4,4,128,128]{4,3,2,1,0:T(8,128)(2,1)S(1)} %collective-permute-done.5.refs_1_.refs_2_, bf16[2,4,4,128,128]{4,3,2,1,0:T(8,128)(2,1)S(1)} %collective-permute-done.5.refs_1_.refs_2_, ...), custom_call_target="tpu_custom_call" | custom-call | flops 17600000000 | bytes 32000000 | tf_op jit(solution)/shard_map/near_panels/pallas_call | solution.py:275
  108.2 3.9 %last_coded.2 = (s16[4,33,16,128]{3,2,1,0:T(8,128)(2,1)S(1)}, s16[4,33,16,128]{3,2,1,0:T(8,128)(2,1)S(1)}) custom-call(s32[4]{0:T(128)S(1)} %copy-done, bf16[1,4,4,128,128]{4,3,2,1,0:T(8,128)(2,1)S(1)} %collective-permute-done.10.refs_1_, bf16[1,4,4,128,128]{4,3,2,1,0:T(8,128)(2,1)S(1)} %collective-permute-done.12.refs_2_, ...), custom_call_target="tpu_custom_call" | custom-call | flops 4400000000 | bytes 8000000 | tf_op jit(solution)/shard_map/last_coded/pallas_call | solution.py:275
  112.1 1.7 collective-permute-start.17
  113.8 2.5 %collective-permute-start.18 = (s16[4,33,16,128]{3,2,1,0:T(8,128)(2,1)S(1)}, s16[4,33,16,128]{3,2,1,0:T(8,128)(2,1)S(1)}, u32[]{:S(2)}, u32[]{:S(2)}) collective-permute-start(s16[4,33,16,128]{3,2,1,0:T(8,128)(2,1)S(1)} %get-tuple-element.56), channel_id=1, source_target_pairs={{0,3},{1,0},{2,1},{3,2},{4,7},{5,4},{6,5},{7,6},{8,11},{9,8},{10,9... | collective-permute-start | bytes 1622024 | tf_op jit(solution)/shard_map/ppermute | solution.py:36
  116.3 3.8 %last_coded.3 = (s16[4,33,16,128]{3,2,1,0:T(8,128)(2,1)S(1)}, s16[4,33,16,128]{3,2,1,0:T(8,128)(2,1)S(1)}) custom-call(s32[4]{0:T(128)S(1)} %copy-done, bf16[1,4,4,128,128]{4,3,2,1,0:T(8,128)(2,1)S(1)} %collective-permute-done.10.refs_1_, bf16[1,4,4,128,128]{4,3,2,1,0:T(8,128)(2,1)S(1)} %collective-permute-done.12.refs_2_, ...), custom_call_target="tpu_custom_call" | custom-call | flops 4400000000 | bytes 8000000 | tf_op jit(solution)/shard_map/last_coded/pallas_call | solution.py:275
  120.2 2.7 %collective-permute-start.21 = (s16[4,33,16,128]{3,2,1,0:T(8,128)(2,1)S(1)}, s16[4,33,16,128]{3,2,1,0:T(8,128)(2,1)S(1)}, u32[]{:S(2)}, u32[]{:S(2)}) collective-permute-start(s16[4,33,16,128]{3,2,1,0:T(8,128)(2,1)S(1)} %get-tuple-element.59), channel_id=1, source_target_pairs={{0,3},{1,0},{2,1},{3,2},{4,7},{5,4},{6,5},{7,6},{8,11},{9,8},{10,9... | collective-permute-start | bytes 1622024 | tf_op jit(solution)/shard_map/ppermute | solution.py:36
  123.3 3.9 %last_sent.1 = (s16[4,33,16,128]{3,2,1,0:T(8,128)(2,1)S(1)}, s16[4,33,16,128]{3,2,1,0:T(8,128)(2,1)S(1)}) custom-call(s32[4]{0:T(128)S(1)} %copy-done, bf16[1,4,4,128,128]{4,3,2,1,0:T(8,128)(2,1)S(1)} %collective-permute-done.10.refs_1_, bf16[1,4,4,128,128]{4,3,2,1,0:T(8,128)(2,1)S(1)} %collective-permute-done.12.refs_2_, ...), custom_call_target="tpu_custom_call" | custom-call | flops 4400000000 | bytes 8000000 | tf_op jit(solution)/shard_map/last_sent/pallas_call | solution.py:275
  128.0 2.2 %collective-permute-start.22 = (s16[4,33,16,128]{3,2,1,0:T(8,128)(2,1)S(1)}, s16[4,33,16,128]{3,2,1,0:T(8,128)(2,1)S(1)}, u32[]{:S(2)}, u32[]{:S(2)}) collective-permute-start(s16[4,33,16,128]{3,2,1,0:T(8,128)(2,1)S(1)} %get-tuple-element.60), channel_id=1, source_target_pairs={{0,3},{1,0},{2,1},{3,2},{4,7},{5,4},{6,5},{7,6},{8,11},{9,8},{10,9... | collective-permute-start | bytes 1622024 | tf_op jit(solution)/shard_map/ppermute | solution.py:36
  130.3 3.3 %last_more.1.own = f32[1,8,32,16,128]{4,3,2,1,0:T(8,128)S(1)} custom-call(s32[4]{0:T(128)S(1)} %copy-done, bf16[1,4,4,128,128]{4,3,2,1,0:T(8,128)(2,1)S(1)} %collective-permute-done.10.refs_1_, bf16[1,4,4,128,128]{4,3,2,1,0:T(8,128)(2,1)S(1)} %collective-permute-done.12.refs_2_, bf16[4160,128]{1,0:T(8,128)(2,1)S(1)} %collective-permute-done.13.refs_3_, ...), custom_call_target="tpu_custom_call" | custom-call | flops 4400000000 | bytes 8000000 | tf_op jit(solution)/shard_map/last_more/pallas_call | solution.py:275
  133.6 3.4 %collective-permute-done.19.prev0 = s16[4,33,16,128]{3,2,1,0:T(8,128)(2,1)S(1)} collective-permute-done((s16[4,33,16,128]{3,2,1,0:T(8,128)(2,1)S(1)}, s16[4,33,16,128]{3,2,1,0:T(8,128)(2,1)S(1)}, u32[]{:S(2)}, u32[]{:S(2)}) %collective-permute-start.19) | collective-permute-done | bytes 540704 | tf_op jit(solution)/shard_map/ppermute | solution.py:36
  137.0 5.9 %pack.1 = s16[128,80,128]{2,1,0:T(8,128)(2,1)S(1)} custom-call(s32[256]{0:T(256)S(1)} %add_bitcast_fusion.slots, f32[1,8,32,16,128]{4,3,2,1,0:T(8,128)S(1)} %last_more.1.own, s16[4,33,16,128]{3,2,1,0:T(8,128)(2,1)S(1)} %collective-permute-done.19.prev0, s16[4,33,16,128]{3,2,1,0:T(8,128)(2,1)S(1)} %collective-permute-done.20.prev1, ...), custom_call_target="tpu_custom_call" | custom-call | tf_op jit(solution)/shard_map/pack/pallas_call | solution.py:369
  142.9 45.9 %all_to_all.5 = s16[128,80,128]{2,1,0:T(8,128)(2,1)S(1)} all-to-all(s16[128,80,128]{2,1,0:T(8,128)(2,1)S(1)} %pack.1), channel_id=1, replica_groups=mesh['x'=4,'core'=2,'z'=4,'y'=4] {'x','core','z','y'}, dimensions={0} | all-to-all | bytes 5242880 | tf_op jit(solution)/shard_map/all_to_all | solution.py:484
  188.8 5.8 %unpack.1 = f32[256,4096]{1,0:T(8,128)} custom-call(s16[4,2,16,80,128]{4,3,2,1,0:T(8,128)(2,1)S(1)} %bitcast.11), custom_call_target="tpu_custom_call" | custom-call | tf_op jit(solution)/shard_map/unpack/pallas_call | solution.py:409
  (53 shorter events, 10.8 us)
Async XLA Ops:
  0.0 5.3 %copy-start.2 = (s32[1,8,8]{2,1,0:T(8,128)S(1)}, s32[1,8,8]{2,1,0:T(8,128)}, u32[]{:S(2)}) copy-start(s32[1,8,8]{2,1,0:T(8,128)} %param.8) | copy-start | bytes 772
  0.0 5.5 %copy-start.3 = (s32[64,1,4]{0,2,1:T(4,128)S(1)}, s32[64,1,4]{0,2,1:T(4,128)}, u32[]{:S(2)}) copy-start(s32[64,1,4]{0,2,1:T(4,128)} %param.6) | copy-start | bytes 3076
  0.0 6.4 %copy-start.1 = (s32[128,1]{0,1:T(1,128)S(1)}, s32[128,1]{0,1:T(1,128)}, u32[]{:S(2)}) copy-start(s32[128,1]{0,1:T(1,128)} %param.9) | copy-start | bytes 1540
  3.8 11.3 %collective-permute-start.1 = (bf16[16,4,128,128]{3,2,1,0:T(8,128)(2,1)S(1)}, bf16[16,4,128,128]{3,2,1,0:T(8,128)(2,1)}, u32[]{:S(2)}, u32[]{:S(2)}) collective-permute-start(bf16[16,4,128,128]{3,2,1,0:T(8,128)(2,1)S(1)} %reshape.33.mine), channel_id=1, source_target_pairs={{0,16},{16,0},{1,17},{17,1},{2,18},{18,2},{3,19},{19,3},{4,20},{20... | collective-permute-start | bytes 6291464 | tf_op jit(solution)/shard_map/ppermute | solution.py:52
  7.0 13.0 %copy-start = (s32[4]{0:T(128)S(1)}, s32[4]{0:T(128)}, u32[]{:S(2)}) copy-start(s32[4]{0:T(128)} %pad_add_fusion.2.core.at.refs_0_) | copy-start | bytes 52
  12.4 1.8 collective-permute-start
  15.2 31.2 %collective-permute-start.4 = (bf16[2080,128]{1,0:T(8,128)(2,1)S(1)}, bf16[2080,128]{1,0:T(8,128)(2,1)S(1)}, u32[]{:S(2)}, u32[]{:S(2)}) collective-permute-start(bf16[2080,128]{1,0:T(8,128)(2,1)S(1)} %pad_maximum_fusion), channel_id=1, source_target_pairs={{0,64},{32,96},{64,0},{96,32},{1,65},{33,97},{65,1},{97,33},{2,66}... | collective-permute-start | bytes 1597448 | tf_op jit(solution)/shard_map/ppermute | solution.py:48
  18.1 24.0 %collective-permute-start.3 = (bf16[2080,128]{1,0:T(8,128)(2,1)S(1)}, bf16[2080,128]{1,0:T(8,128)(2,1)}, u32[]{:S(2)}, u32[]{:S(2)}) collective-permute-start(bf16[2080,128]{1,0:T(8,128)(2,1)S(1)} %pad_maximum_fusion), channel_id=1, source_target_pairs={{0,96},{32,0},{64,32},{96,64},{1,97},{33,1},{65,33},{97,65},{2,98}... | collective-permute-start | bytes 1597448 | tf_op jit(solution)/shard_map/ppermute | solution.py:48
  18.9 28.5 %collective-permute-start.2 = (bf16[2080,128]{1,0:T(8,128)(2,1)S(1)}, bf16[2080,128]{1,0:T(8,128)(2,1)}, u32[]{:S(2)}, u32[]{:S(2)}) collective-permute-start(bf16[2080,128]{1,0:T(8,128)(2,1)S(1)} %pad_maximum_fusion), channel_id=1, source_target_pairs={{0,32},{32,64},{64,96},{96,0},{1,33},{33,65},{65,97},{97,1},{2,34}... | collective-permute-start | bytes 1597448 | tf_op jit(solution)/shard_map/ppermute | solution.py:48
  25.0 20.8 %collective-permute-start.9 = (bf16[1,4,4,128,128]{4,3,2,1,0:T(8,128)(2,1)S(1)}, bf16[1,4,4,128,128]{4,3,2,1,0:T(8,128)(2,1)S(1)}, u32[]{:S(2)}, u32[]{:S(2)}) collective-permute-start(bf16[1,4,4,128,128]{4,3,2,1,0:T(8,128)(2,1)S(1)} %get-tuple-element.45), channel_id=1, source_target_pairs={{0,4},{4,8},{8,12},{12,0},{1,5},{5,9},{9,13},{13,1},{2,6},{6,10},{... | collective-permute-start | bytes 1572872 | tf_op jit(solution)/shard_map/ppermute | solution.py:36
  26.4 22.2 %collective-permute-start.5 = (bf16[2,4,4,128,128]{4,3,2,1,0:T(8,128)(2,1)S(1)}, bf16[2,4,4,128,128]{4,3,2,1,0:T(8,128)(2,1)S(1)}, u32[]{:S(2)}, u32[]{:S(2)}) collective-permute-start(bf16[2,4,4,128,128]{4,3,2,1,0:T(8,128)(2,1)S(1)} %get-tuple-element.40), channel_id=1, source_target_pairs={{0,4},{4,8},{8,12},{12,0},{1,5},{5,9},{9,13},{13,1},{2,6},{6,10},{... | collective-permute-start | bytes 3145736 | tf_op jit(solution)/shard_map/ppermute | solution.py:36
  42.0 14.5 %collective-permute-start.6 = (bf16[2,4,4,128,128]{4,3,2,1,0:T(8,128)(2,1)S(1)}, bf16[2,4,4,128,128]{4,3,2,1,0:T(8,128)(2,1)S(1)}, u32[]{:S(2)}, u32[]{:S(2)}) collective-permute-start(bf16[2,4,4,128,128]{4,3,2,1,0:T(8,128)(2,1)S(1)} %get-tuple-element.41), channel_id=1, source_target_pairs={{0,12},{4,0},{8,4},{12,8},{1,13},{5,1},{9,5},{13,9},{2,14},{6,2},{... | collective-permute-start | bytes 3145736 | tf_op jit(solution)/shard_map/ppermute | solution.py:36
  45.9 16.3 %collective-permute-start.11 = (bf16[1,4,4,128,128]{4,3,2,1,0:T(8,128)(2,1)S(1)}, bf16[1,4,4,128,128]{4,3,2,1,0:T(8,128)(2,1)S(1)}, u32[]{:S(2)}, u32[]{:S(2)}) collective-permute-start(bf16[1,4,4,128,128]{4,3,2,1,0:T(8,128)(2,1)S(1)} %get-tuple-element.46), channel_id=1, source_target_pairs={{0,12},{4,0},{8,4},{12,8},{1,13},{5,1},{9,5},{13,9},{2,14},{6,2},{... | collective-permute-start | bytes 1572872 | tf_op jit(solution)/shard_map/ppermute | solution.py:36
  46.4 16.5 %collective-permute-start.10 = (bf16[1,4,4,128,128]{4,3,2,1,0:T(8,128)(2,1)S(1)}, bf16[1,4,4,128,128]{4,3,2,1,0:T(8,128)(2,1)S(1)}, u32[]{:S(2)}, u32[]{:S(2)}) collective-permute-start(bf16[1,4,4,128,128]{4,3,2,1,0:T(8,128)(2,1)S(1)} %collective-permute-done.9), channel_id=1, source_target_pairs={{0,4},{4,8},{8,12},{12,0},{1,5},{5,9},{9,13},{13,1},{2,6},{6,10},{... | collective-permute-start | bytes 1572872 | tf_op jit(solution)/shard_map/ppermute | solution.py:36
  56.5 34.1 %collective-permute-start.7 = (bf16[4160,128]{1,0:T(8,128)(2,1)S(1)}, bf16[4160,128]{1,0:T(8,128)(2,1)S(1)}, u32[]{:S(2)}, u32[]{:S(2)}) collective-permute-start(bf16[4160,128]{1,0:T(8,128)(2,1)S(1)} %constant_dynamic-update-slice_fusion.refs_3_), channel_id=1, source_target_pairs={{0,4},{4,8},{8,12},{12,0},{1,5},{5,9},{9,13},{13,1},{2,6},{6,10},{... | collective-permute-start | bytes 3194888 | tf_op jit(solution)/shard_map/ppermute | solution.py:36
  57.3 33.3 %collective-permute-start.8 = (bf16[4160,128]{1,0:T(8,128)(2,1)S(1)}, bf16[4160,128]{1,0:T(8,128)(2,1)S(1)}, u32[]{:S(2)}, u32[]{:S(2)}) collective-permute-start(bf16[4160,128]{1,0:T(8,128)(2,1)S(1)} %constant_dynamic-update-slice_fusion.2.refs_4_), channel_id=1, source_target_pairs={{0,12},{4,0},{8,4},{12,8},{1,13},{5,1},{9,5},{13,9},{2,14},{6,2},{... | collective-permute-start | bytes 3194888 | tf_op jit(solution)/shard_map/ppermute | solution.py:36
  59.9 34.0 %collective-permute-start.16 = (bf16[4160,128]{1,0:T(8,128)(2,1)S(1)}, bf16[4160,128]{1,0:T(8,128)(2,1)S(1)}, u32[]{:S(2)}, u32[]{:S(2)}) collective-permute-start(bf16[4160,128]{1,0:T(8,128)(2,1)S(1)} %constant_dynamic-update-slice_fusion.refs_3_), channel_id=1, source_target_pairs={{0,12},{4,0},{8,4},{12,8},{1,13},{5,1},{9,5},{13,9},{2,14},{6,2},{... | collective-permute-start | bytes 3194888 | tf_op jit(solution)/shard_map/ppermute | solution.py:36
  62.1 31.8 %collective-permute-start.15 = (bf16[4160,128]{1,0:T(8,128)(2,1)S(1)}, bf16[4160,128]{1,0:T(8,128)(2,1)S(1)}, u32[]{:S(2)}, u32[]{:S(2)}) collective-permute-start(bf16[4160,128]{1,0:T(8,128)(2,1)S(1)} %constant_dynamic-update-slice_fusion.2.refs_4_), channel_id=1, source_target_pairs={{0,4},{4,8},{8,12},{12,0},{1,5},{5,9},{9,13},{13,1},{2,6},{6,10},{... | collective-permute-start | bytes 3194888 | tf_op jit(solution)/shard_map/ppermute | solution.py:36
  62.9 27.7 %collective-permute-start.12 = (bf16[1,4,4,128,128]{4,3,2,1,0:T(8,128)(2,1)S(1)}, bf16[1,4,4,128,128]{4,3,2,1,0:T(8,128)(2,1)S(1)}, u32[]{:S(2)}, u32[]{:S(2)}) collective-permute-start(bf16[1,4,4,128,128]{4,3,2,1,0:T(8,128)(2,1)S(1)} %collective-permute-done.11), channel_id=1, source_target_pairs={{0,12},{4,0},{8,4},{12,8},{1,13},{5,1},{9,5},{13,9},{2,14},{6,2},{... | collective-permute-start | bytes 1572872 | tf_op jit(solution)/shard_map/ppermute | solution.py:36
  90.6 17.6 %collective-permute-start.13 = (bf16[4160,128]{1,0:T(8,128)(2,1)S(1)}, bf16[4160,128]{1,0:T(8,128)(2,1)S(1)}, u32[]{:S(2)}, u32[]{:S(2)}) collective-permute-start(bf16[4160,128]{1,0:T(8,128)(2,1)S(1)} %collective-permute-done.7.refs_5_), channel_id=1, source_target_pairs={{0,4},{4,8},{8,12},{12,0},{1,5},{5,9},{9,13},{13,1},{2,6},{6,10},{... | collective-permute-start | bytes 3194888 | tf_op jit(solution)/shard_map/ppermute | solution.py:36
  91.3 16.9 %collective-permute-start.14 = (bf16[4160,128]{1,0:T(8,128)(2,1)S(1)}, bf16[4160,128]{1,0:T(8,128)(2,1)S(1)}, u32[]{:S(2)}, u32[]{:S(2)}) collective-permute-start(bf16[4160,128]{1,0:T(8,128)(2,1)S(1)} %collective-permute-done.8.refs_8_), channel_id=1, source_target_pairs={{0,12},{4,0},{8,4},{12,8},{1,13},{5,1},{9,5},{13,9},{2,14},{6,2},{... | collective-permute-start | bytes 3194888 | tf_op jit(solution)/shard_map/ppermute | solution.py:36
  112.1 11.2 %collective-permute-start.17 = (s16[4,33,16,128]{3,2,1,0:T(8,128)(2,1)S(1)}, s16[4,33,16,128]{3,2,1,0:T(8,128)(2,1)S(1)}, u32[]{:S(2)}, u32[]{:S(2)}) collective-permute-start(s16[4,33,16,128]{3,2,1,0:T(8,128)(2,1)S(1)} %get-tuple-element.55), channel_id=1, source_target_pairs={{0,1},{1,2},{2,3},{3,0},{4,5},{5,6},{6,7},{7,4},{8,9},{9,10},{10,1... | collective-permute-start | bytes 1622024 | tf_op jit(solution)/shard_map/ppermute | solution.py:36
  113.8 9.5 %collective-permute-start.18 = (s16[4,33,16,128]{3,2,1,0:T(8,128)(2,1)S(1)}, s16[4,33,16,128]{3,2,1,0:T(8,128)(2,1)S(1)}, u32[]{:S(2)}, u32[]{:S(2)}) collective-permute-start(s16[4,33,16,128]{3,2,1,0:T(8,128)(2,1)S(1)} %get-tuple-element.56), channel_id=1, source_target_pairs={{0,3},{1,0},{2,1},{3,2},{4,7},{5,4},{6,5},{7,6},{8,11},{9,8},{10,9... | collective-permute-start | bytes 1622024 | tf_op jit(solution)/shard_map/ppermute | solution.py:36
  120.1 13.4 %collective-permute-start.20 = (s16[4,33,16,128]{3,2,1,0:T(8,128)(2,1)S(1)}, s16[4,33,16,128]{3,2,1,0:T(8,128)(2,1)S(1)}, u32[]{:S(2)}, u32[]{:S(2)}) collective-permute-start(s16[4,33,16,128]{3,2,1,0:T(8,128)(2,1)S(1)} %get-tuple-element.58), channel_id=1, source_target_pairs={{0,1},{1,2},{2,3},{3,0},{4,5},{5,6},{6,7},{7,4},{8,9},{9,10},{10,1... | collective-permute-start | bytes 1622024 | tf_op jit(solution)/shard_map/ppermute | solution.py:36
  120.2 13.3 %collective-permute-start.21 = (s16[4,33,16,128]{3,2,1,0:T(8,128)(2,1)S(1)}, s16[4,33,16,128]{3,2,1,0:T(8,128)(2,1)S(1)}, u32[]{:S(2)}, u32[]{:S(2)}) collective-permute-start(s16[4,33,16,128]{3,2,1,0:T(8,128)(2,1)S(1)} %get-tuple-element.59), channel_id=1, source_target_pairs={{0,3},{1,0},{2,1},{3,2},{4,7},{5,4},{6,5},{7,6},{8,11},{9,8},{10,9... | collective-permute-start | bytes 1622024 | tf_op jit(solution)/shard_map/ppermute | solution.py:36
  127.1 9.9 %collective-permute-start.19 = (s16[4,33,16,128]{3,2,1,0:T(8,128)(2,1)S(1)}, s16[4,33,16,128]{3,2,1,0:T(8,128)(2,1)S(1)}, u32[]{:S(2)}, u32[]{:S(2)}) collective-permute-start(s16[4,33,16,128]{3,2,1,0:T(8,128)(2,1)S(1)} %get-tuple-element.57), channel_id=1, source_target_pairs={{0,1},{1,2},{2,3},{3,0},{4,5},{5,6},{6,7},{7,4},{8,9},{9,10},{10,1... | collective-permute-start | bytes 1622024 | tf_op jit(solution)/shard_map/ppermute | solution.py:36
  128.0 8.9 %collective-permute-start.22 = (s16[4,33,16,128]{3,2,1,0:T(8,128)(2,1)S(1)}, s16[4,33,16,128]{3,2,1,0:T(8,128)(2,1)S(1)}, u32[]{:S(2)}, u32[]{:S(2)}) collective-permute-start(s16[4,33,16,128]{3,2,1,0:T(8,128)(2,1)S(1)} %get-tuple-element.60), channel_id=1, source_target_pairs={{0,3},{1,0},{2,1},{3,2},{4,7},{5,4},{6,5},{7,6},{8,11},{9,8},{10,9... | collective-permute-start | bytes 1622024 | tf_op jit(solution)/shard_map/ppermute | solution.py:36

commit v10 on v9

--- a/solution.py
+++ b/solution.py
@@ -107,7 +107,7 @@
     )(core, dens, ints)
 
 
-def regroup_kernel(at, mine, other, own, ahead, back, far0, far1, sems):
+def regroup_kernel(at, mine, other, own, ahead, back, sems):
     swapped, line, cross = at[0] == 1, at[1], at[2]
     copies = []
     for step in range(4):
@@ -116,7 +116,7 @@
             o = (cross + rel) % 4
             row = jnp.where(swapped, o * 4 + t, t * 4 + o)
             for m, src in enumerate((mine, other)):
-                dst = (own.at[m, i], ahead.at[m, i], (far0, far1)[m].at[0, i], back.at[m, i])[step]
+                dst = (own.at[m, i], ahead.at[m, i], (ahead, back)[m].at[2, i], back.at[m, i])[step]
                 copies.append(pltpu.make_async_copy(src.at[row], dst, sems.at[len(copies)]))
     for copy in copies:
         copy.start()
@@ -125,7 +125,7 @@
 
 
 def regroup(at, mine, other):
-    shapes = [(2, 4, 4, 128, 128)] * 3 + [(1, 4, 4, 128, 128)] * 2
+    shapes = [(2, 4, 4, 128, 128), (3, 4, 4, 128, 128), (3, 4, 4, 128, 128)]
     return pl.pallas_call(
         regroup_kernel,
         grid_spec=pltpu.PrefetchScalarGridSpec(
@@ -436,12 +436,11 @@
     mine, theirs = split(at, dens, ints)
     shard = jnp.concatenate([mine, over_core(theirs)])
     shard, kohn, kohn_other = lax.optimization_barrier((shard, kohn, kohn_other))
-    left, right, far = over_x(shard, 1), over_x(shard, -1), over_x(shard, 2)
-
-    kohn, ahead, back, opposite0, opposite1 = regroup(at, kohn, kohn_other)
-    opposite0, opposite1 = over_line(opposite0, 1), over_line(opposite1, -1)
+    left, right = over_x(shard, 1), over_x(shard, -1)
+
+    kohn, ahead, back = regroup(at, kohn, kohn_other)
     kohn_prev, kohn_next = over_line(ahead, 1), over_line(back, -1)
-    opposite0, opposite1 = over_line(opposite0, 1), over_line(opposite1, -1)
+    opposite0, opposite1 = over_line(kohn_prev[2:], 1), over_line(kohn_next[2:], -1)
 
     owners = jnp.stack([owner_map.reshape(128), shard[PART + 8 * 128 + 3].astype(jnp.int32)])
     hit = (owners[..., None] == jnp.arange(128, dtype=jnp.int32)).astype(jnp.int32)
@@ -449,7 +448,8 @@
     source = jnp.arange(2, dtype=jnp.int32)[:, None] ^ c
     slots = (owners * 4 + source * 2 + ranks).reshape(-1)
 
-    low, high = jnp.concatenate([shard, left]), jnp.concatenate([right, far])
+    low = jnp.concatenate([shard, left])
+    high = jnp.concatenate([right, over_x(left[:PART], 1), over_x(right[PART:], -1)])
     low_sent, high_sent, kohn_prev, kohn_next, slots = lax.optimization_barrier((low, high, kohn_prev, kohn_next, slots))
     prev_low, next_high = over_line(low_sent, 1), over_line(high_sent, -1)
     prev_high, next_low = over_line(high_sent, 1), over_line(low_sent, -1)
@@ -459,14 +459,14 @@
 
     everything = tuple((target, m) for target in range(4) for m in range(2))
     sums, = panel_sums("own_panel", "first", at, both(kohn), [low, high], everything, us=9.0)
-    prev_low, next_high, opposite0, opposite1, sums = lax.optimization_barrier(
-        (prev_low, next_high, opposite0, opposite1, sums)
-    )
+    prev_low, next_high, sums = lax.optimization_barrier((prev_low, next_high, sums))
     far_low, far_high = over_line(prev_low, 1), over_line(next_high, -1)
     sums, = panel_sums(
         "near_panels", "more", at, both(kohn_prev) + both(kohn_next), [prev_low, prev_high, next_low, next_high],
         everything, sums, us=16.0,
     )
+
+    sums, opposite0, opposite1 = lax.optimization_barrier((sums, opposite0, opposite1))
 
     def last(form, halves, received=()):
         kohn = [(opposite0, 0), (opposite1, 0)]

time: 195 us -> 179 us (0.918)
  waiting for transfers between devices: 45.4 us -> 27.8 us
  starting transfers between devices: 34.3 us -> 28 us
  local copies, waits for them, and re-layouts: 6.48 us -> 10.7 us
    ppermute x3 -> x4, waiting for transfers between devices: 14.3 us -> 1.07 us  [over_x(): return lax.ppermute(v, 'x', [(i, (i + step) % X) for i in range(X)])]
    ppermute x18 -> x16, starting transfers between devices: 28.4 us -> 20.9 us  [over(): lax.ppermute(v, PLANE, [(group[i], group[(i + step) % 4]) for group in gr...]
    ppermute x18 -> x16, waiting for transfers between devices: 29.4 us -> 25.1 us  [over(): lax.ppermute(v, PLANE, [(group[i], group[(i + step) % 4]) for group in gr...]
    unnamed x11 -> x16, local copies, waits for them, and re-layouts: 1.22 us -> 3.32 us
    slice x0 -> x4, local copies, waits for them, and re-layouts: none -> 2.02 us  [the longest x1 0.97 us: local(): left[:PART]]
    ppermute x3 -> x4, starting transfers between devices: 4.37 us -> 5.49 us  [over_x(): return lax.ppermute(v, 'x', [(i, (i + step) % X) for i in range(X)])]
  transfers between devices with their start and end apart: 23 -> 22, of which waited for: 7 -> 9; matrix products, arithmetic and copies ran while one was open for 3% -> 6% of each run, Pallas kernels for 23% -> 25%
where the time goes in v10:
time: 179 us; the launch traced here: 178 us
  Pallas kernels  60.5 us (34%)
  blocking collectives  46.7 us (26%)
  starting transfers between devices  28 us (16%)
  waiting for transfers between devices  27.8 us (16%)
  local copies, waits for them, and re-layouts  10.7 us (6%)
  other arithmetic  4.28 us (2%)
    all_to_all x1, blocking collectives, local(): lax.all_to_all(outgoing, ALL, split_axis=0, concat_axis=0, tiled=True)  46.7 us
    pallas_call x6, Pallas kernels, panel_sums(): pl.pallas_call(lambda *refs: panel_kernel(n, pieces, halves, form, *refs)...  37.4 us
    ppermute x16, waiting for transfers between devices, over(): lax.ppermute(v, PLANE, [(group[i], group[(i + step) % 4]) for group in gr...  25.1 us
    ppermute x16, starting transfers between devices, over(): lax.ppermute(v, PLANE, [(group[i], group[(i + step) % 4]) for group in gr...  20.9 us
    pallas_call x1, Pallas kernels, regroup(): pl.pallas_call(regroup_kernel, grid_spec=pltpu.PrefetchScalarGridSpec(num...  6.2 us
    pallas_call x1, Pallas kernels, pack(): pl.pallas_call(pack_kernel, grid_spec=pltpu.PrefetchScalarGridSpec(num_sc...  5.87 us
    pallas_call x1, Pallas kernels, unpack(): pl.pallas_call(unpack_kernel, grid=(X,), in_specs=[pl.BlockSpec((1, C, 16...  5.77 us
    ppermute x4, starting transfers between devices, over_x(): return lax.ppermute(v, 'x', [(i, (i + step) % X) for i in range(X)])  5.49 us
  transfers between devices with their start and end apart: 22, of which 9 were waited for; matrix products, arithmetic and copies ran while one was open for 6% of the time, Pallas kernels for 25%

profile of v10, /device:TPU:1, one launch (start us, length us, event | category | flops | bytes accessed | tf_op | source)
XLA Modules:
  0.0 178.1 jit_solution(2201895268205279893)
XLA Ops:
  0.0 3.8 %reshape.33.mine = bf16[16,4,128,128]{3,2,1,0:T(8,128)(2,1)S(1)} reshape(bf16[64,1,4,4096]{3,2,1,0:T(4,128)(2,1)} %param.5) | data formatting | bytes 4194304 | tf_op jit(solution)/shard_map/reshape | solution.py:427
  3.8 1.5 collective-permute-start.1
  6.9 5.2 %split.1 = (bf16[1040,128]{1,0:T(8,128)(2,1)}, bf16[1040,128]{1,0:T(8,128)(2,1)}) custom-call(s32[4]{0:T(128)} %pad_add_fusion.2.core.at.refs_0_, bf16[8,8,4096]{2,1,0:T(8,128)(2,1)} %bitcast.12, s32[16,128]{1,0:T(8,128)} %fusion.2.i_ref), custom_call_target="tpu_custom_call" | custom-call | tf_op jit(solution)/shard_map/split/pallas_call | solution.py:95
  12.2 1.7 collective-permute-done
  13.9 1.8 %pad_maximum_fusion = bf16[2080,128]{1,0:T(8,128)(2,1)} fusion(bf16[1040,128]{1,0:T(8,128)(2,1)S(1)} %collective-permute-done, bf16[1040,128]{1,0:T(8,128)(2,1)} %get-tuple-element.33), kind=kLoop, calls=%fused_computation | loop fusion | flops 1064960 | bytes 1064960 | tf_op jit(solution)/shard_map/concatenate | solution.py:437
  17.0 1.4 collective-permute-start.3
  19.1 6.2 %regroup.1 = (bf16[2,4,4,128,128]{4,3,2,1,0:T(8,128)(2,1)S(1)}, bf16[3,4,4,128,128]{4,3,2,1,0:T(8,128)(2,1)}, bf16[3,4,4,128,128]{4,3,2,1,0:T(8,128)(2,1)}) custom-call(s32[4]{0:T(128)S(1)} %copy-done, bf16[16,4,128,128]{3,2,1,0:T(8,128)(2,1)S(1)} %reshape.33.mine, bf16[16,4,128,128]{3,2,1,0:T(8,128)(2,1)} %collective-permute-done.1.other), custom_call_target="tpu_custom_call" | custom-call | tf_op jit(solution)/shard_map/regroup/pallas_call | solution.py:129
  26.3 1.4 collective-permute-start.6
  27.7 1.4 collective-permute-start.7
  32.9 2.7 %collective-permute-start.5 = (bf16[1040,128]{1,0:T(8,128)(2,1)S(1)}, bf16[1040,128]{1,0:T(8,128)(2,1)S(1)}, u32[]{:S(2)}, u32[]{:S(2)}) collective-permute-start(bf16[1040,128]{1,0:T(8,128)(2,1)S(1)} %slice.21), channel_id=1, source_target_pairs={{0,96},{32,0},{64,32},{96,64},{1,97},{33,1},{65,33},{97,65},{2,98}... | collective-permute-start | bytes 798728 | tf_op jit(solution)/shard_map/ppermute | solution.py:48
  39.0 8.4 %collective-permute-done.6.refs_1_.refs_2_ = bf16[3,4,4,128,128]{4,3,2,1,0:T(8,128)(2,1)S(1)} collective-permute-done((bf16[3,4,4,128,128]{4,3,2,1,0:T(8,128)(2,1)}, bf16[3,4,4,128,128]{4,3,2,1,0:T(8,128)(2,1)S(1)}, u32[]{:S(2)}, u32[]{:S(2)}) %collective-permute-start.6) | collective-permute-done | bytes 1572896 | tf_op jit(solution)/shard_map/ppermute | solution.py:36
  48.8 1.4 collective-permute-start.9
  50.2 2.6 %collective-permute-start.11 = (bf16[4160,128]{1,0:T(8,128)(2,1)S(1)}, bf16[4160,128]{1,0:T(8,128)(2,1)S(1)}, u32[]{:S(2)}, u32[]{:S(2)}) collective-permute-start(bf16[4160,128]{1,0:T(8,128)(2,1)S(1)} %constant_dynamic-update-slice_fusion.refs_3_), channel_id=1, source_target_pairs={{0,12},{4,0},{8,4},{12,8},{1,13},{5,1},{9,5},{13,9},{2,14},{6,2},{... | collective-permute-start | bytes 3194888 | tf_op jit(solution)/shard_map/ppermute | solution.py:36
  52.8 8.3 %own_panel.1.refs_9_ = f32[4,8,32,16,128]{4,3,2,1,0:T(8,128)S(1)} custom-call(s32[4]{0:T(128)S(1)} %copy-done, bf16[2,4,4,128,128]{4,3,2,1,0:T(8,128)(2,1)S(1)} %copy-done.2, bf16[2,4,4,128,128]{4,3,2,1,0:T(8,128)(2,1)S(1)} %copy-done.2, bf16[4160,128]{1,0:T(8,128)(2,1)S(1)} %constant_dynamic-update-slice_fusion.refs_3_, ...), custom_call_target="tpu_custom_call" | custom-call | flops 9900000256 | bytes 18000000 | tf_op jit(solution)/shard_map/own_panel/pallas_call | solution.py:275
  61.3 1.5 collective-permute-done.8.refs_5_
  62.8 1.4 collective-permute-start.13
  64.3 9.9 %collective-permute-done.10.refs_6_ = bf16[4160,128]{1,0:T(8,128)(2,1)S(1)} collective-permute-done((bf16[4160,128]{1,0:T(8,128)(2,1)S(1)}, bf16[4160,128]{1,0:T(8,128)(2,1)S(1)}, u32[]{:S(2)}, u32[]{:S(2)}) %collective-permute-start.10) | collective-permute-done | bytes 1064992 | tf_op jit(solution)/shard_map/ppermute | solution.py:36
  74.2 1.4 collective-permute-start.15
  75.7 14.2 %near_panels.1.refs_5_ = f32[4,8,32,16,128]{4,3,2,1,0:T(8,128)S(1)} custom-call(s32[4]{0:T(128)S(1)} %copy-done, bf16[3,4,4,128,128]{4,3,2,1,0:T(8,128)(2,1)S(1)} %collective-permute-done.6.refs_1_.refs_2_, bf16[3,4,4,128,128]{4,3,2,1,0:T(8,128)(2,1)S(1)} %collective-permute-done.6.refs_1_.refs_2_, ...), custom_call_target="tpu_custom_call" | custom-call | flops 17600000000 | bytes 32000000 | tf_op jit(solution)/shard_map/near_panels/pallas_call | solution.py:275
  89.9 1.3 collective-permute-done.14.refs_3_
  91.3 3.8 %last_coded.2 = (s16[4,33,16,128]{3,2,1,0:T(8,128)(2,1)S(1)}, s16[4,33,16,128]{3,2,1,0:T(8,128)(2,1)S(1)}) custom-call(s32[4]{0:T(128)S(1)} %copy-done, bf16[1,4,4,128,128]{4,3,2,1,0:T(8,128)(2,1)S(1)} %collective-permute-done.12.refs_1_, bf16[1,4,4,128,128]{4,3,2,1,0:T(8,128)(2,1)S(1)} %collective-permute-done.13.refs_2_, ...), custom_call_target="tpu_custom_call" | custom-call | flops 4400000000 | bytes 8000000 | tf_op jit(solution)/shard_map/last_coded/pallas_call | solution.py:275
  95.2 1.7 collective-permute-start.16
  96.9 2.2 %collective-permute-start.17 = (s16[4,33,16,128]{3,2,1,0:T(8,128)(2,1)S(1)}, s16[4,33,16,128]{3,2,1,0:T(8,128)(2,1)S(1)}, u32[]{:S(2)}, u32[]{:S(2)}) collective-permute-start(s16[4,33,16,128]{3,2,1,0:T(8,128)(2,1)S(1)} %get-tuple-element.54), channel_id=1, source_target_pairs={{0,3},{1,0},{2,1},{3,2},{4,7},{5,4},{6,5},{7,6},{8,11},{9,8},{10,9... | collective-permute-start | bytes 1622024 | tf_op jit(solution)/shard_map/ppermute | solution.py:36
  99.1 3.8 %last_coded.3 = (s16[4,33,16,128]{3,2,1,0:T(8,128)(2,1)S(1)}, s16[4,33,16,128]{3,2,1,0:T(8,128)(2,1)S(1)}) custom-call(s32[4]{0:T(128)S(1)} %copy-done, bf16[1,4,4,128,128]{4,3,2,1,0:T(8,128)(2,1)S(1)} %collective-permute-done.12.refs_1_, bf16[1,4,4,128,128]{4,3,2,1,0:T(8,128)(2,1)S(1)} %collective-permute-done.13.refs_2_, ...), custom_call_target="tpu_custom_call" | custom-call | flops 4400000000 | bytes 8000000 | tf_op jit(solution)/shard_map/last_coded/pallas_call | solution.py:275
  103.0 2.7 %collective-permute-start.20 = (s16[4,33,16,128]{3,2,1,0:T(8,128)(2,1)S(1)}, s16[4,33,16,128]{3,2,1,0:T(8,128)(2,1)S(1)}, u32[]{:S(2)}, u32[]{:S(2)}) collective-permute-start(s16[4,33,16,128]{3,2,1,0:T(8,128)(2,1)S(1)} %get-tuple-element.57), channel_id=1, source_target_pairs={{0,3},{1,0},{2,1},{3,2},{4,7},{5,4},{6,5},{7,6},{8,11},{9,8},{10,9... | collective-permute-start | bytes 1622024 | tf_op jit(solution)/shard_map/ppermute | solution.py:36
  106.1 3.9 %last_sent.1 = (s16[4,33,16,128]{3,2,1,0:T(8,128)(2,1)S(1)}, s16[4,33,16,128]{3,2,1,0:T(8,128)(2,1)S(1)}) custom-call(s32[4]{0:T(128)S(1)} %copy-done, bf16[1,4,4,128,128]{4,3,2,1,0:T(8,128)(2,1)S(1)} %collective-permute-done.12.refs_1_, bf16[1,4,4,128,128]{4,3,2,1,0:T(8,128)(2,1)S(1)} %collective-permute-done.13.refs_2_, ...), custom_call_target="tpu_custom_call" | custom-call | flops 4400000000 | bytes 8000000 | tf_op jit(solution)/shard_map/last_sent/pallas_call | solution.py:275
  111.0 2.1 %collective-permute-start.21 = (s16[4,33,16,128]{3,2,1,0:T(8,128)(2,1)S(1)}, s16[4,33,16,128]{3,2,1,0:T(8,128)(2,1)S(1)}, u32[]{:S(2)}, u32[]{:S(2)}) collective-permute-start(s16[4,33,16,128]{3,2,1,0:T(8,128)(2,1)S(1)} %get-tuple-element.58), channel_id=1, source_target_pairs={{0,3},{1,0},{2,1},{3,2},{4,7},{5,4},{6,5},{7,6},{8,11},{9,8},{10,9... | collective-permute-start | bytes 1622024 | tf_op jit(solution)/shard_map/ppermute | solution.py:36
  113.1 3.3 %last_more.1.own = f32[1,8,32,16,128]{4,3,2,1,0:T(8,128)S(1)} custom-call(s32[4]{0:T(128)S(1)} %copy-done, bf16[1,4,4,128,128]{4,3,2,1,0:T(8,128)(2,1)S(1)} %collective-permute-done.12.refs_1_, bf16[1,4,4,128,128]{4,3,2,1,0:T(8,128)(2,1)S(1)} %collective-permute-done.13.refs_2_, bf16[4160,128]{1,0:T(8,128)(2,1)S(1)} %collective-permute-done.14.refs_3_, ...), custom_call_target="tpu_custom_call" | custom-call | flops 4400000000 | bytes 8000000 | tf_op jit(solution)/shard_map/last_more/pallas_call | solution.py:275
  116.4 3.4 %collective-permute-done.18.prev0 = s16[4,33,16,128]{3,2,1,0:T(8,128)(2,1)S(1)} collective-permute-done((s16[4,33,16,128]{3,2,1,0:T(8,128)(2,1)S(1)}, s16[4,33,16,128]{3,2,1,0:T(8,128)(2,1)S(1)}, u32[]{:S(2)}, u32[]{:S(2)}) %collective-permute-start.18) | collective-permute-done | bytes 540704 | tf_op jit(solution)/shard_map/ppermute | solution.py:36
  119.8 5.9 %pack.1 = s16[128,80,128]{2,1,0:T(8,128)(2,1)S(1)} custom-call(s32[256]{0:T(256)S(1)} %add_bitcast_fusion.slots, f32[1,8,32,16,128]{4,3,2,1,0:T(8,128)S(1)} %last_more.1.own, s16[4,33,16,128]{3,2,1,0:T(8,128)(2,1)S(1)} %collective-permute-done.18.prev0, s16[4,33,16,128]{3,2,1,0:T(8,128)(2,1)S(1)} %collective-permute-done.19.prev1, ...), custom_call_target="tpu_custom_call" | custom-call | tf_op jit(solution)/shard_map/pack/pallas_call | solution.py:369
  125.7 46.7 %all_to_all.5 = s16[128,80,128]{2,1,0:T(8,128)(2,1)S(1)} all-to-all(s16[128,80,128]{2,1,0:T(8,128)(2,1)S(1)} %pack.1), channel_id=1, replica_groups=mesh['x'=4,'core'=2,'z'=4,'y'=4] {'x','core','z','y'}, dimensions={0} | all-to-all | bytes 5242880 | tf_op jit(solution)/shard_map/all_to_all | solution.py:484
  172.4 5.8 %unpack.1 = f32[256,4096]{1,0:T(8,128)} custom-call(s16[4,2,16,80,128]{4,3,2,1,0:T(8,128)(2,1)S(1)} %bitcast.11), custom_call_target="tpu_custom_call" | custom-call | tf_op jit(solution)/shard_map/unpack/pallas_call | solution.py:409
  (60 shorter events, 15.0 us)
Async XLA Ops:
  0.0 5.3 %copy-start.4 = (s32[1,8,8]{2,1,0:T(8,128)S(1)}, s32[1,8,8]{2,1,0:T(8,128)}, u32[]{:S(2)}) copy-start(s32[1,8,8]{2,1,0:T(8,128)} %param.8) | copy-start | bytes 772
  0.0 5.4 %copy-start.5 = (s32[64,1,4]{0,2,1:T(4,128)S(1)}, s32[64,1,4]{0,2,1:T(4,128)}, u32[]{:S(2)}) copy-start(s32[64,1,4]{0,2,1:T(4,128)} %param.6) | copy-start | bytes 3076
  0.0 6.3 %copy-start.3 = (s32[128,1]{0,1:T(1,128)S(1)}, s32[128,1]{0,1:T(1,128)}, u32[]{:S(2)}) copy-start(s32[128,1]{0,1:T(1,128)} %param.9) | copy-start | bytes 1540
  3.8 11.9 %collective-permute-start.1 = (bf16[16,4,128,128]{3,2,1,0:T(8,128)(2,1)S(1)}, bf16[16,4,128,128]{3,2,1,0:T(8,128)(2,1)}, u32[]{:S(2)}, u32[]{:S(2)}) collective-permute-start(bf16[16,4,128,128]{3,2,1,0:T(8,128)(2,1)S(1)} %reshape.33.mine), channel_id=1, source_target_pairs={{0,16},{16,0},{1,17},{17,1},{2,18},{18,2},{3,19},{19,3},{4,20},{20... | collective-permute-start | bytes 6291464 | tf_op jit(solution)/shard_map/ppermute | solution.py:52
  6.3 12.8 %copy-start = (s32[4]{0:T(128)S(1)}, s32[4]{0:T(128)}, u32[]{:S(2)}) copy-start(s32[4]{0:T(128)} %pad_add_fusion.2.core.at.refs_0_) | copy-start | bytes 52
  12.2 1.8 collective-permute-start
  15.7 15.1 %collective-permute-start.2 = (bf16[2080,128]{1,0:T(8,128)(2,1)}, bf16[2080,128]{1,0:T(8,128)(2,1)}, u32[]{:S(2)}, u32[]{:S(2)}) collective-permute-start(bf16[2080,128]{1,0:T(8,128)(2,1)} %pad_maximum_fusion), channel_id=1, source_target_pairs={{0,32},{32,64},{64,96},{96,0},{1,33},{33,65},{65,97},{97,1},{2,34}... | collective-permute-start | bytes 1597448 | tf_op jit(solution)/shard_map/ppermute | solution.py:48
  17.0 14.9 %collective-permute-start.3 = (bf16[2080,128]{1,0:T(8,128)(2,1)}, bf16[2080,128]{1,0:T(8,128)(2,1)}, u32[]{:S(2)}, u32[]{:S(2)}) collective-permute-start(bf16[2080,128]{1,0:T(8,128)(2,1)} %pad_maximum_fusion), channel_id=1, source_target_pairs={{0,96},{32,0},{64,32},{96,64},{1,97},{33,1},{65,33},{97,65},{2,98}... | collective-permute-start | bytes 1597448 | tf_op jit(solution)/shard_map/ppermute | solution.py:48
  25.3 1.0 copy-start.1
  26.3 21.1 %collective-permute-start.6 = (bf16[3,4,4,128,128]{4,3,2,1,0:T(8,128)(2,1)}, bf16[3,4,4,128,128]{4,3,2,1,0:T(8,128)(2,1)S(1)}, u32[]{:S(2)}, u32[]{:S(2)}) collective-permute-start(bf16[3,4,4,128,128]{4,3,2,1,0:T(8,128)(2,1)} %get-tuple-element.39), channel_id=1, source_target_pairs={{0,4},{4,8},{8,12},{12,0},{1,5},{5,9},{9,13},{13,1},{2,6},{6,10},{... | collective-permute-start | bytes 4718600 | tf_op jit(solution)/shard_map/ppermute | solution.py:36
  27.7 19.8 %collective-permute-start.7 = (bf16[3,4,4,128,128]{4,3,2,1,0:T(8,128)(2,1)}, bf16[3,4,4,128,128]{4,3,2,1,0:T(8,128)(2,1)S(1)}, u32[]{:S(2)}, u32[]{:S(2)}) collective-permute-start(bf16[3,4,4,128,128]{4,3,2,1,0:T(8,128)(2,1)} %get-tuple-element.40), channel_id=1, source_target_pairs={{0,12},{4,0},{8,4},{12,8},{1,13},{5,1},{9,5},{13,9},{2,14},{6,2},{... | collective-permute-start | bytes 4718600 | tf_op jit(solution)/shard_map/ppermute | solution.py:36
  31.8 7.2 %collective-permute-start.4 = (bf16[1040,128]{1,0:T(8,128)(2,1)S(1)}, bf16[1040,128]{1,0:T(8,128)(2,1)S(1)}, u32[]{:S(2)}, u32[]{:S(2)}) collective-permute-start(bf16[1040,128]{1,0:T(8,128)(2,1)S(1)} %slice.20), channel_id=1, source_target_pairs={{0,32},{32,64},{64,96},{96,0},{1,33},{33,65},{65,97},{97,1},{2,34}... | collective-permute-start | bytes 798728 | tf_op jit(solution)/shard_map/ppermute | solution.py:48
  32.9 6.1 %collective-permute-start.5 = (bf16[1040,128]{1,0:T(8,128)(2,1)S(1)}, bf16[1040,128]{1,0:T(8,128)(2,1)S(1)}, u32[]{:S(2)}, u32[]{:S(2)}) collective-permute-start(bf16[1040,128]{1,0:T(8,128)(2,1)S(1)} %slice.21), channel_id=1, source_target_pairs={{0,96},{32,0},{64,32},{96,64},{1,97},{33,1},{65,33},{97,65},{2,98}... | collective-permute-start | bytes 798728 | tf_op jit(solution)/shard_map/ppermute | solution.py:48
  36.7 16.2 %copy-start.2 = (bf16[2,4,4,128,128]{4,3,2,1,0:T(8,128)(2,1)S(1)}, bf16[2,4,4,128,128]{4,3,2,1,0:T(8,128)(2,1)}, u32[]{:S(2)}) copy-start(bf16[2,4,4,128,128]{4,3,2,1,0:T(8,128)(2,1)} %copy-done.1) | copy-start | bytes 3145732
  47.5 15.3 %collective-permute-start.8 = (bf16[4160,128]{1,0:T(8,128)(2,1)S(1)}, bf16[4160,128]{1,0:T(8,128)(2,1)S(1)}, u32[]{:S(2)}, u32[]{:S(2)}) collective-permute-start(bf16[4160,128]{1,0:T(8,128)(2,1)S(1)} %constant_dynamic-update-slice_fusion.refs_3_), channel_id=1, source_target_pairs={{0,4},{4,8},{8,12},{12,0},{1,5},{5,9},{9,13},{13,1},{2,6},{6,10},{... | collective-permute-start | bytes 3194888 | tf_op jit(solution)/shard_map/ppermute | solution.py:36
  48.8 15.5 %collective-permute-start.9 = (bf16[4160,128]{1,0:T(8,128)(2,1)S(1)}, bf16[4160,128]{1,0:T(8,128)(2,1)S(1)}, u32[]{:S(2)}, u32[]{:S(2)}) collective-permute-start(bf16[4160,128]{1,0:T(8,128)(2,1)S(1)} %constant_dynamic-update-slice_fusion.2.refs_4_), channel_id=1, source_target_pairs={{0,12},{4,0},{8,4},{12,8},{1,13},{5,1},{9,5},{13,9},{2,14},{6,2},{... | collective-permute-start | bytes 3194888 | tf_op jit(solution)/shard_map/ppermute | solution.py:36
  50.2 24.1 %collective-permute-start.10 = (bf16[4160,128]{1,0:T(8,128)(2,1)S(1)}, bf16[4160,128]{1,0:T(8,128)(2,1)S(1)}, u32[]{:S(2)}, u32[]{:S(2)}) collective-permute-start(bf16[4160,128]{1,0:T(8,128)(2,1)S(1)} %constant_dynamic-update-slice_fusion.2.refs_4_), channel_id=1, source_target_pairs={{0,4},{4,8},{8,12},{12,0},{1,5},{5,9},{9,13},{13,1},{2,6},{6,10},{... | collective-permute-start | bytes 3194888 | tf_op jit(solution)/shard_map/ppermute | solution.py:36
  50.2 25.4 %collective-permute-start.11 = (bf16[4160,128]{1,0:T(8,128)(2,1)S(1)}, bf16[4160,128]{1,0:T(8,128)(2,1)S(1)}, u32[]{:S(2)}, u32[]{:S(2)}) collective-permute-start(bf16[4160,128]{1,0:T(8,128)(2,1)S(1)} %constant_dynamic-update-slice_fusion.refs_3_), channel_id=1, source_target_pairs={{0,12},{4,0},{8,4},{12,8},{1,13},{5,1},{9,5},{13,9},{2,14},{6,2},{... | collective-permute-start | bytes 3194888 | tf_op jit(solution)/shard_map/ppermute | solution.py:36
  61.2 28.7 %collective-permute-start.12 = (bf16[1,4,4,128,128]{4,3,2,1,0:T(8,128)(2,1)S(1)}, bf16[1,4,4,128,128]{4,3,2,1,0:T(8,128)(2,1)S(1)}, u32[]{:S(2)}, u32[]{:S(2)}) collective-permute-start(bf16[1,4,4,128,128]{4,3,2,1,0:T(8,128)(2,1)S(1)} %slice.22), channel_id=1, source_target_pairs={{0,4},{4,8},{8,12},{12,0},{1,5},{5,9},{9,13},{13,1},{2,6},{6,10},{... | collective-permute-start | bytes 1572872 | tf_op jit(solution)/shard_map/ppermute | solution.py:36
  62.8 27.1 %collective-permute-start.13 = (bf16[1,4,4,128,128]{4,3,2,1,0:T(8,128)(2,1)S(1)}, bf16[1,4,4,128,128]{4,3,2,1,0:T(8,128)(2,1)S(1)}, u32[]{:S(2)}, u32[]{:S(2)}) collective-permute-start(bf16[1,4,4,128,128]{4,3,2,1,0:T(8,128)(2,1)S(1)} %slice.23), channel_id=1, source_target_pairs={{0,12},{4,0},{8,4},{12,8},{1,13},{5,1},{9,5},{13,9},{2,14},{6,2},{... | collective-permute-start | bytes 1572872 | tf_op jit(solution)/shard_map/ppermute | solution.py:36
  64.3 27.0 %collective-permute-start.14 = (bf16[4160,128]{1,0:T(8,128)(2,1)S(1)}, bf16[4160,128]{1,0:T(8,128)(2,1)S(1)}, u32[]{:S(2)}, u32[]{:S(2)}) collective-permute-start(bf16[4160,128]{1,0:T(8,128)(2,1)S(1)} %collective-permute-done.8.refs_5_), channel_id=1, source_target_pairs={{0,4},{4,8},{8,12},{12,0},{1,5},{5,9},{9,13},{13,1},{2,6},{6,10},{... | collective-permute-start | bytes 3194888 | tf_op jit(solution)/shard_map/ppermute | solution.py:36
  74.2 17.1 %collective-permute-start.15 = (bf16[4160,128]{1,0:T(8,128)(2,1)S(1)}, bf16[4160,128]{1,0:T(8,128)(2,1)S(1)}, u32[]{:S(2)}, u32[]{:S(2)}) collective-permute-start(bf16[4160,128]{1,0:T(8,128)(2,1)S(1)} %collective-permute-done.9.refs_8_), channel_id=1, source_target_pairs={{0,12},{4,0},{8,4},{12,8},{1,13},{5,1},{9,5},{13,9},{2,14},{6,2},{... | collective-permute-start | bytes 3194888 | tf_op jit(solution)/shard_map/ppermute | solution.py:36
  95.2 10.9 %collective-permute-start.16 = (s16[4,33,16,128]{3,2,1,0:T(8,128)(2,1)S(1)}, s16[4,33,16,128]{3,2,1,0:T(8,128)(2,1)S(1)}, u32[]{:S(2)}, u32[]{:S(2)}) collective-permute-start(s16[4,33,16,128]{3,2,1,0:T(8,128)(2,1)S(1)} %get-tuple-element.53), channel_id=1, source_target_pairs={{0,1},{1,2},{2,3},{3,0},{4,5},{5,6},{6,7},{7,4},{8,9},{9,10},{10,1... | collective-permute-start | bytes 1622024 | tf_op jit(solution)/shard_map/ppermute | solution.py:36
  96.9 9.2 %collective-permute-start.17 = (s16[4,33,16,128]{3,2,1,0:T(8,128)(2,1)S(1)}, s16[4,33,16,128]{3,2,1,0:T(8,128)(2,1)S(1)}, u32[]{:S(2)}, u32[]{:S(2)}) collective-permute-start(s16[4,33,16,128]{3,2,1,0:T(8,128)(2,1)S(1)} %get-tuple-element.54), channel_id=1, source_target_pairs={{0,3},{1,0},{2,1},{3,2},{4,7},{5,4},{6,5},{7,6},{8,11},{9,8},{10,9... | collective-permute-start | bytes 1622024 | tf_op jit(solution)/shard_map/ppermute | solution.py:36
  103.0 13.4 %collective-permute-start.19 = (s16[4,33,16,128]{3,2,1,0:T(8,128)(2,1)S(1)}, s16[4,33,16,128]{3,2,1,0:T(8,128)(2,1)S(1)}, u32[]{:S(2)}, u32[]{:S(2)}) collective-permute-start(s16[4,33,16,128]{3,2,1,0:T(8,128)(2,1)S(1)} %get-tuple-element.56), channel_id=1, source_target_pairs={{0,1},{1,2},{2,3},{3,0},{4,5},{5,6},{6,7},{7,4},{8,9},{9,10},{10,1... | collective-permute-start | bytes 1622024 | tf_op jit(solution)/shard_map/ppermute | solution.py:36
  103.0 13.3 %collective-permute-start.20 = (s16[4,33,16,128]{3,2,1,0:T(8,128)(2,1)S(1)}, s16[4,33,16,128]{3,2,1,0:T(8,128)(2,1)S(1)}, u32[]{:S(2)}, u32[]{:S(2)}) collective-permute-start(s16[4,33,16,128]{3,2,1,0:T(8,128)(2,1)S(1)} %get-tuple-element.57), channel_id=1, source_target_pairs={{0,3},{1,0},{2,1},{3,2},{4,7},{5,4},{6,5},{7,6},{8,11},{9,8},{10,9... | collective-permute-start | bytes 1622024 | tf_op jit(solution)/shard_map/ppermute | solution.py:36
  109.9 9.9 %collective-permute-start.18 = (s16[4,33,16,128]{3,2,1,0:T(8,128)(2,1)S(1)}, s16[4,33,16,128]{3,2,1,0:T(8,128)(2,1)S(1)}, u32[]{:S(2)}, u32[]{:S(2)}) collective-permute-start(s16[4,33,16,128]{3,2,1,0:T(8,128)(2,1)S(1)} %get-tuple-element.55), channel_id=1, source_target_pairs={{0,1},{1,2},{2,3},{3,0},{4,5},{5,6},{6,7},{7,4},{8,9},{9,10},{10,1... | collective-permute-start | bytes 1622024 | tf_op jit(solution)/shard_map/ppermute | solution.py:36
  111.0 8.8 %collective-permute-start.21 = (s16[4,33,16,128]{3,2,1,0:T(8,128)(2,1)S(1)}, s16[4,33,16,128]{3,2,1,0:T(8,128)(2,1)S(1)}, u32[]{:S(2)}, u32[]{:S(2)}) collective-permute-start(s16[4,33,16,128]{3,2,1,0:T(8,128)(2,1)S(1)} %get-tuple-element.58), channel_id=1, source_target_pairs={{0,3},{1,0},{2,1},{3,2},{4,7},{5,4},{6,5},{7,6},{8,11},{9,8},{10,9... | collective-permute-start | bytes 1622024 | tf_op jit(solution)/shard_map/ppermute | solution.py:36

commit v11 on v10

--- a/solution.py
+++ b/solution.py
@@ -14,7 +14,7 @@
 ALL = ("x", "core", "z", "y")
 PLANE = ("core", "z", "y")
 TOP = 32766.0
-MSG = 80
+MSG = 72
 LIMIT = 16
 PART = 8 * 128 + 16
 ORDER = (2, 1, 3, 0)
@@ -52,15 +52,14 @@
     return lax.ppermute(v, "core", [(0, 1), (1, 0)])
 
 
-def split_kernel(core, d_ref, i_ref, mine, theirs, flat, wide):
+def split_kernel(core, d_ref, i_ref, mine, theirs, flat0, wide0, flat1, wide1):
     lane32 = lax.broadcasted_iota(jnp.int32, (32, 128), 1)
     lane64 = lax.broadcasted_iota(jnp.int32, (64, 128), 1)
 
-    def one(k, _):
+    def one(k, flat, wide):
         rows = d_ref[k].astype(jnp.float32)
         for p in range(32):
             flat[p * 8:(p + 1) * 8, :] = rows[:, p * 128:(p + 1) * 128]
-        v = []
         for b in range(4):
             lo, hi = flat[pl.ds(b, 32, stride=8), :], flat[pl.ds(b + 4, 32, stride=8), :]
             wide[b, pl.ds(0, 32, stride=2), :] = jnp.where(lane32 < 64, lo, pltpu.roll(hi, 64, 1))
@@ -81,9 +80,13 @@
         at = pl.ds(pl.multiple_of(k * 128, 128), 128)
         mine[at, :] = jnp.where(swapped, second, first).astype(jnp.bfloat16)
         theirs[at, :] = jnp.where(swapped, first, second).astype(jnp.bfloat16)
+
+    def two(i, _):
+        one(i * 2, flat0, wide0)
+        one(i * 2 + 1, flat1, wide1)
         return 0
 
-    lax.fori_loop(0, 8, one, 0)
+    lax.fori_loop(0, 4, two, 0)
     ints = i_ref[...].astype(jnp.float32).astype(jnp.bfloat16)
     mine[8 * 128:, :] = ints
     theirs[8 * 128:, :] = ints
@@ -100,7 +103,7 @@
                 pl.BlockSpec((8, SP, B * B), lambda i, *_: (0, 0, 0)), pl.BlockSpec((16, 128), lambda i, *_: (0, 0))
             ],
             out_specs=[whole, whole],
-            scratch_shapes=[pltpu.VMEM((256, 128), jnp.float32), pltpu.VMEM((4, B, 128), jnp.float32)],
+            scratch_shapes=[pltpu.VMEM((256, 128), jnp.float32), pltpu.VMEM((4, B, 128), jnp.float32)] * 2,
         ),
         out_shape=[half, half],
         name="split",
@@ -161,7 +164,8 @@
     panels, refs = refs[:pieces], refs[pieces:]
     if form != "first":
         sums_in, refs = refs[0], refs[1:]
-    if form == "sent":
+    received = ()
+    if form in ("sent", "own"):
         received, refs = refs[:2], refs[2:]
     outs, (dens, sems, acc, in_sems, out_sems, staged, ints) = refs[:-7], refs[-7:]
     size = n * 8 * PART // pieces
@@ -174,7 +178,7 @@
             src = sums_in.at[target, pl.ds(m * 4, 4)]
             sums.append(pltpu.make_async_copy(src, acc.at[h], in_sems.at[h]))
     stores = []
-    if form in ("first", "more"):
+    if form in ("first", "more", "own"):
         for h, (target, m) in enumerate(halves):
             dst = outs[0].at[target if len(halves) > 2 else 0, pl.ds(m * 4, 4)]
             stores.append(pltpu.make_async_copy(acc.at[h], dst, out_sems.at[h]))
@@ -225,7 +229,7 @@
             total = acc.at[h, r]
             if form == "first":
                 total[...] = jnp.zeros((NCW, 16, 128), jnp.float32)
-            elif form == "sent":
+            elif received:
                 scale = decoded_scale(received[h][r, NCW])
                 for j in range(NCW):
                     total[j] = total[j] + received[h][r, j].astype(jnp.int32).astype(jnp.float32) * scale
@@ -299,27 +303,26 @@
     )(at, *[array for array, _ in kohn], *panels, *([] if sums is None else [sums]), *received)
 
 
-def pack_kernel(slots, own, prev0, prev1, next0, next1, o_ref, total, codes):
-    rows = lax.broadcasted_iota(jnp.int32, (16, 128), 0)
+def pack_kernel(slots, own, prev0, next1, o_ref, total, codes):
+    rows = lax.broadcasted_iota(jnp.int32, (8, 128), 0)
     lane = lax.broadcasted_iota(jnp.int32, (16, 128), 1)
 
     def clear(n, _):
         for m in range(4):
             o_ref[n * 4 + m] = jnp.zeros((MSG, 128), jnp.int16)
-            codes[n * 4 + m] = jnp.zeros((16, 128), jnp.int32)
+            codes[n * 4 + m] = jnp.zeros((8, 128), jnp.int32)
         return 0
 
     lax.fori_loop(0, 32, clear, 0)
 
     def one(m, r):
         row = m * 4 + r
-        coded = [((prev0, prev1)[m], r), ((next0, next1)[m], r)]
-        scales = [decoded_scale(ref[at, NCW]) for ref, at in coded]
+        coded = (prev0, next1)[m]
+        scale = decoded_scale(coded[r, NCW])
         for group in range(NCW // 8):
             blocks = []
             for j in range(group * 8, group * 8 + 8):
-                g = [ref[at, j].astype(jnp.int32).astype(jnp.float32) * scale for (ref, at), scale in zip(coded, scales)]
-                blocks.append(own[0, row, j] + g[0] + g[1])
+                blocks.append(own[0, row, j] + coded[r, j].astype(jnp.int32).astype(jnp.float32) * scale)
             turned = jnp.concatenate(blocks, axis=0).T
             v = []
             for q in range(8):
@@ -345,7 +348,7 @@
         def write_code(code):
             for j in range(NCW):
                 slot = slots[row * NCW + j]
-                codes[slot // 4] = jnp.where(rows == slot % 4, code, codes[slot // 4])
+                codes[slot // 4] = jnp.where(rows == slot % 4, code[:8], codes[slot // 4])
 
         encode(total, put, write_code)
 
@@ -354,7 +357,7 @@
 
     def finish(n, _):
         for m in range(4):
-            o_ref[n * 4 + m, 64:80, :] = codes[n * 4 + m].astype(jnp.int16)
+            o_ref[n * 4 + m, 64:72, :] = codes[n * 4 + m].astype(jnp.int16)
         return 0
 
     lax.fori_loop(0, 32, finish, 0)
@@ -373,7 +376,7 @@
             grid=(1,),
             in_specs=[whole(array) for array in parts],
             out_specs=pl.BlockSpec((128, MSG, 128), lambda i, *_: (0, 0, 0), pipeline_mode=pl.Buffered(1)),
-            scratch_shapes=[pltpu.VMEM((NCW, 16, 128), jnp.float32), pltpu.VMEM((128, 16, 128), jnp.int32)],
+            scratch_shapes=[pltpu.VMEM((NCW, 16, 128), jnp.float32), pltpu.VMEM((128, 8, 128), jnp.int32)],
         ),
         out_shape=jax.ShapeDtypeStruct((128, MSG, 128), jnp.int16),
         compiler_params=pltpu.CompilerParams(vmem_limit_bytes=32 << 20),
@@ -385,7 +388,7 @@
     low32 = (lax.broadcasted_iota(jnp.int32, (16, 128), 1) & 32) == 0
     for n in range(16):
         for c in range(2):
-            scales[n * 2 + c] = decoded_scale(r_ref[0, c, n, 64:80, :])[:8]
+            scales[n * 2 + c] = decoded_scale(r_ref[0, c, n, 64:72, :])
 
     def one(n, _):
         for s in range(2):
@@ -451,7 +454,7 @@
     low = jnp.concatenate([shard, left])
     high = jnp.concatenate([right, over_x(left[:PART], 1), over_x(right[PART:], -1)])
     low_sent, high_sent, kohn_prev, kohn_next, slots = lax.optimization_barrier((low, high, kohn_prev, kohn_next, slots))
-    prev_low, next_high = over_line(low_sent, 1), over_line(high_sent, -1)
+    prev_low, next_high = over_line(low, 1), over_line(high, -1)
     prev_high, next_low = over_line(high_sent, 1), over_line(low_sent, -1)
 
     def both(array):
@@ -478,9 +481,9 @@
     prev_1, next_0 = over_cross(next1, 1), over_cross(prev0, -1)
     next0, prev1 = last("sent", ((1, 0), (2, 1)), (via_next, via_prev))
     prev_0, next_1 = over_cross(next0, 1), over_cross(prev1, -1)
-    own, = last("more", ((3, 0), (3, 1)))
-
-    outgoing = pack(slots, own, prev_0, prev_1, next_0, next_1)
+    own, = last("own", ((3, 0), (3, 1)), (next_0, prev_1))
+
+    outgoing = pack(slots, own, prev_0, next_1)
     received = lax.all_to_all(outgoing, ALL, split_axis=0, concat_axis=0, tiled=True)
     return unpack(received.reshape(X, C, 16, MSG, 128))
 

time: 179 us -> 170 us (0.950)
  waiting for transfers between devices: 27.8 us -> 22.6 us
  blocking collectives: 46.7 us -> 43 us
    ppermute x16, waiting for transfers between devices: 25.1 us -> 20.9 us  [over(): lax.ppermute(v, PLANE, [(group[i], group[(i + step) % 4]) for group in gr...]
    all_to_all x1, blocking collectives: 46.7 us -> 43 us  [local(): lax.all_to_all(outgoing, ALL, split_axis=0, concat_axis=0, tiled=True)]
  transfers between devices with their start and end apart: 22 -> 22, of which waited for: 9 -> 8; matrix products, arithmetic and copies ran while one was open for 6% -> 6% of each run, Pallas kernels for 25% -> 26%
where the time goes in v11:
time: 170 us; the launch traced here: 169 us
  Pallas kernels  59.3 us (35%)
  blocking collectives  43 us (25%)
  starting transfers between devices  29.4 us (17%)
  waiting for transfers between devices  22.6 us (13%)
  local copies, waits for them, and re-layouts  10.6 us (6%)
  other arithmetic  4.24 us (2%)
    all_to_all x1, blocking collectives, local(): lax.all_to_all(outgoing, ALL, split_axis=0, concat_axis=0, tiled=True)  43 us
    pallas_call x6, Pallas kernels, panel_sums(): pl.pallas_call(lambda *refs: panel_kernel(n, pieces, halves, form, *refs)...  37.4 us
    ppermute x16, starting transfers between devices, over(): lax.ppermute(v, PLANE, [(group[i], group[(i + step) % 4]) for group in gr...  22.3 us
    ppermute x16, waiting for transfers between devices, over(): lax.ppermute(v, PLANE, [(group[i], group[(i + step) % 4]) for group in gr...  20.9 us
    pallas_call x1, Pallas kernels, regroup(): pl.pallas_call(regroup_kernel, grid_spec=pltpu.PrefetchScalarGridSpec(num...  6.2 us
    pallas_call x1, Pallas kernels, unpack(): pl.pallas_call(unpack_kernel, grid=(X,), in_specs=[pl.BlockSpec((1, C, 16...  5.78 us
    pallas_call x1, Pallas kernels, pack(): pl.pallas_call(pack_kernel, grid_spec=pltpu.PrefetchScalarGridSpec(num_sc...  5.52 us
    ppermute x4, starting transfers between devices, over_x(): return lax.ppermute(v, 'x', [(i, (i + step) % X) for i in range(X)])  5.49 us
  transfers between devices with their start and end apart: 22, of which 8 were waited for; matrix products, arithmetic and copies ran while one was open for 6% of the time, Pallas kernels for 26%

profile of v11, /device:TPU:1, one launch (start us, length us, event | category | flops | bytes accessed | tf_op | source)
XLA Modules:
  0.0 169.4 jit_solution(8456748685163760675)
XLA Ops:
  0.0 3.8 %reshape.33.mine = bf16[16,4,128,128]{3,2,1,0:T(8,128)(2,1)S(1)} reshape(bf16[64,1,4,4096]{3,2,1,0:T(4,128)(2,1)} %param.5) | data formatting | bytes 4194304 | tf_op jit(solution)/shard_map/reshape | solution.py:430
  3.8 1.5 collective-permute-start.1
  6.9 4.4 %split.1 = (bf16[1040,128]{1,0:T(8,128)(2,1)}, bf16[1040,128]{1,0:T(8,128)(2,1)}) custom-call(s32[4]{0:T(128)} %pad_add_fusion.2.core.at.refs_0_, bf16[8,8,4096]{2,1,0:T(8,128)(2,1)} %bitcast.12, s32[16,128]{1,0:T(8,128)} %fusion.2.i_ref), custom_call_target="tpu_custom_call" | custom-call | tf_op jit(solution)/shard_map/split/pallas_call | solution.py:98
  11.4 1.7 %collective-permute-done = bf16[1040,128]{1,0:T(8,128)(2,1)S(1)} collective-permute-done((bf16[1040,128]{1,0:T(8,128)(2,1)}, bf16[1040,128]{1,0:T(8,128)(2,1)S(1)}, u32[]{:S(2)}, u32[]{:S(2)}) %collective-permute-start) | collective-permute-done | bytes 266272 | tf_op jit(solution)/shard_map/ppermute | solution.py:52
  13.1 1.8 %pad_maximum_fusion = bf16[2080,128]{1,0:T(8,128)(2,1)} fusion(bf16[1040,128]{1,0:T(8,128)(2,1)S(1)} %collective-permute-done, bf16[1040,128]{1,0:T(8,128)(2,1)} %get-tuple-element.33), kind=kLoop, calls=%fused_computation | loop fusion | flops 1064960 | bytes 1064960 | tf_op jit(solution)/shard_map/concatenate | solution.py:440
  16.2 1.4 collective-permute-start.3
  18.2 6.2 %regroup.1 = (bf16[2,4,4,128,128]{4,3,2,1,0:T(8,128)(2,1)S(1)}, bf16[3,4,4,128,128]{4,3,2,1,0:T(8,128)(2,1)}, bf16[3,4,4,128,128]{4,3,2,1,0:T(8,128)(2,1)}) custom-call(s32[4]{0:T(128)S(1)} %copy-done, bf16[16,4,128,128]{3,2,1,0:T(8,128)(2,1)S(1)} %reshape.33.mine, bf16[16,4,128,128]{3,2,1,0:T(8,128)(2,1)} %collective-permute-done.1.other), custom_call_target="tpu_custom_call" | custom-call | tf_op jit(solution)/shard_map/regroup/pallas_call | solution.py:132
  25.5 1.4 collective-permute-start.6
  26.8 1.4 collective-permute-start.7
  32.1 2.7 %collective-permute-start.5 = (bf16[1040,128]{1,0:T(8,128)(2,1)S(1)}, bf16[1040,128]{1,0:T(8,128)(2,1)S(1)}, u32[]{:S(2)}, u32[]{:S(2)}) collective-permute-start(bf16[1040,128]{1,0:T(8,128)(2,1)S(1)} %slice.21), channel_id=1, source_target_pairs={{0,96},{32,0},{64,32},{96,64},{1,97},{33,1},{65,33},{97,65},{2,98}... | collective-permute-start | bytes 798728 | tf_op jit(solution)/shard_map/ppermute | solution.py:48
  35.8 1.4 collective-permute-start.8
  38.5 2.7 %collective-permute-start.9 = (bf16[4160,128]{1,0:T(8,128)(2,1)S(1)}, bf16[4160,128]{1,0:T(8,128)(2,1)S(1)}, u32[]{:S(2)}, u32[]{:S(2)}) collective-permute-start(bf16[4160,128]{1,0:T(8,128)(2,1)S(1)} %constant_dynamic-update-slice_fusion.2.refs_4_), channel_id=1, source_target_pairs={{0,12},{4,0},{8,4},{12,8},{1,13},{5,1},{9,5},{13,9},{2,14},{6,2},{... | collective-permute-start | bytes 3194888 | tf_op jit(solution)/shard_map/ppermute | solution.py:36
  41.1 5.4 %collective-permute-done.6.refs_1_.refs_2_ = bf16[3,4,4,128,128]{4,3,2,1,0:T(8,128)(2,1)S(1)} collective-permute-done((bf16[3,4,4,128,128]{4,3,2,1,0:T(8,128)(2,1)}, bf16[3,4,4,128,128]{4,3,2,1,0:T(8,128)(2,1)S(1)}, u32[]{:S(2)}, u32[]{:S(2)}) %collective-permute-start.6) | collective-permute-done | bytes 1572896 | tf_op jit(solution)/shard_map/ppermute | solution.py:36
  47.9 1.4 collective-permute-start.11
  49.3 8.3 %own_panel.1.refs_9_ = f32[4,8,32,16,128]{4,3,2,1,0:T(8,128)S(1)} custom-call(s32[4]{0:T(128)S(1)} %copy-done, bf16[2,4,4,128,128]{4,3,2,1,0:T(8,128)(2,1)S(1)} %copy-done.2, bf16[2,4,4,128,128]{4,3,2,1,0:T(8,128)(2,1)S(1)} %copy-done.2, bf16[4160,128]{1,0:T(8,128)(2,1)S(1)} %constant_dynamic-update-slice_fusion.refs_3_, ...), custom_call_target="tpu_custom_call" | custom-call | flops 9900000256 | bytes 18000000 | tf_op jit(solution)/shard_map/own_panel/pallas_call | solution.py:279
  58.0 2.5 %collective-permute-start.13 = (bf16[1,4,4,128,128]{4,3,2,1,0:T(8,128)(2,1)S(1)}, bf16[1,4,4,128,128]{4,3,2,1,0:T(8,128)(2,1)S(1)}, u32[]{:S(2)}, u32[]{:S(2)}) collective-permute-start(bf16[1,4,4,128,128]{4,3,2,1,0:T(8,128)(2,1)S(1)} %slice.23), channel_id=1, source_target_pairs={{0,12},{4,0},{8,4},{12,8},{1,13},{5,1},{9,5},{13,9},{2,14},{6,2},{... | collective-permute-start | bytes 1572872 | tf_op jit(solution)/shard_map/ppermute | solution.py:36
  60.5 8.9 %collective-permute-done.10.refs_6_ = bf16[4160,128]{1,0:T(8,128)(2,1)S(1)} collective-permute-done((bf16[4160,128]{1,0:T(8,128)(2,1)S(1)}, bf16[4160,128]{1,0:T(8,128)(2,1)S(1)}, u32[]{:S(2)}, u32[]{:S(2)}) %collective-permute-start.10) | collective-permute-done | bytes 1064992 | tf_op jit(solution)/shard_map/ppermute | solution.py:36
  69.4 1.5 collective-permute-start.15
  70.9 14.2 %near_panels.1.refs_5_ = f32[4,8,32,16,128]{4,3,2,1,0:T(8,128)S(1)} custom-call(s32[4]{0:T(128)S(1)} %copy-done, bf16[3,4,4,128,128]{4,3,2,1,0:T(8,128)(2,1)S(1)} %collective-permute-done.6.refs_1_.refs_2_, bf16[3,4,4,128,128]{4,3,2,1,0:T(8,128)(2,1)S(1)} %collective-permute-done.6.refs_1_.refs_2_, ...), custom_call_target="tpu_custom_call" | custom-call | flops 17600000000 | bytes 32000000 | tf_op jit(solution)/shard_map/near_panels/pallas_call | solution.py:279
  86.5 3.9 %last_coded.3 = (s16[4,33,16,128]{3,2,1,0:T(8,128)(2,1)S(1)}, s16[4,33,16,128]{3,2,1,0:T(8,128)(2,1)S(1)}) custom-call(s32[4]{0:T(128)S(1)} %copy-done, bf16[1,4,4,128,128]{4,3,2,1,0:T(8,128)(2,1)S(1)} %collective-permute-done.12.refs_1_, bf16[1,4,4,128,128]{4,3,2,1,0:T(8,128)(2,1)S(1)} %collective-permute-done.13.refs_2_, ...), custom_call_target="tpu_custom_call" | custom-call | flops 4400000000 | bytes 8000000 | tf_op jit(solution)/shard_map/last_coded/pallas_call | solution.py:279
  90.3 1.7 %collective-permute-start.18 = (s16[4,33,16,128]{3,2,1,0:T(8,128)(2,1)S(1)}, s16[4,33,16,128]{3,2,1,0:T(8,128)(2,1)S(1)}, u32[]{:S(2)}, u32[]{:S(2)}) collective-permute-start(s16[4,33,16,128]{3,2,1,0:T(8,128)(2,1)S(1)} %get-tuple-element.55), channel_id=1, source_target_pairs={{0,1},{1,2},{2,3},{3,0},{4,5},{5,6},{6,7},{7,4},{8,9},{9,10},{10,1... | collective-permute-start | bytes 1622024 | tf_op jit(solution)/shard_map/ppermute | solution.py:36
  92.0 2.2 %collective-permute-start.19 = (s16[4,33,16,128]{3,2,1,0:T(8,128)(2,1)S(1)}, s16[4,33,16,128]{3,2,1,0:T(8,128)(2,1)S(1)}, u32[]{:S(2)}, u32[]{:S(2)}) collective-permute-start(s16[4,33,16,128]{3,2,1,0:T(8,128)(2,1)S(1)} %get-tuple-element.56), channel_id=1, source_target_pairs={{0,3},{1,0},{2,1},{3,2},{4,7},{5,4},{6,5},{7,6},{8,11},{9,8},{10,9... | collective-permute-start | bytes 1622024 | tf_op jit(solution)/shard_map/ppermute | solution.py:36
  94.2 3.8 %last_coded.2 = (s16[4,33,16,128]{3,2,1,0:T(8,128)(2,1)S(1)}, s16[4,33,16,128]{3,2,1,0:T(8,128)(2,1)S(1)}) custom-call(s32[4]{0:T(128)S(1)} %copy-done, bf16[1,4,4,128,128]{4,3,2,1,0:T(8,128)(2,1)S(1)} %collective-permute-done.12.refs_1_, bf16[1,4,4,128,128]{4,3,2,1,0:T(8,128)(2,1)S(1)} %collective-permute-done.13.refs_2_, ...), custom_call_target="tpu_custom_call" | custom-call | flops 4400000000 | bytes 8000000 | tf_op jit(solution)/shard_map/last_coded/pallas_call | solution.py:279
  98.1 1.5 collective-permute-start.16
  99.6 1.6 collective-permute-done.18.refs_6_
  101.2 3.9 %last_sent.1 = (s16[4,33,16,128]{3,2,1,0:T(8,128)(2,1)S(1)}, s16[4,33,16,128]{3,2,1,0:T(8,128)(2,1)S(1)}) custom-call(s32[4]{0:T(128)S(1)} %copy-done, bf16[1,4,4,128,128]{4,3,2,1,0:T(8,128)(2,1)S(1)} %collective-permute-done.12.refs_1_, bf16[1,4,4,128,128]{4,3,2,1,0:T(8,128)(2,1)S(1)} %collective-permute-done.13.refs_2_, ...), custom_call_target="tpu_custom_call" | custom-call | flops 4400000000 | bytes 8000000 | tf_op jit(solution)/shard_map/last_sent/pallas_call | solution.py:279
  106.1 2.1 %collective-permute-start.21 = (s16[4,33,16,128]{3,2,1,0:T(8,128)(2,1)S(1)}, s16[4,33,16,128]{3,2,1,0:T(8,128)(2,1)S(1)}, u32[]{:S(2)}, u32[]{:S(2)}) collective-permute-start(s16[4,33,16,128]{3,2,1,0:T(8,128)(2,1)S(1)} %get-tuple-element.58), channel_id=1, source_target_pairs={{0,3},{1,0},{2,1},{3,2},{4,7},{5,4},{6,5},{7,6},{8,11},{9,8},{10,9... | collective-permute-start | bytes 1622024 | tf_op jit(solution)/shard_map/ppermute | solution.py:36
  109.3 3.3 %last_own.1.own = f32[1,8,32,16,128]{4,3,2,1,0:T(8,128)S(1)} custom-call(s32[4]{0:T(128)S(1)} %copy-done, bf16[1,4,4,128,128]{4,3,2,1,0:T(8,128)(2,1)S(1)} %collective-permute-done.12.refs_1_, bf16[1,4,4,128,128]{4,3,2,1,0:T(8,128)(2,1)S(1)} %collective-permute-done.13.refs_2_, bf16[4160,128]{1,0:T(8,128)(2,1)S(1)} %collective-permute-done.14.refs_3_, ...), custom_call_target="tpu_custom_call" | custom-call | flops 4400000000 | bytes 8000000 | tf_op jit(solution)/shard_map/last_own/pallas_call | solution.py:279
  112.6 2.5 %collective-permute-done.20.prev0 = s16[4,33,16,128]{3,2,1,0:T(8,128)(2,1)S(1)} collective-permute-done((s16[4,33,16,128]{3,2,1,0:T(8,128)(2,1)S(1)}, s16[4,33,16,128]{3,2,1,0:T(8,128)(2,1)S(1)}, u32[]{:S(2)}, u32[]{:S(2)}) %collective-permute-start.20) | collective-permute-done | bytes 540704 | tf_op jit(solution)/shard_map/ppermute | solution.py:36
  115.1 5.5 %pack.1 = s16[128,72,128]{2,1,0:T(8,128)(2,1)S(1)} custom-call(s32[256]{0:T(256)S(1)} %add_bitcast_fusion.slots, f32[1,8,32,16,128]{4,3,2,1,0:T(8,128)S(1)} %last_own.1.own, s16[4,33,16,128]{3,2,1,0:T(8,128)(2,1)S(1)} %collective-permute-done.20.prev0, s16[4,33,16,128]{3,2,1,0:T(8,128)(2,1)S(1)} %collective-permute-done.21.next1), custom_call_target="tpu_custom_call" | custom-call | tf_op jit(solution)/shard_map/pack/pallas_call | solution.py:372
  120.6 43.0 %all_to_all.5 = s16[128,72,128]{2,1,0:T(8,128)(2,1)S(1)} all-to-all(s16[128,72,128]{2,1,0:T(8,128)(2,1)S(1)} %pack.1), channel_id=1, replica_groups=mesh['x'=4,'core'=2,'z'=4,'y'=4] {'x','core','z','y'}, dimensions={0} | all-to-all | bytes 4718592 | tf_op jit(solution)/shard_map/all_to_all | solution.py:487
  163.6 5.8 %unpack.1 = f32[256,4096]{1,0:T(8,128)} custom-call(s16[4,2,16,72,128]{4,3,2,1,0:T(8,128)(2,1)S(1)} %bitcast.11), custom_call_target="tpu_custom_call" | custom-call | tf_op jit(solution)/shard_map/unpack/pallas_call | solution.py:412
  (60 shorter events, 15.8 us)
Async XLA Ops:
  0.0 5.3 %copy-start.4 = (s32[1,8,8]{2,1,0:T(8,128)S(1)}, s32[1,8,8]{2,1,0:T(8,128)}, u32[]{:S(2)}) copy-start(s32[1,8,8]{2,1,0:T(8,128)} %param.8) | copy-start | bytes 772
  0.0 5.4 %copy-start.5 = (s32[64,1,4]{0,2,1:T(4,128)S(1)}, s32[64,1,4]{0,2,1:T(4,128)}, u32[]{:S(2)}) copy-start(s32[64,1,4]{0,2,1:T(4,128)} %param.6) | copy-start | bytes 3076
  0.0 6.3 %copy-start.3 = (s32[128,1]{0,1:T(1,128)S(1)}, s32[128,1]{0,1:T(1,128)}, u32[]{:S(2)}) copy-start(s32[128,1]{0,1:T(1,128)} %param.9) | copy-start | bytes 1540
  3.8 11.0 %collective-permute-start.1 = (bf16[16,4,128,128]{3,2,1,0:T(8,128)(2,1)S(1)}, bf16[16,4,128,128]{3,2,1,0:T(8,128)(2,1)}, u32[]{:S(2)}, u32[]{:S(2)}) collective-permute-start(bf16[16,4,128,128]{3,2,1,0:T(8,128)(2,1)S(1)} %reshape.33.mine), channel_id=1, source_target_pairs={{0,16},{16,0},{1,17},{17,1},{2,18},{18,2},{3,19},{19,3},{4,20},{20... | collective-permute-start | bytes 6291464 | tf_op jit(solution)/shard_map/ppermute | solution.py:52
  6.3 12.0 %copy-start = (s32[4]{0:T(128)S(1)}, s32[4]{0:T(128)}, u32[]{:S(2)}) copy-start(s32[4]{0:T(128)} %pad_add_fusion.2.core.at.refs_0_) | copy-start | bytes 52
  11.3 1.8 %collective-permute-start = (bf16[1040,128]{1,0:T(8,128)(2,1)}, bf16[1040,128]{1,0:T(8,128)(2,1)S(1)}, u32[]{:S(2)}, u32[]{:S(2)}) collective-permute-start(bf16[1040,128]{1,0:T(8,128)(2,1)} %get-tuple-element.34), channel_id=1, source_target_pairs={{0,16},{16,0},{1,17},{17,1},{2,18},{18,2},{3,19},{19,3},{4,20},{20... | collective-permute-start | bytes 798728 | tf_op jit(solution)/shard_map/ppermute | solution.py:52
  14.9 15.1 %collective-permute-start.2 = (bf16[2080,128]{1,0:T(8,128)(2,1)}, bf16[2080,128]{1,0:T(8,128)(2,1)}, u32[]{:S(2)}, u32[]{:S(2)}) collective-permute-start(bf16[2080,128]{1,0:T(8,128)(2,1)} %pad_maximum_fusion), channel_id=1, source_target_pairs={{0,32},{32,64},{64,96},{96,0},{1,33},{33,65},{65,97},{97,1},{2,34}... | collective-permute-start | bytes 1597448 | tf_op jit(solution)/shard_map/ppermute | solution.py:48
  16.2 14.9 %collective-permute-start.3 = (bf16[2080,128]{1,0:T(8,128)(2,1)}, bf16[2080,128]{1,0:T(8,128)(2,1)}, u32[]{:S(2)}, u32[]{:S(2)}) collective-permute-start(bf16[2080,128]{1,0:T(8,128)(2,1)} %pad_maximum_fusion), channel_id=1, source_target_pairs={{0,96},{32,0},{64,32},{96,64},{1,97},{33,1},{65,33},{97,65},{2,98}... | collective-permute-start | bytes 1597448 | tf_op jit(solution)/shard_map/ppermute | solution.py:48
  24.5 1.0 copy-start.1
  25.5 21.1 %collective-permute-start.6 = (bf16[3,4,4,128,128]{4,3,2,1,0:T(8,128)(2,1)}, bf16[3,4,4,128,128]{4,3,2,1,0:T(8,128)(2,1)S(1)}, u32[]{:S(2)}, u32[]{:S(2)}) collective-permute-start(bf16[3,4,4,128,128]{4,3,2,1,0:T(8,128)(2,1)} %get-tuple-element.39), channel_id=1, source_target_pairs={{0,4},{4,8},{8,12},{12,0},{1,5},{5,9},{9,13},{13,1},{2,6},{6,10},{... | collective-permute-start | bytes 4718600 | tf_op jit(solution)/shard_map/ppermute | solution.py:36
  26.8 19.8 %collective-permute-start.7 = (bf16[3,4,4,128,128]{4,3,2,1,0:T(8,128)(2,1)}, bf16[3,4,4,128,128]{4,3,2,1,0:T(8,128)(2,1)S(1)}, u32[]{:S(2)}, u32[]{:S(2)}) collective-permute-start(bf16[3,4,4,128,128]{4,3,2,1,0:T(8,128)(2,1)} %get-tuple-element.40), channel_id=1, source_target_pairs={{0,12},{4,0},{8,4},{12,8},{1,13},{5,1},{9,5},{13,9},{2,14},{6,2},{... | collective-permute-start | bytes 4718600 | tf_op jit(solution)/shard_map/ppermute | solution.py:36
  30.9 7.5 %collective-permute-start.4 = (bf16[1040,128]{1,0:T(8,128)(2,1)S(1)}, bf16[1040,128]{1,0:T(8,128)(2,1)S(1)}, u32[]{:S(2)}, u32[]{:S(2)}) collective-permute-start(bf16[1040,128]{1,0:T(8,128)(2,1)S(1)} %slice.20), channel_id=1, source_target_pairs={{0,32},{32,64},{64,96},{96,0},{1,33},{33,65},{65,97},{97,1},{2,34}... | collective-permute-start | bytes 798728 | tf_op jit(solution)/shard_map/ppermute | solution.py:48
  32.1 6.4 %collective-permute-start.5 = (bf16[1040,128]{1,0:T(8,128)(2,1)S(1)}, bf16[1040,128]{1,0:T(8,128)(2,1)S(1)}, u32[]{:S(2)}, u32[]{:S(2)}) collective-permute-start(bf16[1040,128]{1,0:T(8,128)(2,1)S(1)} %slice.21), channel_id=1, source_target_pairs={{0,96},{32,0},{64,32},{96,64},{1,97},{33,1},{65,33},{97,65},{2,98}... | collective-permute-start | bytes 798728 | tf_op jit(solution)/shard_map/ppermute | solution.py:48
  35.8 13.5 %copy-start.2 = (bf16[2,4,4,128,128]{4,3,2,1,0:T(8,128)(2,1)S(1)}, bf16[2,4,4,128,128]{4,3,2,1,0:T(8,128)(2,1)}, u32[]{:S(2)}) copy-start(bf16[2,4,4,128,128]{4,3,2,1,0:T(8,128)(2,1)} %copy-done.1) | copy-start | bytes 3145732
  35.8 22.2 %collective-permute-start.8 = (bf16[4160,128]{1,0:T(8,128)(2,1)S(1)}, bf16[4160,128]{1,0:T(8,128)(2,1)S(1)}, u32[]{:S(2)}, u32[]{:S(2)}) collective-permute-start(bf16[4160,128]{1,0:T(8,128)(2,1)S(1)} %constant_dynamic-update-slice_fusion.refs_3_), channel_id=1, source_target_pairs={{0,4},{4,8},{8,12},{12,0},{1,5},{5,9},{9,13},{13,1},{2,6},{6,10},{... | collective-permute-start | bytes 3194888 | tf_op jit(solution)/shard_map/ppermute | solution.py:36
  38.5 22.1 %collective-permute-start.9 = (bf16[4160,128]{1,0:T(8,128)(2,1)S(1)}, bf16[4160,128]{1,0:T(8,128)(2,1)S(1)}, u32[]{:S(2)}, u32[]{:S(2)}) collective-permute-start(bf16[4160,128]{1,0:T(8,128)(2,1)S(1)} %constant_dynamic-update-slice_fusion.2.refs_4_), channel_id=1, source_target_pairs={{0,12},{4,0},{8,4},{12,8},{1,13},{5,1},{9,5},{13,9},{2,14},{6,2},{... | collective-permute-start | bytes 3194888 | tf_op jit(solution)/shard_map/ppermute | solution.py:36
  46.6 22.8 %collective-permute-start.10 = (bf16[4160,128]{1,0:T(8,128)(2,1)S(1)}, bf16[4160,128]{1,0:T(8,128)(2,1)S(1)}, u32[]{:S(2)}, u32[]{:S(2)}) collective-permute-start(bf16[4160,128]{1,0:T(8,128)(2,1)S(1)} %constant_dynamic-update-slice_fusion.2.refs_4_), channel_id=1, source_target_pairs={{0,4},{4,8},{8,12},{12,0},{1,5},{5,9},{9,13},{13,1},{2,6},{6,10},{... | collective-permute-start | bytes 3194888 | tf_op jit(solution)/shard_map/ppermute | solution.py:36
  47.9 23.0 %collective-permute-start.11 = (bf16[4160,128]{1,0:T(8,128)(2,1)S(1)}, bf16[4160,128]{1,0:T(8,128)(2,1)S(1)}, u32[]{:S(2)}, u32[]{:S(2)}) collective-permute-start(bf16[4160,128]{1,0:T(8,128)(2,1)S(1)} %constant_dynamic-update-slice_fusion.refs_3_), channel_id=1, source_target_pairs={{0,12},{4,0},{8,4},{12,8},{1,13},{5,1},{9,5},{13,9},{2,14},{6,2},{... | collective-permute-start | bytes 3194888 | tf_op jit(solution)/shard_map/ppermute | solution.py:36
  57.7 27.5 %collective-permute-start.12 = (bf16[1,4,4,128,128]{4,3,2,1,0:T(8,128)(2,1)S(1)}, bf16[1,4,4,128,128]{4,3,2,1,0:T(8,128)(2,1)S(1)}, u32[]{:S(2)}, u32[]{:S(2)}) collective-permute-start(bf16[1,4,4,128,128]{4,3,2,1,0:T(8,128)(2,1)S(1)} %slice.22), channel_id=1, source_target_pairs={{0,4},{4,8},{8,12},{12,0},{1,5},{5,9},{9,13},{13,1},{2,6},{6,10},{... | collective-permute-start | bytes 1572872 | tf_op jit(solution)/shard_map/ppermute | solution.py:36
  58.0 27.1 %collective-permute-start.13 = (bf16[1,4,4,128,128]{4,3,2,1,0:T(8,128)(2,1)S(1)}, bf16[1,4,4,128,128]{4,3,2,1,0:T(8,128)(2,1)S(1)}, u32[]{:S(2)}, u32[]{:S(2)}) collective-permute-start(bf16[1,4,4,128,128]{4,3,2,1,0:T(8,128)(2,1)S(1)} %slice.23), channel_id=1, source_target_pairs={{0,12},{4,0},{8,4},{12,8},{1,13},{5,1},{9,5},{13,9},{2,14},{6,2},{... | collective-permute-start | bytes 1572872 | tf_op jit(solution)/shard_map/ppermute | solution.py:36
  60.5 25.9 %collective-permute-start.14 = (bf16[4160,128]{1,0:T(8,128)(2,1)S(1)}, bf16[4160,128]{1,0:T(8,128)(2,1)S(1)}, u32[]{:S(2)}, u32[]{:S(2)}) collective-permute-start(bf16[4160,128]{1,0:T(8,128)(2,1)S(1)} %collective-permute-done.8.refs_5_), channel_id=1, source_target_pairs={{0,4},{4,8},{8,12},{12,0},{1,5},{5,9},{9,13},{13,1},{2,6},{6,10},{... | collective-permute-start | bytes 3194888 | tf_op jit(solution)/shard_map/ppermute | solution.py:36
  69.4 17.1 %collective-permute-start.15 = (bf16[4160,128]{1,0:T(8,128)(2,1)S(1)}, bf16[4160,128]{1,0:T(8,128)(2,1)S(1)}, u32[]{:S(2)}, u32[]{:S(2)}) collective-permute-start(bf16[4160,128]{1,0:T(8,128)(2,1)S(1)} %collective-permute-done.9.refs_8_), channel_id=1, source_target_pairs={{0,12},{4,0},{8,4},{12,8},{1,13},{5,1},{9,5},{13,9},{2,14},{6,2},{... | collective-permute-start | bytes 3194888 | tf_op jit(solution)/shard_map/ppermute | solution.py:36
  90.3 10.9 %collective-permute-start.18 = (s16[4,33,16,128]{3,2,1,0:T(8,128)(2,1)S(1)}, s16[4,33,16,128]{3,2,1,0:T(8,128)(2,1)S(1)}, u32[]{:S(2)}, u32[]{:S(2)}) collective-permute-start(s16[4,33,16,128]{3,2,1,0:T(8,128)(2,1)S(1)} %get-tuple-element.55), channel_id=1, source_target_pairs={{0,1},{1,2},{2,3},{3,0},{4,5},{5,6},{6,7},{7,4},{8,9},{9,10},{10,1... | collective-permute-start | bytes 1622024 | tf_op jit(solution)/shard_map/ppermute | solution.py:36
  92.0 9.2 %collective-permute-start.19 = (s16[4,33,16,128]{3,2,1,0:T(8,128)(2,1)S(1)}, s16[4,33,16,128]{3,2,1,0:T(8,128)(2,1)S(1)}, u32[]{:S(2)}, u32[]{:S(2)}) collective-permute-start(s16[4,33,16,128]{3,2,1,0:T(8,128)(2,1)S(1)} %get-tuple-element.56), channel_id=1, source_target_pairs={{0,3},{1,0},{2,1},{3,2},{4,7},{5,4},{6,5},{7,6},{8,11},{9,8},{10,9... | collective-permute-start | bytes 1622024 | tf_op jit(solution)/shard_map/ppermute | solution.py:36
  98.1 10.1 %collective-permute-start.16 = (s16[4,33,16,128]{3,2,1,0:T(8,128)(2,1)S(1)}, s16[4,33,16,128]{3,2,1,0:T(8,128)(2,1)S(1)}, u32[]{:S(2)}, u32[]{:S(2)}) collective-permute-start(s16[4,33,16,128]{3,2,1,0:T(8,128)(2,1)S(1)} %get-tuple-element.53), channel_id=1, source_target_pairs={{0,3},{1,0},{2,1},{3,2},{4,7},{5,4},{6,5},{7,6},{8,11},{9,8},{10,9... | collective-permute-start | bytes 1622024 | tf_op jit(solution)/shard_map/ppermute | solution.py:36
  99.5 9.7 %collective-permute-start.17 = (s16[4,33,16,128]{3,2,1,0:T(8,128)(2,1)S(1)}, s16[4,33,16,128]{3,2,1,0:T(8,128)(2,1)S(1)}, u32[]{:S(2)}, u32[]{:S(2)}) collective-permute-start(s16[4,33,16,128]{3,2,1,0:T(8,128)(2,1)S(1)} %get-tuple-element.54), channel_id=1, source_target_pairs={{0,1},{1,2},{2,3},{3,0},{4,5},{5,6},{6,7},{7,4},{8,9},{9,10},{10,1... | collective-permute-start | bytes 1622024 | tf_op jit(solution)/shard_map/ppermute | solution.py:36
  105.1 10.0 %collective-permute-start.20 = (s16[4,33,16,128]{3,2,1,0:T(8,128)(2,1)S(1)}, s16[4,33,16,128]{3,2,1,0:T(8,128)(2,1)S(1)}, u32[]{:S(2)}, u32[]{:S(2)}) collective-permute-start(s16[4,33,16,128]{3,2,1,0:T(8,128)(2,1)S(1)} %get-tuple-element.57), channel_id=1, source_target_pairs={{0,1},{1,2},{2,3},{3,0},{4,5},{5,6},{6,7},{7,4},{8,9},{9,10},{10,1... | collective-permute-start | bytes 1622024 | tf_op jit(solution)/shard_map/ppermute | solution.py:36
  106.1 8.9 %collective-permute-start.21 = (s16[4,33,16,128]{3,2,1,0:T(8,128)(2,1)S(1)}, s16[4,33,16,128]{3,2,1,0:T(8,128)(2,1)S(1)}, u32[]{:S(2)}, u32[]{:S(2)}) collective-permute-start(s16[4,33,16,128]{3,2,1,0:T(8,128)(2,1)S(1)} %get-tuple-element.58), channel_id=1, source_target_pairs={{0,3},{1,0},{2,1},{3,2},{4,7},{5,4},{6,5},{7,6},{8,11},{9,8},{10,9... | collective-permute-start | bytes 1622024 | tf_op jit(solution)/shard_map/ppermute | solution.py:36

commit v12 on v11

--- a/solution.py
+++ b/solution.py
@@ -167,7 +167,8 @@
     received = ()
     if form in ("sent", "own"):
         received, refs = refs[:2], refs[2:]
-    outs, (dens, sems, acc, in_sems, out_sems, staged, ints) = refs[:-7], refs[-7:]
+    outs, (dens, sems, acc0, acc1, in_sems, out_sems, staged, ints) = refs[:-8], refs[-8:]
+    accs = (acc0, acc1)
     size = n * 8 * PART // pieces
     core, line, cross, x = at[0], at[1], at[2], at[3]
 
@@ -175,13 +176,15 @@
     sums = []
     if form != "first":
         for h, (target, m) in enumerate(halves):
-            src = sums_in.at[target, pl.ds(m * 4, 4)]
-            sums.append(pltpu.make_async_copy(src, acc.at[h], in_sems.at[h]))
+            for q in range(2):
+                src = sums_in.at[target, pl.ds(m * 4 + q * 2, 2)]
+                sums.append(pltpu.make_async_copy(src, accs[q].at[h], in_sems.at[h * 2 + q]))
     stores = []
     if form in ("first", "more", "own"):
         for h, (target, m) in enumerate(halves):
-            dst = outs[0].at[target if len(halves) > 2 else 0, pl.ds(m * 4, 4)]
-            stores.append(pltpu.make_async_copy(acc.at[h], dst, out_sems.at[h]))
+            for q in range(2):
+                dst = outs[0].at[target if len(halves) > 2 else 0, pl.ds(m * 4 + q * 2, 2)]
+                stores.append(pltpu.make_async_copy(accs[q].at[h], dst, out_sems.at[h * 2 + q]))
     for copy in loads + sums:
         copy.start()
     for copy in loads:
@@ -222,11 +225,11 @@
             total[js[b]] = old[b] + r[b * 16:(b + 1) * 16, :]
 
     def two_rows(h, pair):
-        work, totals = [], []
+        totals = []
+        work = [(q, q * 2 + pair, s, a) for s in range(n) for a in range(SK) for q in range(2)]
         for q in range(2):
-            r = pair * 2 + q
-            work += [(q, r, s, a) for s in range(n) for a in range(SK)]
-            total = acc.at[h, r]
+            r = q * 2 + pair
+            total = accs[q].at[h, pair]
             if form == "first":
                 total[...] = jnp.zeros((NCW, 16, 128), jnp.float32)
             elif received:
@@ -234,14 +237,14 @@
                 for j in range(NCW):
                     total[j] = total[j] + received[h][r, j].astype(jnp.int32).astype(jnp.float32) * scale
             totals.append(total)
-        held = [product(h, *work[i][1:]) for i in range(3)]
+        held = [product(h, *work[i][1:]) for i in range(4)]
         for i in range(len(work)):
-            if i + 3 < len(work):
-                held.append(product(h, *work[i + 3][1:]))
+            if i + 4 < len(work):
+                held.append(product(h, *work[i + 4][1:]))
             add(totals[work[i][0]], *held[i])
         if form in ("coded", "sent"):
             for q in range(2):
-                r = pair * 2 + q
+                r = q * 2 + pair
 
                 def put(j, value, r=r):
                     outs[h][r, j] = value
@@ -249,11 +252,11 @@
                 encode(totals[q], put, lambda code, put=put: put(NCW, code.astype(jnp.int16)))
 
     for h in range(len(halves)):
-        if sums:
-            sums[h].wait()
+        for copy in sums[2 * h:2 * h + 2]:
+            copy.wait()
         lax.fori_loop(0, 2, lambda pair, _, h=h: (two_rows(h, pair), 0)[1], 0)
-        if stores:
-            stores[h].start()
+        for copy in stores[2 * h:2 * h + 2]:
+            copy.start()
     for copy in stores:
         copy.wait()
 
@@ -289,9 +292,10 @@
             scratch_shapes=[
                 pltpu.VMEM((n * 8 * PART, 128), jnp.bfloat16),
                 pltpu.SemaphoreType.DMA((pieces + 1,)),
-                pltpu.VMEM((groups, 4, NCW, 16, 128), jnp.float32),
-                pltpu.SemaphoreType.DMA((groups,)),
-                pltpu.SemaphoreType.DMA((groups,)),
+                pltpu.VMEM((groups, 2, NCW, 16, 128), jnp.float32),
+                pltpu.VMEM((groups, 2, NCW, 16, 128), jnp.float32),
+                pltpu.SemaphoreType.DMA((groups * 2,)),
+                pltpu.SemaphoreType.DMA((groups * 2,)),
                 pltpu.VMEM((n * 16, 128), jnp.int32),
                 pltpu.SMEM((n * 16, 128), jnp.int32),
             ],
@@ -403,7 +407,7 @@
                 full[pl.ds(base + 16, 16), :] = jnp.where(low32, pltpu.roll(h[0], 96, 1), h[1])
         return 0
 
-    lax.fori_loop(0, 16, one, 0, unroll=4)
+    lax.fori_loop(0, 16, one, 0, unroll=8)
     for p in range(32):
         o_ref[:, p * 128:(p + 1) * 128] = full[pl.ds(p, 64, stride=32), :]
 

time: 170 us -> 169 us (level)
  no operation moved by 1% of the time
where the time goes in v12:
time: 169 us
  Pallas kernels  59.2 us (35%)
  blocking collectives  43.1 us (26%)
  starting transfers between devices  29.4 us (17%)
  waiting for transfers between devices  22.3 us (13%)
  local copies, waits for them, and re-layouts  10.6 us (6%)
  other arithmetic  4.24 us (3%)
    all_to_all x1, blocking collectives, local(): lax.all_to_all(outgoing, ALL, split_axis=0, concat_axis=0, tiled=True)  43.1 us
    pallas_call x6, Pallas kernels, panel_sums(): pl.pallas_call(lambda *refs: panel_kernel(n, pieces, halves, form, *refs)...  37.8 us
    ppermute x16, starting transfers between devices, over(): lax.ppermute(v, PLANE, [(group[i], group[(i + step) % 4]) for group in gr...  22.3 us
    ppermute x16, waiting for transfers between devices, over(): lax.ppermute(v, PLANE, [(group[i], group[(i + step) % 4]) for group in gr...  20.6 us
    pallas_call x1, Pallas kernels, regroup(): pl.pallas_call(regroup_kernel, grid_spec=pltpu.PrefetchScalarGridSpec(num...  6.2 us
    pallas_call x1, Pallas kernels, pack(): pl.pallas_call(pack_kernel, grid_spec=pltpu.PrefetchScalarGridSpec(num_sc...  5.52 us
    ppermute x4, starting transfers between devices, over_x(): return lax.ppermute(v, 'x', [(i, (i + step) % X) for i in range(X)])  5.49 us
    pallas_call x1, Pallas kernels, unpack(): pl.pallas_call(unpack_kernel, grid=(X,), in_specs=[pl.BlockSpec((1, C, 16...  5.22 us
  transfers between devices with their start and end apart: 22, of which 8 were waited for; matrix products, arithmetic and copies ran while one was open for 6% of the time, Pallas kernels for 26%

profile of v12, /device:TPU:1, one launch (start us, length us, event | category | flops | bytes accessed | tf_op | source)
XLA Modules:
  0.0 168.9 jit_solution(4517077577192890364)
XLA Ops:
  0.0 3.8 %reshape.33.mine = bf16[16,4,128,128]{3,2,1,0:T(8,128)(2,1)S(1)} reshape(bf16[64,1,4,4096]{3,2,1,0:T(4,128)(2,1)} %param.5) | data formatting | bytes 4194304 | tf_op jit(solution)/shard_map/reshape | solution.py:434
  3.8 1.5 collective-permute-start.1
  6.9 4.4 %split.1 = (bf16[1040,128]{1,0:T(8,128)(2,1)}, bf16[1040,128]{1,0:T(8,128)(2,1)}) custom-call(s32[4]{0:T(128)} %pad_add_fusion.2.core.at.refs_0_, bf16[8,8,4096]{2,1,0:T(8,128)(2,1)} %bitcast.12, s32[16,128]{1,0:T(8,128)} %fusion.2.i_ref), custom_call_target="tpu_custom_call" | custom-call | tf_op jit(solution)/shard_map/split/pallas_call | solution.py:98
  11.4 1.7 %collective-permute-done = bf16[1040,128]{1,0:T(8,128)(2,1)S(1)} collective-permute-done((bf16[1040,128]{1,0:T(8,128)(2,1)}, bf16[1040,128]{1,0:T(8,128)(2,1)S(1)}, u32[]{:S(2)}, u32[]{:S(2)}) %collective-permute-start) | collective-permute-done | bytes 266272 | tf_op jit(solution)/shard_map/ppermute | solution.py:52
  13.1 1.8 %pad_maximum_fusion = bf16[2080,128]{1,0:T(8,128)(2,1)} fusion(bf16[1040,128]{1,0:T(8,128)(2,1)S(1)} %collective-permute-done, bf16[1040,128]{1,0:T(8,128)(2,1)} %get-tuple-element.33), kind=kLoop, calls=%fused_computation | loop fusion | flops 1064960 | bytes 1064960 | tf_op jit(solution)/shard_map/concatenate | solution.py:444
  16.2 1.4 collective-permute-start.3
  18.2 6.2 %regroup.1 = (bf16[2,4,4,128,128]{4,3,2,1,0:T(8,128)(2,1)S(1)}, bf16[3,4,4,128,128]{4,3,2,1,0:T(8,128)(2,1)}, bf16[3,4,4,128,128]{4,3,2,1,0:T(8,128)(2,1)}) custom-call(s32[4]{0:T(128)S(1)} %copy-done, bf16[16,4,128,128]{3,2,1,0:T(8,128)(2,1)S(1)} %reshape.33.mine, bf16[16,4,128,128]{3,2,1,0:T(8,128)(2,1)} %collective-permute-done.1.other), custom_call_target="tpu_custom_call" | custom-call | tf_op jit(solution)/shard_map/regroup/pallas_call | solution.py:132
  25.5 1.4 collective-permute-start.6
  26.8 1.4 collective-permute-start.7
  32.1 2.7 %collective-permute-start.5 = (bf16[1040,128]{1,0:T(8,128)(2,1)S(1)}, bf16[1040,128]{1,0:T(8,128)(2,1)S(1)}, u32[]{:S(2)}, u32[]{:S(2)}) collective-permute-start(bf16[1040,128]{1,0:T(8,128)(2,1)S(1)} %slice.21), channel_id=1, source_target_pairs={{0,96},{32,0},{64,32},{96,64},{1,97},{33,1},{65,33},{97,65},{2,98}... | collective-permute-start | bytes 798728 | tf_op jit(solution)/shard_map/ppermute | solution.py:48
  35.8 1.4 collective-permute-start.8
  38.5 2.7 %collective-permute-start.9 = (bf16[4160,128]{1,0:T(8,128)(2,1)S(1)}, bf16[4160,128]{1,0:T(8,128)(2,1)S(1)}, u32[]{:S(2)}, u32[]{:S(2)}) collective-permute-start(bf16[4160,128]{1,0:T(8,128)(2,1)S(1)} %constant_dynamic-update-slice_fusion.2.refs_4_), channel_id=1, source_target_pairs={{0,12},{4,0},{8,4},{12,8},{1,13},{5,1},{9,5},{13,9},{2,14},{6,2},{... | collective-permute-start | bytes 3194888 | tf_op jit(solution)/shard_map/ppermute | solution.py:36
  41.1 5.4 %collective-permute-done.6.refs_1_.refs_2_ = bf16[3,4,4,128,128]{4,3,2,1,0:T(8,128)(2,1)S(1)} collective-permute-done((bf16[3,4,4,128,128]{4,3,2,1,0:T(8,128)(2,1)}, bf16[3,4,4,128,128]{4,3,2,1,0:T(8,128)(2,1)S(1)}, u32[]{:S(2)}, u32[]{:S(2)}) %collective-permute-start.6) | collective-permute-done | bytes 1572896 | tf_op jit(solution)/shard_map/ppermute | solution.py:36
  47.9 1.4 collective-permute-start.11
  49.3 8.3 %own_panel.1.refs_9_ = f32[4,8,32,16,128]{4,3,2,1,0:T(8,128)S(1)} custom-call(s32[4]{0:T(128)S(1)} %copy-done, bf16[2,4,4,128,128]{4,3,2,1,0:T(8,128)(2,1)S(1)} %copy-done.2, bf16[2,4,4,128,128]{4,3,2,1,0:T(8,128)(2,1)S(1)} %copy-done.2, bf16[4160,128]{1,0:T(8,128)(2,1)S(1)} %constant_dynamic-update-slice_fusion.refs_3_, ...), custom_call_target="tpu_custom_call" | custom-call | flops 9900000256 | bytes 18000000 | tf_op jit(solution)/shard_map/own_panel/pallas_call | solution.py:282
  58.0 2.5 %collective-permute-start.13 = (bf16[1,4,4,128,128]{4,3,2,1,0:T(8,128)(2,1)S(1)}, bf16[1,4,4,128,128]{4,3,2,1,0:T(8,128)(2,1)S(1)}, u32[]{:S(2)}, u32[]{:S(2)}) collective-permute-start(bf16[1,4,4,128,128]{4,3,2,1,0:T(8,128)(2,1)S(1)} %slice.23), channel_id=1, source_target_pairs={{0,12},{4,0},{8,4},{12,8},{1,13},{5,1},{9,5},{13,9},{2,14},{6,2},{... | collective-permute-start | bytes 1572872 | tf_op jit(solution)/shard_map/ppermute | solution.py:36
  60.5 8.9 %collective-permute-done.10.refs_6_ = bf16[4160,128]{1,0:T(8,128)(2,1)S(1)} collective-permute-done((bf16[4160,128]{1,0:T(8,128)(2,1)S(1)}, bf16[4160,128]{1,0:T(8,128)(2,1)S(1)}, u32[]{:S(2)}, u32[]{:S(2)}) %collective-permute-start.10) | collective-permute-done | bytes 1064992 | tf_op jit(solution)/shard_map/ppermute | solution.py:36
  69.4 1.5 collective-permute-start.15
  70.9 14.5 %near_panels.1.refs_5_ = f32[4,8,32,16,128]{4,3,2,1,0:T(8,128)S(1)} custom-call(s32[4]{0:T(128)S(1)} %copy-done, bf16[3,4,4,128,128]{4,3,2,1,0:T(8,128)(2,1)S(1)} %collective-permute-done.6.refs_1_.refs_2_, bf16[3,4,4,128,128]{4,3,2,1,0:T(8,128)(2,1)S(1)} %collective-permute-done.6.refs_1_.refs_2_, ...), custom_call_target="tpu_custom_call" | custom-call | flops 17600000000 | bytes 32000000 | tf_op jit(solution)/shard_map/near_panels/pallas_call | solution.py:282
  86.5 3.9 %last_coded.3 = (s16[4,33,16,128]{3,2,1,0:T(8,128)(2,1)S(1)}, s16[4,33,16,128]{3,2,1,0:T(8,128)(2,1)S(1)}) custom-call(s32[4]{0:T(128)S(1)} %copy-done, bf16[1,4,4,128,128]{4,3,2,1,0:T(8,128)(2,1)S(1)} %collective-permute-done.12.refs_1_, bf16[1,4,4,128,128]{4,3,2,1,0:T(8,128)(2,1)S(1)} %collective-permute-done.13.refs_2_, ...), custom_call_target="tpu_custom_call" | custom-call | flops 4400000000 | bytes 8000000 | tf_op jit(solution)/shard_map/last_coded/pallas_call | solution.py:282
  90.3 1.7 %collective-permute-start.18 = (s16[4,33,16,128]{3,2,1,0:T(8,128)(2,1)S(1)}, s16[4,33,16,128]{3,2,1,0:T(8,128)(2,1)S(1)}, u32[]{:S(2)}, u32[]{:S(2)}) collective-permute-start(s16[4,33,16,128]{3,2,1,0:T(8,128)(2,1)S(1)} %get-tuple-element.55), channel_id=1, source_target_pairs={{0,1},{1,2},{2,3},{3,0},{4,5},{5,6},{6,7},{7,4},{8,9},{9,10},{10,1... | collective-permute-start | bytes 1622024 | tf_op jit(solution)/shard_map/ppermute | solution.py:36
  92.0 2.2 %collective-permute-start.19 = (s16[4,33,16,128]{3,2,1,0:T(8,128)(2,1)S(1)}, s16[4,33,16,128]{3,2,1,0:T(8,128)(2,1)S(1)}, u32[]{:S(2)}, u32[]{:S(2)}) collective-permute-start(s16[4,33,16,128]{3,2,1,0:T(8,128)(2,1)S(1)} %get-tuple-element.56), channel_id=1, source_target_pairs={{0,3},{1,0},{2,1},{3,2},{4,7},{5,4},{6,5},{7,6},{8,11},{9,8},{10,9... | collective-permute-start | bytes 1622024 | tf_op jit(solution)/shard_map/ppermute | solution.py:36
  94.3 3.9 %last_coded.2 = (s16[4,33,16,128]{3,2,1,0:T(8,128)(2,1)S(1)}, s16[4,33,16,128]{3,2,1,0:T(8,128)(2,1)S(1)}) custom-call(s32[4]{0:T(128)S(1)} %copy-done, bf16[1,4,4,128,128]{4,3,2,1,0:T(8,128)(2,1)S(1)} %collective-permute-done.12.refs_1_, bf16[1,4,4,128,128]{4,3,2,1,0:T(8,128)(2,1)S(1)} %collective-permute-done.13.refs_2_, ...), custom_call_target="tpu_custom_call" | custom-call | flops 4400000000 | bytes 8000000 | tf_op jit(solution)/shard_map/last_coded/pallas_call | solution.py:282
  98.1 1.5 collective-permute-start.16
  99.7 1.5 collective-permute-done.18.refs_6_
  101.2 3.9 %last_sent.1 = (s16[4,33,16,128]{3,2,1,0:T(8,128)(2,1)S(1)}, s16[4,33,16,128]{3,2,1,0:T(8,128)(2,1)S(1)}) custom-call(s32[4]{0:T(128)S(1)} %copy-done, bf16[1,4,4,128,128]{4,3,2,1,0:T(8,128)(2,1)S(1)} %collective-permute-done.12.refs_1_, bf16[1,4,4,128,128]{4,3,2,1,0:T(8,128)(2,1)S(1)} %collective-permute-done.13.refs_2_, ...), custom_call_target="tpu_custom_call" | custom-call | flops 4400000000 | bytes 8000000 | tf_op jit(solution)/shard_map/last_sent/pallas_call | solution.py:282
  106.2 2.1 %collective-permute-start.21 = (s16[4,33,16,128]{3,2,1,0:T(8,128)(2,1)S(1)}, s16[4,33,16,128]{3,2,1,0:T(8,128)(2,1)S(1)}, u32[]{:S(2)}, u32[]{:S(2)}) collective-permute-start(s16[4,33,16,128]{3,2,1,0:T(8,128)(2,1)S(1)} %get-tuple-element.58), channel_id=1, source_target_pairs={{0,3},{1,0},{2,1},{3,2},{4,7},{5,4},{6,5},{7,6},{8,11},{9,8},{10,9... | collective-permute-start | bytes 1622024 | tf_op jit(solution)/shard_map/ppermute | solution.py:36
  109.3 3.3 %last_own.1.own = f32[1,8,32,16,128]{4,3,2,1,0:T(8,128)S(1)} custom-call(s32[4]{0:T(128)S(1)} %copy-done, bf16[1,4,4,128,128]{4,3,2,1,0:T(8,128)(2,1)S(1)} %collective-permute-done.12.refs_1_, bf16[1,4,4,128,128]{4,3,2,1,0:T(8,128)(2,1)S(1)} %collective-permute-done.13.refs_2_, bf16[4160,128]{1,0:T(8,128)(2,1)S(1)} %collective-permute-done.14.refs_3_, ...), custom_call_target="tpu_custom_call" | custom-call | flops 4400000000 | bytes 8000000 | tf_op jit(solution)/shard_map/last_own/pallas_call | solution.py:282
  112.7 2.4 %collective-permute-done.20.prev0 = s16[4,33,16,128]{3,2,1,0:T(8,128)(2,1)S(1)} collective-permute-done((s16[4,33,16,128]{3,2,1,0:T(8,128)(2,1)S(1)}, s16[4,33,16,128]{3,2,1,0:T(8,128)(2,1)S(1)}, u32[]{:S(2)}, u32[]{:S(2)}) %collective-permute-start.20) | collective-permute-done | bytes 540704 | tf_op jit(solution)/shard_map/ppermute | solution.py:36
  115.1 5.5 %pack.1 = s16[128,72,128]{2,1,0:T(8,128)(2,1)S(1)} custom-call(s32[256]{0:T(256)S(1)} %add_bitcast_fusion.slots, f32[1,8,32,16,128]{4,3,2,1,0:T(8,128)S(1)} %last_own.1.own, s16[4,33,16,128]{3,2,1,0:T(8,128)(2,1)S(1)} %collective-permute-done.20.prev0, s16[4,33,16,128]{3,2,1,0:T(8,128)(2,1)S(1)} %collective-permute-done.21.next1), custom_call_target="tpu_custom_call" | custom-call | tf_op jit(solution)/shard_map/pack/pallas_call | solution.py:376
  120.6 43.1 %all_to_all.5 = s16[128,72,128]{2,1,0:T(8,128)(2,1)S(1)} all-to-all(s16[128,72,128]{2,1,0:T(8,128)(2,1)S(1)} %pack.1), channel_id=1, replica_groups=mesh['x'=4,'core'=2,'z'=4,'y'=4] {'x','core','z','y'}, dimensions={0} | all-to-all | bytes 4718592 | tf_op jit(solution)/shard_map/all_to_all | solution.py:491
  163.7 5.2 %unpack.1 = f32[256,4096]{1,0:T(8,128)} custom-call(s16[4,2,16,72,128]{4,3,2,1,0:T(8,128)(2,1)S(1)} %bitcast.11), custom_call_target="tpu_custom_call" | custom-call | tf_op jit(solution)/shard_map/unpack/pallas_call | solution.py:416
  (60 shorter events, 15.6 us)
Async XLA Ops:
  0.0 5.3 %copy-start.4 = (s32[1,8,8]{2,1,0:T(8,128)S(1)}, s32[1,8,8]{2,1,0:T(8,128)}, u32[]{:S(2)}) copy-start(s32[1,8,8]{2,1,0:T(8,128)} %param.8) | copy-start | bytes 772
  0.0 5.4 %copy-start.5 = (s32[64,1,4]{0,2,1:T(4,128)S(1)}, s32[64,1,4]{0,2,1:T(4,128)}, u32[]{:S(2)}) copy-start(s32[64,1,4]{0,2,1:T(4,128)} %param.6) | copy-start | bytes 3076
  0.0 6.3 %copy-start.3 = (s32[128,1]{0,1:T(1,128)S(1)}, s32[128,1]{0,1:T(1,128)}, u32[]{:S(2)}) copy-start(s32[128,1]{0,1:T(1,128)} %param.9) | copy-start | bytes 1540
  3.8 11.0 %collective-permute-start.1 = (bf16[16,4,128,128]{3,2,1,0:T(8,128)(2,1)S(1)}, bf16[16,4,128,128]{3,2,1,0:T(8,128)(2,1)}, u32[]{:S(2)}, u32[]{:S(2)}) collective-permute-start(bf16[16,4,128,128]{3,2,1,0:T(8,128)(2,1)S(1)} %reshape.33.mine), channel_id=1, source_target_pairs={{0,16},{16,0},{1,17},{17,1},{2,18},{18,2},{3,19},{19,3},{4,20},{20... | collective-permute-start | bytes 6291464 | tf_op jit(solution)/shard_map/ppermute | solution.py:52
  6.3 12.0 %copy-start = (s32[4]{0:T(128)S(1)}, s32[4]{0:T(128)}, u32[]{:S(2)}) copy-start(s32[4]{0:T(128)} %pad_add_fusion.2.core.at.refs_0_) | copy-start | bytes 52
  11.3 1.8 %collective-permute-start = (bf16[1040,128]{1,0:T(8,128)(2,1)}, bf16[1040,128]{1,0:T(8,128)(2,1)S(1)}, u32[]{:S(2)}, u32[]{:S(2)}) collective-permute-start(bf16[1040,128]{1,0:T(8,128)(2,1)} %get-tuple-element.34), channel_id=1, source_target_pairs={{0,16},{16,0},{1,17},{17,1},{2,18},{18,2},{3,19},{19,3},{4,20},{20... | collective-permute-start | bytes 798728 | tf_op jit(solution)/shard_map/ppermute | solution.py:52
  14.9 15.1 %collective-permute-start.2 = (bf16[2080,128]{1,0:T(8,128)(2,1)}, bf16[2080,128]{1,0:T(8,128)(2,1)}, u32[]{:S(2)}, u32[]{:S(2)}) collective-permute-start(bf16[2080,128]{1,0:T(8,128)(2,1)} %pad_maximum_fusion), channel_id=1, source_target_pairs={{0,32},{32,64},{64,96},{96,0},{1,33},{33,65},{65,97},{97,1},{2,34}... | collective-permute-start | bytes 1597448 | tf_op jit(solution)/shard_map/ppermute | solution.py:48
  16.2 14.9 %collective-permute-start.3 = (bf16[2080,128]{1,0:T(8,128)(2,1)}, bf16[2080,128]{1,0:T(8,128)(2,1)}, u32[]{:S(2)}, u32[]{:S(2)}) collective-permute-start(bf16[2080,128]{1,0:T(8,128)(2,1)} %pad_maximum_fusion), channel_id=1, source_target_pairs={{0,96},{32,0},{64,32},{96,64},{1,97},{33,1},{65,33},{97,65},{2,98}... | collective-permute-start | bytes 1597448 | tf_op jit(solution)/shard_map/ppermute | solution.py:48
  24.5 1.0 copy-start.1
  25.5 21.1 %collective-permute-start.6 = (bf16[3,4,4,128,128]{4,3,2,1,0:T(8,128)(2,1)}, bf16[3,4,4,128,128]{4,3,2,1,0:T(8,128)(2,1)S(1)}, u32[]{:S(2)}, u32[]{:S(2)}) collective-permute-start(bf16[3,4,4,128,128]{4,3,2,1,0:T(8,128)(2,1)} %get-tuple-element.39), channel_id=1, source_target_pairs={{0,4},{4,8},{8,12},{12,0},{1,5},{5,9},{9,13},{13,1},{2,6},{6,10},{... | collective-permute-start | bytes 4718600 | tf_op jit(solution)/shard_map/ppermute | solution.py:36
  26.8 19.8 %collective-permute-start.7 = (bf16[3,4,4,128,128]{4,3,2,1,0:T(8,128)(2,1)}, bf16[3,4,4,128,128]{4,3,2,1,0:T(8,128)(2,1)S(1)}, u32[]{:S(2)}, u32[]{:S(2)}) collective-permute-start(bf16[3,4,4,128,128]{4,3,2,1,0:T(8,128)(2,1)} %get-tuple-element.40), channel_id=1, source_target_pairs={{0,12},{4,0},{8,4},{12,8},{1,13},{5,1},{9,5},{13,9},{2,14},{6,2},{... | collective-permute-start | bytes 4718600 | tf_op jit(solution)/shard_map/ppermute | solution.py:36
  30.9 7.5 %collective-permute-start.4 = (bf16[1040,128]{1,0:T(8,128)(2,1)S(1)}, bf16[1040,128]{1,0:T(8,128)(2,1)S(1)}, u32[]{:S(2)}, u32[]{:S(2)}) collective-permute-start(bf16[1040,128]{1,0:T(8,128)(2,1)S(1)} %slice.20), channel_id=1, source_target_pairs={{0,32},{32,64},{64,96},{96,0},{1,33},{33,65},{65,97},{97,1},{2,34}... | collective-permute-start | bytes 798728 | tf_op jit(solution)/shard_map/ppermute | solution.py:48
  32.1 6.4 %collective-permute-start.5 = (bf16[1040,128]{1,0:T(8,128)(2,1)S(1)}, bf16[1040,128]{1,0:T(8,128)(2,1)S(1)}, u32[]{:S(2)}, u32[]{:S(2)}) collective-permute-start(bf16[1040,128]{1,0:T(8,128)(2,1)S(1)} %slice.21), channel_id=1, source_target_pairs={{0,96},{32,0},{64,32},{96,64},{1,97},{33,1},{65,33},{97,65},{2,98}... | collective-permute-start | bytes 798728 | tf_op jit(solution)/shard_map/ppermute | solution.py:48
  35.8 13.5 %copy-start.2 = (bf16[2,4,4,128,128]{4,3,2,1,0:T(8,128)(2,1)S(1)}, bf16[2,4,4,128,128]{4,3,2,1,0:T(8,128)(2,1)}, u32[]{:S(2)}) copy-start(bf16[2,4,4,128,128]{4,3,2,1,0:T(8,128)(2,1)} %copy-done.1) | copy-start | bytes 3145732
  35.8 22.2 %collective-permute-start.8 = (bf16[4160,128]{1,0:T(8,128)(2,1)S(1)}, bf16[4160,128]{1,0:T(8,128)(2,1)S(1)}, u32[]{:S(2)}, u32[]{:S(2)}) collective-permute-start(bf16[4160,128]{1,0:T(8,128)(2,1)S(1)} %constant_dynamic-update-slice_fusion.refs_3_), channel_id=1, source_target_pairs={{0,4},{4,8},{8,12},{12,0},{1,5},{5,9},{9,13},{13,1},{2,6},{6,10},{... | collective-permute-start | bytes 3194888 | tf_op jit(solution)/shard_map/ppermute | solution.py:36
  38.5 22.1 %collective-permute-start.9 = (bf16[4160,128]{1,0:T(8,128)(2,1)S(1)}, bf16[4160,128]{1,0:T(8,128)(2,1)S(1)}, u32[]{:S(2)}, u32[]{:S(2)}) collective-permute-start(bf16[4160,128]{1,0:T(8,128)(2,1)S(1)} %constant_dynamic-update-slice_fusion.2.refs_4_), channel_id=1, source_target_pairs={{0,12},{4,0},{8,4},{12,8},{1,13},{5,1},{9,5},{13,9},{2,14},{6,2},{... | collective-permute-start | bytes 3194888 | tf_op jit(solution)/shard_map/ppermute | solution.py:36
  46.6 22.8 %collective-permute-start.10 = (bf16[4160,128]{1,0:T(8,128)(2,1)S(1)}, bf16[4160,128]{1,0:T(8,128)(2,1)S(1)}, u32[]{:S(2)}, u32[]{:S(2)}) collective-permute-start(bf16[4160,128]{1,0:T(8,128)(2,1)S(1)} %constant_dynamic-update-slice_fusion.2.refs_4_), channel_id=1, source_target_pairs={{0,4},{4,8},{8,12},{12,0},{1,5},{5,9},{9,13},{13,1},{2,6},{6,10},{... | collective-permute-start | bytes 3194888 | tf_op jit(solution)/shard_map/ppermute | solution.py:36
  47.9 23.0 %collective-permute-start.11 = (bf16[4160,128]{1,0:T(8,128)(2,1)S(1)}, bf16[4160,128]{1,0:T(8,128)(2,1)S(1)}, u32[]{:S(2)}, u32[]{:S(2)}) collective-permute-start(bf16[4160,128]{1,0:T(8,128)(2,1)S(1)} %constant_dynamic-update-slice_fusion.refs_3_), channel_id=1, source_target_pairs={{0,12},{4,0},{8,4},{12,8},{1,13},{5,1},{9,5},{13,9},{2,14},{6,2},{... | collective-permute-start | bytes 3194888 | tf_op jit(solution)/shard_map/ppermute | solution.py:36
  57.7 27.7 %collective-permute-start.12 = (bf16[1,4,4,128,128]{4,3,2,1,0:T(8,128)(2,1)S(1)}, bf16[1,4,4,128,128]{4,3,2,1,0:T(8,128)(2,1)S(1)}, u32[]{:S(2)}, u32[]{:S(2)}) collective-permute-start(bf16[1,4,4,128,128]{4,3,2,1,0:T(8,128)(2,1)S(1)} %slice.22), channel_id=1, source_target_pairs={{0,4},{4,8},{8,12},{12,0},{1,5},{5,9},{9,13},{13,1},{2,6},{6,10},{... | collective-permute-start | bytes 1572872 | tf_op jit(solution)/shard_map/ppermute | solution.py:36
  58.0 27.4 %collective-permute-start.13 = (bf16[1,4,4,128,128]{4,3,2,1,0:T(8,128)(2,1)S(1)}, bf16[1,4,4,128,128]{4,3,2,1,0:T(8,128)(2,1)S(1)}, u32[]{:S(2)}, u32[]{:S(2)}) collective-permute-start(bf16[1,4,4,128,128]{4,3,2,1,0:T(8,128)(2,1)S(1)} %slice.23), channel_id=1, source_target_pairs={{0,12},{4,0},{8,4},{12,8},{1,13},{5,1},{9,5},{13,9},{2,14},{6,2},{... | collective-permute-start | bytes 1572872 | tf_op jit(solution)/shard_map/ppermute | solution.py:36
  60.5 25.9 %collective-permute-start.14 = (bf16[4160,128]{1,0:T(8,128)(2,1)S(1)}, bf16[4160,128]{1,0:T(8,128)(2,1)S(1)}, u32[]{:S(2)}, u32[]{:S(2)}) collective-permute-start(bf16[4160,128]{1,0:T(8,128)(2,1)S(1)} %collective-permute-done.8.refs_5_), channel_id=1, source_target_pairs={{0,4},{4,8},{8,12},{12,0},{1,5},{5,9},{9,13},{13,1},{2,6},{6,10},{... | collective-permute-start | bytes 3194888 | tf_op jit(solution)/shard_map/ppermute | solution.py:36
  69.4 17.1 %collective-permute-start.15 = (bf16[4160,128]{1,0:T(8,128)(2,1)S(1)}, bf16[4160,128]{1,0:T(8,128)(2,1)S(1)}, u32[]{:S(2)}, u32[]{:S(2)}) collective-permute-start(bf16[4160,128]{1,0:T(8,128)(2,1)S(1)} %collective-permute-done.9.refs_8_), channel_id=1, source_target_pairs={{0,12},{4,0},{8,4},{12,8},{1,13},{5,1},{9,5},{13,9},{2,14},{6,2},{... | collective-permute-start | bytes 3194888 | tf_op jit(solution)/shard_map/ppermute | solution.py:36
  90.3 10.9 %collective-permute-start.18 = (s16[4,33,16,128]{3,2,1,0:T(8,128)(2,1)S(1)}, s16[4,33,16,128]{3,2,1,0:T(8,128)(2,1)S(1)}, u32[]{:S(2)}, u32[]{:S(2)}) collective-permute-start(s16[4,33,16,128]{3,2,1,0:T(8,128)(2,1)S(1)} %get-tuple-element.55), channel_id=1, source_target_pairs={{0,1},{1,2},{2,3},{3,0},{4,5},{5,6},{6,7},{7,4},{8,9},{9,10},{10,1... | collective-permute-start | bytes 1622024 | tf_op jit(solution)/shard_map/ppermute | solution.py:36
  92.0 9.2 %collective-permute-start.19 = (s16[4,33,16,128]{3,2,1,0:T(8,128)(2,1)S(1)}, s16[4,33,16,128]{3,2,1,0:T(8,128)(2,1)S(1)}, u32[]{:S(2)}, u32[]{:S(2)}) collective-permute-start(s16[4,33,16,128]{3,2,1,0:T(8,128)(2,1)S(1)} %get-tuple-element.56), channel_id=1, source_target_pairs={{0,3},{1,0},{2,1},{3,2},{4,7},{5,4},{6,5},{7,6},{8,11},{9,8},{10,9... | collective-permute-start | bytes 1622024 | tf_op jit(solution)/shard_map/ppermute | solution.py:36
  98.1 10.1 %collective-permute-start.16 = (s16[4,33,16,128]{3,2,1,0:T(8,128)(2,1)S(1)}, s16[4,33,16,128]{3,2,1,0:T(8,128)(2,1)S(1)}, u32[]{:S(2)}, u32[]{:S(2)}) collective-permute-start(s16[4,33,16,128]{3,2,1,0:T(8,128)(2,1)S(1)} %get-tuple-element.53), channel_id=1, source_target_pairs={{0,3},{1,0},{2,1},{3,2},{4,7},{5,4},{6,5},{7,6},{8,11},{9,8},{10,9... | collective-permute-start | bytes 1622024 | tf_op jit(solution)/shard_map/ppermute | solution.py:36
  99.6 9.7 %collective-permute-start.17 = (s16[4,33,16,128]{3,2,1,0:T(8,128)(2,1)S(1)}, s16[4,33,16,128]{3,2,1,0:T(8,128)(2,1)S(1)}, u32[]{:S(2)}, u32[]{:S(2)}) collective-permute-start(s16[4,33,16,128]{3,2,1,0:T(8,128)(2,1)S(1)} %get-tuple-element.54), channel_id=1, source_target_pairs={{0,1},{1,2},{2,3},{3,0},{4,5},{5,6},{6,7},{7,4},{8,9},{9,10},{10,1... | collective-permute-start | bytes 1622024 | tf_op jit(solution)/shard_map/ppermute | solution.py:36
  105.1 10.0 %collective-permute-start.20 = (s16[4,33,16,128]{3,2,1,0:T(8,128)(2,1)S(1)}, s16[4,33,16,128]{3,2,1,0:T(8,128)(2,1)S(1)}, u32[]{:S(2)}, u32[]{:S(2)}) collective-permute-start(s16[4,33,16,128]{3,2,1,0:T(8,128)(2,1)S(1)} %get-tuple-element.57), channel_id=1, source_target_pairs={{0,1},{1,2},{2,3},{3,0},{4,5},{5,6},{6,7},{7,4},{8,9},{9,10},{10,1... | collective-permute-start | bytes 1622024 | tf_op jit(solution)/shard_map/ppermute | solution.py:36
  106.2 8.9 %collective-permute-start.21 = (s16[4,33,16,128]{3,2,1,0:T(8,128)(2,1)S(1)}, s16[4,33,16,128]{3,2,1,0:T(8,128)(2,1)S(1)}, u32[]{:S(2)}, u32[]{:S(2)}) collective-permute-start(s16[4,33,16,128]{3,2,1,0:T(8,128)(2,1)S(1)} %get-tuple-element.58), channel_id=1, source_target_pairs={{0,3},{1,0},{2,1},{3,2},{4,7},{5,4},{6,5},{7,6},{8,11},{9,8},{10,9... | collective-permute-start | bytes 1622024 | tf_op jit(solution)/shard_map/ppermute | solution.py:36

commit v13 on v12

--- a/solution.py
+++ b/solution.py
@@ -110,16 +110,16 @@
     )(core, dens, ints)
 
 
-def regroup_kernel(at, mine, other, own, ahead, back, sems):
+def regroup_kernel(at, mine, other, ahead, back, sems):
     swapped, line, cross = at[0] == 1, at[1], at[2]
     copies = []
-    for step in range(4):
+    for step in (1, 2, 3):
         t = (line + step) % 4
         for i, rel in enumerate(ORDER):
             o = (cross + rel) % 4
             row = jnp.where(swapped, o * 4 + t, t * 4 + o)
             for m, src in enumerate((mine, other)):
-                dst = (own.at[m, i], ahead.at[m, i], (ahead, back)[m].at[2, i], back.at[m, i])[step]
+                dst = (ahead.at[m, i], (ahead, back)[m].at[2, i], back.at[m, i])[step - 1]
                 copies.append(pltpu.make_async_copy(src.at[row], dst, sems.at[len(copies)]))
     for copy in copies:
         copy.start()
@@ -128,14 +128,14 @@
 
 
 def regroup(at, mine, other):
-    shapes = [(2, 4, 4, 128, 128), (3, 4, 4, 128, 128), (3, 4, 4, 128, 128)]
+    shapes = [(3, 4, 4, 128, 128)] * 2
     return pl.pallas_call(
         regroup_kernel,
         grid_spec=pltpu.PrefetchScalarGridSpec(
             num_scalar_prefetch=1, grid=(1,),
             in_specs=[pl.BlockSpec(memory_space=pl.ANY)] * 2,
             out_specs=[pl.BlockSpec(s, lambda i, *_: (0,) * 5, pipeline_mode=pl.Buffered(1)) for s in shapes],
-            scratch_shapes=[pltpu.SemaphoreType.DMA((32,))],
+            scratch_shapes=[pltpu.SemaphoreType.DMA((24,))],
         ),
         out_shape=[jax.ShapeDtypeStruct(shape, jnp.bfloat16) for shape in shapes],
         compiler_params=pltpu.CompilerParams(vmem_limit_bytes=12 << 20),
@@ -162,6 +162,8 @@
 def panel_kernel(n, pieces, halves, form, at, *refs):
     kohn, refs = refs[:2 * n], refs[2 * n:]
     panels, refs = refs[:pieces], refs[pieces:]
+    if form == "first":
+        picked, picked_sems, refs = refs[-2], refs[-1], refs[:-2]
     if form != "first":
         sums_in, refs = refs[0], refs[1:]
     received = ()
@@ -174,7 +176,13 @@
 
     loads = [pltpu.make_async_copy(panels[s], dens.at[pl.ds(s * size, size)], sems.at[s]) for s in range(pieces)]
     sums = []
-    if form != "first":
+    if form == "first":
+        for i, rel in enumerate(ORDER):
+            goal = (cross + rel) & 3
+            row = jnp.where(core == 1, goal * 4 + line, line * 4 + goal)
+            for m in range(2):
+                loads.append(pltpu.make_async_copy(kohn[m].at[row], picked.at[m, i], picked_sems.at[m * 4 + i]))
+    else:
         for h, (target, m) in enumerate(halves):
             for q in range(2):
                 src = sums_in.at[target, pl.ds(m * 4 + q * 2, 2)]
@@ -213,8 +221,11 @@
         k = slot * 16 + ((k & 15) ^ (8 * core))
         part = s * 8 + (k >> 3)
         left = dens[pl.ds(pl.multiple_of(part * PART + (k & 7) * 128, 16), 128), :]
-        ref, index = kohn[2 * s + m], target if kohn[2 * s + m].shape[1] == 4 else 0
-        right = twice(ref[0, index, r, a * 32:(a + 1) * 32, :])
+        if form == "first":
+            ref, index = picked.at[m], target
+        else:
+            ref, index = kohn[2 * s + m].at[0], target if kohn[2 * s + m].shape[1] == 4 else 0
+        right = twice(ref[index, r, a * 32:(a + 1) * 32, :])
         r = lax.dot_general(left, right, (((1,), (1,)), ((), ())), preferred_element_type=jnp.float32)
         return s * 16 + (k >> 3), (k & 7) * SP, r
 
@@ -285,7 +296,8 @@
             num_scalar_prefetch=1,
             grid=(1,),
             in_specs=(
-                [k_spec(i, place) for i, (_, place) in enumerate(kohn)] + [any_spec] * pieces
+                [any_spec if form == "first" else k_spec(i, place) for i, (_, place) in enumerate(kohn)]
+                + [any_spec] * pieces
                 + ([] if sums is None else [sums_spec]) + [coded] * len(received)
             ),
             out_specs=o_specs,
@@ -298,7 +310,9 @@
                 pltpu.SemaphoreType.DMA((groups * 2,)),
                 pltpu.VMEM((n * 16, 128), jnp.int32),
                 pltpu.SMEM((n * 16, 128), jnp.int32),
-            ],
+            ] + [
+                pltpu.VMEM((2, 4, 4, 128, 128), jnp.bfloat16), pltpu.SemaphoreType.DMA((8,))
+            ] * (form == "first"),
         ),
         out_shape=shapes,
         compiler_params=pltpu.CompilerParams(vmem_limit_bytes=LIMIT << 20),
@@ -431,21 +445,20 @@
     on_line, on_cross = jnp.where(c == 0, z, y), jnp.where(c == 0, y, z)
     at = jnp.stack([c, on_line, on_cross, x])
 
-    kohn = kohn_blocks.reshape(16, 4, SK * 32, 128)
-    kohn_other = over_core(kohn)
-
     ints = jnp.concatenate([
         kohn_columns.reshape(2, 128), jnp.pad(density_columns.reshape(1, 64), ((0, 0), (0, 64))),
         owner_map.reshape(1, 128), jnp.zeros((12, 128), jnp.int32),
     ])
-    dens, kohn = lax.optimization_barrier((density_blocks[0], kohn))
-
-    mine, theirs = split(at, dens, ints)
+
+    mine, theirs = split(at, density_blocks[0], ints)
+    kohn, mine, theirs = lax.optimization_barrier((kohn_blocks, mine, theirs))
+    kohn = kohn.reshape(16, 4, SK * 32, 128)
+    kohn_other = over_core(kohn)
     shard = jnp.concatenate([mine, over_core(theirs)])
     shard, kohn, kohn_other = lax.optimization_barrier((shard, kohn, kohn_other))
     left, right = over_x(shard, 1), over_x(shard, -1)
 
-    kohn, ahead, back = regroup(at, kohn, kohn_other)
+    ahead, back = regroup(at, kohn, kohn_other)
     kohn_prev, kohn_next = over_line(ahead, 1), over_line(back, -1)
     opposite0, opposite1 = over_line(kohn_prev[2:], 1), over_line(kohn_next[2:], -1)
 
@@ -465,7 +478,7 @@
         return [(array, 0), (array, 1)]
 
     everything = tuple((target, m) for target in range(4) for m in range(2))
-    sums, = panel_sums("own_panel", "first", at, both(kohn), [low, high], everything, us=9.0)
+    sums, = panel_sums("own_panel", "first", at, [(kohn, 0), (kohn_other, 0)], [low, high], everything, us=9.0)
     prev_low, next_high, sums = lax.optimization_barrier((prev_low, next_high, sums))
     far_low, far_high = over_line(prev_low, 1), over_line(next_high, -1)
     sums, = panel_sums(

time: 169 us -> 171 us (1.012)
  Pallas kernels: 59.2 us -> 62.4 us
  other arithmetic: 4.24 us -> 2.48 us
    ppermute x16, waiting for transfers between devices: 20.6 us -> 14.2 us  [over(): lax.ppermute(v, PLANE, [(group[i], group[(i + step) % 4]) for group in gr...]
    ppermute x4, waiting for transfers between devices: 0.03 us -> 4.45 us  [over_x(): return lax.ppermute(v, 'x', [(i, (i + step) % X) for i in range(X)])]
    pallas_call x6, Pallas kernels: 37.8 us -> 40.7 us  [panel_sums(): pl.pallas_call(lambda *refs: panel_kernel(n, pieces, halves, form, *refs)...]
    unnamed x16, local copies, waits for them, and re-layouts: 3.32 us -> 0.91 us
    ppermute x2, waiting for transfers between devices: 1.71 us -> 4.06 us  [over_core(): return lax.ppermute(v, 'core', [(0, 1), (1, 0)])]
    concatenate x1, other arithmetic: 1.77 us -> 0.04 us  [local(): shard = jnp.concatenate([mine, over_core(theirs)])]
  transfers between devices with their start and end apart: 22 -> 22, of which waited for: 8 -> 8; matrix products, arithmetic and copies ran while one was open for 6% -> 3% of each run, Pallas kernels for 26% -> 25%
where the time goes in v13:
time: 171 us
  Pallas kernels  62.4 us (36%)
  blocking collectives  42.8 us (25%)
  starting transfers between devices  30 us (18%)
  waiting for transfers between devices  22.7 us (13%)
  local copies, waits for them, and re-layouts  9.98 us (6%)
  other arithmetic  2.48 us (1%)
    all_to_all x1, blocking collectives, local(): lax.all_to_all(outgoing, ALL, split_axis=0, concat_axis=0, tiled=True)  42.8 us
    pallas_call x6, Pallas kernels, panel_sums(): pl.pallas_call(lambda *refs: panel_kernel(n, pieces, halves, form, *refs)...  40.7 us
    ppermute x16, starting transfers between devices, over(): lax.ppermute(v, PLANE, [(group[i], group[(i + step) % 4]) for group in gr...  22.9 us
    ppermute x16, waiting for transfers between devices, over(): lax.ppermute(v, PLANE, [(group[i], group[(i + step) % 4]) for group in gr...  14.2 us
    pallas_call x1, Pallas kernels, regroup(): pl.pallas_call(regroup_kernel, grid_spec=pltpu.PrefetchScalarGridSpec(num...  6.51 us
    ppermute x4, starting transfers between devices, over_x(): return lax.ppermute(v, 'x', [(i, (i + step) % X) for i in range(X)])  5.56 us
    pallas_call x1, Pallas kernels, pack(): pl.pallas_call(pack_kernel, grid_spec=pltpu.PrefetchScalarGridSpec(num_sc...  5.51 us
    pallas_call x1, Pallas kernels, unpack(): pl.pallas_call(unpack_kernel, grid=(X,), in_specs=[pl.BlockSpec((1, C, 16...  5.22 us
  transfers between devices with their start and end apart: 22, of which 8 were waited for; matrix products, arithmetic and copies ran while one was open for 3% of the time, Pallas kernels for 25%

profile of v13, /device:TPU:1, one launch (start us, length us, event | category | flops | bytes accessed | tf_op | source)
XLA Modules:
  0.0 170.6 jit_solution(7652860941627367247)
XLA Ops:
  3.6 4.4 %split.1 = (bf16[1040,128]{1,0:T(8,128)(2,1)}, bf16[1040,128]{1,0:T(8,128)(2,1)}) custom-call(s32[4]{0:T(128)} %pad_add_fusion.2.core.at.refs_0_, bf16[8,8,4096]{2,1,0:T(8,128)(2,1)} %bitcast.12, s32[16,128]{1,0:T(8,128)} %fusion.2.i_ref), custom_call_target="tpu_custom_call" | custom-call | tf_op jit(solution)/shard_map/split/pallas_call | solution.py:98
  8.0 3.8 %reshape.36.mine.refs_1_ = bf16[16,4,128,128]{3,2,1,0:T(8,128)(2,1)S(1)} reshape(bf16[64,1,4,4096]{3,2,1,0:T(4,128)(2,1)} %param.5) | data formatting | bytes 4194304 | tf_op jit(solution)/shard_map/reshape | solution.py:455
  11.9 1.5 collective-permute-start.1
  13.5 4.1 %collective-permute-done = bf16[1040,128]{1,0:T(8,128)(2,1)S(1)} collective-permute-done((bf16[1040,128]{1,0:T(8,128)(2,1)S(1)}, bf16[1040,128]{1,0:T(8,128)(2,1)S(1)}, u32[]{:S(2)}, u32[]{:S(2)}) %collective-permute-start) | collective-permute-done | bytes 266272 | tf_op jit(solution)/shard_map/ppermute | solution.py:52
  20.4 6.5 %regroup.1 = (bf16[3,4,4,128,128]{4,3,2,1,0:T(8,128)(2,1)}, bf16[3,4,4,128,128]{4,3,2,1,0:T(8,128)(2,1)}) custom-call(s32[4]{0:T(128)S(1)} %copy-done.2, bf16[16,4,128,128]{3,2,1,0:T(8,128)(2,1)S(1)} %reshape.36.mine.refs_1_, bf16[16,4,128,128]{3,2,1,0:T(8,128)(2,1)S(1)} %collective-permute-done.1.other.refs_2_), custom_call_target="tpu_custom_call" | custom-call | tf_op jit(solution)/shard_map/regroup/pallas_call | solution.py:132
  26.9 1.4 collective-permute-start.6
  28.3 1.5 collective-permute-start.7
  30.5 1.8 %collective-permute-done.2 = bf16[2080,128]{1,0:T(8,128)(2,1)} collective-permute-done((bf16[2080,128]{1,0:T(8,128)(2,1)S(1)}, bf16[2080,128]{1,0:T(8,128)(2,1)}, u32[]{:S(2)}, u32[]{:S(2)}) %collective-permute-start.2) | collective-permute-done | bytes 532512 | tf_op jit(solution)/shard_map/ppermute | solution.py:48
  33.4 2.7 %collective-permute-start.5 = (bf16[1040,128]{1,0:T(8,128)(2,1)S(1)}, bf16[1040,128]{1,0:T(8,128)(2,1)S(1)}, u32[]{:S(2)}, u32[]{:S(2)}) collective-permute-start(bf16[1040,128]{1,0:T(8,128)(2,1)S(1)} %slice.21), channel_id=1, source_target_pairs={{0,96},{32,0},{64,32},{96,64},{1,97},{33,1},{65,33},{97,65},{2,98}... | collective-permute-start | bytes 798728 | tf_op jit(solution)/shard_map/ppermute | solution.py:48
  37.2 1.4 collective-permute-start.8
  38.7 2.6 %collective-permute-done.4 = bf16[1040,128]{1,0:T(8,128)(2,1)S(1)} collective-permute-done((bf16[1040,128]{1,0:T(8,128)(2,1)S(1)}, bf16[1040,128]{1,0:T(8,128)(2,1)S(1)}, u32[]{:S(2)}, u32[]{:S(2)}) %collective-permute-start.4) | collective-permute-done | bytes 266272 | tf_op jit(solution)/shard_map/ppermute | solution.py:48
  41.4 2.9 %collective-permute-start.9 = (bf16[4160,128]{1,0:T(8,128)(2,1)S(1)}, bf16[4160,128]{1,0:T(8,128)(2,1)S(1)}, u32[]{:S(2)}, u32[]{:S(2)}) collective-permute-start(bf16[4160,128]{1,0:T(8,128)(2,1)S(1)} %constant_dynamic-update-slice_fusion.2.refs_4_), channel_id=1, source_target_pairs={{0,12},{4,0},{8,4},{12,8},{1,13},{5,1},{9,5},{13,9},{2,14},{6,2},{... | collective-permute-start | bytes 3194888 | tf_op jit(solution)/shard_map/ppermute | solution.py:36
  44.3 3.9 %collective-permute-done.6.refs_1_.refs_2_ = bf16[3,4,4,128,128]{4,3,2,1,0:T(8,128)(2,1)} collective-permute-done((bf16[3,4,4,128,128]{4,3,2,1,0:T(8,128)(2,1)}, bf16[3,4,4,128,128]{4,3,2,1,0:T(8,128)(2,1)}, u32[]{:S(2)}, u32[]{:S(2)}) %collective-permute-start.6) | collective-permute-done | bytes 1572896 | tf_op jit(solution)/shard_map/ppermute | solution.py:36
  49.5 1.4 collective-permute-start.11
  51.0 9.7 %own_panel.1.refs_9_ = f32[4,8,32,16,128]{4,3,2,1,0:T(8,128)S(1)} custom-call(s32[4]{0:T(128)S(1)} %copy-done.2, bf16[16,4,128,128]{3,2,1,0:T(8,128)(2,1)S(1)} %reshape.36.mine.refs_1_, bf16[16,4,128,128]{3,2,1,0:T(8,128)(2,1)S(1)} %copy-done.1, bf16[4160,128]{1,0:T(8,128)(2,1)S(1)} %constant_dynamic-update-slice_fusion.refs_3_, ...), custom_call_target="tpu_custom_call" | custom-call | flops 9900000256 | bytes 18000000 | tf_op jit(solution)/shard_map/own_panel/pallas_call | solution.py:293
  63.0 2.7 %collective-permute-start.13 = (bf16[1,4,4,128,128]{4,3,2,1,0:T(8,128)(2,1)S(1)}, bf16[1,4,4,128,128]{4,3,2,1,0:T(8,128)(2,1)S(1)}, u32[]{:S(2)}, u32[]{:S(2)}) collective-permute-start(bf16[1,4,4,128,128]{4,3,2,1,0:T(8,128)(2,1)S(1)} %slice.23), channel_id=1, source_target_pairs={{0,12},{4,0},{8,4},{12,8},{1,13},{5,1},{9,5},{13,9},{2,14},{6,2},{... | collective-permute-start | bytes 1572872 | tf_op jit(solution)/shard_map/ppermute | solution.py:36
  65.7 5.2 %collective-permute-done.10.refs_6_ = bf16[4160,128]{1,0:T(8,128)(2,1)S(1)} collective-permute-done((bf16[4160,128]{1,0:T(8,128)(2,1)S(1)}, bf16[4160,128]{1,0:T(8,128)(2,1)S(1)}, u32[]{:S(2)}, u32[]{:S(2)}) %collective-permute-start.10) | collective-permute-done | bytes 1064992 | tf_op jit(solution)/shard_map/ppermute | solution.py:36
  70.9 1.5 collective-permute-start.15
  72.4 16.0 %near_panels.1.refs_5_ = f32[4,8,32,16,128]{4,3,2,1,0:T(8,128)S(1)} custom-call(s32[4]{0:T(128)S(1)} %copy-done.2, bf16[3,4,4,128,128]{4,3,2,1,0:T(8,128)(2,1)} %collective-permute-done.6.refs_1_.refs_2_, bf16[3,4,4,128,128]{4,3,2,1,0:T(8,128)(2,1)} %collective-permute-done.6.refs_1_.refs_2_, ...), custom_call_target="tpu_custom_call" | custom-call | flops 17600000000 | bytes 32000000 | tf_op jit(solution)/shard_map/near_panels/pallas_call | solution.py:293
  88.4 3.9 %last_coded.3 = (s16[4,33,16,128]{3,2,1,0:T(8,128)(2,1)S(1)}, s16[4,33,16,128]{3,2,1,0:T(8,128)(2,1)S(1)}) custom-call(s32[4]{0:T(128)S(1)} %copy-done.2, bf16[1,4,4,128,128]{4,3,2,1,0:T(8,128)(2,1)S(1)} %collective-permute-done.12.refs_1_, bf16[1,4,4,128,128]{4,3,2,1,0:T(8,128)(2,1)S(1)} %collective-permute-done.13.refs_2_, ...), custom_call_target="tpu_custom_call" | custom-call | flops 4400000000 | bytes 8000000 | tf_op jit(solution)/shard_map/last_coded/pallas_call | solution.py:293
  92.3 1.7 collective-permute-start.18
  94.0 2.2 %collective-permute-start.19 = (s16[4,33,16,128]{3,2,1,0:T(8,128)(2,1)S(1)}, s16[4,33,16,128]{3,2,1,0:T(8,128)(2,1)S(1)}, u32[]{:S(2)}, u32[]{:S(2)}) collective-permute-start(s16[4,33,16,128]{3,2,1,0:T(8,128)(2,1)S(1)} %get-tuple-element.56), channel_id=1, source_target_pairs={{0,3},{1,0},{2,1},{3,2},{4,7},{5,4},{6,5},{7,6},{8,11},{9,8},{10,9... | collective-permute-start | bytes 1622024 | tf_op jit(solution)/shard_map/ppermute | solution.py:36
  96.2 3.9 %last_coded.2 = (s16[4,33,16,128]{3,2,1,0:T(8,128)(2,1)S(1)}, s16[4,33,16,128]{3,2,1,0:T(8,128)(2,1)S(1)}) custom-call(s32[4]{0:T(128)S(1)} %copy-done.2, bf16[1,4,4,128,128]{4,3,2,1,0:T(8,128)(2,1)S(1)} %collective-permute-done.12.refs_1_, bf16[1,4,4,128,128]{4,3,2,1,0:T(8,128)(2,1)S(1)} %collective-permute-done.13.refs_2_, ...), custom_call_target="tpu_custom_call" | custom-call | flops 4400000000 | bytes 8000000 | tf_op jit(solution)/shard_map/last_coded/pallas_call | solution.py:293
  100.1 1.4 collective-permute-start.16
  101.6 1.5 collective-permute-done.18.refs_6_
  103.2 3.9 %last_sent.1 = (s16[4,33,16,128]{3,2,1,0:T(8,128)(2,1)S(1)}, s16[4,33,16,128]{3,2,1,0:T(8,128)(2,1)S(1)}) custom-call(s32[4]{0:T(128)S(1)} %copy-done.2, bf16[1,4,4,128,128]{4,3,2,1,0:T(8,128)(2,1)S(1)} %collective-permute-done.12.refs_1_, bf16[1,4,4,128,128]{4,3,2,1,0:T(8,128)(2,1)S(1)} %collective-permute-done.13.refs_2_, ...), custom_call_target="tpu_custom_call" | custom-call | flops 4400000000 | bytes 8000000 | tf_op jit(solution)/shard_map/last_sent/pallas_call | solution.py:293
  108.1 2.1 %collective-permute-start.21 = (s16[4,33,16,128]{3,2,1,0:T(8,128)(2,1)S(1)}, s16[4,33,16,128]{3,2,1,0:T(8,128)(2,1)S(1)}, u32[]{:S(2)}, u32[]{:S(2)}) collective-permute-start(s16[4,33,16,128]{3,2,1,0:T(8,128)(2,1)S(1)} %get-tuple-element.58), channel_id=1, source_target_pairs={{0,3},{1,0},{2,1},{3,2},{4,7},{5,4},{6,5},{7,6},{8,11},{9,8},{10,9... | collective-permute-start | bytes 1622024 | tf_op jit(solution)/shard_map/ppermute | solution.py:36
  111.3 3.3 %last_own.1.own = f32[1,8,32,16,128]{4,3,2,1,0:T(8,128)S(1)} custom-call(s32[4]{0:T(128)S(1)} %copy-done.2, bf16[1,4,4,128,128]{4,3,2,1,0:T(8,128)(2,1)S(1)} %collective-permute-done.12.refs_1_, bf16[1,4,4,128,128]{4,3,2,1,0:T(8,128)(2,1)S(1)} %collective-permute-done.13.refs_2_, bf16[4160,128]{1,0:T(8,128)(2,1)S(1)} %collective-permute-done.14.refs_3_, ...), custom_call_target="tpu_custom_call" | custom-call | flops 4400000000 | bytes 8000000 | tf_op jit(solution)/shard_map/last_own/pallas_call | solution.py:293
  114.6 2.5 %collective-permute-done.20.prev0 = s16[4,33,16,128]{3,2,1,0:T(8,128)(2,1)S(1)} collective-permute-done((s16[4,33,16,128]{3,2,1,0:T(8,128)(2,1)S(1)}, s16[4,33,16,128]{3,2,1,0:T(8,128)(2,1)S(1)}, u32[]{:S(2)}, u32[]{:S(2)}) %collective-permute-start.20) | collective-permute-done | bytes 540704 | tf_op jit(solution)/shard_map/ppermute | solution.py:36
  117.1 5.5 %pack.1 = s16[128,72,128]{2,1,0:T(8,128)(2,1)S(1)} custom-call(s32[256]{0:T(256)S(1)} %add_bitcast_fusion.slots, f32[1,8,32,16,128]{4,3,2,1,0:T(8,128)S(1)} %last_own.1.own, s16[4,33,16,128]{3,2,1,0:T(8,128)(2,1)S(1)} %collective-permute-done.20.prev0, s16[4,33,16,128]{3,2,1,0:T(8,128)(2,1)S(1)} %collective-permute-done.21.next1), custom_call_target="tpu_custom_call" | custom-call | tf_op jit(solution)/shard_map/pack/pallas_call | solution.py:390
  122.6 42.8 %all_to_all.5 = s16[128,72,128]{2,1,0:T(8,128)(2,1)S(1)} all-to-all(s16[128,72,128]{2,1,0:T(8,128)(2,1)S(1)} %pack.1), channel_id=1, replica_groups=mesh['x'=4,'core'=2,'z'=4,'y'=4] {'x','core','z','y'}, dimensions={0} | all-to-all | bytes 4718592 | tf_op jit(solution)/shard_map/all_to_all | solution.py:504
  165.4 5.2 %unpack.1 = f32[256,4096]{1,0:T(8,128)} custom-call(s16[4,2,16,72,128]{4,3,2,1,0:T(8,128)(2,1)S(1)} %bitcast.11), custom_call_target="tpu_custom_call" | custom-call | tf_op jit(solution)/shard_map/unpack/pallas_call | solution.py:430
  (60 shorter events, 15.3 us)
Async XLA Ops:
  8.0 5.4 %copy-start.5 = (bf16[1040,128]{1,0:T(8,128)(2,1)S(1)}, bf16[1040,128]{1,0:T(8,128)(2,1)}, u32[]{:S(2)}) copy-start(bf16[1040,128]{1,0:T(8,128)(2,1)} %get-tuple-element.35) | copy-start | bytes 798724
  8.0 9.5 %copy-start.3 = (bf16[1040,128]{1,0:T(8,128)(2,1)S(1)}, bf16[1040,128]{1,0:T(8,128)(2,1)}, u32[]{:S(2)}) copy-start(bf16[1040,128]{1,0:T(8,128)(2,1)} %get-tuple-element.34) | copy-start | bytes 798724
  11.9 8.5 %copy-start.2 = (s32[4]{0:T(128)S(1)}, s32[4]{0:T(128)}, u32[]{:S(2)}) copy-start(s32[4]{0:T(128)} %pad_add_fusion.2.core.at.refs_0_) | copy-start | bytes 52
  11.9 5.7 %collective-permute-start.1 = (bf16[16,4,128,128]{3,2,1,0:T(8,128)(2,1)S(1)}, bf16[16,4,128,128]{3,2,1,0:T(8,128)(2,1)S(1)}, u32[]{:S(2)}, u32[]{:S(2)}) collective-permute-start(bf16[16,4,128,128]{3,2,1,0:T(8,128)(2,1)S(1)} %reshape.36.mine.refs_1_), channel_id=1, source_target_pairs={{0,16},{16,0},{1,17},{17,1},{2,18},{18,2},{3,19},{19,3},{4,20},{20... | collective-permute-start | bytes 6291464 | tf_op jit(solution)/shard_map/ppermute | solution.py:52
  13.4 4.2 %collective-permute-start = (bf16[1040,128]{1,0:T(8,128)(2,1)S(1)}, bf16[1040,128]{1,0:T(8,128)(2,1)S(1)}, u32[]{:S(2)}, u32[]{:S(2)}) collective-permute-start(bf16[1040,128]{1,0:T(8,128)(2,1)S(1)} %copy-done.5), channel_id=1, source_target_pairs={{0,16},{16,0},{1,17},{17,1},{2,18},{18,2},{3,19},{19,3},{4,20},{20... | collective-permute-start | bytes 798728 | tf_op jit(solution)/shard_map/ppermute | solution.py:52
  17.6 9.3 %copy-start = (bf16[16,4,128,128]{3,2,1,0:T(8,128)(2,1)}, bf16[16,4,128,128]{3,2,1,0:T(8,128)(2,1)S(1)}, u32[]{:S(2)}) copy-start(bf16[16,4,128,128]{3,2,1,0:T(8,128)(2,1)S(1)} %collective-permute-done.1.other.refs_2_) | copy-start | bytes 6291460
  17.6 14.7 %collective-permute-start.2 = (bf16[2080,128]{1,0:T(8,128)(2,1)S(1)}, bf16[2080,128]{1,0:T(8,128)(2,1)}, u32[]{:S(2)}, u32[]{:S(2)}) collective-permute-start(bf16[2080,128]{1,0:T(8,128)(2,1)S(1)} %pad_maximum_fusion), channel_id=1, source_target_pairs={{0,32},{32,64},{64,96},{96,0},{1,33},{33,65},{65,97},{97,1},{2,34}... | collective-permute-start | bytes 1597448 | tf_op jit(solution)/shard_map/ppermute | solution.py:48
  19.0 14.5 %collective-permute-start.3 = (bf16[2080,128]{1,0:T(8,128)(2,1)S(1)}, bf16[2080,128]{1,0:T(8,128)(2,1)S(1)}, u32[]{:S(2)}, u32[]{:S(2)}) collective-permute-start(bf16[2080,128]{1,0:T(8,128)(2,1)S(1)} %pad_maximum_fusion), channel_id=1, source_target_pairs={{0,96},{32,0},{64,32},{96,64},{1,97},{33,1},{65,33},{97,65},{2,98}... | collective-permute-start | bytes 1597448 | tf_op jit(solution)/shard_map/ppermute | solution.py:48
  20.4 9.5 %copy-start.4 = (s32[128,1]{0,1:T(1,128)S(1)}, s32[128,1]{0,1:T(1,128)}, u32[]{:S(2)}) copy-start(s32[128,1]{0,1:T(1,128)} %param.9) | copy-start | bytes 1540
  26.9 21.3 %collective-permute-start.6 = (bf16[3,4,4,128,128]{4,3,2,1,0:T(8,128)(2,1)}, bf16[3,4,4,128,128]{4,3,2,1,0:T(8,128)(2,1)}, u32[]{:S(2)}, u32[]{:S(2)}) collective-permute-start(bf16[3,4,4,128,128]{4,3,2,1,0:T(8,128)(2,1)} %get-tuple-element.40), channel_id=1, source_target_pairs={{0,4},{4,8},{8,12},{12,0},{1,5},{5,9},{9,13},{13,1},{2,6},{6,10},{... | collective-permute-start | bytes 4718600 | tf_op jit(solution)/shard_map/ppermute | solution.py:36
  28.3 19.9 %collective-permute-start.7 = (bf16[3,4,4,128,128]{4,3,2,1,0:T(8,128)(2,1)}, bf16[3,4,4,128,128]{4,3,2,1,0:T(8,128)(2,1)}, u32[]{:S(2)}, u32[]{:S(2)}) collective-permute-start(bf16[3,4,4,128,128]{4,3,2,1,0:T(8,128)(2,1)} %get-tuple-element.41), channel_id=1, source_target_pairs={{0,12},{4,0},{8,4},{12,8},{1,13},{5,1},{9,5},{13,9},{2,14},{6,2},{... | collective-permute-start | bytes 4718600 | tf_op jit(solution)/shard_map/ppermute | solution.py:36
  33.3 8.1 %collective-permute-start.4 = (bf16[1040,128]{1,0:T(8,128)(2,1)S(1)}, bf16[1040,128]{1,0:T(8,128)(2,1)S(1)}, u32[]{:S(2)}, u32[]{:S(2)}) collective-permute-start(bf16[1040,128]{1,0:T(8,128)(2,1)S(1)} %slice.20), channel_id=1, source_target_pairs={{0,32},{32,64},{64,96},{96,0},{1,33},{33,65},{65,97},{97,1},{2,34}... | collective-permute-start | bytes 798728 | tf_op jit(solution)/shard_map/ppermute | solution.py:48
  33.4 7.9 %collective-permute-start.5 = (bf16[1040,128]{1,0:T(8,128)(2,1)S(1)}, bf16[1040,128]{1,0:T(8,128)(2,1)S(1)}, u32[]{:S(2)}, u32[]{:S(2)}) collective-permute-start(bf16[1040,128]{1,0:T(8,128)(2,1)S(1)} %slice.21), channel_id=1, source_target_pairs={{0,96},{32,0},{64,32},{96,64},{1,97},{33,1},{65,33},{97,65},{2,98}... | collective-permute-start | bytes 798728 | tf_op jit(solution)/shard_map/ppermute | solution.py:48
  37.2 13.7 %copy-start.1 = (bf16[16,4,128,128]{3,2,1,0:T(8,128)(2,1)S(1)}, bf16[16,4,128,128]{3,2,1,0:T(8,128)(2,1)}, u32[]{:S(2)}) copy-start(bf16[16,4,128,128]{3,2,1,0:T(8,128)(2,1)} %copy-done) | copy-start | bytes 6291460
  37.2 25.7 %collective-permute-start.8 = (bf16[4160,128]{1,0:T(8,128)(2,1)S(1)}, bf16[4160,128]{1,0:T(8,128)(2,1)S(1)}, u32[]{:S(2)}, u32[]{:S(2)}) collective-permute-start(bf16[4160,128]{1,0:T(8,128)(2,1)S(1)} %constant_dynamic-update-slice_fusion.refs_3_), channel_id=1, source_target_pairs={{0,4},{4,8},{8,12},{12,0},{1,5},{5,9},{9,13},{13,1},{2,6},{6,10},{... | collective-permute-start | bytes 3194888 | tf_op jit(solution)/shard_map/ppermute | solution.py:36
  41.4 24.3 %collective-permute-start.9 = (bf16[4160,128]{1,0:T(8,128)(2,1)S(1)}, bf16[4160,128]{1,0:T(8,128)(2,1)S(1)}, u32[]{:S(2)}, u32[]{:S(2)}) collective-permute-start(bf16[4160,128]{1,0:T(8,128)(2,1)S(1)} %constant_dynamic-update-slice_fusion.2.refs_4_), channel_id=1, source_target_pairs={{0,12},{4,0},{8,4},{12,8},{1,13},{5,1},{9,5},{13,9},{2,14},{6,2},{... | collective-permute-start | bytes 3194888 | tf_op jit(solution)/shard_map/ppermute | solution.py:36
  48.2 22.7 %collective-permute-start.10 = (bf16[4160,128]{1,0:T(8,128)(2,1)S(1)}, bf16[4160,128]{1,0:T(8,128)(2,1)S(1)}, u32[]{:S(2)}, u32[]{:S(2)}) collective-permute-start(bf16[4160,128]{1,0:T(8,128)(2,1)S(1)} %constant_dynamic-update-slice_fusion.2.refs_4_), channel_id=1, source_target_pairs={{0,4},{4,8},{8,12},{12,0},{1,5},{5,9},{9,13},{13,1},{2,6},{6,10},{... | collective-permute-start | bytes 3194888 | tf_op jit(solution)/shard_map/ppermute | solution.py:36
  49.5 22.9 %collective-permute-start.11 = (bf16[4160,128]{1,0:T(8,128)(2,1)S(1)}, bf16[4160,128]{1,0:T(8,128)(2,1)S(1)}, u32[]{:S(2)}, u32[]{:S(2)}) collective-permute-start(bf16[4160,128]{1,0:T(8,128)(2,1)S(1)} %constant_dynamic-update-slice_fusion.refs_3_), channel_id=1, source_target_pairs={{0,12},{4,0},{8,4},{12,8},{1,13},{5,1},{9,5},{13,9},{2,14},{6,2},{... | collective-permute-start | bytes 3194888 | tf_op jit(solution)/shard_map/ppermute | solution.py:36
  61.8 26.6 %collective-permute-start.12 = (bf16[1,4,4,128,128]{4,3,2,1,0:T(8,128)(2,1)S(1)}, bf16[1,4,4,128,128]{4,3,2,1,0:T(8,128)(2,1)S(1)}, u32[]{:S(2)}, u32[]{:S(2)}) collective-permute-start(bf16[1,4,4,128,128]{4,3,2,1,0:T(8,128)(2,1)S(1)} %slice.22), channel_id=1, source_target_pairs={{0,4},{4,8},{8,12},{12,0},{1,5},{5,9},{9,13},{13,1},{2,6},{6,10},{... | collective-permute-start | bytes 1572872 | tf_op jit(solution)/shard_map/ppermute | solution.py:36
  63.0 25.4 %collective-permute-start.13 = (bf16[1,4,4,128,128]{4,3,2,1,0:T(8,128)(2,1)S(1)}, bf16[1,4,4,128,128]{4,3,2,1,0:T(8,128)(2,1)S(1)}, u32[]{:S(2)}, u32[]{:S(2)}) collective-permute-start(bf16[1,4,4,128,128]{4,3,2,1,0:T(8,128)(2,1)S(1)} %slice.23), channel_id=1, source_target_pairs={{0,12},{4,0},{8,4},{12,8},{1,13},{5,1},{9,5},{13,9},{2,14},{6,2},{... | collective-permute-start | bytes 1572872 | tf_op jit(solution)/shard_map/ppermute | solution.py:36
  65.7 22.7 %collective-permute-start.14 = (bf16[4160,128]{1,0:T(8,128)(2,1)S(1)}, bf16[4160,128]{1,0:T(8,128)(2,1)S(1)}, u32[]{:S(2)}, u32[]{:S(2)}) collective-permute-start(bf16[4160,128]{1,0:T(8,128)(2,1)S(1)} %collective-permute-done.8.refs_5_), channel_id=1, source_target_pairs={{0,4},{4,8},{8,12},{12,0},{1,5},{5,9},{9,13},{13,1},{2,6},{6,10},{... | collective-permute-start | bytes 3194888 | tf_op jit(solution)/shard_map/ppermute | solution.py:36
  70.9 17.5 %collective-permute-start.15 = (bf16[4160,128]{1,0:T(8,128)(2,1)S(1)}, bf16[4160,128]{1,0:T(8,128)(2,1)S(1)}, u32[]{:S(2)}, u32[]{:S(2)}) collective-permute-start(bf16[4160,128]{1,0:T(8,128)(2,1)S(1)} %collective-permute-done.9.refs_8_), channel_id=1, source_target_pairs={{0,12},{4,0},{8,4},{12,8},{1,13},{5,1},{9,5},{13,9},{2,14},{6,2},{... | collective-permute-start | bytes 3194888 | tf_op jit(solution)/shard_map/ppermute | solution.py:36
  92.3 10.9 %collective-permute-start.18 = (s16[4,33,16,128]{3,2,1,0:T(8,128)(2,1)S(1)}, s16[4,33,16,128]{3,2,1,0:T(8,128)(2,1)S(1)}, u32[]{:S(2)}, u32[]{:S(2)}) collective-permute-start(s16[4,33,16,128]{3,2,1,0:T(8,128)(2,1)S(1)} %get-tuple-element.55), channel_id=1, source_target_pairs={{0,1},{1,2},{2,3},{3,0},{4,5},{5,6},{6,7},{7,4},{8,9},{9,10},{10,1... | collective-permute-start | bytes 1622024 | tf_op jit(solution)/shard_map/ppermute | solution.py:36
  94.0 9.2 %collective-permute-start.19 = (s16[4,33,16,128]{3,2,1,0:T(8,128)(2,1)S(1)}, s16[4,33,16,128]{3,2,1,0:T(8,128)(2,1)S(1)}, u32[]{:S(2)}, u32[]{:S(2)}) collective-permute-start(s16[4,33,16,128]{3,2,1,0:T(8,128)(2,1)S(1)} %get-tuple-element.56), channel_id=1, source_target_pairs={{0,3},{1,0},{2,1},{3,2},{4,7},{5,4},{6,5},{7,6},{8,11},{9,8},{10,9... | collective-permute-start | bytes 1622024 | tf_op jit(solution)/shard_map/ppermute | solution.py:36
  100.1 10.1 %collective-permute-start.16 = (s16[4,33,16,128]{3,2,1,0:T(8,128)(2,1)S(1)}, s16[4,33,16,128]{3,2,1,0:T(8,128)(2,1)S(1)}, u32[]{:S(2)}, u32[]{:S(2)}) collective-permute-start(s16[4,33,16,128]{3,2,1,0:T(8,128)(2,1)S(1)} %get-tuple-element.53), channel_id=1, source_target_pairs={{0,3},{1,0},{2,1},{3,2},{4,7},{5,4},{6,5},{7,6},{8,11},{9,8},{10,9... | collective-permute-start | bytes 1622024 | tf_op jit(solution)/shard_map/ppermute | solution.py:36
  101.5 9.7 %collective-permute-start.17 = (s16[4,33,16,128]{3,2,1,0:T(8,128)(2,1)S(1)}, s16[4,33,16,128]{3,2,1,0:T(8,128)(2,1)S(1)}, u32[]{:S(2)}, u32[]{:S(2)}) collective-permute-start(s16[4,33,16,128]{3,2,1,0:T(8,128)(2,1)S(1)} %get-tuple-element.54), channel_id=1, source_target_pairs={{0,1},{1,2},{2,3},{3,0},{4,5},{5,6},{6,7},{7,4},{8,9},{9,10},{10,1... | collective-permute-start | bytes 1622024 | tf_op jit(solution)/shard_map/ppermute | solution.py:36
  107.1 10.0 %collective-permute-start.20 = (s16[4,33,16,128]{3,2,1,0:T(8,128)(2,1)S(1)}, s16[4,33,16,128]{3,2,1,0:T(8,128)(2,1)S(1)}, u32[]{:S(2)}, u32[]{:S(2)}) collective-permute-start(s16[4,33,16,128]{3,2,1,0:T(8,128)(2,1)S(1)} %get-tuple-element.57), channel_id=1, source_target_pairs={{0,1},{1,2},{2,3},{3,0},{4,5},{5,6},{6,7},{7,4},{8,9},{9,10},{10,1... | collective-permute-start | bytes 1622024 | tf_op jit(solution)/shard_map/ppermute | solution.py:36
  108.1 8.9 %collective-permute-start.21 = (s16[4,33,16,128]{3,2,1,0:T(8,128)(2,1)S(1)}, s16[4,33,16,128]{3,2,1,0:T(8,128)(2,1)S(1)}, u32[]{:S(2)}, u32[]{:S(2)}) collective-permute-start(s16[4,33,16,128]{3,2,1,0:T(8,128)(2,1)S(1)} %get-tuple-element.58), channel_id=1, source_target_pairs={{0,3},{1,0},{2,1},{3,2},{4,7},{5,4},{6,5},{7,6},{8,11},{9,8},{10,9... | collective-permute-start | bytes 1622024 | tf_op jit(solution)/shard_map/ppermute | solution.py:36

commit v14 on v12

--- a/solution.py
+++ b/solution.py
@@ -254,7 +254,11 @@
     for h in range(len(halves)):
         for copy in sums[2 * h:2 * h + 2]:
             copy.wait()
-        lax.fori_loop(0, 2, lambda pair, _, h=h: (two_rows(h, pair), 0)[1], 0)
+        if len(halves) > 2:
+            lax.fori_loop(0, 2, lambda pair, _, h=h: (two_rows(h, pair), 0)[1], 0)
+        else:
+            two_rows(h, 0)
+            two_rows(h, 1)
         for copy in stores[2 * h:2 * h + 2]:
             copy.start()
     for copy in stores:
@@ -307,7 +311,7 @@
     )(at, *[array for array, _ in kohn], *panels, *([] if sums is None else [sums]), *received)
 
 
-def pack_kernel(slots, own, prev0, next1, o_ref, total, codes):
+def pack_kernel(slots, own, prev0, next1, o_ref, total0, total1, codes):
     rows = lax.broadcasted_iota(jnp.int32, (8, 128), 0)
     lane = lax.broadcasted_iota(jnp.int32, (16, 128), 1)
 
@@ -321,7 +325,7 @@
 
     def one(m, r):
         row = m * 4 + r
-        coded = (prev0, next1)[m]
+        coded, total = (prev0, next1)[m], (total0, total1)[m]
         scale = decoded_scale(coded[r, NCW])
         for group in range(NCW // 8):
             blocks = []
@@ -354,10 +358,14 @@
                 slot = slots[row * NCW + j]
                 codes[slot // 4] = jnp.where(rows == slot % 4, code[:8], codes[slot // 4])
 
-        encode(total, put, write_code)
-
-    for m in range(2):
-        lax.fori_loop(0, 4, lambda r, _, m=m: (one(m, r), 0)[1], 0)
+        return lambda: encode(total, put, write_code)
+
+    def both(r, _):
+        for finish_row in [one(m, r) for m in range(2)]:
+            finish_row()
+        return 0
+
+    lax.fori_loop(0, 4, both, 0)
 
     def finish(n, _):
         for m in range(4):
@@ -380,7 +388,7 @@
             grid=(1,),
             in_specs=[whole(array) for array in parts],
             out_specs=pl.BlockSpec((128, MSG, 128), lambda i, *_: (0, 0, 0), pipeline_mode=pl.Buffered(1)),
-            scratch_shapes=[pltpu.VMEM((NCW, 16, 128), jnp.float32), pltpu.VMEM((128, 8, 128), jnp.int32)],
+            scratch_shapes=[pltpu.VMEM((NCW, 16, 128), jnp.float32)] * 2 + [pltpu.VMEM((128, 8, 128), jnp.int32)],
         ),
         out_shape=jax.ShapeDtypeStruct((128, MSG, 128), jnp.int16),
         compiler_params=pltpu.CompilerParams(vmem_limit_bytes=32 << 20),

time: 169 us -> 170 us (level)
  no operation moved by 1% of the time
where the time goes in v14:
time: 170 us; the launch traced here: 169 us
  Pallas kernels  59.2 us (35%)
  blocking collectives  43.2 us (25%)
  starting transfers between devices  29.1 us (17%)
  waiting for transfers between devices  22.8 us (13%)
  local copies, waits for them, and re-layouts  10.6 us (6%)
  other arithmetic  4.24 us (2%)
    all_to_all x1, blocking collectives, local(): lax.all_to_all(outgoing, ALL, split_axis=0, concat_axis=0, tiled=True)  43.2 us
    pallas_call x6, Pallas kernels, panel_sums(): pl.pallas_call(lambda *refs: panel_kernel(n, pieces, halves, form, *refs)...  36.9 us
    ppermute x16, starting transfers between devices, over(): lax.ppermute(v, PLANE, [(group[i], group[(i + step) % 4]) for group in gr...  22.1 us
    ppermute x16, waiting for transfers between devices, over(): lax.ppermute(v, PLANE, [(group[i], group[(i + step) % 4]) for group in gr...  21.1 us
    pallas_call x1, Pallas kernels, pack(): pl.pallas_call(pack_kernel, grid_spec=pltpu.PrefetchScalarGridSpec(num_sc...  6.54 us
    pallas_call x1, Pallas kernels, regroup(): pl.pallas_call(regroup_kernel, grid_spec=pltpu.PrefetchScalarGridSpec(num...  6.2 us
    ppermute x4, starting transfers between devices, over_x(): return lax.ppermute(v, 'x', [(i, (i + step) % X) for i in range(X)])  5.49 us
    pallas_call x1, Pallas kernels, unpack(): pl.pallas_call(unpack_kernel, grid=(X,), in_specs=[pl.BlockSpec((1, C, 16...  5.22 us
  transfers between devices with their start and end apart: 22, of which 8 were waited for; matrix products, arithmetic and copies ran while one was open for 6% of the time, Pallas kernels for 26%

profile of v14, /device:TPU:1, one launch (start us, length us, event | category | flops | bytes accessed | tf_op | source)
XLA Modules:
  0.0 169.3 jit_solution(13980699173405601508)
XLA Ops:
  0.0 3.8 %reshape.33.mine = bf16[16,4,128,128]{3,2,1,0:T(8,128)(2,1)S(1)} reshape(bf16[64,1,4,4096]{3,2,1,0:T(4,128)(2,1)} %param.5) | data formatting | bytes 4194304 | tf_op jit(solution)/shard_map/reshape | solution.py:442
  3.8 1.5 collective-permute-start.1
  6.9 4.4 %split.1 = (bf16[1040,128]{1,0:T(8,128)(2,1)}, bf16[1040,128]{1,0:T(8,128)(2,1)}) custom-call(s32[4]{0:T(128)} %pad_add_fusion.2.core.at.refs_0_, bf16[8,8,4096]{2,1,0:T(8,128)(2,1)} %bitcast.12, s32[16,128]{1,0:T(8,128)} %fusion.2.i_ref), custom_call_target="tpu_custom_call" | custom-call | tf_op jit(solution)/shard_map/split/pallas_call | solution.py:98
  11.4 1.7 %collective-permute-done = bf16[1040,128]{1,0:T(8,128)(2,1)S(1)} collective-permute-done((bf16[1040,128]{1,0:T(8,128)(2,1)}, bf16[1040,128]{1,0:T(8,128)(2,1)S(1)}, u32[]{:S(2)}, u32[]{:S(2)}) %collective-permute-start) | collective-permute-done | bytes 266272 | tf_op jit(solution)/shard_map/ppermute | solution.py:52
  13.1 1.8 %pad_maximum_fusion = bf16[2080,128]{1,0:T(8,128)(2,1)} fusion(bf16[1040,128]{1,0:T(8,128)(2,1)S(1)} %collective-permute-done, bf16[1040,128]{1,0:T(8,128)(2,1)} %get-tuple-element.33), kind=kLoop, calls=%fused_computation | loop fusion | flops 1064960 | bytes 1064960 | tf_op jit(solution)/shard_map/concatenate | solution.py:452
  16.2 1.4 collective-permute-start.3
  18.2 6.2 %regroup.1 = (bf16[2,4,4,128,128]{4,3,2,1,0:T(8,128)(2,1)S(1)}, bf16[3,4,4,128,128]{4,3,2,1,0:T(8,128)(2,1)}, bf16[3,4,4,128,128]{4,3,2,1,0:T(8,128)(2,1)}) custom-call(s32[4]{0:T(128)S(1)} %copy-done, bf16[16,4,128,128]{3,2,1,0:T(8,128)(2,1)S(1)} %reshape.33.mine, bf16[16,4,128,128]{3,2,1,0:T(8,128)(2,1)} %collective-permute-done.1.other), custom_call_target="tpu_custom_call" | custom-call | tf_op jit(solution)/shard_map/regroup/pallas_call | solution.py:132
  25.5 1.4 collective-permute-start.6
  26.8 1.4 collective-permute-start.7
  32.1 2.7 %collective-permute-start.5 = (bf16[1040,128]{1,0:T(8,128)(2,1)S(1)}, bf16[1040,128]{1,0:T(8,128)(2,1)S(1)}, u32[]{:S(2)}, u32[]{:S(2)}) collective-permute-start(bf16[1040,128]{1,0:T(8,128)(2,1)S(1)} %slice.21), channel_id=1, source_target_pairs={{0,96},{32,0},{64,32},{96,64},{1,97},{33,1},{65,33},{97,65},{2,98}... | collective-permute-start | bytes 798728 | tf_op jit(solution)/shard_map/ppermute | solution.py:48
  35.8 1.4 collective-permute-start.8
  38.5 2.7 %collective-permute-start.9 = (bf16[4160,128]{1,0:T(8,128)(2,1)S(1)}, bf16[4160,128]{1,0:T(8,128)(2,1)S(1)}, u32[]{:S(2)}, u32[]{:S(2)}) collective-permute-start(bf16[4160,128]{1,0:T(8,128)(2,1)S(1)} %constant_dynamic-update-slice_fusion.2.refs_4_), channel_id=1, source_target_pairs={{0,12},{4,0},{8,4},{12,8},{1,13},{5,1},{9,5},{13,9},{2,14},{6,2},{... | collective-permute-start | bytes 3194888 | tf_op jit(solution)/shard_map/ppermute | solution.py:36
  41.1 5.4 %collective-permute-done.6.refs_1_.refs_2_ = bf16[3,4,4,128,128]{4,3,2,1,0:T(8,128)(2,1)S(1)} collective-permute-done((bf16[3,4,4,128,128]{4,3,2,1,0:T(8,128)(2,1)}, bf16[3,4,4,128,128]{4,3,2,1,0:T(8,128)(2,1)S(1)}, u32[]{:S(2)}, u32[]{:S(2)}) %collective-permute-start.6) | collective-permute-done | bytes 1572896 | tf_op jit(solution)/shard_map/ppermute | solution.py:36
  47.9 1.4 collective-permute-start.11
  49.3 8.3 %own_panel.1.refs_9_ = f32[4,8,32,16,128]{4,3,2,1,0:T(8,128)S(1)} custom-call(s32[4]{0:T(128)S(1)} %copy-done, bf16[2,4,4,128,128]{4,3,2,1,0:T(8,128)(2,1)S(1)} %copy-done.2, bf16[2,4,4,128,128]{4,3,2,1,0:T(8,128)(2,1)S(1)} %copy-done.2, bf16[4160,128]{1,0:T(8,128)(2,1)S(1)} %constant_dynamic-update-slice_fusion.refs_3_, ...), custom_call_target="tpu_custom_call" | custom-call | flops 9900000256 | bytes 18000000 | tf_op jit(solution)/shard_map/own_panel/pallas_call | solution.py:286
  58.0 2.5 %collective-permute-start.13 = (bf16[1,4,4,128,128]{4,3,2,1,0:T(8,128)(2,1)S(1)}, bf16[1,4,4,128,128]{4,3,2,1,0:T(8,128)(2,1)S(1)}, u32[]{:S(2)}, u32[]{:S(2)}) collective-permute-start(bf16[1,4,4,128,128]{4,3,2,1,0:T(8,128)(2,1)S(1)} %slice.23), channel_id=1, source_target_pairs={{0,12},{4,0},{8,4},{12,8},{1,13},{5,1},{9,5},{13,9},{2,14},{6,2},{... | collective-permute-start | bytes 1572872 | tf_op jit(solution)/shard_map/ppermute | solution.py:36
  60.5 8.9 %collective-permute-done.10.refs_6_ = bf16[4160,128]{1,0:T(8,128)(2,1)S(1)} collective-permute-done((bf16[4160,128]{1,0:T(8,128)(2,1)S(1)}, bf16[4160,128]{1,0:T(8,128)(2,1)S(1)}, u32[]{:S(2)}, u32[]{:S(2)}) %collective-permute-start.10) | collective-permute-done | bytes 1064992 | tf_op jit(solution)/shard_map/ppermute | solution.py:36
  69.4 1.5 collective-permute-start.15
  70.9 14.5 %near_panels.1.refs_5_ = f32[4,8,32,16,128]{4,3,2,1,0:T(8,128)S(1)} custom-call(s32[4]{0:T(128)S(1)} %copy-done, bf16[3,4,4,128,128]{4,3,2,1,0:T(8,128)(2,1)S(1)} %collective-permute-done.6.refs_1_.refs_2_, bf16[3,4,4,128,128]{4,3,2,1,0:T(8,128)(2,1)S(1)} %collective-permute-done.6.refs_1_.refs_2_, ...), custom_call_target="tpu_custom_call" | custom-call | flops 17600000000 | bytes 32000000 | tf_op jit(solution)/shard_map/near_panels/pallas_call | solution.py:286
  86.5 3.4 %last_coded.3 = (s16[4,33,16,128]{3,2,1,0:T(8,128)(2,1)S(1)}, s16[4,33,16,128]{3,2,1,0:T(8,128)(2,1)S(1)}) custom-call(s32[4]{0:T(128)S(1)} %copy-done, bf16[1,4,4,128,128]{4,3,2,1,0:T(8,128)(2,1)S(1)} %collective-permute-done.12.refs_1_, bf16[1,4,4,128,128]{4,3,2,1,0:T(8,128)(2,1)S(1)} %collective-permute-done.13.refs_2_, ...), custom_call_target="tpu_custom_call" | custom-call | flops 4400000000 | bytes 8000000 | tf_op jit(solution)/shard_map/last_coded/pallas_call | solution.py:286
  89.9 1.7 collective-permute-start.18
  91.6 2.2 %collective-permute-start.19 = (s16[4,33,16,128]{3,2,1,0:T(8,128)(2,1)S(1)}, s16[4,33,16,128]{3,2,1,0:T(8,128)(2,1)S(1)}, u32[]{:S(2)}, u32[]{:S(2)}) collective-permute-start(s16[4,33,16,128]{3,2,1,0:T(8,128)(2,1)S(1)} %get-tuple-element.56), channel_id=1, source_target_pairs={{0,3},{1,0},{2,1},{3,2},{4,7},{5,4},{6,5},{7,6},{8,11},{9,8},{10,9... | collective-permute-start | bytes 1622024 | tf_op jit(solution)/shard_map/ppermute | solution.py:36
  93.8 3.4 %last_coded.2 = (s16[4,33,16,128]{3,2,1,0:T(8,128)(2,1)S(1)}, s16[4,33,16,128]{3,2,1,0:T(8,128)(2,1)S(1)}) custom-call(s32[4]{0:T(128)S(1)} %copy-done, bf16[1,4,4,128,128]{4,3,2,1,0:T(8,128)(2,1)S(1)} %collective-permute-done.12.refs_1_, bf16[1,4,4,128,128]{4,3,2,1,0:T(8,128)(2,1)S(1)} %collective-permute-done.13.refs_2_, ...), custom_call_target="tpu_custom_call" | custom-call | flops 4400000000 | bytes 8000000 | tf_op jit(solution)/shard_map/last_coded/pallas_call | solution.py:286
  97.3 1.5 collective-permute-start.16
  98.8 2.0 %collective-permute-done.18.refs_6_ = s16[4,33,16,128]{3,2,1,0:T(8,128)(2,1)S(1)} collective-permute-done((s16[4,33,16,128]{3,2,1,0:T(8,128)(2,1)S(1)}, s16[4,33,16,128]{3,2,1,0:T(8,128)(2,1)S(1)}, u32[]{:S(2)}, u32[]{:S(2)}) %collective-permute-start.18) | collective-permute-done | bytes 540704 | tf_op jit(solution)/shard_map/ppermute | solution.py:36
  100.8 3.8 %last_sent.1 = (s16[4,33,16,128]{3,2,1,0:T(8,128)(2,1)S(1)}, s16[4,33,16,128]{3,2,1,0:T(8,128)(2,1)S(1)}) custom-call(s32[4]{0:T(128)S(1)} %copy-done, bf16[1,4,4,128,128]{4,3,2,1,0:T(8,128)(2,1)S(1)} %collective-permute-done.12.refs_1_, bf16[1,4,4,128,128]{4,3,2,1,0:T(8,128)(2,1)S(1)} %collective-permute-done.13.refs_2_, ...), custom_call_target="tpu_custom_call" | custom-call | flops 4400000000 | bytes 8000000 | tf_op jit(solution)/shard_map/last_sent/pallas_call | solution.py:286
  105.6 1.9 %collective-permute-start.21 = (s16[4,33,16,128]{3,2,1,0:T(8,128)(2,1)S(1)}, s16[4,33,16,128]{3,2,1,0:T(8,128)(2,1)S(1)}, u32[]{:S(2)}, u32[]{:S(2)}) collective-permute-start(s16[4,33,16,128]{3,2,1,0:T(8,128)(2,1)S(1)} %get-tuple-element.58), channel_id=1, source_target_pairs={{0,3},{1,0},{2,1},{3,2},{4,7},{5,4},{6,5},{7,6},{8,11},{9,8},{10,9... | collective-permute-start | bytes 1622024 | tf_op jit(solution)/shard_map/ppermute | solution.py:36
  108.4 3.4 %last_own.1.own = f32[1,8,32,16,128]{4,3,2,1,0:T(8,128)S(1)} custom-call(s32[4]{0:T(128)S(1)} %copy-done, bf16[1,4,4,128,128]{4,3,2,1,0:T(8,128)(2,1)S(1)} %collective-permute-done.12.refs_1_, bf16[1,4,4,128,128]{4,3,2,1,0:T(8,128)(2,1)S(1)} %collective-permute-done.13.refs_2_, bf16[4160,128]{1,0:T(8,128)(2,1)S(1)} %collective-permute-done.14.refs_3_, ...), custom_call_target="tpu_custom_call" | custom-call | flops 4400000000 | bytes 8000000 | tf_op jit(solution)/shard_map/last_own/pallas_call | solution.py:286
  111.8 2.6 %collective-permute-done.20.prev0 = s16[4,33,16,128]{3,2,1,0:T(8,128)(2,1)S(1)} collective-permute-done((s16[4,33,16,128]{3,2,1,0:T(8,128)(2,1)S(1)}, s16[4,33,16,128]{3,2,1,0:T(8,128)(2,1)S(1)}, u32[]{:S(2)}, u32[]{:S(2)}) %collective-permute-start.20) | collective-permute-done | bytes 540704 | tf_op jit(solution)/shard_map/ppermute | solution.py:36
  114.4 6.5 %pack.1 = s16[128,72,128]{2,1,0:T(8,128)(2,1)S(1)} custom-call(s32[256]{0:T(256)S(1)} %add_bitcast_fusion.slots, f32[1,8,32,16,128]{4,3,2,1,0:T(8,128)S(1)} %last_own.1.own, s16[4,33,16,128]{3,2,1,0:T(8,128)(2,1)S(1)} %collective-permute-done.20.prev0, s16[4,33,16,128]{3,2,1,0:T(8,128)(2,1)S(1)} %collective-permute-done.21.next1), custom_call_target="tpu_custom_call" | custom-call | tf_op jit(solution)/shard_map/pack/pallas_call | solution.py:384
  121.0 43.2 %all_to_all.5 = s16[128,72,128]{2,1,0:T(8,128)(2,1)S(1)} all-to-all(s16[128,72,128]{2,1,0:T(8,128)(2,1)S(1)} %pack.1), channel_id=1, replica_groups=mesh['x'=4,'core'=2,'z'=4,'y'=4] {'x','core','z','y'}, dimensions={0} | all-to-all | bytes 4718592 | tf_op jit(solution)/shard_map/all_to_all | solution.py:499
  164.1 5.2 %unpack.1 = f32[256,4096]{1,0:T(8,128)} custom-call(s16[4,2,16,72,128]{4,3,2,1,0:T(8,128)(2,1)S(1)} %bitcast.11), custom_call_target="tpu_custom_call" | custom-call | tf_op jit(solution)/shard_map/unpack/pallas_call | solution.py:424
  (60 shorter events, 15.5 us)
Async XLA Ops:
  0.0 5.3 %copy-start.4 = (s32[1,8,8]{2,1,0:T(8,128)S(1)}, s32[1,8,8]{2,1,0:T(8,128)}, u32[]{:S(2)}) copy-start(s32[1,8,8]{2,1,0:T(8,128)} %param.8) | copy-start | bytes 772
  0.0 5.4 %copy-start.5 = (s32[64,1,4]{0,2,1:T(4,128)S(1)}, s32[64,1,4]{0,2,1:T(4,128)}, u32[]{:S(2)}) copy-start(s32[64,1,4]{0,2,1:T(4,128)} %param.6) | copy-start | bytes 3076
  0.0 6.3 %copy-start.3 = (s32[128,1]{0,1:T(1,128)S(1)}, s32[128,1]{0,1:T(1,128)}, u32[]{:S(2)}) copy-start(s32[128,1]{0,1:T(1,128)} %param.9) | copy-start | bytes 1540
  3.8 11.0 %collective-permute-start.1 = (bf16[16,4,128,128]{3,2,1,0:T(8,128)(2,1)S(1)}, bf16[16,4,128,128]{3,2,1,0:T(8,128)(2,1)}, u32[]{:S(2)}, u32[]{:S(2)}) collective-permute-start(bf16[16,4,128,128]{3,2,1,0:T(8,128)(2,1)S(1)} %reshape.33.mine), channel_id=1, source_target_pairs={{0,16},{16,0},{1,17},{17,1},{2,18},{18,2},{3,19},{19,3},{4,20},{20... | collective-permute-start | bytes 6291464 | tf_op jit(solution)/shard_map/ppermute | solution.py:52
  6.3 12.0 %copy-start = (s32[4]{0:T(128)S(1)}, s32[4]{0:T(128)}, u32[]{:S(2)}) copy-start(s32[4]{0:T(128)} %pad_add_fusion.2.core.at.refs_0_) | copy-start | bytes 52
  11.3 1.8 %collective-permute-start = (bf16[1040,128]{1,0:T(8,128)(2,1)}, bf16[1040,128]{1,0:T(8,128)(2,1)S(1)}, u32[]{:S(2)}, u32[]{:S(2)}) collective-permute-start(bf16[1040,128]{1,0:T(8,128)(2,1)} %get-tuple-element.34), channel_id=1, source_target_pairs={{0,16},{16,0},{1,17},{17,1},{2,18},{18,2},{3,19},{19,3},{4,20},{20... | collective-permute-start | bytes 798728 | tf_op jit(solution)/shard_map/ppermute | solution.py:52
  14.9 15.1 %collective-permute-start.2 = (bf16[2080,128]{1,0:T(8,128)(2,1)}, bf16[2080,128]{1,0:T(8,128)(2,1)}, u32[]{:S(2)}, u32[]{:S(2)}) collective-permute-start(bf16[2080,128]{1,0:T(8,128)(2,1)} %pad_maximum_fusion), channel_id=1, source_target_pairs={{0,32},{32,64},{64,96},{96,0},{1,33},{33,65},{65,97},{97,1},{2,34}... | collective-permute-start | bytes 1597448 | tf_op jit(solution)/shard_map/ppermute | solution.py:48
  16.2 14.9 %collective-permute-start.3 = (bf16[2080,128]{1,0:T(8,128)(2,1)}, bf16[2080,128]{1,0:T(8,128)(2,1)}, u32[]{:S(2)}, u32[]{:S(2)}) collective-permute-start(bf16[2080,128]{1,0:T(8,128)(2,1)} %pad_maximum_fusion), channel_id=1, source_target_pairs={{0,96},{32,0},{64,32},{96,64},{1,97},{33,1},{65,33},{97,65},{2,98}... | collective-permute-start | bytes 1597448 | tf_op jit(solution)/shard_map/ppermute | solution.py:48
  24.5 1.0 copy-start.1
  25.5 21.1 %collective-permute-start.6 = (bf16[3,4,4,128,128]{4,3,2,1,0:T(8,128)(2,1)}, bf16[3,4,4,128,128]{4,3,2,1,0:T(8,128)(2,1)S(1)}, u32[]{:S(2)}, u32[]{:S(2)}) collective-permute-start(bf16[3,4,4,128,128]{4,3,2,1,0:T(8,128)(2,1)} %get-tuple-element.39), channel_id=1, source_target_pairs={{0,4},{4,8},{8,12},{12,0},{1,5},{5,9},{9,13},{13,1},{2,6},{6,10},{... | collective-permute-start | bytes 4718600 | tf_op jit(solution)/shard_map/ppermute | solution.py:36
  26.8 19.8 %collective-permute-start.7 = (bf16[3,4,4,128,128]{4,3,2,1,0:T(8,128)(2,1)}, bf16[3,4,4,128,128]{4,3,2,1,0:T(8,128)(2,1)S(1)}, u32[]{:S(2)}, u32[]{:S(2)}) collective-permute-start(bf16[3,4,4,128,128]{4,3,2,1,0:T(8,128)(2,1)} %get-tuple-element.40), channel_id=1, source_target_pairs={{0,12},{4,0},{8,4},{12,8},{1,13},{5,1},{9,5},{13,9},{2,14},{6,2},{... | collective-permute-start | bytes 4718600 | tf_op jit(solution)/shard_map/ppermute | solution.py:36
  30.9 7.5 %collective-permute-start.4 = (bf16[1040,128]{1,0:T(8,128)(2,1)S(1)}, bf16[1040,128]{1,0:T(8,128)(2,1)S(1)}, u32[]{:S(2)}, u32[]{:S(2)}) collective-permute-start(bf16[1040,128]{1,0:T(8,128)(2,1)S(1)} %slice.20), channel_id=1, source_target_pairs={{0,32},{32,64},{64,96},{96,0},{1,33},{33,65},{65,97},{97,1},{2,34}... | collective-permute-start | bytes 798728 | tf_op jit(solution)/shard_map/ppermute | solution.py:48
  32.1 6.4 %collective-permute-start.5 = (bf16[1040,128]{1,0:T(8,128)(2,1)S(1)}, bf16[1040,128]{1,0:T(8,128)(2,1)S(1)}, u32[]{:S(2)}, u32[]{:S(2)}) collective-permute-start(bf16[1040,128]{1,0:T(8,128)(2,1)S(1)} %slice.21), channel_id=1, source_target_pairs={{0,96},{32,0},{64,32},{96,64},{1,97},{33,1},{65,33},{97,65},{2,98}... | collective-permute-start | bytes 798728 | tf_op jit(solution)/shard_map/ppermute | solution.py:48
  35.8 13.5 %copy-start.2 = (bf16[2,4,4,128,128]{4,3,2,1,0:T(8,128)(2,1)S(1)}, bf16[2,4,4,128,128]{4,3,2,1,0:T(8,128)(2,1)}, u32[]{:S(2)}) copy-start(bf16[2,4,4,128,128]{4,3,2,1,0:T(8,128)(2,1)} %copy-done.1) | copy-start | bytes 3145732
  35.8 22.2 %collective-permute-start.8 = (bf16[4160,128]{1,0:T(8,128)(2,1)S(1)}, bf16[4160,128]{1,0:T(8,128)(2,1)S(1)}, u32[]{:S(2)}, u32[]{:S(2)}) collective-permute-start(bf16[4160,128]{1,0:T(8,128)(2,1)S(1)} %constant_dynamic-update-slice_fusion.refs_3_), channel_id=1, source_target_pairs={{0,4},{4,8},{8,12},{12,0},{1,5},{5,9},{9,13},{13,1},{2,6},{6,10},{... | collective-permute-start | bytes 3194888 | tf_op jit(solution)/shard_map/ppermute | solution.py:36
  38.5 22.1 %collective-permute-start.9 = (bf16[4160,128]{1,0:T(8,128)(2,1)S(1)}, bf16[4160,128]{1,0:T(8,128)(2,1)S(1)}, u32[]{:S(2)}, u32[]{:S(2)}) collective-permute-start(bf16[4160,128]{1,0:T(8,128)(2,1)S(1)} %constant_dynamic-update-slice_fusion.2.refs_4_), channel_id=1, source_target_pairs={{0,12},{4,0},{8,4},{12,8},{1,13},{5,1},{9,5},{13,9},{2,14},{6,2},{... | collective-permute-start | bytes 3194888 | tf_op jit(solution)/shard_map/ppermute | solution.py:36
  46.6 22.8 %collective-permute-start.10 = (bf16[4160,128]{1,0:T(8,128)(2,1)S(1)}, bf16[4160,128]{1,0:T(8,128)(2,1)S(1)}, u32[]{:S(2)}, u32[]{:S(2)}) collective-permute-start(bf16[4160,128]{1,0:T(8,128)(2,1)S(1)} %constant_dynamic-update-slice_fusion.2.refs_4_), channel_id=1, source_target_pairs={{0,4},{4,8},{8,12},{12,0},{1,5},{5,9},{9,13},{13,1},{2,6},{6,10},{... | collective-permute-start | bytes 3194888 | tf_op jit(solution)/shard_map/ppermute | solution.py:36
  47.9 23.0 %collective-permute-start.11 = (bf16[4160,128]{1,0:T(8,128)(2,1)S(1)}, bf16[4160,128]{1,0:T(8,128)(2,1)S(1)}, u32[]{:S(2)}, u32[]{:S(2)}) collective-permute-start(bf16[4160,128]{1,0:T(8,128)(2,1)S(1)} %constant_dynamic-update-slice_fusion.refs_3_), channel_id=1, source_target_pairs={{0,12},{4,0},{8,4},{12,8},{1,13},{5,1},{9,5},{13,9},{2,14},{6,2},{... | collective-permute-start | bytes 3194888 | tf_op jit(solution)/shard_map/ppermute | solution.py:36
  57.7 27.7 %collective-permute-start.12 = (bf16[1,4,4,128,128]{4,3,2,1,0:T(8,128)(2,1)S(1)}, bf16[1,4,4,128,128]{4,3,2,1,0:T(8,128)(2,1)S(1)}, u32[]{:S(2)}, u32[]{:S(2)}) collective-permute-start(bf16[1,4,4,128,128]{4,3,2,1,0:T(8,128)(2,1)S(1)} %slice.22), channel_id=1, source_target_pairs={{0,4},{4,8},{8,12},{12,0},{1,5},{5,9},{9,13},{13,1},{2,6},{6,10},{... | collective-permute-start | bytes 1572872 | tf_op jit(solution)/shard_map/ppermute | solution.py:36
  58.0 27.4 %collective-permute-start.13 = (bf16[1,4,4,128,128]{4,3,2,1,0:T(8,128)(2,1)S(1)}, bf16[1,4,4,128,128]{4,3,2,1,0:T(8,128)(2,1)S(1)}, u32[]{:S(2)}, u32[]{:S(2)}) collective-permute-start(bf16[1,4,4,128,128]{4,3,2,1,0:T(8,128)(2,1)S(1)} %slice.23), channel_id=1, source_target_pairs={{0,12},{4,0},{8,4},{12,8},{1,13},{5,1},{9,5},{13,9},{2,14},{6,2},{... | collective-permute-start | bytes 1572872 | tf_op jit(solution)/shard_map/ppermute | solution.py:36
  60.5 25.9 %collective-permute-start.14 = (bf16[4160,128]{1,0:T(8,128)(2,1)S(1)}, bf16[4160,128]{1,0:T(8,128)(2,1)S(1)}, u32[]{:S(2)}, u32[]{:S(2)}) collective-permute-start(bf16[4160,128]{1,0:T(8,128)(2,1)S(1)} %collective-permute-done.8.refs_5_), channel_id=1, source_target_pairs={{0,4},{4,8},{8,12},{12,0},{1,5},{5,9},{9,13},{13,1},{2,6},{6,10},{... | collective-permute-start | bytes 3194888 | tf_op jit(solution)/shard_map/ppermute | solution.py:36
  69.4 17.1 %collective-permute-start.15 = (bf16[4160,128]{1,0:T(8,128)(2,1)S(1)}, bf16[4160,128]{1,0:T(8,128)(2,1)S(1)}, u32[]{:S(2)}, u32[]{:S(2)}) collective-permute-start(bf16[4160,128]{1,0:T(8,128)(2,1)S(1)} %collective-permute-done.9.refs_8_), channel_id=1, source_target_pairs={{0,12},{4,0},{8,4},{12,8},{1,13},{5,1},{9,5},{13,9},{2,14},{6,2},{... | collective-permute-start | bytes 3194888 | tf_op jit(solution)/shard_map/ppermute | solution.py:36
  89.9 10.9 %collective-permute-start.18 = (s16[4,33,16,128]{3,2,1,0:T(8,128)(2,1)S(1)}, s16[4,33,16,128]{3,2,1,0:T(8,128)(2,1)S(1)}, u32[]{:S(2)}, u32[]{:S(2)}) collective-permute-start(s16[4,33,16,128]{3,2,1,0:T(8,128)(2,1)S(1)} %get-tuple-element.55), channel_id=1, source_target_pairs={{0,1},{1,2},{2,3},{3,0},{4,5},{5,6},{6,7},{7,4},{8,9},{9,10},{10,1... | collective-permute-start | bytes 1622024 | tf_op jit(solution)/shard_map/ppermute | solution.py:36
  91.6 9.2 %collective-permute-start.19 = (s16[4,33,16,128]{3,2,1,0:T(8,128)(2,1)S(1)}, s16[4,33,16,128]{3,2,1,0:T(8,128)(2,1)S(1)}, u32[]{:S(2)}, u32[]{:S(2)}) collective-permute-start(s16[4,33,16,128]{3,2,1,0:T(8,128)(2,1)S(1)} %get-tuple-element.56), channel_id=1, source_target_pairs={{0,3},{1,0},{2,1},{3,2},{4,7},{5,4},{6,5},{7,6},{8,11},{9,8},{10,9... | collective-permute-start | bytes 1622024 | tf_op jit(solution)/shard_map/ppermute | solution.py:36
  97.3 10.2 %collective-permute-start.16 = (s16[4,33,16,128]{3,2,1,0:T(8,128)(2,1)S(1)}, s16[4,33,16,128]{3,2,1,0:T(8,128)(2,1)S(1)}, u32[]{:S(2)}, u32[]{:S(2)}) collective-permute-start(s16[4,33,16,128]{3,2,1,0:T(8,128)(2,1)S(1)} %get-tuple-element.53), channel_id=1, source_target_pairs={{0,3},{1,0},{2,1},{3,2},{4,7},{5,4},{6,5},{7,6},{8,11},{9,8},{10,9... | collective-permute-start | bytes 1622024 | tf_op jit(solution)/shard_map/ppermute | solution.py:36
  98.7 9.7 %collective-permute-start.17 = (s16[4,33,16,128]{3,2,1,0:T(8,128)(2,1)S(1)}, s16[4,33,16,128]{3,2,1,0:T(8,128)(2,1)S(1)}, u32[]{:S(2)}, u32[]{:S(2)}) collective-permute-start(s16[4,33,16,128]{3,2,1,0:T(8,128)(2,1)S(1)} %get-tuple-element.54), channel_id=1, source_target_pairs={{0,1},{1,2},{2,3},{3,0},{4,5},{5,6},{6,7},{7,4},{8,9},{9,10},{10,1... | collective-permute-start | bytes 1622024 | tf_op jit(solution)/shard_map/ppermute | solution.py:36
  104.6 9.9 %collective-permute-start.20 = (s16[4,33,16,128]{3,2,1,0:T(8,128)(2,1)S(1)}, s16[4,33,16,128]{3,2,1,0:T(8,128)(2,1)S(1)}, u32[]{:S(2)}, u32[]{:S(2)}) collective-permute-start(s16[4,33,16,128]{3,2,1,0:T(8,128)(2,1)S(1)} %get-tuple-element.57), channel_id=1, source_target_pairs={{0,1},{1,2},{2,3},{3,0},{4,5},{5,6},{6,7},{7,4},{8,9},{9,10},{10,1... | collective-permute-start | bytes 1622024 | tf_op jit(solution)/shard_map/ppermute | solution.py:36
  105.6 8.8 %collective-permute-start.21 = (s16[4,33,16,128]{3,2,1,0:T(8,128)(2,1)S(1)}, s16[4,33,16,128]{3,2,1,0:T(8,128)(2,1)S(1)}, u32[]{:S(2)}, u32[]{:S(2)}) collective-permute-start(s16[4,33,16,128]{3,2,1,0:T(8,128)(2,1)S(1)} %get-tuple-element.58), channel_id=1, source_target_pairs={{0,3},{1,0},{2,1},{3,2},{4,7},{5,4},{6,5},{7,6},{8,11},{9,8},{10,9... | collective-permute-start | bytes 1622024 | tf_op jit(solution)/shard_map/ppermute | solution.py:36

commit v15 on v12

--- a/solution.py
+++ b/solution.py
@@ -254,7 +254,11 @@
     for h in range(len(halves)):
         for copy in sums[2 * h:2 * h + 2]:
             copy.wait()
-        lax.fori_loop(0, 2, lambda pair, _, h=h: (two_rows(h, pair), 0)[1], 0)
+        if len(halves) > 2:
+            lax.fori_loop(0, 2, lambda pair, _, h=h: (two_rows(h, pair), 0)[1], 0)
+        else:
+            two_rows(h, 0)
+            two_rows(h, 1)
         for copy in stores[2 * h:2 * h + 2]:
             copy.start()
     for copy in stores:

time: 169 us -> 169 us (level)
  no operation moved by 1% of the time
where the time goes in v15:
time: 169 us; the launch traced here: 168 us
  Pallas kernels  58.2 us (34%)
  blocking collectives  43.2 us (26%)
  starting transfers between devices  29.1 us (17%)
  waiting for transfers between devices  22.8 us (13%)
  local copies, waits for them, and re-layouts  10.6 us (6%)
  other arithmetic  4.24 us (3%)
    all_to_all x1, blocking collectives, local(): lax.all_to_all(outgoing, ALL, split_axis=0, concat_axis=0, tiled=True)  43.2 us
    pallas_call x6, Pallas kernels, panel_sums(): pl.pallas_call(lambda *refs: panel_kernel(n, pieces, halves, form, *refs)...  36.9 us
    ppermute x16, starting transfers between devices, over(): lax.ppermute(v, PLANE, [(group[i], group[(i + step) % 4]) for group in gr...  22.1 us
    ppermute x16, waiting for transfers between devices, over(): lax.ppermute(v, PLANE, [(group[i], group[(i + step) % 4]) for group in gr...  21.1 us
    pallas_call x1, Pallas kernels, regroup(): pl.pallas_call(regroup_kernel, grid_spec=pltpu.PrefetchScalarGridSpec(num...  6.2 us
    pallas_call x1, Pallas kernels, pack(): pl.pallas_call(pack_kernel, grid_spec=pltpu.PrefetchScalarGridSpec(num_sc...  5.52 us
    ppermute x4, starting transfers between devices, over_x(): return lax.ppermute(v, 'x', [(i, (i + step) % X) for i in range(X)])  5.49 us
    pallas_call x1, Pallas kernels, unpack(): pl.pallas_call(unpack_kernel, grid=(X,), in_specs=[pl.BlockSpec((1, C, 16...  5.22 us
  transfers between devices with their start and end apart: 22, of which 8 were waited for; matrix products, arithmetic and copies ran while one was open for 6% of the time, Pallas kernels for 26%

profile of v15, /device:TPU:1, one launch (start us, length us, event | category | flops | bytes accessed | tf_op | source)
XLA Modules:
  0.0 168.3 jit_solution(11084026392495804607)
XLA Ops:
  0.0 3.8 %reshape.33.mine = bf16[16,4,128,128]{3,2,1,0:T(8,128)(2,1)S(1)} reshape(bf16[64,1,4,4096]{3,2,1,0:T(4,128)(2,1)} %param.5) | data formatting | bytes 4194304 | tf_op jit(solution)/shard_map/reshape | solution.py:438
  3.8 1.5 collective-permute-start.1
  6.9 4.4 %split.1 = (bf16[1040,128]{1,0:T(8,128)(2,1)}, bf16[1040,128]{1,0:T(8,128)(2,1)}) custom-call(s32[4]{0:T(128)} %pad_add_fusion.2.core.at.refs_0_, bf16[8,8,4096]{2,1,0:T(8,128)(2,1)} %bitcast.12, s32[16,128]{1,0:T(8,128)} %fusion.2.i_ref), custom_call_target="tpu_custom_call" | custom-call | tf_op jit(solution)/shard_map/split/pallas_call | solution.py:98
  11.4 1.7 %collective-permute-done = bf16[1040,128]{1,0:T(8,128)(2,1)S(1)} collective-permute-done((bf16[1040,128]{1,0:T(8,128)(2,1)}, bf16[1040,128]{1,0:T(8,128)(2,1)S(1)}, u32[]{:S(2)}, u32[]{:S(2)}) %collective-permute-start) | collective-permute-done | bytes 266272 | tf_op jit(solution)/shard_map/ppermute | solution.py:52
  13.1 1.8 %pad_maximum_fusion = bf16[2080,128]{1,0:T(8,128)(2,1)} fusion(bf16[1040,128]{1,0:T(8,128)(2,1)S(1)} %collective-permute-done, bf16[1040,128]{1,0:T(8,128)(2,1)} %get-tuple-element.33), kind=kLoop, calls=%fused_computation | loop fusion | flops 1064960 | bytes 1064960 | tf_op jit(solution)/shard_map/concatenate | solution.py:448
  16.2 1.4 collective-permute-start.3
  18.2 6.2 %regroup.1 = (bf16[2,4,4,128,128]{4,3,2,1,0:T(8,128)(2,1)S(1)}, bf16[3,4,4,128,128]{4,3,2,1,0:T(8,128)(2,1)}, bf16[3,4,4,128,128]{4,3,2,1,0:T(8,128)(2,1)}) custom-call(s32[4]{0:T(128)S(1)} %copy-done, bf16[16,4,128,128]{3,2,1,0:T(8,128)(2,1)S(1)} %reshape.33.mine, bf16[16,4,128,128]{3,2,1,0:T(8,128)(2,1)} %collective-permute-done.1.other), custom_call_target="tpu_custom_call" | custom-call | tf_op jit(solution)/shard_map/regroup/pallas_call | solution.py:132
  25.5 1.4 collective-permute-start.6
  26.8 1.4 collective-permute-start.7
  32.1 2.7 %collective-permute-start.5 = (bf16[1040,128]{1,0:T(8,128)(2,1)S(1)}, bf16[1040,128]{1,0:T(8,128)(2,1)S(1)}, u32[]{:S(2)}, u32[]{:S(2)}) collective-permute-start(bf16[1040,128]{1,0:T(8,128)(2,1)S(1)} %slice.21), channel_id=1, source_target_pairs={{0,96},{32,0},{64,32},{96,64},{1,97},{33,1},{65,33},{97,65},{2,98}... | collective-permute-start | bytes 798728 | tf_op jit(solution)/shard_map/ppermute | solution.py:48
  35.8 1.4 collective-permute-start.8
  38.5 2.7 %collective-permute-start.9 = (bf16[4160,128]{1,0:T(8,128)(2,1)S(1)}, bf16[4160,128]{1,0:T(8,128)(2,1)S(1)}, u32[]{:S(2)}, u32[]{:S(2)}) collective-permute-start(bf16[4160,128]{1,0:T(8,128)(2,1)S(1)} %constant_dynamic-update-slice_fusion.2.refs_4_), channel_id=1, source_target_pairs={{0,12},{4,0},{8,4},{12,8},{1,13},{5,1},{9,5},{13,9},{2,14},{6,2},{... | collective-permute-start | bytes 3194888 | tf_op jit(solution)/shard_map/ppermute | solution.py:36
  41.1 5.4 %collective-permute-done.6.refs_1_.refs_2_ = bf16[3,4,4,128,128]{4,3,2,1,0:T(8,128)(2,1)S(1)} collective-permute-done((bf16[3,4,4,128,128]{4,3,2,1,0:T(8,128)(2,1)}, bf16[3,4,4,128,128]{4,3,2,1,0:T(8,128)(2,1)S(1)}, u32[]{:S(2)}, u32[]{:S(2)}) %collective-permute-start.6) | collective-permute-done | bytes 1572896 | tf_op jit(solution)/shard_map/ppermute | solution.py:36
  47.9 1.4 collective-permute-start.11
  49.3 8.3 %own_panel.1.refs_9_ = f32[4,8,32,16,128]{4,3,2,1,0:T(8,128)S(1)} custom-call(s32[4]{0:T(128)S(1)} %copy-done, bf16[2,4,4,128,128]{4,3,2,1,0:T(8,128)(2,1)S(1)} %copy-done.2, bf16[2,4,4,128,128]{4,3,2,1,0:T(8,128)(2,1)S(1)} %copy-done.2, bf16[4160,128]{1,0:T(8,128)(2,1)S(1)} %constant_dynamic-update-slice_fusion.refs_3_, ...), custom_call_target="tpu_custom_call" | custom-call | flops 9900000256 | bytes 18000000 | tf_op jit(solution)/shard_map/own_panel/pallas_call | solution.py:286
  58.0 2.5 %collective-permute-start.13 = (bf16[1,4,4,128,128]{4,3,2,1,0:T(8,128)(2,1)S(1)}, bf16[1,4,4,128,128]{4,3,2,1,0:T(8,128)(2,1)S(1)}, u32[]{:S(2)}, u32[]{:S(2)}) collective-permute-start(bf16[1,4,4,128,128]{4,3,2,1,0:T(8,128)(2,1)S(1)} %slice.23), channel_id=1, source_target_pairs={{0,12},{4,0},{8,4},{12,8},{1,13},{5,1},{9,5},{13,9},{2,14},{6,2},{... | collective-permute-start | bytes 1572872 | tf_op jit(solution)/shard_map/ppermute | solution.py:36
  60.5 8.9 %collective-permute-done.10.refs_6_ = bf16[4160,128]{1,0:T(8,128)(2,1)S(1)} collective-permute-done((bf16[4160,128]{1,0:T(8,128)(2,1)S(1)}, bf16[4160,128]{1,0:T(8,128)(2,1)S(1)}, u32[]{:S(2)}, u32[]{:S(2)}) %collective-permute-start.10) | collective-permute-done | bytes 1064992 | tf_op jit(solution)/shard_map/ppermute | solution.py:36
  69.4 1.5 collective-permute-start.15
  70.9 14.5 %near_panels.1.refs_5_ = f32[4,8,32,16,128]{4,3,2,1,0:T(8,128)S(1)} custom-call(s32[4]{0:T(128)S(1)} %copy-done, bf16[3,4,4,128,128]{4,3,2,1,0:T(8,128)(2,1)S(1)} %collective-permute-done.6.refs_1_.refs_2_, bf16[3,4,4,128,128]{4,3,2,1,0:T(8,128)(2,1)S(1)} %collective-permute-done.6.refs_1_.refs_2_, ...), custom_call_target="tpu_custom_call" | custom-call | flops 17600000000 | bytes 32000000 | tf_op jit(solution)/shard_map/near_panels/pallas_call | solution.py:286
  86.5 3.4 %last_coded.3 = (s16[4,33,16,128]{3,2,1,0:T(8,128)(2,1)S(1)}, s16[4,33,16,128]{3,2,1,0:T(8,128)(2,1)S(1)}) custom-call(s32[4]{0:T(128)S(1)} %copy-done, bf16[1,4,4,128,128]{4,3,2,1,0:T(8,128)(2,1)S(1)} %collective-permute-done.12.refs_1_, bf16[1,4,4,128,128]{4,3,2,1,0:T(8,128)(2,1)S(1)} %collective-permute-done.13.refs_2_, ...), custom_call_target="tpu_custom_call" | custom-call | flops 4400000000 | bytes 8000000 | tf_op jit(solution)/shard_map/last_coded/pallas_call | solution.py:286
  89.9 1.7 %collective-permute-start.18 = (s16[4,33,16,128]{3,2,1,0:T(8,128)(2,1)S(1)}, s16[4,33,16,128]{3,2,1,0:T(8,128)(2,1)S(1)}, u32[]{:S(2)}, u32[]{:S(2)}) collective-permute-start(s16[4,33,16,128]{3,2,1,0:T(8,128)(2,1)S(1)} %get-tuple-element.55), channel_id=1, source_target_pairs={{0,1},{1,2},{2,3},{3,0},{4,5},{5,6},{6,7},{7,4},{8,9},{9,10},{10,1... | collective-permute-start | bytes 1622024 | tf_op jit(solution)/shard_map/ppermute | solution.py:36
  91.6 2.2 %collective-permute-start.19 = (s16[4,33,16,128]{3,2,1,0:T(8,128)(2,1)S(1)}, s16[4,33,16,128]{3,2,1,0:T(8,128)(2,1)S(1)}, u32[]{:S(2)}, u32[]{:S(2)}) collective-permute-start(s16[4,33,16,128]{3,2,1,0:T(8,128)(2,1)S(1)} %get-tuple-element.56), channel_id=1, source_target_pairs={{0,3},{1,0},{2,1},{3,2},{4,7},{5,4},{6,5},{7,6},{8,11},{9,8},{10,9... | collective-permute-start | bytes 1622024 | tf_op jit(solution)/shard_map/ppermute | solution.py:36
  93.8 3.4 %last_coded.2 = (s16[4,33,16,128]{3,2,1,0:T(8,128)(2,1)S(1)}, s16[4,33,16,128]{3,2,1,0:T(8,128)(2,1)S(1)}) custom-call(s32[4]{0:T(128)S(1)} %copy-done, bf16[1,4,4,128,128]{4,3,2,1,0:T(8,128)(2,1)S(1)} %collective-permute-done.12.refs_1_, bf16[1,4,4,128,128]{4,3,2,1,0:T(8,128)(2,1)S(1)} %collective-permute-done.13.refs_2_, ...), custom_call_target="tpu_custom_call" | custom-call | flops 4400000000 | bytes 8000000 | tf_op jit(solution)/shard_map/last_coded/pallas_call | solution.py:286
  97.3 1.5 collective-permute-start.16
  98.8 2.0 %collective-permute-done.18.refs_6_ = s16[4,33,16,128]{3,2,1,0:T(8,128)(2,1)S(1)} collective-permute-done((s16[4,33,16,128]{3,2,1,0:T(8,128)(2,1)S(1)}, s16[4,33,16,128]{3,2,1,0:T(8,128)(2,1)S(1)}, u32[]{:S(2)}, u32[]{:S(2)}) %collective-permute-start.18) | collective-permute-done | bytes 540704 | tf_op jit(solution)/shard_map/ppermute | solution.py:36
  100.8 3.8 %last_sent.1 = (s16[4,33,16,128]{3,2,1,0:T(8,128)(2,1)S(1)}, s16[4,33,16,128]{3,2,1,0:T(8,128)(2,1)S(1)}) custom-call(s32[4]{0:T(128)S(1)} %copy-done, bf16[1,4,4,128,128]{4,3,2,1,0:T(8,128)(2,1)S(1)} %collective-permute-done.12.refs_1_, bf16[1,4,4,128,128]{4,3,2,1,0:T(8,128)(2,1)S(1)} %collective-permute-done.13.refs_2_, ...), custom_call_target="tpu_custom_call" | custom-call | flops 4400000000 | bytes 8000000 | tf_op jit(solution)/shard_map/last_sent/pallas_call | solution.py:286
  105.6 1.9 %collective-permute-start.21 = (s16[4,33,16,128]{3,2,1,0:T(8,128)(2,1)S(1)}, s16[4,33,16,128]{3,2,1,0:T(8,128)(2,1)S(1)}, u32[]{:S(2)}, u32[]{:S(2)}) collective-permute-start(s16[4,33,16,128]{3,2,1,0:T(8,128)(2,1)S(1)} %get-tuple-element.58), channel_id=1, source_target_pairs={{0,3},{1,0},{2,1},{3,2},{4,7},{5,4},{6,5},{7,6},{8,11},{9,8},{10,9... | collective-permute-start | bytes 1622024 | tf_op jit(solution)/shard_map/ppermute | solution.py:36
  108.4 3.4 %last_own.1.own = f32[1,8,32,16,128]{4,3,2,1,0:T(8,128)S(1)} custom-call(s32[4]{0:T(128)S(1)} %copy-done, bf16[1,4,4,128,128]{4,3,2,1,0:T(8,128)(2,1)S(1)} %collective-permute-done.12.refs_1_, bf16[1,4,4,128,128]{4,3,2,1,0:T(8,128)(2,1)S(1)} %collective-permute-done.13.refs_2_, bf16[4160,128]{1,0:T(8,128)(2,1)S(1)} %collective-permute-done.14.refs_3_, ...), custom_call_target="tpu_custom_call" | custom-call | flops 4400000000 | bytes 8000000 | tf_op jit(solution)/shard_map/last_own/pallas_call | solution.py:286
  111.8 2.6 %collective-permute-done.20.prev0 = s16[4,33,16,128]{3,2,1,0:T(8,128)(2,1)S(1)} collective-permute-done((s16[4,33,16,128]{3,2,1,0:T(8,128)(2,1)S(1)}, s16[4,33,16,128]{3,2,1,0:T(8,128)(2,1)S(1)}, u32[]{:S(2)}, u32[]{:S(2)}) %collective-permute-start.20) | collective-permute-done | bytes 540704 | tf_op jit(solution)/shard_map/ppermute | solution.py:36
  114.4 5.5 %pack.1 = s16[128,72,128]{2,1,0:T(8,128)(2,1)S(1)} custom-call(s32[256]{0:T(256)S(1)} %add_bitcast_fusion.slots, f32[1,8,32,16,128]{4,3,2,1,0:T(8,128)S(1)} %last_own.1.own, s16[4,33,16,128]{3,2,1,0:T(8,128)(2,1)S(1)} %collective-permute-done.20.prev0, s16[4,33,16,128]{3,2,1,0:T(8,128)(2,1)S(1)} %collective-permute-done.21.next1), custom_call_target="tpu_custom_call" | custom-call | tf_op jit(solution)/shard_map/pack/pallas_call | solution.py:380
  119.9 43.2 %all_to_all.5 = s16[128,72,128]{2,1,0:T(8,128)(2,1)S(1)} all-to-all(s16[128,72,128]{2,1,0:T(8,128)(2,1)S(1)} %pack.1), channel_id=1, replica_groups=mesh['x'=4,'core'=2,'z'=4,'y'=4] {'x','core','z','y'}, dimensions={0} | all-to-all | bytes 4718592 | tf_op jit(solution)/shard_map/all_to_all | solution.py:495
  163.1 5.2 %unpack.1 = f32[256,4096]{1,0:T(8,128)} custom-call(s16[4,2,16,72,128]{4,3,2,1,0:T(8,128)(2,1)S(1)} %bitcast.11), custom_call_target="tpu_custom_call" | custom-call | tf_op jit(solution)/shard_map/unpack/pallas_call | solution.py:420
  (60 shorter events, 15.5 us)
Async XLA Ops:
  0.0 5.3 %copy-start.4 = (s32[1,8,8]{2,1,0:T(8,128)S(1)}, s32[1,8,8]{2,1,0:T(8,128)}, u32[]{:S(2)}) copy-start(s32[1,8,8]{2,1,0:T(8,128)} %param.8) | copy-start | bytes 772
  0.0 5.4 %copy-start.5 = (s32[64,1,4]{0,2,1:T(4,128)S(1)}, s32[64,1,4]{0,2,1:T(4,128)}, u32[]{:S(2)}) copy-start(s32[64,1,4]{0,2,1:T(4,128)} %param.6) | copy-start | bytes 3076
  0.0 6.3 %copy-start.3 = (s32[128,1]{0,1:T(1,128)S(1)}, s32[128,1]{0,1:T(1,128)}, u32[]{:S(2)}) copy-start(s32[128,1]{0,1:T(1,128)} %param.9) | copy-start | bytes 1540
  3.8 11.0 %collective-permute-start.1 = (bf16[16,4,128,128]{3,2,1,0:T(8,128)(2,1)S(1)}, bf16[16,4,128,128]{3,2,1,0:T(8,128)(2,1)}, u32[]{:S(2)}, u32[]{:S(2)}) collective-permute-start(bf16[16,4,128,128]{3,2,1,0:T(8,128)(2,1)S(1)} %reshape.33.mine), channel_id=1, source_target_pairs={{0,16},{16,0},{1,17},{17,1},{2,18},{18,2},{3,19},{19,3},{4,20},{20... | collective-permute-start | bytes 6291464 | tf_op jit(solution)/shard_map/ppermute | solution.py:52
  6.3 12.0 %copy-start = (s32[4]{0:T(128)S(1)}, s32[4]{0:T(128)}, u32[]{:S(2)}) copy-start(s32[4]{0:T(128)} %pad_add_fusion.2.core.at.refs_0_) | copy-start | bytes 52
  11.3 1.8 %collective-permute-start = (bf16[1040,128]{1,0:T(8,128)(2,1)}, bf16[1040,128]{1,0:T(8,128)(2,1)S(1)}, u32[]{:S(2)}, u32[]{:S(2)}) collective-permute-start(bf16[1040,128]{1,0:T(8,128)(2,1)} %get-tuple-element.34), channel_id=1, source_target_pairs={{0,16},{16,0},{1,17},{17,1},{2,18},{18,2},{3,19},{19,3},{4,20},{20... | collective-permute-start | bytes 798728 | tf_op jit(solution)/shard_map/ppermute | solution.py:52
  14.9 15.1 %collective-permute-start.2 = (bf16[2080,128]{1,0:T(8,128)(2,1)}, bf16[2080,128]{1,0:T(8,128)(2,1)}, u32[]{:S(2)}, u32[]{:S(2)}) collective-permute-start(bf16[2080,128]{1,0:T(8,128)(2,1)} %pad_maximum_fusion), channel_id=1, source_target_pairs={{0,32},{32,64},{64,96},{96,0},{1,33},{33,65},{65,97},{97,1},{2,34}... | collective-permute-start | bytes 1597448 | tf_op jit(solution)/shard_map/ppermute | solution.py:48
  16.2 14.9 %collective-permute-start.3 = (bf16[2080,128]{1,0:T(8,128)(2,1)}, bf16[2080,128]{1,0:T(8,128)(2,1)}, u32[]{:S(2)}, u32[]{:S(2)}) collective-permute-start(bf16[2080,128]{1,0:T(8,128)(2,1)} %pad_maximum_fusion), channel_id=1, source_target_pairs={{0,96},{32,0},{64,32},{96,64},{1,97},{33,1},{65,33},{97,65},{2,98}... | collective-permute-start | bytes 1597448 | tf_op jit(solution)/shard_map/ppermute | solution.py:48
  24.5 1.0 copy-start.1
  25.5 21.1 %collective-permute-start.6 = (bf16[3,4,4,128,128]{4,3,2,1,0:T(8,128)(2,1)}, bf16[3,4,4,128,128]{4,3,2,1,0:T(8,128)(2,1)S(1)}, u32[]{:S(2)}, u32[]{:S(2)}) collective-permute-start(bf16[3,4,4,128,128]{4,3,2,1,0:T(8,128)(2,1)} %get-tuple-element.39), channel_id=1, source_target_pairs={{0,4},{4,8},{8,12},{12,0},{1,5},{5,9},{9,13},{13,1},{2,6},{6,10},{... | collective-permute-start | bytes 4718600 | tf_op jit(solution)/shard_map/ppermute | solution.py:36
  26.8 19.8 %collective-permute-start.7 = (bf16[3,4,4,128,128]{4,3,2,1,0:T(8,128)(2,1)}, bf16[3,4,4,128,128]{4,3,2,1,0:T(8,128)(2,1)S(1)}, u32[]{:S(2)}, u32[]{:S(2)}) collective-permute-start(bf16[3,4,4,128,128]{4,3,2,1,0:T(8,128)(2,1)} %get-tuple-element.40), channel_id=1, source_target_pairs={{0,12},{4,0},{8,4},{12,8},{1,13},{5,1},{9,5},{13,9},{2,14},{6,2},{... | collective-permute-start | bytes 4718600 | tf_op jit(solution)/shard_map/ppermute | solution.py:36
  30.9 7.5 %collective-permute-start.4 = (bf16[1040,128]{1,0:T(8,128)(2,1)S(1)}, bf16[1040,128]{1,0:T(8,128)(2,1)S(1)}, u32[]{:S(2)}, u32[]{:S(2)}) collective-permute-start(bf16[1040,128]{1,0:T(8,128)(2,1)S(1)} %slice.20), channel_id=1, source_target_pairs={{0,32},{32,64},{64,96},{96,0},{1,33},{33,65},{65,97},{97,1},{2,34}... | collective-permute-start | bytes 798728 | tf_op jit(solution)/shard_map/ppermute | solution.py:48
  32.1 6.4 %collective-permute-start.5 = (bf16[1040,128]{1,0:T(8,128)(2,1)S(1)}, bf16[1040,128]{1,0:T(8,128)(2,1)S(1)}, u32[]{:S(2)}, u32[]{:S(2)}) collective-permute-start(bf16[1040,128]{1,0:T(8,128)(2,1)S(1)} %slice.21), channel_id=1, source_target_pairs={{0,96},{32,0},{64,32},{96,64},{1,97},{33,1},{65,33},{97,65},{2,98}... | collective-permute-start | bytes 798728 | tf_op jit(solution)/shard_map/ppermute | solution.py:48
  35.8 13.5 %copy-start.2 = (bf16[2,4,4,128,128]{4,3,2,1,0:T(8,128)(2,1)S(1)}, bf16[2,4,4,128,128]{4,3,2,1,0:T(8,128)(2,1)}, u32[]{:S(2)}) copy-start(bf16[2,4,4,128,128]{4,3,2,1,0:T(8,128)(2,1)} %copy-done.1) | copy-start | bytes 3145732
  35.8 22.2 %collective-permute-start.8 = (bf16[4160,128]{1,0:T(8,128)(2,1)S(1)}, bf16[4160,128]{1,0:T(8,128)(2,1)S(1)}, u32[]{:S(2)}, u32[]{:S(2)}) collective-permute-start(bf16[4160,128]{1,0:T(8,128)(2,1)S(1)} %constant_dynamic-update-slice_fusion.refs_3_), channel_id=1, source_target_pairs={{0,4},{4,8},{8,12},{12,0},{1,5},{5,9},{9,13},{13,1},{2,6},{6,10},{... | collective-permute-start | bytes 3194888 | tf_op jit(solution)/shard_map/ppermute | solution.py:36
  38.5 22.1 %collective-permute-start.9 = (bf16[4160,128]{1,0:T(8,128)(2,1)S(1)}, bf16[4160,128]{1,0:T(8,128)(2,1)S(1)}, u32[]{:S(2)}, u32[]{:S(2)}) collective-permute-start(bf16[4160,128]{1,0:T(8,128)(2,1)S(1)} %constant_dynamic-update-slice_fusion.2.refs_4_), channel_id=1, source_target_pairs={{0,12},{4,0},{8,4},{12,8},{1,13},{5,1},{9,5},{13,9},{2,14},{6,2},{... | collective-permute-start | bytes 3194888 | tf_op jit(solution)/shard_map/ppermute | solution.py:36
  46.6 22.8 %collective-permute-start.10 = (bf16[4160,128]{1,0:T(8,128)(2,1)S(1)}, bf16[4160,128]{1,0:T(8,128)(2,1)S(1)}, u32[]{:S(2)}, u32[]{:S(2)}) collective-permute-start(bf16[4160,128]{1,0:T(8,128)(2,1)S(1)} %constant_dynamic-update-slice_fusion.2.refs_4_), channel_id=1, source_target_pairs={{0,4},{4,8},{8,12},{12,0},{1,5},{5,9},{9,13},{13,1},{2,6},{6,10},{... | collective-permute-start | bytes 3194888 | tf_op jit(solution)/shard_map/ppermute | solution.py:36
  47.9 23.0 %collective-permute-start.11 = (bf16[4160,128]{1,0:T(8,128)(2,1)S(1)}, bf16[4160,128]{1,0:T(8,128)(2,1)S(1)}, u32[]{:S(2)}, u32[]{:S(2)}) collective-permute-start(bf16[4160,128]{1,0:T(8,128)(2,1)S(1)} %constant_dynamic-update-slice_fusion.refs_3_), channel_id=1, source_target_pairs={{0,12},{4,0},{8,4},{12,8},{1,13},{5,1},{9,5},{13,9},{2,14},{6,2},{... | collective-permute-start | bytes 3194888 | tf_op jit(solution)/shard_map/ppermute | solution.py:36
  57.7 27.8 %collective-permute-start.12 = (bf16[1,4,4,128,128]{4,3,2,1,0:T(8,128)(2,1)S(1)}, bf16[1,4,4,128,128]{4,3,2,1,0:T(8,128)(2,1)S(1)}, u32[]{:S(2)}, u32[]{:S(2)}) collective-permute-start(bf16[1,4,4,128,128]{4,3,2,1,0:T(8,128)(2,1)S(1)} %slice.22), channel_id=1, source_target_pairs={{0,4},{4,8},{8,12},{12,0},{1,5},{5,9},{9,13},{13,1},{2,6},{6,10},{... | collective-permute-start | bytes 1572872 | tf_op jit(solution)/shard_map/ppermute | solution.py:36
  58.0 27.4 %collective-permute-start.13 = (bf16[1,4,4,128,128]{4,3,2,1,0:T(8,128)(2,1)S(1)}, bf16[1,4,4,128,128]{4,3,2,1,0:T(8,128)(2,1)S(1)}, u32[]{:S(2)}, u32[]{:S(2)}) collective-permute-start(bf16[1,4,4,128,128]{4,3,2,1,0:T(8,128)(2,1)S(1)} %slice.23), channel_id=1, source_target_pairs={{0,12},{4,0},{8,4},{12,8},{1,13},{5,1},{9,5},{13,9},{2,14},{6,2},{... | collective-permute-start | bytes 1572872 | tf_op jit(solution)/shard_map/ppermute | solution.py:36
  60.5 25.9 %collective-permute-start.14 = (bf16[4160,128]{1,0:T(8,128)(2,1)S(1)}, bf16[4160,128]{1,0:T(8,128)(2,1)S(1)}, u32[]{:S(2)}, u32[]{:S(2)}) collective-permute-start(bf16[4160,128]{1,0:T(8,128)(2,1)S(1)} %collective-permute-done.8.refs_5_), channel_id=1, source_target_pairs={{0,4},{4,8},{8,12},{12,0},{1,5},{5,9},{9,13},{13,1},{2,6},{6,10},{... | collective-permute-start | bytes 3194888 | tf_op jit(solution)/shard_map/ppermute | solution.py:36
  69.4 17.1 %collective-permute-start.15 = (bf16[4160,128]{1,0:T(8,128)(2,1)S(1)}, bf16[4160,128]{1,0:T(8,128)(2,1)S(1)}, u32[]{:S(2)}, u32[]{:S(2)}) collective-permute-start(bf16[4160,128]{1,0:T(8,128)(2,1)S(1)} %collective-permute-done.9.refs_8_), channel_id=1, source_target_pairs={{0,12},{4,0},{8,4},{12,8},{1,13},{5,1},{9,5},{13,9},{2,14},{6,2},{... | collective-permute-start | bytes 3194888 | tf_op jit(solution)/shard_map/ppermute | solution.py:36
  89.9 10.9 %collective-permute-start.18 = (s16[4,33,16,128]{3,2,1,0:T(8,128)(2,1)S(1)}, s16[4,33,16,128]{3,2,1,0:T(8,128)(2,1)S(1)}, u32[]{:S(2)}, u32[]{:S(2)}) collective-permute-start(s16[4,33,16,128]{3,2,1,0:T(8,128)(2,1)S(1)} %get-tuple-element.55), channel_id=1, source_target_pairs={{0,1},{1,2},{2,3},{3,0},{4,5},{5,6},{6,7},{7,4},{8,9},{9,10},{10,1... | collective-permute-start | bytes 1622024 | tf_op jit(solution)/shard_map/ppermute | solution.py:36
  91.6 9.2 %collective-permute-start.19 = (s16[4,33,16,128]{3,2,1,0:T(8,128)(2,1)S(1)}, s16[4,33,16,128]{3,2,1,0:T(8,128)(2,1)S(1)}, u32[]{:S(2)}, u32[]{:S(2)}) collective-permute-start(s16[4,33,16,128]{3,2,1,0:T(8,128)(2,1)S(1)} %get-tuple-element.56), channel_id=1, source_target_pairs={{0,3},{1,0},{2,1},{3,2},{4,7},{5,4},{6,5},{7,6},{8,11},{9,8},{10,9... | collective-permute-start | bytes 1622024 | tf_op jit(solution)/shard_map/ppermute | solution.py:36
  97.3 10.2 %collective-permute-start.16 = (s16[4,33,16,128]{3,2,1,0:T(8,128)(2,1)S(1)}, s16[4,33,16,128]{3,2,1,0:T(8,128)(2,1)S(1)}, u32[]{:S(2)}, u32[]{:S(2)}) collective-permute-start(s16[4,33,16,128]{3,2,1,0:T(8,128)(2,1)S(1)} %get-tuple-element.53), channel_id=1, source_target_pairs={{0,3},{1,0},{2,1},{3,2},{4,7},{5,4},{6,5},{7,6},{8,11},{9,8},{10,9... | collective-permute-start | bytes 1622024 | tf_op jit(solution)/shard_map/ppermute | solution.py:36
  98.7 9.7 %collective-permute-start.17 = (s16[4,33,16,128]{3,2,1,0:T(8,128)(2,1)S(1)}, s16[4,33,16,128]{3,2,1,0:T(8,128)(2,1)S(1)}, u32[]{:S(2)}, u32[]{:S(2)}) collective-permute-start(s16[4,33,16,128]{3,2,1,0:T(8,128)(2,1)S(1)} %get-tuple-element.54), channel_id=1, source_target_pairs={{0,1},{1,2},{2,3},{3,0},{4,5},{5,6},{6,7},{7,4},{8,9},{9,10},{10,1... | collective-permute-start | bytes 1622024 | tf_op jit(solution)/shard_map/ppermute | solution.py:36
  104.5 9.9 %collective-permute-start.20 = (s16[4,33,16,128]{3,2,1,0:T(8,128)(2,1)S(1)}, s16[4,33,16,128]{3,2,1,0:T(8,128)(2,1)S(1)}, u32[]{:S(2)}, u32[]{:S(2)}) collective-permute-start(s16[4,33,16,128]{3,2,1,0:T(8,128)(2,1)S(1)} %get-tuple-element.57), channel_id=1, source_target_pairs={{0,1},{1,2},{2,3},{3,0},{4,5},{5,6},{6,7},{7,4},{8,9},{9,10},{10,1... | collective-permute-start | bytes 1622024 | tf_op jit(solution)/shard_map/ppermute | solution.py:36
  105.6 8.8 %collective-permute-start.21 = (s16[4,33,16,128]{3,2,1,0:T(8,128)(2,1)S(1)}, s16[4,33,16,128]{3,2,1,0:T(8,128)(2,1)S(1)}, u32[]{:S(2)}, u32[]{:S(2)}) collective-permute-start(s16[4,33,16,128]{3,2,1,0:T(8,128)(2,1)S(1)} %get-tuple-element.58), channel_id=1, source_target_pairs={{0,3},{1,0},{2,1},{3,2},{4,7},{5,4},{6,5},{7,6},{8,11},{9,8},{10,9... | collective-permute-start | bytes 1622024 | tf_op jit(solution)/shard_map/ppermute | solution.py:36
